TPU v7x, 512 devices: a whole 4x4x16 slice. The times are simulated.
512 devices in a mesh: row: 8 (over x_hi, y), col: 32 (over x_lo, z), head: 2 (over core).
Axes of the slice: x: 4 (x_hi: 2, x_lo: 2; x = x_hi * 2 + x_lo), y: 4, z: 16, core: 2. Of those that a mesh axis runs over, the one named last changes fastest.
Arguments:
- pair: bfloat16 [32, 4096, 128], P('row', 'col'), may hold values from -6 to 6
- layer_norm_gain: float32 [128], replicated, may hold values from 0.1 to 1.9
- w_proj: bfloat16 [128, 512], P(None, 'head'), may hold values from -0.5 to 0.5
- w_out: bfloat16 [128, 128], P('head'), may hold values from -0.5 to 0.5
- tri_bias: bfloat16 [4, 4096, 4096], P('head', 'col', 'row'), may hold values from -6 to 300
- active: int32 [16, 16], replicated, may hold values from 0 to 1, as said below
- d_out: bfloat16 [32, 4096, 128], P('row', 'col'), may hold values from -6 to 6
Outputs:
- out: bfloat16 [32, 4096, 128], P('row', 'col', 'head')
- pair_gradient: bfloat16 [32, 4096, 128], P('row', 'col')
Inputs may be any that keep to these rules, and one draw needn't show every extreme that they name: Entry [a, b] is 1 where key tile b is computed for query tile a; the table is symmetric and every tile is active with itself.
All inputs are finite; a program needn't handle non-finite values.
Results may differ from a plain program's by a relative error of at most 0.02.
Values may be sent and summed in bfloat16 or wider, within the bound.
No kernel may reach another device: no remote copies, remote signals or barrier semaphores. Data moves between devices by JAX's collectives and lax.ppermute only.
A program may use at most 64 MiB of HBM per device.

v0:
```python
import math

import jax
import jax.numpy as jnp
from jax import lax
from jax.sharding import PartitionSpec as P

DH = 32
TILE = 256


EPS = 1e-05
NEG = -1e30


def tile_onehot(first, count, tiles_total):
    index = (first + jnp.arange(count, dtype=jnp.int32)) // TILE
    return (index[:, None] == jnp.arange(tiles_total, dtype=jnp.int32)[None, :]).astype(jnp.float32)


def per_device(pair, layer_norm_gain, w_proj, w_out, tri_bias, active, d_out):
    rows, cols, width = pair.shape
    heads = w_out.shape[0] // DH
    scale = DH ** (-0.5)
    tiles_total = active.shape[0]
    x = pair.astype(jnp.float32)
    channel_average = jnp.mean(x, axis=-1, keepdims=True)
    centered_input = x - channel_average
    inverse_deviation = lax.rsqrt(
        jnp.mean(centered_input * centered_input, axis=-1, keepdims=True) + EPS
    )
    standardized_input = centered_input * inverse_deviation
    normalized_pair = (standardized_input * layer_norm_gain).astype(jnp.bfloat16)
    proj = jnp.einsum("rjc,cf->rjf", normalized_pair, w_proj, preferred_element_type=jnp.float32)
    proj = proj.reshape(rows, cols, heads, 4, DH)
    query = (proj[:, :, :, 0] * scale).astype(jnp.bfloat16)
    kv_local = proj[:, :, :, 1:3].astype(jnp.bfloat16).reshape(rows, cols, heads * 2 * DH)
    gate = jax.nn.sigmoid(proj[:, :, :, 3])
    col_start = lax.axis_index("col") * cols
    row_active = jnp.dot(tile_onehot(col_start, cols, tiles_total), active.astype(jnp.float32))
    gathered = lax.all_gather(kv_local, "col", axis=1, tiled=True)

    def block_parts(keys_values, piece, offset, first, step):
        bias_blk = lax.dynamic_slice_in_dim(piece, offset, step, 2)
        kv_blk = lax.dynamic_slice_in_dim(keys_values, first, step, 1).reshape(
            rows, step, heads, 2, DH
        )
        mask = jnp.dot(row_active, tile_onehot(first, step, tiles_total).T) > 0.5
        return (bias_blk, kv_blk[:, :, :, 0], kv_blk[:, :, :, 1], mask)

    def scores(key_blk, bias_blk, mask):
        score = jnp.einsum("rjhd,rkhd->rhjk", query, key_blk, preferred_element_type=jnp.float32)
        score = score + bias_blk[None].astype(jnp.float32)
        return jnp.where(mask[None, None], score, NEG)

    start_state = (
        jnp.full((rows, heads, cols), NEG, jnp.float32),
        jnp.zeros((rows, heads, cols), jnp.float32),
        jnp.zeros((rows, heads, cols, DH), jnp.float32),
    )
    piece = lax.all_gather(tri_bias, "row", axis=2, tiled=True)
    length = piece.shape[2]
    step = math.gcd(length, 2 * TILE)

    def forward_one_block(number, inner):
        offset = number * step
        bias_blk, key_blk, value_blk, mask = block_parts(gathered, piece, offset, offset, step)

        def forward_update(carry):
            run_max, run_sum, acc = carry
            score = scores(key_blk, bias_blk, mask)
            new_max = jnp.maximum(run_max, jnp.max(score, axis=-1))
            weights = jnp.where(mask[None, None], jnp.exp(score - new_max[..., None]), 0.0)
            factor = jnp.exp(run_max - new_max)
            run_sum = run_sum * factor + jnp.sum(weights, axis=-1)
            acc = acc * factor[..., None] + jnp.einsum(
                "rhjk,rkhd->rhjd",
                weights.astype(jnp.bfloat16),
                value_blk,
                preferred_element_type=jnp.float32,
            )
            return (new_max, run_sum, acc)

        return lax.cond(jnp.any(mask), forward_update, lambda carry: carry, inner)

    run_max, run_sum, acc = lax.fori_loop(0, length // step, forward_one_block, start_state)
    lse = run_max + jnp.log(run_sum)
    attended = jnp.transpose(acc / run_sum[..., None], (0, 2, 1, 3))
    gated = (gate * attended).astype(jnp.bfloat16).reshape(rows, cols, heads * DH)
    partial_out = jnp.einsum("rjf,fc->rjc", gated, w_out, preferred_element_type=jnp.float32)
    out = lax.psum_scatter(
        partial_out.astype(jnp.bfloat16), "head", scatter_dimension=2, tiled=True
    )
    d_go = jnp.einsum("rjc,fc->rjf", d_out, w_out, preferred_element_type=jnp.float32).reshape(
        rows, cols, heads, DH
    )
    d_o = d_go * gate
    delta = jnp.transpose(jnp.sum(d_o * attended, axis=-1), (0, 2, 1))
    grad_out = d_o.astype(jnp.bfloat16)
    d_gate = d_go * attended * gate * (1.0 - gate)
    gathered_back = lax.all_gather(kv_local, "col", axis=1, tiled=True)

    def backward_piece(state, piece):
        length = piece.shape[2]
        step = math.gcd(length, 2 * TILE)

        def backward_one_block(number, inner):
            offset = number * step
            first = offset
            bias_blk, key_blk, value_blk, mask = block_parts(
                gathered_back, piece, offset, first, step
            )

            def backward_update(carry):
                dq_acc, dkv_acc = carry
                score = scores(key_blk, bias_blk, mask)
                prob = jnp.where(mask[None, None], jnp.exp(score - lse[..., None]), 0.0)
                d_value = jnp.einsum(
                    "rhjk,rjhd->rkhd",
                    prob.astype(jnp.bfloat16),
                    grad_out,
                    preferred_element_type=jnp.float32,
                )
                d_prob = jnp.einsum(
                    "rjhd,rkhd->rhjk", grad_out, value_blk, preferred_element_type=jnp.float32
                )
                d_score = (prob * (d_prob - delta[..., None])).astype(jnp.bfloat16)
                dq_acc = dq_acc + jnp.einsum(
                    "rhjk,rkhd->rhjd", d_score, key_blk, preferred_element_type=jnp.float32
                )
                d_key = jnp.einsum(
                    "rhjk,rjhd->rkhd", d_score, query, preferred_element_type=jnp.float32
                )
                both = jnp.stack([d_key, d_value], axis=3).reshape(rows, step, heads * 2 * DH)
                current = lax.dynamic_slice_in_dim(dkv_acc, first, step, 1)
                dkv_acc = lax.dynamic_update_slice_in_dim(dkv_acc, current + both, first, 1)
                return (dq_acc, dkv_acc)

            return lax.cond(jnp.any(mask), backward_update, lambda carry: carry, inner)

        return lax.fori_loop(0, length // step, backward_one_block, state)

    back_state = (
        jnp.zeros((rows, heads, cols, DH), jnp.float32),
        jnp.zeros(gathered_back.shape, jnp.float32),
    )
    dq_acc, dkv_acc = backward_piece(
        back_state, lax.all_gather(tri_bias, "row", axis=2, tiled=True)
    )
    dkv_own = lax.psum_scatter(
        dkv_acc.astype(jnp.bfloat16), "col", scatter_dimension=1, tiled=True
    ).astype(jnp.float32)
    dkv_own = dkv_own.reshape(rows, cols, heads, 2, DH)
    d_query = jnp.transpose(dq_acc, (0, 2, 1, 3)) * scale
    d_proj = jnp.stack([d_query, dkv_own[:, :, :, 0], dkv_own[:, :, :, 1], d_gate], axis=3)
    d_proj = d_proj.astype(jnp.bfloat16).reshape(rows, cols, heads * 4 * DH)
    d_norm = jnp.einsum("rjf,cf->rjc", d_proj, w_proj, preferred_element_type=jnp.float32)
    d_norm = lax.psum(d_norm.astype(jnp.bfloat16), "head").astype(jnp.float32)
    input_gradient = d_norm * layer_norm_gain
    pair_gradient = inverse_deviation * (
        input_gradient
        - jnp.mean(input_gradient, axis=-1, keepdims=True)
        - standardized_input * jnp.mean(input_gradient * standardized_input, axis=-1, keepdims=True)
    )
    pair_gradient = pair_gradient.astype(jnp.bfloat16)
    return (out, pair_gradient)


def solution(mesh):
    in_specs = (
        P("row", "col", None),
        P(),
        P(None, "head"),
        P("head", None),
        P("head", "col", "row"),
        P(),
        P("row", "col", None),
    )
    out_specs = (P("row", "col", "head"), P("row", "col", None))
    return jax.shard_map(
        per_device, mesh=mesh, in_specs=in_specs, out_specs=out_specs, check_vma=False
    )
```

profile of v0, /device:TPU:1, one launch (start us, length us, event | category | flops | bytes accessed | tf_op | source)
XLA Modules:
  0.0 569.7 jit_solution(15667866155526611855)
XLA Ops:
  13.9 71.6 %all-gather.5.cloned.1.call-done = bf16[2,128,4096]{1,2,0:T(8,128)(2,1)} async-done(((bf16[2,128,512]{1,2,0:T(8,128)(2,1)}), bf16[2,128,4096]{1,2,0:T(8,128)(2,1)}) %all-gather.5.cloned.1.call-update) | async-done | bytes 2097168 | tf_op jit(solution)/shard_map/all_gather | solution.py:61
  85.5 123.1 %all-gather.3.cloned.1.call-done = bf16[4,4096,128]{1,2,0:T(8,128)(2,1)} async-done(((bf16[4,128,128]{1,2,0:T(8,128)(2,1)}), bf16[4,4096,128]{1,2,0:T(8,128)(2,1)}) %all-gather.3.cloned.1.call-update) | async-done | bytes 4194320 | tf_op jit(solution)/shard_map/all_gather | solution.py:41
  208.6 44.3 %while.36 = (s32[]{:T(128)}, f32[4,2,128]{2,1,0:T(2,128)S(1)}, f32[4,2,128]{2,1,0:T(2,128)S(1)}, f32[4,2,128,32]{2,3,1,0:T(8,128)S(1)}, bf16[128,16]{0,1:T(8,128...) while((s32[]{:T(128)}, f32[4,2,128]{2,1,0:T(2,128)S(1)}, ...), condition=%wide.region_8.9_spmd, body=%wide.region_2.8_spmd.sunk | while | flops 76367872 | bytes 10887453 | solution.py:86
  210.1 4.1 conditional.4
  215.6 4.1 conditional.4
  221.2 4.1 conditional.4
  226.7 4.1 conditional.4
  237.8 4.1 conditional.4
  253.1 4.2 broadcast_in_dim.98
  257.3 70.4 %while.37 = (s32[]{:T(128)}, f32[4,2,128,32]{2,3,1,0:T(8,128)S(1)}, f32[4,4096,128]{1,2,0:T(8,128)}, bf16[128,16]{0,1:T(8,128)(2,1)S(1)}, bf16[4,4096,128]{1,2,0...) while((s32[]{:T(128)}, f32[4,2,128,32]{2,3,1,0:T(8,128)S(1)}, ...), condition=%wide.region_15.16_spmd, body=%wide.region_11.15_spmd.sunk | while | flops 174899200 | bytes 21643568 | solution.py:141
  258.9 7.3 %conditional.5 = ((f32[4,2,128,32]{2,3,1,0:T(8,128)S(1)}, f32[4,4096,128]{1,2,0:T(8,128)})) conditional(s32[]{:T(128)} %convert_element_type.174, (f32[4,2,128,32]{2,3,1,0:T(8,128)S(1)}, f32[4,4096,128]{1,2,0:T(8,128)}) %tuple.125, (pred[128,512]{0,1:T(8,128)(4,1)S(1)}, s32[]{:T(128)}, bf16[4,4096,128]{1,2,0:T(8,128)(2,1)}, ...), branch_computations={%region_13.13_spmd, %region_14.14_spmd} | conditional | flops 172654592 | bytes 21569606 | solution.py:139
  267.7 7.2 %conditional.5 = ((f32[4,2,128,32]{2,3,1,0:T(8,128)S(1)}, f32[4,4096,128]{1,2,0:T(8,128)})) conditional(s32[]{:T(128)} %convert_element_type.174, (f32[4,2,128,32]{2,3,1,0:T(8,128)S(1)}, f32[4,4096,128]{1,2,0:T(8,128)}) %tuple.125, (pred[128,512]{0,1:T(8,128)(4,1)S(1)}, s32[]{:T(128)}, bf16[4,4096,128]{1,2,0:T(8,128)(2,1)}, ...), branch_computations={%region_13.13_spmd, %region_14.14_spmd} | conditional | flops 172654592 | bytes 21569606 | solution.py:139
  276.5 7.2 %conditional.5 = ((f32[4,2,128,32]{2,3,1,0:T(8,128)S(1)}, f32[4,4096,128]{1,2,0:T(8,128)})) conditional(s32[]{:T(128)} %convert_element_type.174, (f32[4,2,128,32]{2,3,1,0:T(8,128)S(1)}, f32[4,4096,128]{1,2,0:T(8,128)}) %tuple.125, (pred[128,512]{0,1:T(8,128)(4,1)S(1)}, s32[]{:T(128)}, bf16[4,4096,128]{1,2,0:T(8,128)(2,1)}, ...), branch_computations={%region_13.13_spmd, %region_14.14_spmd} | conditional | flops 172654592 | bytes 21569606 | solution.py:139
  285.3 7.3 %conditional.5 = ((f32[4,2,128,32]{2,3,1,0:T(8,128)S(1)}, f32[4,4096,128]{1,2,0:T(8,128)})) conditional(s32[]{:T(128)} %convert_element_type.174, (f32[4,2,128,32]{2,3,1,0:T(8,128)S(1)}, f32[4,4096,128]{1,2,0:T(8,128)}) %tuple.125, (pred[128,512]{0,1:T(8,128)(4,1)S(1)}, s32[]{:T(128)}, bf16[4,4096,128]{1,2,0:T(8,128)(2,1)}, ...), branch_computations={%region_13.13_spmd, %region_14.14_spmd} | conditional | flops 172654592 | bytes 21569606 | solution.py:139
  294.1 7.2 %conditional.5 = ((f32[4,2,128,32]{2,3,1,0:T(8,128)S(1)}, f32[4,4096,128]{1,2,0:T(8,128)})) conditional(s32[]{:T(128)} %convert_element_type.174, (f32[4,2,128,32]{2,3,1,0:T(8,128)S(1)}, f32[4,4096,128]{1,2,0:T(8,128)}) %tuple.125, (pred[128,512]{0,1:T(8,128)(4,1)S(1)}, s32[]{:T(128)}, bf16[4,4096,128]{1,2,0:T(8,128)(2,1)}, ...), branch_computations={%region_13.13_spmd, %region_14.14_spmd} | conditional | flops 172654592 | bytes 21569606 | solution.py:139
  302.8 7.2 %conditional.5 = ((f32[4,2,128,32]{2,3,1,0:T(8,128)S(1)}, f32[4,4096,128]{1,2,0:T(8,128)})) conditional(s32[]{:T(128)} %convert_element_type.174, (f32[4,2,128,32]{2,3,1,0:T(8,128)S(1)}, f32[4,4096,128]{1,2,0:T(8,128)}) %tuple.125, (pred[128,512]{0,1:T(8,128)(4,1)S(1)}, s32[]{:T(128)}, bf16[4,4096,128]{1,2,0:T(8,128)(2,1)}, ...), branch_computations={%region_13.13_spmd, %region_14.14_spmd} | conditional | flops 172654592 | bytes 21569606 | solution.py:139
  311.6 7.2 %conditional.5 = ((f32[4,2,128,32]{2,3,1,0:T(8,128)S(1)}, f32[4,4096,128]{1,2,0:T(8,128)})) conditional(s32[]{:T(128)} %convert_element_type.174, (f32[4,2,128,32]{2,3,1,0:T(8,128)S(1)}, f32[4,4096,128]{1,2,0:T(8,128)}) %tuple.125, (pred[128,512]{0,1:T(8,128)(4,1)S(1)}, s32[]{:T(128)}, bf16[4,4096,128]{1,2,0:T(8,128)(2,1)}, ...), branch_computations={%region_13.13_spmd, %region_14.14_spmd} | conditional | flops 172654592 | bytes 21569606 | solution.py:139
  320.4 7.3 %conditional.5 = ((f32[4,2,128,32]{2,3,1,0:T(8,128)S(1)}, f32[4,4096,128]{1,2,0:T(8,128)})) conditional(s32[]{:T(128)} %convert_element_type.174, (f32[4,2,128,32]{2,3,1,0:T(8,128)S(1)}, f32[4,4096,128]{1,2,0:T(8,128)}) %tuple.125, (pred[128,512]{0,1:T(8,128)(4,1)S(1)}, s32[]{:T(128)}, bf16[4,4096,128]{1,2,0:T(8,128)(2,1)}, ...), branch_computations={%region_13.13_spmd, %region_14.14_spmd} | conditional | flops 172654592 | bytes 21569606 | solution.py:139
  327.7 6.0 %convert_element_type.115 = bf16[4,4096,128]{1,2,0:T(8,128)(2,1)} convert(f32[4,4096,128]{1,2,0:T(8,128)} %get-tuple-element.755) | non-fusion elementwise | flops 2097152 | bytes 12582912 | tf_op jit(solution)/shard_map/convert_element_type | solution.py:151
  333.7 7.5 %copy.50 = bf16[4,4096,128]{2,0,1:T(4,128)(2,1)} copy(bf16[4,4096,128]{1,2,0:T(8,128)(2,1)} %convert_element_type.115) | data formatting | bytes 8388608
  341.2 4.9 copy.58
  346.2 138.4 %reduce-scatter.7.cloned.1.call-done = bf16[128,512]{1,0:T(8,128)(2,1)} async-done(((bf16[4096,512]{1,0:T(8,128)(2,1)}), bf16[128,512]{1,0:T(8,128)(2,1)}) %reduce-scatter.7.cloned.1.call-update) | async-done | bytes 131088
  487.6 53.1 %all-reduce.2.cloned.1.call-done = bf16[4,128,128]{2,1,0:T(8,128)(2,1)} async-done(((bf16[4,128,128]{2,1,0:T(8,128)(2,1)}), bf16[4,128,128]{2,1,0:T(8,128)(2,1)}) %all-reduce.2.cloned.1.call-update) | async-done | bytes 131088 | tf_op jit(solution)/shard_map/psum | solution.py:158
  543.9 19.3 %reduce-scatter.5.cloned.1.call-done = bf16[4,128,64]{1,2,0:T(8,128)(2,1)} async-done(((bf16[4,128,128]{1,2,0:T(8,128)(2,1)}), bf16[4,128,64]{1,2,0:T(8,128)(2,1)}) %reduce-scatter.5.cloned.1.call-update) | async-done | bytes 65552 | tf_op jit(solution)/shard_map/reduce_scatter | solution.py:91
  (227 shorter events, 129.0 us)
Async XLA Ops:
  7.2 6.5 %copy-start = (bf16[4,128,128]{2,1,0:T(8,128)(2,1)S(1)}, bf16[4,128,128]{2,1,0:T(8,128)(2,1)}, u32[]{:S(2)}) copy-start(bf16[4,128,128]{2,1,0:T(8,128)(2,1)} %param.21) | copy-start | bytes 393220
  7.2 6.3 %copy-start.5 = (s32[16,16]{1,0:T(8,128)S(1)}, s32[16,16]{1,0:T(8,128)}, u32[]{:S(2)}) copy-start(s32[16,16]{1,0:T(8,128)} %param.20) | copy-start | bytes 3076
  7.2 6.5 %copy-start.3 = (bf16[64,128]{1,0:T(8,128)(2,1)S(1)}, bf16[64,128]{1,0:T(8,128)(2,1)}, u32[]{:S(2)}) copy-start(bf16[64,128]{1,0:T(8,128)(2,1)} %param.18) | copy-start | bytes 49156
  7.2 78.3 %all-gather.5.cloned.1.call-start = ((), (), s32[]{:S(2)}) async-start(), calls=%async_computation.3 | async-start | bytes 2359296 | tf_op jit(solution)/shard_map/all_gather | solution.py:61
  9.1 199.5 %all-gather.3.cloned.1.call-start = ((), (), s32[]{:S(2)}) async-start(), calls=%async_computation.2 | async-start | bytes 4325376 | tf_op jit(solution)/shard_map/all_gather | solution.py:41
  13.4 471.2 %reduce-scatter.7.cloned.1.call-start = ((), (), s32[]{:S(2)}) async-start(), calls=%async_computation.6 | async-start | bytes 4325376
  346.0 139.7 %copy-start.2 = (bf16[128,256]{1,0:T(8,128)(2,1)S(1)}, bf16[128,256]{1,0:T(8,128)(2,1)}, u32[]{:S(2)}) copy-start(bf16[128,256]{1,0:T(8,128)(2,1)} %param.17) | copy-start | bytes 196612
  346.1 194.7 %copy-start.1 = (bf16[4,128,128]{2,1,0:T(8,128)(2,1)S(1)}, bf16[4,128,128]{2,1,0:T(8,128)(2,1)}, u32[]{:S(2)}) copy-start(bf16[4,128,128]{2,1,0:T(8,128)(2,1)} %param.15) | copy-start | bytes 393220
  346.1 194.6 %copy-start.4 = (f32[128]{0:T(128)S(1)}, f32[128]{0:T(128)}, u32[]{:S(2)}) copy-start(f32[128]{0:T(128)} %param.16) | copy-start | bytes 1540
  346.1 194.6 %all-reduce.2.cloned.1.call-start = ((), (), s32[]{:S(2)}) async-start(), calls=%async_computation.5 | async-start | bytes 262144 | tf_op jit(solution)/shard_map/psum | solution.py:158
  486.7 76.5 %reduce-scatter.5.cloned.1.call-start = ((), (), s32[]{:S(2)}) async-start(), calls=%async_computation.4 | async-start | bytes 196608 | tf_op jit(solution)/shard_map/reduce_scatter | solution.py:91
Sparse Core Ops, SparseCore 0:
  11.2 74.2 all-gather.4
  88.0 120.4 all-gather.2
  346.2 138.3 reduce-scatter.6
  487.9 52.8 all-reduce.1
  543.9 19.2 reduce-scatter.4
where the time goes:
time: 572 us; the launch traced here: 570 us
  waiting for transfers between devices  406 us (71%)
  other arithmetic  51.8 us (9%)
  matrix products  49.1 us (9%)
  local copies, waits for them, and re-layouts  38.2 us (7%)
  between operations  14 us (2%)
  loops' own time  10.8 us (2%)
    unnamed x6, waiting for transfers between devices  139 us
    all_gather x1, waiting for transfers between devices, per_device(): gathered = lax.all_gather(kv_local, 'col', axis=1, tiled=True)  123 us
    all_gather x1, waiting for transfers between devices, per_device(): piece = lax.all_gather(tri_bias, 'row', axis=2, tiled=True)  71.6 us
    psum x1, waiting for transfers between devices, per_device(): d_norm = lax.psum(d_norm.astype(jnp.bfloat16), 'head').astype(jnp.float32)  53.1 us
    reduce_scatter x1, waiting for transfers between devices, per_device(): lax.psum_scatter(partial_out.astype(jnp.bfloat16), 'head', scatter_dimens...  19.3 us
    dynamic_update_slice x8, other arithmetic, backward_update(): dkv_acc = lax.dynamic_update_slice_in_dim(dkv_acc, current + both, first, 1)  19.1 us
    dynamic_slice x16, local copies, waits for them, and re-layouts, block_parts(): lax.dynamic_slice_in_dim(keys_values, first, step, 1)  17.3 us
    convert_element_type x16, other arithmetic, scores(): score = score + bias_blk[None].astype(jnp.float32)  15.9 us
  transfers between devices with their start and end apart: 5, of which 5 were waited for; matrix products, arithmetic and copies ran while one was open for 2% of the time, Pallas kernels for 0%

commit v1 on v0

v1 whole, which is shorter than its diff:
```python
import functools

import jax
import jax.numpy as jnp
import numpy as np
from jax import lax
from jax.experimental import pallas as pl
from jax.experimental.pallas import tpu as pltpu
from jax.sharding import Mesh
from jax.sharding import PartitionSpec as P

DH = 32
SCALE = DH ** (-0.5)
EPS = 1e-05
NEG = -1e30
F32 = jnp.float32
BF16 = jnp.bfloat16
SWAP = [(0, 1), (1, 0)]


def vmem():
    return pl.BlockSpec(memory_space=pltpu.VMEM)


def smem():
    return pl.BlockSpec(memory_space=pltpu.SMEM)


def shapes(*items):
    return [jax.ShapeDtypeStruct(s, d) for s, d in items]


def call(kernel, outs, n_smem, n_vmem, scratch=(), flops=0, nbytes=0):
    return pl.pallas_call(
        kernel,
        out_shape=shapes(*outs),
        in_specs=[smem()] * n_smem + [vmem()] * n_vmem,
        out_specs=[vmem()] * len(outs),
        scratch_shapes=list(scratch),
        compiler_params=pltpu.CompilerParams(vmem_limit_bytes=48 * 1024 * 1024),
        cost_estimate=pl.CostEstimate(flops=flops, bytes_accessed=nbytes, transcendentals=0),
    )


def nt(a, b):
    return lax.dot_general(a, b, (((1,), (1,)), ((), ())), preferred_element_type=F32)


def nn(a, b):
    return jnp.dot(a, b, preferred_element_type=F32)


def bias_kernel(ids, bias, keep, send):
    xl = ids[1]
    for j in range(4):
        cols = pl.ds(j * 128, 128)
        keep[j] = bias[xl, :, cols].T
        send[j] = bias[1 - xl, :, cols].T


def norm(x):
    mean = jnp.mean(x, axis=-1, keepdims=True)
    centred = x - mean
    inv = lax.rsqrt(jnp.mean(centred * centred, axis=-1, keepdims=True) + EPS)
    return centred * inv, inv


def prep_kernel(ids, pair, gain, w_proj, w_out, d_out, keep, send, gate_out, go_out, proj_s):
    xl = ids[1]
    w_t = w_proj[...].T
    for p in range(2):
        for i in range(2):
            r = 2 * p + i
            xhat, _ = norm(pair[r].astype(F32))
            normed = (xhat * gain[...]).astype(BF16)
            proj = nt(w_t, normed)
            go = nt(w_out[...], d_out[r])
            go_out[r] = go
            for h in range(2):
                gate = jax.nn.sigmoid(proj[h * 128 + 96 : h * 128 + 128])
                gate_out[r, h * DH : (h + 1) * DH] = gate
                proj_s[h, i * 64 : (i + 1) * 64] = proj[h * 128 + 32 : h * 128 + 96]
                proj_s[h, 128 + i * 64 : 160 + i * 64] = proj[h * 128 : h * 128 + 32] * SCALE
                proj_s[h, 160 + i * 64 : 192 + i * 64] = go[h * DH : (h + 1) * DH] * gate
        for ref, h in ((keep, xl), (send, 1 - xl)):
            ref[p * 128 : (p + 1) * 128] = proj_s[h, 0:128].T.astype(BF16)
            ref[256 + p * 128 : 384 + p * 128] = proj_s[h, 128:256].astype(BF16)


def fill_queries(qd, packs):
    qd[...] = jnp.zeros_like(qd)
    for half, pack in enumerate(packs):
        for r in range(4):
            low = 64 * (r % 2)
            qd[half, r, low : low + 32, 0:128] = pack[256 + 64 * r : 288 + 64 * r]
            qd[half, r, low + 32 : low + 64, 128:256] = pack[288 + 64 * r : 320 + 64 * r]


def side(ids, which):
    xl = ids[1]
    return xl if which == 0 else 1 - xl


def tile_of(zk, xk):
    return zk // 2 + 8 * xk


def stats_kernel(ids, act, kv, bias, pack0, pack1, stats, qd, ms, ls, ds):
    fill_queries(qd, (pack0, pack1))
    z = ids[0]
    nz = kv.shape[0]
    for half in range(2):
        a = tile_of(z, side(ids, half))
        ms[...] = jnp.full_like(ms, NEG)
        ls[...] = jnp.zeros_like(ls)
        ds[...] = jnp.zeros_like(ds)
        for rel in range(2):
            xk = side(ids, rel)

            @pl.loop(0, nz)
            def _(zk):
                @pl.when(act[a, tile_of(zk, xk)] == 1)
                def _():
                    b = bias[zk // 4, xk, half, zk % 4].astype(F32)
                    for r in range(4):
                        sd = nn(kv[zk, rel, r // 2], qd[half, r])
                        s = (sd[:, :128] + b).reshape(16, 8, 128)
                        dp = sd[:, 128:].reshape(16, 8, 128)
                        m_old = ms[r]
                        m_new = jnp.maximum(m_old, jnp.max(s, axis=0))
                        e = jnp.exp(s - m_new[None])
                        c = jnp.exp(m_old - m_new)
                        ls[r] = ls[r] * c + jnp.sum(e, axis=0)
                        ds[r] = ds[r] * c + jnp.sum(e * dp, axis=0)
                        ms[r] = m_new

        for r in range(4):
            m = ms[r]
            top = jnp.max(m, axis=0, keepdims=True)
            f = jnp.exp(m - top)
            total = jnp.sum(ls[r] * f, axis=0, keepdims=True)
            stats[half, r, 0:1] = top + jnp.log(total)
            stats[half, r, 1:2] = jnp.sum(ds[r] * f, axis=0, keepdims=True) / total


def back_kernel(ids, act, kv, bias, pack0, pack1, stats, dkv, oq, qd, acc):
    fill_queries(qd, (pack0, pack1))
    oq[...] = jnp.zeros_like(oq)
    z = ids[0]
    nz = kv.shape[0]
    for rel in range(2):
        xk = side(ids, rel)

        @pl.loop(0, nz)
        def _(zk):
            acc[...] = jnp.zeros_like(acc)
            for half in range(2):
                a = tile_of(z, side(ids, half))

                @pl.when(act[a, tile_of(zk, xk)] == 1)
                def _():
                    b = bias[zk // 4, xk, half, zk % 4].astype(F32)
                    for p in range(2):
                        kvp = kv[zk, rel, p]
                        kvt = kvp.T
                        for i in range(2):
                            r = 2 * p + i
                            q = qd[half, r]
                            sd = nn(kvp, q)
                            prob = jnp.exp(sd[:, :128] + b - stats[half, r, 0:1])
                            dsc = prob * (sd[:, 128:] - stats[half, r, 1:2])
                            pd = jnp.concatenate([dsc.astype(BF16), prob.astype(BF16)], axis=1)
                            acc[p] += nt(pd, q)
                            t = nn(kvt[64 * i : 64 * i + 64], pd)
                            oq[half, r, 0:32] += t[0:32, 0:128]
                            oq[half, r, 32:64] += t[32:64, 128:256]

            for p in range(2):
                dkv[zk, rel, p] = acc[p].astype(BF16)

    for half in range(2):
        for r in range(4):
            oq[half, r, 0:32] *= SCALE


def out_kernel(ids, oq_own, oq_other, gate, w_out, keep, send):
    xl, c = ids[1], ids[2]
    w_t = w_out[...].T
    for r in range(4):
        mine, theirs = oq_own[0, r, 32:64], oq_other[r, 32:64].astype(F32)
        att = jnp.concatenate(
            [jnp.where(xl == 0, mine, theirs), jnp.where(xl == 0, theirs, mine)], axis=0
        )
        part = nn(w_t, (gate[r] * att).astype(BF16))
        low, high = part[0:64], part[64:128]
        keep[r] = jnp.where(c == 0, low, high)
        send[r] = jnp.where(c == 0, high, low).astype(BF16)


def proj_kernel(ids, oq_own, oq_other, dkv_own, dkv_other, gate, go, w_proj, keep, send, dp):
    xl = ids[1]
    for p in range(2):
        mine_kv, theirs_kv = dkv_own[p].astype(F32).T, dkv_other[p].astype(F32).T
        for i in range(2):
            r = 2 * p + i
            for oq, kvt, h in (
                (oq_own[0, r], mine_kv, xl),
                (oq_other[r].astype(F32), theirs_kv, 1 - xl),
            ):
                low = pl.multiple_of(h * DH, DH)
                g = gate[r, pl.ds(low, DH)]
                base = pl.multiple_of(h * 128, 128)
                dp[pl.ds(base, 32)] = oq[0:32]
                dp[pl.ds(base + 32, 64)] = kvt[64 * i : 64 * i + 64]
                dp[pl.ds(base + 96, 32)] = go[r, pl.ds(low, DH)] * oq[32:64] * g * (1.0 - g)
            part = nn(w_proj[...], dp[...].astype(BF16)).T
            keep[r] = part
            send[r] = part.astype(BF16)


def final_kernel(pair, gain, part, other, out):
    for r in range(4):
        xhat, inv = norm(pair[r].astype(F32))
        g = (part[r].astype(BF16).astype(F32) + other[r].astype(F32)) * gain[...]
        mean = jnp.mean(g, axis=-1, keepdims=True)
        along = jnp.mean(g * xhat, axis=-1, keepdims=True)
        out[r] = (inv * (g - mean - xhat * along)).astype(BF16)


def per_device(pair, gain, w_proj, w_out, tri_bias, active, d_out):
    z, xl, c = lax.axis_index("z"), lax.axis_index("xl"), lax.axis_index("c")
    ids = jnp.stack([z, xl, c, c]).astype(jnp.int32)
    gain = gain.reshape(1, 128)
    bias_keep, bias_send = call(bias_kernel, [((4, 128, 128), BF16)] * 2, 1, 1)(ids, tri_bias)
    bias = jnp.stack([bias_keep, lax.ppermute(bias_send, "xl", SWAP)])
    pack, pack_send, gate, go = call(
        prep_kernel,
        [((512, 128), BF16)] * 2 + [((4, 64, 128), F32)] * 2,
        1,
        5,
        [pltpu.VMEM((2, 256, 128), F32)],
    )(ids, pair, gain, w_proj, w_out, d_out)
    pack_other = lax.ppermute(pack_send, "xl", SWAP)
    kv = jnp.stack([pack[:256].reshape(2, 128, 128), pack_other[:256].reshape(2, 128, 128)])
    kv = lax.all_gather(kv, "z")
    bias = lax.all_gather(bias, "xh")
    bias = lax.all_gather(bias, "y")
    (stats,) = call(
        stats_kernel,
        [((2, 4, 2, 128), F32)],
        2,
        4,
        [pltpu.VMEM((2, 4, 128, 256), BF16)] + [pltpu.VMEM((4, 8, 128), F32)] * 3,
    )(ids, active, kv, bias, pack, pack_other)
    dkv, oq = call(
        back_kernel,
        [((16, 2, 2, 128, 128), BF16), ((2, 4, 64, 128), F32)],
        2,
        5,
        [pltpu.VMEM((2, 4, 128, 256), BF16), pltpu.VMEM((2, 128, 128), F32)],
    )(ids, active, kv, bias, pack, pack_other, stats)
    oq_other = lax.ppermute(oq[1].astype(BF16), "xl", SWAP)
    out_keep, out_send = call(
        out_kernel, [((4, 64, 128), F32), ((4, 64, 128), BF16)], 1, 4
    )(ids, oq, oq_other, gate, w_out)
    out = (out_keep + lax.ppermute(out_send, "c", SWAP).astype(F32)).astype(BF16)
    dkv = lax.psum_scatter(dkv, "z", scatter_dimension=0, tiled=False)
    dkv_other = lax.ppermute(dkv[1], "xl", SWAP)
    part, part_send = call(
        proj_kernel,
        [((4, 128, 128), F32), ((4, 128, 128), BF16)],
        1,
        7,
        [pltpu.VMEM((256, 128), F32)],
    )(ids, oq, oq_other, dkv[0], dkv_other, gate, go, w_proj)
    (pair_gradient,) = call(final_kernel, [((4, 128, 128), BF16)], 0, 4)(
        pair, gain, part, lax.ppermute(part_send, "c", SWAP)
    )
    return jnp.swapaxes(out, 1, 2), pair_gradient


def solution(mesh):
    fine = Mesh(np.asarray(mesh.devices).reshape(2, 4, 2, 16, 2), ("xh", "y", "xl", "z", "c"))
    row, col = ("xh", "y"), ("xl", "z")
    return jax.shard_map(
        per_device,
        mesh=fine,
        in_specs=(
            P(row, col, None),
            P(),
            P(None, "c"),
            P("c", None),
            P("c", col, row),
            P(),
            P(row, col, None),
        ),
        out_specs=(P(row, col, "c"), P(row, col, None)),
        check_vma=False,
    )
```

time: 572 us -> 278 us (0.49)
  waiting for transfers between devices: 406 us -> 179 us
  other arithmetic: 51.8 us -> 1.42 us
  matrix products: 49.1 us -> 0 us
  Pallas kernels: 0 us -> 41 us
  local copies, waits for them, and re-layouts: 38.2 us -> 5.06 us
  starting transfers between devices: 0.2 us -> 28.5 us
  loops' own time: 10.8 us -> 0 us
  blocking collectives: 0 us -> 8.05 us
    unnamed x6 -> x3, waiting for transfers between devices: 139 us -> 0.05 us
    all_gather x2, waiting for transfers between devices: 195 us -> 105 us  [the longest x1 66.8 us: per_device(): kv = lax.all_gather(kv, 'z')]
    psum x1 -> x0, waiting for transfers between devices: 53.1 us -> none  [per_device(): d_norm = lax.psum(d_norm.astype(jnp.bfloat16), 'head').astype(jnp.float32)]
    reduce_scatter x1, waiting for transfers between devices: 19.3 us -> 68.4 us  [per_device(): dkv = lax.psum_scatter(dkv, 'z', scatter_dimension=0, tiled=False)]
    dot_general x77 -> x0, matrix products: 49.1 us -> none  [the longest x16 14.3 us: block_parts(): mask = jnp.dot(row_active, tile_onehot(first, step, tiles_total).T) > 0.5]
    pallas_call x0 -> x7, Pallas kernels: none -> 41 us  [the longest x1 27.2 us: per_device(): call(back_kernel, [((16, 2, 2, 128, 128), BF16), ((2, 4, 64, 128), F32)],...]
    ppermute x0 -> x6, starting transfers between devices: none -> 28.4 us  [the longest x1 13.3 us: per_device(): lax.ppermute(out_send, 'c', SWAP).astype(F32)]
    convert_element_type x19 -> x0, other arithmetic: 23.9 us -> none  [the longest x16 15.9 us: scores(): score = score + bias_blk[None].astype(jnp.float32)]
  transfers between devices with their start and end apart: 5 -> 9, of which waited for: 5 -> 6; matrix products, arithmetic and copies ran while one was open for 2% -> 1% of each run, Pallas kernels for 0% -> 1%
where the time goes in v1:
time: 278 us; the launch traced here: 277 us
  waiting for transfers between devices  179 us (64%)
  Pallas kernels  41 us (15%)
  starting transfers between devices  28.5 us (10%)
  between operations  13.9 us (5%)
  blocking collectives  8.05 us (3%)
  local copies, waits for them, and re-layouts  5.06 us (2%)
    reduce_scatter x1, waiting for transfers between devices, per_device(): dkv = lax.psum_scatter(dkv, 'z', scatter_dimension=0, tiled=False)  68.4 us
    all_gather x1, waiting for transfers between devices, per_device(): kv = lax.all_gather(kv, 'z')  66.8 us
    all_gather x1, waiting for transfers between devices, per_device(): bias = lax.all_gather(bias, 'y')  38.1 us
    pallas_call x1, Pallas kernels, per_device(): call(back_kernel, [((16, 2, 2, 128, 128), BF16), ((2, 4, 64, 128), F32)],...  27.2 us
    ppermute x1, starting transfers between devices, per_device(): lax.ppermute(out_send, 'c', SWAP).astype(F32)  13.3 us
    pallas_call x1, Pallas kernels, per_device(): call(stats_kernel, [((2, 4, 2, 128), F32)], 2, 4, [pltpu.VMEM((2, 4, 128,...  9.16 us
    all_gather x1, blocking collectives, per_device(): bias = lax.all_gather(bias, 'xh')  8.05 us
  transfers between devices with their start and end apart: 9, of which 6 were waited for; matrix products, arithmetic and copies ran while one was open for 1% of the time, Pallas kernels for 1%

profile of v1, /device:TPU:1, one launch (start us, length us, event | category | flops | bytes accessed | tf_op | source)
XLA Modules:
  0.0 277.4 jit_solution(7041128251844755252)
XLA Ops:
  7.3 0.9 copy-done.3
  8.3 0.7 shard_map.87
  8.9 3.9 %collective-permute-start.1 = (bf16[4,128,128]{2,1,0:T(8,128)(2,1)S(1)}, bf16[4,128,128]{2,1,0:T(8,128)(2,1)S(1)}, u32[]{:S(2)}, u32[]{:S(2)}) collective-permute-start(bf16[4,128,128]{2,1,0:T(8,128)(2,1)S(1)} %get-tuple-element.17), channel_id=1, source_target_pairs={{0,32},{32,0},{1,33},{33,1},{2,34},{34,2},{3,35},{35,3},{4,36},{36... | collective-permute-start | bytes 393224 | tf_op jit(solution)/shard_map/ppermute | solution.py:235
  12.9 2.3 collective-permute-done.1
  15.3 8.1 %all-gather.1 = bf16[4,4,128,128]{3,2,1,0:T(8,128)(2,1)} all-gather(bf16[2,4,128,128]{3,2,1,0:T(8,128)(2,1)S(1)} %pad_maximum_fusion), channel_id=3, replica_groups=mesh['xh'=2,'y'=4,'xl'=2,'z'=16,'c'=2] {'xh'}, dimensions={0}, use_global_device_ids=true | all-gather | bytes 786432 | tf_op jit(solution)/shard_map/all_gather | solution.py:246
  23.5 1.2 shard_map.86
  24.6 3.0 %collective-permute-start = (bf16[512,128]{1,0:T(8,128)(2,1)S(1)}, bf16[512,128]{1,0:T(8,128)(2,1)S(1)}, u32[]{:S(2)}, u32[]{:S(2)}) collective-permute-start(bf16[512,128]{1,0:T(8,128)(2,1)S(1)} %get-tuple-element.15), channel_id=1, source_target_pairs={{0,32},{32,0},{1,33},{33,1},{2,34},{34,2},{3,35},{35,3},{4,36},{36... | collective-permute-start | bytes 393224 | tf_op jit(solution)/shard_map/ppermute | solution.py:243
  27.6 3.1 %collective-permute-done.pack1 = bf16[512,128]{1,0:T(8,128)(2,1)S(1)} collective-permute-done((bf16[512,128]{1,0:T(8,128)(2,1)S(1)}, bf16[512,128]{1,0:T(8,128)(2,1)S(1)}, u32[]{:S(2)}, u32[]{:S(2)}) %collective-permute-start) | collective-permute-done | bytes 131104 | tf_op jit(solution)/shard_map/ppermute | solution.py:243
  30.7 0.7 pad_maximum_fusion.1
  31.5 38.1 %all-gather.8.cloned.1.call-done = bf16[8,2,4,128,128]{4,3,2,1,0:T(8,128)(2,1)} async-done(((bf16[2,2,4,128,128]{4,3,2,1,0:T(8,128)(2,1)}), bf16[8,2,4,128,128]{4,3,2,1,0:T(8,128)(2,1)}) %all-gather.8.cloned.1.call-update) | async-done | bytes 2097168 | tf_op jit(solution)/shard_map/all_gather | solution.py:247
  69.6 66.8 %all-gather.6.cloned.1.call-done = bf16[32,2,128,128]{3,2,1,0:T(8,128)(2,1)} async-done(((bf16[2,2,128,128]{3,2,1,0:T(8,128)(2,1)}), bf16[32,2,128,128]{3,2,1,0:T(8,128)(2,1)}) %all-gather.6.cloned.1.call-update) | async-done | bytes 2097168 | tf_op jit(solution)/shard_map/all_gather | solution.py:245
  136.4 1.6 copy-done
  138.0 1.6 copy-done.1
  139.6 9.2 %shard_map.88.stats = f32[2,4,2,128]{3,2,1,0:T(2,128)S(1)} custom-call(s32[4]{0:T(128)S(1)} %pad_add_fusion.ids, s32[16,16]{1,0:T(8,128)S(1)} %copy-done.7, bf16[16,2,2,128,128]{4,3,2,1,0:T(8,128)(2,1)S(1)} %bitcast.21, bf16[4,2,2,4,128,128]{5,4,3,2,1,0:T(8,128)(2,1)S(1)} %bitcast.20, bf16[512,128]{1,0:T(8,128)(2,1)S(1)} %get-tuple-element.14.pack0, ...), custom_call_target="tpu_custom_call" | custom-call | tf_op jit(solution)/shard_map/pallas_call | solution.py:248
  148.8 27.2 %shard_map.89 = (bf16[16,2,2,128,128]{4,3,2,1,0:T(8,128)(2,1)}, f32[2,4,64,128]{3,2,1,0:T(8,128)S(1)}) custom-call(s32[4]{0:T(128)S(1)} %pad_add_fusion.ids, s32[16,16]{1,0:T(8,128)S(1)} %copy-done.7, bf16[16,2,2,128,128]{4,3,2,1,0:T(8,128)(2,1)S(1)} %bitcast.22, bf16[4,2,2,4,128,128]{5,4,3,2,1,0:T(8,128)(2,1)} %bitcast.19, ...), custom_call_target="tpu_custom_call" | custom-call | tf_op jit(solution)/shard_map/pallas_call | solution.py:255
  176.0 3.1 %collective-permute-start.2 = (bf16[4,64,128]{2,1,0:T(8,128)(2,1)S(1)}, bf16[4,64,128]{2,1,0:T(8,128)(2,1)S(1)}, u32[]{:S(2)}, u32[]{:S(2)}) collective-permute-start(bf16[4,64,128]{2,1,0:T(8,128)(2,1)S(1)} %fusion.1), channel_id=1, source_target_pairs={{0,32},{32,0},{1,33},{33,1},{2,34},{34,2},{3,35},{35,3},{4,36},{36... | collective-permute-start | bytes 196616 | tf_op jit(solution)/shard_map/ppermute | solution.py:262
  179.1 68.4 %reduce-scatter.2.cloned.1.call-done = bf16[1,2,2,128,128]{4,3,2,1,0:T(8,128)(2,1)} async-done(((bf16[16,2,2,128,128]{4,3,2,1,0:T(8,128)(2,1)}), bf16[1,2,2,128,128]{4,3,2,1,0:T(8,128)(2,1)}) %reduce-scatter.2.cloned.1.call-update) | async-done | bytes 131088 | tf_op jit(solution)/shard_map/reduce_scatter | solution.py:267
  247.6 0.9 slice_bitcast_fusion
  248.4 3.0 %collective-permute-start.4 = (bf16[2,128,128]{2,1,0:T(8,128)(2,1)S(1)}, bf16[2,128,128]{2,1,0:T(8,128)(2,1)S(1)}, u32[]{:S(2)}, u32[]{:S(2)}) collective-permute-start(bf16[2,128,128]{2,1,0:T(8,128)(2,1)S(1)} %get-tuple-element.26), channel_id=1, source_target_pairs={{0,32},{32,0},{1,33},{33,1},{2,34},{34,2},{3,35},{35,3},{4,36},{36... | collective-permute-start | bytes 196616 | tf_op jit(solution)/shard_map/ppermute | solution.py:268
  251.5 0.8 shard_map.90
  252.2 13.3 %collective-permute-start.3 = (bf16[4,64,128]{2,1,0:T(8,128)(2,1)S(1)}, bf16[4,64,128]{2,1,0:T(8,128)(2,1)S(1)}, u32[]{:S(2)}, u32[]{:S(2)}) collective-permute-start(bf16[4,64,128]{2,1,0:T(8,128)(2,1)S(1)} %get-tuple-element.21), channel_id=1, source_target_pairs={{0,1},{1,0},{2,3},{3,2},{4,5},{5,4},{6,7},{7,6},{8,9},{9,8},{10,11... | collective-permute-start | bytes 196616 | tf_op jit(solution)/shard_map/ppermute | solution.py:266
  265.6 0.9 shard_map.91
  266.5 2.0 collective-permute-start.5
  269.8 1.1 shard_map.92
  (31 shorter events, 1.6 us)
Async XLA Ops:
  7.2 16.2 %copy-start.2 = (bf16[4,128,128]{2,1,0:T(8,128)(2,1)S(1)}, bf16[4,128,128]{2,1,0:T(8,128)(2,1)}, u32[]{:S(2)}) copy-start(bf16[4,128,128]{2,1,0:T(8,128)(2,1)} %pair.3) | copy-start | bytes 393220
  7.2 62.4 %all-gather.8.cloned.1.call-start = ((), (), s32[]{:S(2)}) async-start(), calls=%async_computation.3 | async-start | bytes 2621440 | tf_op jit(solution)/shard_map/all_gather | solution.py:247
  7.3 1.0 copy-start.3
  8.3 15.2 %copy-start.4 = (bf16[128,256]{1,0:T(8,128)(2,1)S(1)}, bf16[128,256]{1,0:T(8,128)(2,1)}, u32[]{:S(2)}) copy-start(bf16[128,256]{1,0:T(8,128)(2,1)} %w_proj.3) | copy-start | bytes 196612
  8.3 15.2 %copy-start.5 = (bf16[4,128,128]{2,1,0:T(8,128)(2,1)S(1)}, bf16[4,128,128]{2,1,0:T(8,128)(2,1)}, u32[]{:S(2)}) copy-start(bf16[4,128,128]{2,1,0:T(8,128)(2,1)} %d_out.1) | copy-start | bytes 393220
  8.3 15.2 %copy-start.6 = (bf16[64,128]{1,0:T(8,128)(2,1)S(1)}, bf16[64,128]{1,0:T(8,128)(2,1)}, u32[]{:S(2)}) copy-start(bf16[64,128]{1,0:T(8,128)(2,1)} %w_out.3) | copy-start | bytes 49156
  8.3 15.2 %copy-start.8 = (f32[128]{0:T(128)S(1)}, f32[128]{0:T(128)}, u32[]{:S(2)}) copy-start(f32[128]{0:T(128)} %param.8) | copy-start | bytes 1540
  8.3 128.1 %copy-start.7 = (s32[16,16]{1,0:T(8,128)S(1)}, s32[16,16]{1,0:T(8,128)}, u32[]{:S(2)}) copy-start(s32[16,16]{1,0:T(8,128)} %act.3) | copy-start | bytes 3076
  8.9 6.3 %collective-permute-start.1 = (bf16[4,128,128]{2,1,0:T(8,128)(2,1)S(1)}, bf16[4,128,128]{2,1,0:T(8,128)(2,1)S(1)}, u32[]{:S(2)}, u32[]{:S(2)}) collective-permute-start(bf16[4,128,128]{2,1,0:T(8,128)(2,1)S(1)} %get-tuple-element.17), channel_id=1, source_target_pairs={{0,32},{32,0},{1,33},{33,1},{2,34},{34,2},{3,35},{35,3},{4,36},{36... | collective-permute-start | bytes 393224 | tf_op jit(solution)/shard_map/ppermute | solution.py:235
  23.4 113.0 %all-gather.6.cloned.1.call-start = ((), (), s32[]{:S(2)}) async-start(), calls=%async_computation.2 | async-start | bytes 2228224 | tf_op jit(solution)/shard_map/all_gather | solution.py:245
  24.6 6.1 %collective-permute-start = (bf16[512,128]{1,0:T(8,128)(2,1)S(1)}, bf16[512,128]{1,0:T(8,128)(2,1)S(1)}, u32[]{:S(2)}, u32[]{:S(2)}) collective-permute-start(bf16[512,128]{1,0:T(8,128)(2,1)S(1)} %get-tuple-element.15), channel_id=1, source_target_pairs={{0,32},{32,0},{1,33},{33,1},{2,34},{34,2},{3,35},{35,3},{4,36},{36... | collective-permute-start | bytes 393224 | tf_op jit(solution)/shard_map/ppermute | solution.py:243
  31.4 216.1 %reduce-scatter.2.cloned.1.call-start = ((), (), s32[]{:S(2)}) async-start(), calls=%async_computation.1 | async-start | bytes 2228224 | tf_op jit(solution)/shard_map/reduce_scatter | solution.py:267
  136.4 1.6 copy-start
  138.0 1.6 copy-start.1
  176.0 75.5 %collective-permute-start.2 = (bf16[4,64,128]{2,1,0:T(8,128)(2,1)S(1)}, bf16[4,64,128]{2,1,0:T(8,128)(2,1)S(1)}, u32[]{:S(2)}, u32[]{:S(2)}) collective-permute-start(bf16[4,64,128]{2,1,0:T(8,128)(2,1)S(1)} %fusion.1), channel_id=1, source_target_pairs={{0,32},{32,0},{1,33},{33,1},{2,34},{34,2},{3,35},{35,3},{4,36},{36... | collective-permute-start | bytes 196616 | tf_op jit(solution)/shard_map/ppermute | solution.py:262
  248.4 17.1 %collective-permute-start.4 = (bf16[2,128,128]{2,1,0:T(8,128)(2,1)S(1)}, bf16[2,128,128]{2,1,0:T(8,128)(2,1)S(1)}, u32[]{:S(2)}, u32[]{:S(2)}) collective-permute-start(bf16[2,128,128]{2,1,0:T(8,128)(2,1)S(1)} %get-tuple-element.26), channel_id=1, source_target_pairs={{0,32},{32,0},{1,33},{33,1},{2,34},{34,2},{3,35},{35,3},{4,36},{36... | collective-permute-start | bytes 196616 | tf_op jit(solution)/shard_map/ppermute | solution.py:268
  252.2 16.3 %collective-permute-start.3 = (bf16[4,64,128]{2,1,0:T(8,128)(2,1)S(1)}, bf16[4,64,128]{2,1,0:T(8,128)(2,1)S(1)}, u32[]{:S(2)}, u32[]{:S(2)}) collective-permute-start(bf16[4,64,128]{2,1,0:T(8,128)(2,1)S(1)} %get-tuple-element.21), channel_id=1, source_target_pairs={{0,1},{1,0},{2,3},{3,2},{4,5},{5,4},{6,7},{7,6},{8,9},{9,8},{10,11... | collective-permute-start | bytes 196616 | tf_op jit(solution)/shard_map/ppermute | solution.py:266
  266.5 3.2 %collective-permute-start.5 = (bf16[4,128,128]{2,1,0:T(8,128)(2,1)S(1)}, bf16[4,128,128]{2,1,0:T(8,128)(2,1)S(1)}, u32[]{:S(2)}, u32[]{:S(2)}) collective-permute-start(bf16[4,128,128]{2,1,0:T(8,128)(2,1)S(1)} %get-tuple-element.25), channel_id=1, source_target_pairs={{0,1},{1,0},{2,3},{3,2},{4,5},{5,4},{6,7},{7,6},{8,9},{9,8},{10,11... | collective-permute-start | bytes 393224 | tf_op jit(solution)/shard_map/ppermute | solution.py:277
Sparse Core Ops, SparseCore 0:
  23.5 46.0 all-gather.7
  72.2 64.1 all-gather.5
  176.1 71.4 reduce-scatter.1

commit v2 on v1

--- a/solution.py
+++ b/solution.py
@@ -37,7 +37,7 @@
         in_specs=[smem()] * n_smem + [vmem()] * n_vmem,
         out_specs=[vmem()] * len(outs),
         scratch_shapes=list(scratch),
-        compiler_params=pltpu.CompilerParams(vmem_limit_bytes=48 * 1024 * 1024),
+        compiler_params=pltpu.CompilerParams(vmem_limit_bytes=24 * 1024 * 1024),
         cost_estimate=pl.CostEstimate(flops=flops, bytes_accessed=nbytes, transcendentals=0),
     )
 
@@ -96,91 +96,128 @@
             qd[half, r, low + 32 : low + 64, 128:256] = pack[288 + 64 * r : 320 + 64 * r]
 
 
-def side(ids, which):
-    xl = ids[1]
-    return xl if which == 0 else 1 - xl
-
-
 def tile_of(zk, xk):
     return zk // 2 + 8 * xk
 
 
-def stats_kernel(ids, act, kv, bias, pack0, pack1, stats, qd, ms, ls, ds):
+def list_units(ids, act, lst, a, first, count):
+    def step(u, n):
+        zk = (ids[0] + first + 4 * (u // 2) + 32) % 16
+        xk = jnp.where(u % 2 == 0, ids[1], 1 - ids[1])
+        lst[n] = u
+        return n + act[a, tile_of(zk, xk)]
+
+    return lax.fori_loop(0, 2 * count, step, 0)
+
+
+def load_units(ids, kv, bias, first, half, units):
+    keys = [[kv[u // 2, u % 2, p] for u in units] for p in range(2)]
+    b = []
+    for u in units:
+        zk = (ids[0] + first + 4 * (u // 2) + 32) % 16
+        xk = jnp.where(u % 2 == 0, ids[1], 1 - ids[1])
+        b.append(bias[zk // 4, jnp.where(xk == ids[3], 0, 1), half, zk % 4].astype(F32))
+    keys = [k[0] if len(k) == 1 else jnp.concatenate(k, axis=0) for k in keys]
+    return keys, b[0] if len(b) == 1 else jnp.concatenate(b, axis=0)
+
+
+def over_units(ids, act, lst, first, count, half, body):
+    a = tile_of(ids[0], jnp.where(half == 0, ids[1], 1 - ids[1]))
+    n = list_units(ids, act, lst, a, first, count)
+
+    @pl.loop(0, n // 2)
+    def _(k):
+        body([lst[2 * k], lst[2 * k + 1]])
+
+    @pl.when(n % 2 == 1)
+    def _():
+        body([lst[n - 1]])
+
+
+def stats_kernel(firsts, begin, end, ids, act, *refs):
+    n = len(firsts)
+    kvs, (bias, pack0, pack1), refs = refs[:n], refs[n : n + 3], refs[n + 3 :]
+    before, refs = (None, refs) if begin else (refs[0], refs[1:])
+    out, qd, lst, st = refs
     fill_queries(qd, (pack0, pack1))
-    z = ids[0]
-    nz = kv.shape[0]
-    for half in range(2):
-        a = tile_of(z, side(ids, half))
-        ms[...] = jnp.full_like(ms, NEG)
-        ls[...] = jnp.zeros_like(ls)
-        ds[...] = jnp.zeros_like(ds)
-        for rel in range(2):
-            xk = side(ids, rel)
-
-            @pl.loop(0, nz)
-            def _(zk):
-                @pl.when(act[a, tile_of(zk, xk)] == 1)
-                def _():
-                    b = bias[zk // 4, xk, half, zk % 4].astype(F32)
-                    for r in range(4):
-                        sd = nn(kv[zk, rel, r // 2], qd[half, r])
-                        s = (sd[:, :128] + b).reshape(16, 8, 128)
-                        dp = sd[:, 128:].reshape(16, 8, 128)
-                        m_old = ms[r]
+    if begin:
+        st[0] = jnp.full(st.shape[1:], NEG, F32)
+        st[1:3] = jnp.zeros((2,) + st.shape[1:], F32)
+    else:
+        st[...] = before[...]
+
+    @pl.loop(0, 2)
+    def _(half):
+        for kv, first in zip(kvs, firsts):
+
+            def body(units, kv=kv, first=first):
+                keys, b = load_units(ids, kv, bias, first, half, units)
+                rows = b.shape[0] // 8
+                for p in range(2):
+                    sd = [nn(keys[p], qd[half, 2 * p + i]) for i in range(2)]
+                    for i in range(2):
+                        r = 2 * p + i
+                        s = (sd[i][:, :128] + b).reshape(rows, 8, 128)
+                        dp = sd[i][:, 128:].reshape(rows, 8, 128)
+                        m_old = st[0, half, r]
                         m_new = jnp.maximum(m_old, jnp.max(s, axis=0))
                         e = jnp.exp(s - m_new[None])
                         c = jnp.exp(m_old - m_new)
-                        ls[r] = ls[r] * c + jnp.sum(e, axis=0)
-                        ds[r] = ds[r] * c + jnp.sum(e * dp, axis=0)
-                        ms[r] = m_new
-
+                        st[1, half, r] = st[1, half, r] * c + jnp.sum(e, axis=0)
+                        st[2, half, r] = st[2, half, r] * c + jnp.sum(e * dp, axis=0)
+                        st[0, half, r] = m_new
+
+            over_units(ids, act, lst, first, kv.shape[0], half, body)
+
+    if not end:
+        out[...] = st[...]
+        return
+    for half in range(2):
         for r in range(4):
-            m = ms[r]
+            m = st[0, half, r]
             top = jnp.max(m, axis=0, keepdims=True)
             f = jnp.exp(m - top)
-            total = jnp.sum(ls[r] * f, axis=0, keepdims=True)
-            stats[half, r, 0:1] = top + jnp.log(total)
-            stats[half, r, 1:2] = jnp.sum(ds[r] * f, axis=0, keepdims=True) / total
-
-
-def back_kernel(ids, act, kv, bias, pack0, pack1, stats, dkv, oq, qd, acc):
+            total = jnp.sum(st[1, half, r] * f, axis=0, keepdims=True)
+            out[half, r, 0:1] = top + jnp.log(total)
+            out[half, r, 1:2] = jnp.sum(st[2, half, r] * f, axis=0, keepdims=True) / total
+
+
+def back_kernel(firsts, ids, act, *refs):
+    n = len(firsts)
+    kvs, (bias, pack0, pack1, stats) = refs[:n], refs[n : n + 4]
+    dkvs, (oq, qd, lst, acc) = refs[n + 4 : 2 * n + 4], refs[2 * n + 4 :]
     fill_queries(qd, (pack0, pack1))
     oq[...] = jnp.zeros_like(oq)
-    z = ids[0]
-    nz = kv.shape[0]
-    for rel in range(2):
-        xk = side(ids, rel)
-
-        @pl.loop(0, nz)
-        def _(zk):
-            acc[...] = jnp.zeros_like(acc)
-            for half in range(2):
-                a = tile_of(z, side(ids, half))
-
-                @pl.when(act[a, tile_of(zk, xk)] == 1)
-                def _():
-                    b = bias[zk // 4, xk, half, zk % 4].astype(F32)
-                    for p in range(2):
-                        kvp = kv[zk, rel, p]
-                        kvt = kvp.T
-                        for i in range(2):
-                            r = 2 * p + i
-                            q = qd[half, r]
-                            sd = nn(kvp, q)
-                            prob = jnp.exp(sd[:, :128] + b - stats[half, r, 0:1])
-                            dsc = prob * (sd[:, 128:] - stats[half, r, 1:2])
-                            pd = jnp.concatenate([dsc.astype(BF16), prob.astype(BF16)], axis=1)
-                            acc[p] += nt(pd, q)
-                            t = nn(kvt[64 * i : 64 * i + 64], pd)
-                            oq[half, r, 0:32] += t[0:32, 0:128]
-                            oq[half, r, 32:64] += t[32:64, 128:256]
-
-            for p in range(2):
-                dkv[zk, rel, p] = acc[p].astype(BF16)
-
-    for half in range(2):
-        for r in range(4):
-            oq[half, r, 0:32] *= SCALE
+    for kv, dkv, first in zip(kvs, dkvs, firsts):
+        count = kv.shape[0]
+        acc[0:count] = jnp.zeros((count,) + acc.shape[1:], F32)
+
+        @pl.loop(0, 2)
+        def _(half):
+            def body(units):
+                keys, b = load_units(ids, kv, bias, first, half, units)
+                for p in range(2):
+                    keys_t = keys[p].T
+                    qs = [qd[half, 2 * p + i] for i in range(2)]
+                    sd = [nn(keys[p], q) for q in qs]
+                    pds = []
+                    for i in range(2):
+                        r = 2 * p + i
+                        prob = jnp.exp(sd[i][:, :128] + (b - stats[half, r, 0:1]))
+                        dsc = prob * (sd[i][:, 128:] - stats[half, r, 1:2])
+                        pds.append(jnp.concatenate([dsc.astype(BF16), prob.astype(BF16)], axis=1))
+                    both = nt(jnp.concatenate(pds, axis=1), jnp.concatenate(qs, axis=1))
+                    for k, u in enumerate(units):
+                        acc[u // 2, u % 2, p] += both[128 * k : 128 * k + 128]
+                    for i in range(2):
+                        r = 2 * p + i
+                        t = nn(keys_t[64 * i : 64 * i + 64], pds[i])
+                        oq[half, r, 0:32] += t[0:32, 0:128]
+                        oq[half, r, 32:64] += t[32:64, 128:256]
+
+            over_units(ids, act, lst, first, count, half, body)
+
+        dkv[...] = acc[0:count].astype(BF16)
 
 
 def out_kernel(ids, oq_own, oq_other, gate, w_out, keep, send):
@@ -227,12 +264,48 @@
         out[r] = (inv * (g - mean - xhat * along)).astype(BF16)
 
 
+def stats_call(firsts, begin, end, ids, active, kvs, rest):
+    out = ((2, 4, 2, 128), F32) if end else ((3, 2, 4, 8, 128), F32)
+    return call(
+        functools.partial(stats_kernel, firsts, begin, end),
+        [out],
+        2,
+        len(kvs) + len(rest),
+        [
+            pltpu.VMEM((2, 4, 128, 256), BF16),
+            pltpu.SMEM((9,), jnp.int32),
+            pltpu.VMEM((3, 2, 4, 8, 128), F32),
+        ],
+        flops=10 ** 9,
+        nbytes=10 ** 7,
+    )(ids, active, *kvs, *rest)[0]
+
+
+def back_call(firsts, ids, active, kvs, rest):
+    res = call(
+        functools.partial(back_kernel, firsts),
+        [(kv.shape, BF16) for kv in kvs] + [((2, 4, 64, 128), F32)],
+        2,
+        len(kvs) + len(rest),
+        [
+            pltpu.VMEM((2, 4, 128, 256), BF16),
+            pltpu.SMEM((9,), jnp.int32),
+            pltpu.VMEM((4, 2, 2, 128, 128), F32),
+        ],
+        flops=2 * 10 ** 9,
+        nbytes=2 * 10 ** 7,
+    )(ids, active, *kvs, *rest)
+    return res[:-1], res[-1]
+
+
+def to_z(x, step):
+    return lax.ppermute(x, "z", [(j, (j + step) % 16) for j in range(16)])
+
+
 def per_device(pair, gain, w_proj, w_out, tri_bias, active, d_out):
-    z, xl, c = lax.axis_index("z"), lax.axis_index("xl"), lax.axis_index("c")
-    ids = jnp.stack([z, xl, c, c]).astype(jnp.int32)
+    z, xl, c, xh = (lax.axis_index(name) for name in ("z", "xl", "c", "xh"))
+    ids = jnp.stack([z, xl, c, xh]).astype(jnp.int32)
     gain = gain.reshape(1, 128)
-    bias_keep, bias_send = call(bias_kernel, [((4, 128, 128), BF16)] * 2, 1, 1)(ids, tri_bias)
-    bias = jnp.stack([bias_keep, lax.ppermute(bias_send, "xl", SWAP)])
     pack, pack_send, gate, go = call(
         prep_kernel,
         [((512, 128), BF16)] * 2 + [((4, 64, 128), F32)] * 2,
@@ -241,31 +314,41 @@
         [pltpu.VMEM((2, 256, 128), F32)],
     )(ids, pair, gain, w_proj, w_out, d_out)
     pack_other = lax.ppermute(pack_send, "xl", SWAP)
+    bias_keep, bias_send = call(bias_kernel, [((4, 128, 128), BF16)] * 2, 1, 1)(ids, tri_bias)
+    bias = jnp.stack([bias_keep, lax.ppermute(bias_send, "xl", SWAP)])
+    bias = jnp.stack([bias, lax.ppermute(bias, "xh", SWAP)])
+    bias = lax.all_gather(bias, "y")
     kv = jnp.stack([pack[:256].reshape(2, 128, 128), pack_other[:256].reshape(2, 128, 128)])
-    kv = lax.all_gather(kv, "z")
-    bias = lax.all_gather(bias, "xh")
-    bias = lax.all_gather(bias, "y")
-    (stats,) = call(
-        stats_kernel,
-        [((2, 4, 2, 128), F32)],
-        2,
-        4,
-        [pltpu.VMEM((2, 4, 128, 256), BF16)] + [pltpu.VMEM((4, 8, 128), F32)] * 3,
-    )(ids, active, kv, bias, pack, pack_other)
-    dkv, oq = call(
-        back_kernel,
-        [((16, 2, 2, 128, 128), BF16), ((2, 4, 64, 128), F32)],
-        2,
-        5,
-        [pltpu.VMEM((2, 4, 128, 256), BF16), pltpu.VMEM((2, 128, 128), F32)],
-    )(ids, active, kv, bias, pack, pack_other, stats)
+    own = jnp.stack([to_z(kv, 4), kv, to_z(kv, -4), to_z(kv, 8)])
+    up, down = to_z(own, -1), to_z(own, 1)
+    up2, down2 = to_z(own[1:3], -2), to_z(own[0:2], 2)
+    rest = (bias, pack, pack_other)
+    state = stats_call((-4,), True, False, ids, active, (own,), rest)
+    state = stats_call((-3, -5), False, False, ids, active, (up, down), rest + (state,))
+    stats = stats_call((2, -6), False, True, ids, active, (up2, down2), rest + (state,))
+    rest = rest + (stats,)
+    (d_up2, d_down2), oq2 = back_call((2, -6), ids, active, (up2, down2), rest)
+    r_up2, r_down2 = to_z(d_up2, 2), to_z(d_down2, -2)
+    (d_up,), oq1 = back_call((-3,), ids, active, (up,), rest)
+    r_up = to_z(d_up, 1)
+    (d_down,), oq3 = back_call((-5,), ids, active, (down,), rest)
+    r_down = to_z(d_down, -1)
+    (d_own,), oq0 = back_call((-4,), ids, active, (own,), rest)
+    oq = oq0 + oq1 + oq2 + oq3
+    oq = jnp.concatenate([oq[:, :, :32] * SCALE, oq[:, :, 32:]], axis=2)
     oq_other = lax.ppermute(oq[1].astype(BF16), "xl", SWAP)
     out_keep, out_send = call(
         out_kernel, [((4, 64, 128), F32), ((4, 64, 128), BF16)], 1, 4
     )(ids, oq, oq_other, gate, w_out)
     out = (out_keep + lax.ppermute(out_send, "c", SWAP).astype(F32)).astype(BF16)
-    dkv = lax.psum_scatter(dkv, "z", scatter_dimension=0, tiled=False)
-    dkv_other = lax.ppermute(dkv[1], "xl", SWAP)
+    f = lambda x: x.astype(F32)
+    sums = f(d_own) + f(r_up) + f(r_down)
+    s0 = (sums[0] + f(r_down2[0])).astype(BF16)
+    s1 = sums[1] + f(r_up2[0]) + f(r_down2[1])
+    s2 = (sums[2] + f(r_up2[1])).astype(BF16)
+    s3 = sums[3].astype(BF16)
+    dkv = s1 + f(to_z(s0, -4)) + f(to_z(s2, 4)) + f(to_z(s3, 8))
+    dkv_other = lax.ppermute(dkv[1].astype(BF16), "xl", SWAP)
     part, part_send = call(
         proj_kernel,
         [((4, 128, 128), F32), ((4, 128, 128), BF16)],

time: 278 us -> 202 us (0.73)
  waiting for transfers between devices: 179 us -> 38.2 us
  starting transfers between devices: 28.5 us -> 103 us
  blocking collectives: 8.05 us -> 0 us
    ppermute x1 -> x16, starting transfers between devices: 3.02 us -> 83.1 us  [the longest x14 75.7 us: to_z(): return lax.ppermute(x, 'z', [(j, (j + step) % 16) for j in range(16)])]
    reduce_scatter x1 -> x0, waiting for transfers between devices: 68.4 us -> none  [per_device(): dkv = lax.psum_scatter(dkv, 'z', scatter_dimension=0, tiled=False)]
    all_gather x1 -> x0, waiting for transfers between devices: 66.8 us -> none  [per_device(): kv = lax.all_gather(kv, 'z')]
    all_gather x1, waiting for transfers between devices: 38.1 us -> 0.02 us  [per_device(): bias = lax.all_gather(bias, 'y')]
    ppermute x1 -> x16, waiting for transfers between devices: 0.01 us -> 30.4 us  [the longest x14 23.6 us: to_z(): return lax.ppermute(x, 'z', [(j, (j + step) % 16) for j in range(16)])]
    all_gather x1 -> x0, blocking collectives: 8.05 us -> none  [per_device(): bias = lax.all_gather(bias, 'xh')]
    ppermute x1, starting transfers between devices: 13.3 us -> 6.2 us  [per_device(): lax.ppermute(out_send, 'c', SWAP).astype(F32)]
    pallas_call x2 -> x7, Pallas kernels: 36.3 us -> 36.3 us  [the longest x4 22.1 us: back_call(): call(functools.partial(back_kernel, firsts), [(kv.shape, BF16) for kv in...]
  transfers between devices with their start and end apart: 9 -> 22, of which waited for: 6 -> 11; matrix products, arithmetic and copies ran while one was open for 1% -> 1% of each run, Pallas kernels for 1% -> 15%
where the time goes in v2:
time: 202 us; the launch traced here: 201 us
  starting transfers between devices  103 us (51%)
  Pallas kernels  40.9 us (20%)
  waiting for transfers between devices  38.2 us (19%)
  between operations  14.5 us (7%)
  local copies, waits for them, and re-layouts  2.61 us (1%)
  other arithmetic  2.24 us (1%)
    ppermute x14, starting transfers between devices, to_z(): return lax.ppermute(x, 'z', [(j, (j + step) % 16) for j in range(16)])  75.7 us
    ppermute x14, waiting for transfers between devices, to_z(): return lax.ppermute(x, 'z', [(j, (j + step) % 16) for j in range(16)])  23.6 us
    pallas_call x4, Pallas kernels, back_call(): call(functools.partial(back_kernel, firsts), [(kv.shape, BF16) for kv in...  22.1 us
    pallas_call x3, Pallas kernels, stats_call(): call(functools.partial(stats_kernel, firsts, begin, end), [out], 2, len(k...  14.2 us
    ppermute x1, starting transfers between devices, per_device(): lax.ppermute(out_send, 'c', SWAP).astype(F32)  6.2 us
    ppermute x1, starting transfers between devices, per_device(): bias = jnp.stack([bias, lax.ppermute(bias, 'xh', SWAP)])  5.44 us
  transfers between devices with their start and end apart: 22, of which 11 were waited for; matrix products, arithmetic and copies ran while one was open for 1% of the time, Pallas kernels for 15%

profile of v2, /device:TPU:1, one launch (start us, length us, event | category | flops | bytes accessed | tf_op | source)
XLA Modules:
  0.0 201.1 jit_solution(3366014096471985653)
XLA Ops:
  8.9 3.9 %collective-permute-start.4 = (bf16[4,128,128]{2,1,0:T(8,128)(2,1)S(1)}, bf16[4,128,128]{2,1,0:T(8,128)(2,1)S(1)}, u32[]{:S(2)}, u32[]{:S(2)}) collective-permute-start(bf16[4,128,128]{2,1,0:T(8,128)(2,1)S(1)} %get-tuple-element.24), channel_id=1, source_target_pairs={{0,32},{32,0},{1,33},{33,1},{2,34},{34,2},{3,35},{35,3},{4,36},{36... | collective-permute-start | bytes 393224 | tf_op jit(solution)/shard_map/ppermute | solution.py:318
  15.3 5.4 %collective-permute-start.5 = (bf16[2,4,128,128]{3,2,1,0:T(8,128)(2,1)S(1)}, bf16[2,4,128,128]{3,2,1,0:T(8,128)(2,1)S(1)}, u32[]{:S(2)}, u32[]{:S(2)}) collective-permute-start(bf16[2,4,128,128]{3,2,1,0:T(8,128)(2,1)S(1)} %get-tuple-element.45), channel_id=1, source_target_pairs={{0,256},{256,0},{1,257},{257,1},{2,258},{258,2},{3,259},{259,3},{4... | collective-permute-start | bytes 786440 | tf_op jit(solution)/shard_map/ppermute | solution.py:319
  20.7 3.7 %collective-permute-done.5 = bf16[2,4,128,128]{3,2,1,0:T(8,128)(2,1)S(1)} collective-permute-done((bf16[2,4,128,128]{3,2,1,0:T(8,128)(2,1)S(1)}, bf16[2,4,128,128]{3,2,1,0:T(8,128)(2,1)S(1)}, u32[]{:S(2)}, u32[]{:S(2)}) %collective-permute-start.5) | collective-permute-done | bytes 262176 | tf_op jit(solution)/shard_map/ppermute | solution.py:319
  32.3 13.7 %collective-permute-start.2 = (bf16[2,2,128,128]{3,2,1,0:T(8,128)(2,1)S(1)}, bf16[2,2,128,128]{3,2,1,0:T(8,128)(2,1)S(1)}, u32[]{:S(2)}, u32[]{:S(2)}) collective-permute-start(bf16[2,2,128,128]{3,2,1,0:T(8,128)(2,1)S(1)} %get-tuple-element.49), channel_id=1, source_target_pairs={{0,24},{2,26},{4,28},{6,30},{8,0},{10,2},{12,4},{14,6},{16,8},{18,... | collective-permute-start | bytes 393224 | tf_op jit(solution)/shard_map/ppermute | solution.py:302
  46.0 4.9 %collective-permute-start.3 = (bf16[2,2,128,128]{3,2,1,0:T(8,128)(2,1)S(1)}, bf16[2,2,128,128]{3,2,1,0:T(8,128)(2,1)S(1)}, u32[]{:S(2)}, u32[]{:S(2)}) collective-permute-start(bf16[2,2,128,128]{3,2,1,0:T(8,128)(2,1)S(1)} %get-tuple-element.49), channel_id=1, source_target_pairs={{0,16},{2,18},{4,20},{6,22},{8,24},{10,26},{12,28},{14,30},{16,0},... | collective-permute-start | bytes 393224 | tf_op jit(solution)/shard_map/ppermute | solution.py:302
  50.9 7.3 %collective-permute-start.1 = (bf16[2,2,128,128]{3,2,1,0:T(8,128)(2,1)S(1)}, bf16[2,2,128,128]{3,2,1,0:T(8,128)(2,1)S(1)}, u32[]{:S(2)}, u32[]{:S(2)}) collective-permute-start(bf16[2,2,128,128]{3,2,1,0:T(8,128)(2,1)S(1)} %get-tuple-element.49), channel_id=1, source_target_pairs={{0,8},{2,10},{4,12},{6,14},{8,16},{10,18},{12,20},{14,22},{16,24},... | collective-permute-start | bytes 393224 | tf_op jit(solution)/shard_map/ppermute | solution.py:302
  60.9 6.9 %collective-permute-done.1 = bf16[2,2,128,128]{3,2,1,0:T(8,128)(2,1)S(1)} collective-permute-done((bf16[2,2,128,128]{3,2,1,0:T(8,128)(2,1)S(1)}, bf16[2,2,128,128]{3,2,1,0:T(8,128)(2,1)S(1)}, u32[]{:S(2)}, u32[]{:S(2)}) %collective-permute-start.1) | collective-permute-done | bytes 131104 | tf_op jit(solution)/shard_map/ppermute | solution.py:302
  67.9 7.9 %collective-permute-start.9 = (bf16[4,2,2,128,128]{4,3,2,1,0:T(8,128)(2,1)S(1)}, bf16[4,2,2,128,128]{4,3,2,1,0:T(8,128)(2,1)S(1)}, u32[]{:S(2)}, u32[]{:S(2)}) collective-permute-start(bf16[4,2,2,128,128]{4,3,2,1,0:T(8,128)(2,1)S(1)} %pad_maximum_fusion.refs_0_), channel_id=1, source_target_pairs={{0,2},{2,4},{4,6},{6,8},{8,10},{10,12},{12,14},{14,16},{16,18},{18... | collective-permute-start | bytes 1572872 | tf_op jit(solution)/shard_map/ppermute | solution.py:302
  75.8 9.2 %collective-permute-start.8 = (bf16[4,2,2,128,128]{4,3,2,1,0:T(8,128)(2,1)S(1)}, bf16[4,2,2,128,128]{4,3,2,1,0:T(8,128)(2,1)S(1)}, u32[]{:S(2)}, u32[]{:S(2)}) collective-permute-start(bf16[4,2,2,128,128]{4,3,2,1,0:T(8,128)(2,1)S(1)} %pad_maximum_fusion.refs_0_), channel_id=1, source_target_pairs={{0,30},{2,0},{4,2},{6,4},{8,6},{10,8},{12,10},{14,12},{16,14},{18,... | collective-permute-start | bytes 1572872 | tf_op jit(solution)/shard_map/ppermute | solution.py:302
  87.0 5.5 %collective-permute-start.6 = (bf16[2,2,2,128,128]{4,3,2,1,0:T(8,128)(2,1)S(1)}, bf16[2,2,2,128,128]{4,3,2,1,0:T(8,128)(2,1)S(1)}, u32[]{:S(2)}, u32[]{:S(2)}) collective-permute-start(bf16[2,2,2,128,128]{4,3,2,1,0:T(8,128)(2,1)S(1)} %get-tuple-element.47), channel_id=1, source_target_pairs={{0,28},{2,30},{4,0},{6,2},{8,4},{10,6},{12,8},{14,10},{16,12},{18,... | collective-permute-start | bytes 786440 | tf_op jit(solution)/shard_map/ppermute | solution.py:302
  94.1 3.8 %shard_map.88.refs_5_ = f32[3,2,4,8,128]{4,3,2,1,0:T(8,128)S(1)} custom-call(s32[4]{0:T(128)S(1)} %pad_add_fusion.ids, s32[16,16]{1,0:T(8,128)S(1)} %copy-done.7, bf16[4,2,2,128,128]{4,3,2,1,0:T(8,128)(2,1)S(1)} %pad_maximum_fusion.refs_0_, bf16[4,2,2,4,128,128]{5,4,3,2,1,0:T(8,128)(2,1)S(1)} %bitcast.43, ...), custom_call_target="tpu_custom_call" | custom-call | flops 1000000000 | bytes 10000000 | tf_op jit(solution)/shard_map/pallas_call | solution.py:269
  101.3 6.7 %shard_map.89.refs_5_ = f32[3,2,4,8,128]{4,3,2,1,0:T(8,128)S(1)} custom-call(s32[4]{0:T(128)S(1)} %pad_add_fusion.ids, s32[16,16]{1,0:T(8,128)S(1)} %copy-done.7, bf16[4,2,2,128,128]{4,3,2,1,0:T(8,128)(2,1)S(1)} %collective-permute-done.8.refs_0_, bf16[4,2,2,128,128]{4,3,2,1,0:T(8,128)(2,1)S(1)} %collective-permute-done.9.refs_1_.refs_0_, ...), custom_call_target="tpu_custom_call" | custom-call | flops 1000000000 | bytes 10000000 | tf_op jit(solution)/shard_map/pallas_call | solution.py:269
  108.0 3.7 %shard_map.90.refs_4_.refs_5_ = f32[2,4,2,128]{3,2,1,0:T(2,128)S(1)} custom-call(s32[4]{0:T(128)S(1)} %pad_add_fusion.ids, s32[16,16]{1,0:T(8,128)S(1)} %copy-done.7, bf16[2,2,2,128,128]{4,3,2,1,0:T(8,128)(2,1)S(1)} %collective-permute-done.6.refs_0_, bf16[2,2,2,128,128]{4,3,2,1,0:T(8,128)(2,1)S(1)} %collective-permute-done.7.refs_1_, ...), custom_call_target="tpu_custom_call" | custom-call | flops 1000000000 | bytes 10000000 | tf_op jit(solution)/shard_map/pallas_call | solution.py:269
  111.7 5.5 %shard_map.93 = (bf16[2,2,2,128,128]{4,3,2,1,0:T(8,128)(2,1)S(1)}, bf16[2,2,2,128,128]{4,3,2,1,0:T(8,128)(2,1)S(1)}, f32[2,4,64,128]{3,2,1,0:T(8,128)S(1)}) custom-call(s32[4]{0:T(128)S(1)} %pad_add_fusion.ids, s32[16,16]{1,0:T(8,128)S(1)} %copy-done.7, bf16[2,2,2,128,128]{4,3,2,1,0:T(8,128)(2,1)S(1)} %collective-permute-done.6.refs_0_, ...), custom_call_target="tpu_custom_call" | custom-call | flops 2000000000 | bytes 20000000 | tf_op jit(solution)/shard_map/pallas_call | solution.py:285
  119.1 5.5 %collective-permute-start.15 = (bf16[2,2,2,128,128]{4,3,2,1,0:T(8,128)(2,1)S(1)}, bf16[2,2,2,128,128]{4,3,2,1,0:T(8,128)(2,1)S(1)}, u32[]{:S(2)}, u32[]{:S(2)}) collective-permute-start(bf16[2,2,2,128,128]{4,3,2,1,0:T(8,128)(2,1)S(1)} %get-tuple-element.36), channel_id=1, source_target_pairs={{0,28},{2,30},{4,0},{6,2},{8,4},{10,6},{12,8},{14,10},{16,12},{18,... | collective-permute-start | bytes 786440 | tf_op jit(solution)/shard_map/ppermute | solution.py:302
  124.6 5.6 %shard_map.92 = (bf16[4,2,2,128,128]{4,3,2,1,0:T(8,128)(2,1)S(1)}, f32[2,4,64,128]{3,2,1,0:T(8,128)S(1)}) custom-call(s32[4]{0:T(128)S(1)} %pad_add_fusion.ids, s32[16,16]{1,0:T(8,128)S(1)} %copy-done.7, bf16[4,2,2,128,128]{4,3,2,1,0:T(8,128)(2,1)S(1)} %collective-permute-done.8.refs_0_, bf16[4,2,2,4,128,128]{5,4,3,2,1,0:T(8,128)(2,1)S(1)} %bitcast.47, ...), custom_call_target="tpu_custom_call" | custom-call | flops 2000000000 | bytes 20000000 | tf_op jit(solution)/shard_map/pallas_call | solution.py:285
  132.1 5.4 %shard_map.94 = (bf16[4,2,2,128,128]{4,3,2,1,0:T(8,128)(2,1)S(1)}, f32[2,4,64,128]{3,2,1,0:T(8,128)S(1)}) custom-call(s32[4]{0:T(128)S(1)} %pad_add_fusion.ids, s32[16,16]{1,0:T(8,128)S(1)} %copy-done.7, bf16[4,2,2,128,128]{4,3,2,1,0:T(8,128)(2,1)S(1)} %collective-permute-done.9.refs_1_.refs_0_, bf16[4,2,2,4,128,128]{5,4,3,2,1,0:T(8,128)(2,1)S(1)} %bitcast.48, ...), custom_call_target="tpu_custom_call" | custom-call | flops 2000000000 | bytes 20000000 | tf_op jit(solution)/shard_map/pallas_call | solution.py:285
  139.5 5.6 %shard_map.91 = (bf16[4,2,2,128,128]{4,3,2,1,0:T(8,128)(2,1)S(1)}, f32[2,4,64,128]{3,2,1,0:T(8,128)S(1)}) custom-call(s32[4]{0:T(128)S(1)} %pad_add_fusion.ids, s32[16,16]{1,0:T(8,128)S(1)} %copy-done.7, bf16[4,2,2,128,128]{4,3,2,1,0:T(8,128)(2,1)S(1)} %pad_maximum_fusion.refs_0_, bf16[4,2,2,4,128,128]{5,4,3,2,1,0:T(8,128)(2,1)S(1)} %bitcast.49, ...), custom_call_target="tpu_custom_call" | custom-call | flops 2000000000 | bytes 20000000 | tf_op jit(solution)/shard_map/pallas_call | solution.py:285
  145.2 4.5 %collective-permute-done.13 = bf16[4,2,2,128,128]{4,3,2,1,0:T(8,128)(2,1)S(1)} collective-permute-done((bf16[4,2,2,128,128]{4,3,2,1,0:T(8,128)(2,1)S(1)}, bf16[4,2,2,128,128]{4,3,2,1,0:T(8,128)(2,1)S(1)}, u32[]{:S(2)}, u32[]{:S(2)}) %collective-permute-start.13) | collective-permute-done | bytes 524320 | tf_op jit(solution)/shard_map/ppermute | solution.py:302
  150.0 4.6 %collective-permute-start.18 = (bf16[2,2,128,128]{3,2,1,0:T(8,128)(2,1)S(1)}, bf16[2,2,128,128]{3,2,1,0:T(8,128)(2,1)S(1)}, u32[]{:S(2)}, u32[]{:S(2)}) collective-permute-start(bf16[2,2,128,128]{3,2,1,0:T(8,128)(2,1)S(1)} %fusion.9), channel_id=1, source_target_pairs={{0,16},{2,18},{4,20},{6,22},{8,24},{10,26},{12,28},{14,30},{16,0},... | collective-permute-start | bytes 393224 | tf_op jit(solution)/shard_map/ppermute | solution.py:302
  157.2 7.0 %collective-permute-start.17 = (bf16[2,2,128,128]{3,2,1,0:T(8,128)(2,1)S(1)}, bf16[2,2,128,128]{3,2,1,0:T(8,128)(2,1)S(1)}, u32[]{:S(2)}, u32[]{:S(2)}) collective-permute-start(bf16[2,2,128,128]{3,2,1,0:T(8,128)(2,1)S(1)} %get-tuple-element.41), channel_id=1, source_target_pairs={{0,8},{2,10},{4,12},{6,14},{8,16},{10,18},{12,20},{14,22},{16,24},... | collective-permute-start | bytes 393224 | tf_op jit(solution)/shard_map/ppermute | solution.py:302
  170.3 6.2 %collective-permute-start.11 = (bf16[4,64,128]{2,1,0:T(8,128)(2,1)S(1)}, bf16[4,64,128]{2,1,0:T(8,128)(2,1)S(1)}, u32[]{:S(2)}, u32[]{:S(2)}) collective-permute-start(bf16[4,64,128]{2,1,0:T(8,128)(2,1)S(1)} %get-tuple-element.31), channel_id=1, source_target_pairs={{0,1},{1,0},{2,3},{3,2},{4,5},{5,4},{6,7},{7,6},{8,9},{9,8},{10,11... | collective-permute-start | bytes 196616 | tf_op jit(solution)/shard_map/ppermute | solution.py:343
  176.5 6.1 %collective-permute-done.16 = bf16[2,2,128,128]{3,2,1,0:T(8,128)(2,1)S(1)} collective-permute-done((bf16[2,2,128,128]{3,2,1,0:T(8,128)(2,1)S(1)}, bf16[2,2,128,128]{3,2,1,0:T(8,128)(2,1)S(1)}, u32[]{:S(2)}, u32[]{:S(2)}) %collective-permute-start.16) | collective-permute-done | bytes 131104 | tf_op jit(solution)/shard_map/ppermute | solution.py:302
  188.6 3.6 %collective-permute-start.20 = (bf16[4,128,128]{2,1,0:T(8,128)(2,1)S(1)}, bf16[4,128,128]{2,1,0:T(8,128)(2,1)S(1)}, u32[]{:S(2)}, u32[]{:S(2)}) collective-permute-start(bf16[4,128,128]{2,1,0:T(8,128)(2,1)S(1)} %get-tuple-element.39), channel_id=1, source_target_pairs={{0,1},{1,0},{2,3},{3,2},{4,5},{5,4},{6,7},{7,6},{8,9},{9,8},{10,11... | collective-permute-start | bytes 393224 | tf_op jit(solution)/shard_map/ppermute | solution.py:360
  (68 shorter events, 44.4 us)
Async XLA Ops:
  7.2 18.2 %copy-start = (bf16[4,128,128]{2,1,0:T(8,128)(2,1)S(1)}, bf16[4,128,128]{2,1,0:T(8,128)(2,1)}, u32[]{:S(2)}) copy-start(bf16[4,128,128]{2,1,0:T(8,128)(2,1)} %pair.3) | copy-start | bytes 393220
  7.2 85.4 %all-gather.3.cloned.1.call-start = ((), (), s32[]{:S(2)}) async-start(), calls=%async_computation | async-start | bytes 2621440 | tf_op jit(solution)/shard_map/all_gather | solution.py:320
  8.9 6.3 %collective-permute-start.4 = (bf16[4,128,128]{2,1,0:T(8,128)(2,1)S(1)}, bf16[4,128,128]{2,1,0:T(8,128)(2,1)S(1)}, u32[]{:S(2)}, u32[]{:S(2)}) collective-permute-start(bf16[4,128,128]{2,1,0:T(8,128)(2,1)S(1)} %get-tuple-element.24), channel_id=1, source_target_pairs={{0,32},{32,0},{1,33},{33,1},{2,34},{34,2},{3,35},{35,3},{4,36},{36... | collective-permute-start | bytes 393224 | tf_op jit(solution)/shard_map/ppermute | solution.py:318
  15.3 9.2 %collective-permute-start.5 = (bf16[2,4,128,128]{3,2,1,0:T(8,128)(2,1)S(1)}, bf16[2,4,128,128]{3,2,1,0:T(8,128)(2,1)S(1)}, u32[]{:S(2)}, u32[]{:S(2)}) collective-permute-start(bf16[2,4,128,128]{3,2,1,0:T(8,128)(2,1)S(1)} %get-tuple-element.45), channel_id=1, source_target_pairs={{0,256},{256,0},{1,257},{257,1},{2,258},{258,2},{3,259},{259,3},{4... | collective-permute-start | bytes 786440 | tf_op jit(solution)/shard_map/ppermute | solution.py:319
  24.5 68.1 %copy-start.7 = (s32[16,16]{1,0:T(8,128)S(1)}, s32[16,16]{1,0:T(8,128)}, u32[]{:S(2)}) copy-start(s32[16,16]{1,0:T(8,128)} %act.13) | copy-start | bytes 3076
  26.6 5.7 %collective-permute-start = (bf16[512,128]{1,0:T(8,128)(2,1)S(1)}, bf16[512,128]{1,0:T(8,128)(2,1)S(1)}, u32[]{:S(2)}, u32[]{:S(2)}) collective-permute-start(bf16[512,128]{1,0:T(8,128)(2,1)S(1)} %get-tuple-element.22), channel_id=1, source_target_pairs={{0,32},{32,0},{1,33},{33,1},{2,34},{34,2},{3,35},{35,3},{4,36},{36... | collective-permute-start | bytes 393224 | tf_op jit(solution)/shard_map/ppermute | solution.py:316
  32.3 25.9 %collective-permute-start.2 = (bf16[2,2,128,128]{3,2,1,0:T(8,128)(2,1)S(1)}, bf16[2,2,128,128]{3,2,1,0:T(8,128)(2,1)S(1)}, u32[]{:S(2)}, u32[]{:S(2)}) collective-permute-start(bf16[2,2,128,128]{3,2,1,0:T(8,128)(2,1)S(1)} %get-tuple-element.49), channel_id=1, source_target_pairs={{0,24},{2,26},{4,28},{6,30},{8,0},{10,2},{12,4},{14,6},{16,8},{18,... | collective-permute-start | bytes 393224 | tf_op jit(solution)/shard_map/ppermute | solution.py:302
  46.0 14.9 %collective-permute-start.3 = (bf16[2,2,128,128]{3,2,1,0:T(8,128)(2,1)S(1)}, bf16[2,2,128,128]{3,2,1,0:T(8,128)(2,1)S(1)}, u32[]{:S(2)}, u32[]{:S(2)}) collective-permute-start(bf16[2,2,128,128]{3,2,1,0:T(8,128)(2,1)S(1)} %get-tuple-element.49), channel_id=1, source_target_pairs={{0,16},{2,18},{4,20},{6,22},{8,24},{10,26},{12,28},{14,30},{16,0},... | collective-permute-start | bytes 393224 | tf_op jit(solution)/shard_map/ppermute | solution.py:302
  50.9 16.9 %collective-permute-start.1 = (bf16[2,2,128,128]{3,2,1,0:T(8,128)(2,1)S(1)}, bf16[2,2,128,128]{3,2,1,0:T(8,128)(2,1)S(1)}, u32[]{:S(2)}, u32[]{:S(2)}) collective-permute-start(bf16[2,2,128,128]{3,2,1,0:T(8,128)(2,1)S(1)} %get-tuple-element.49), channel_id=1, source_target_pairs={{0,8},{2,10},{4,12},{6,14},{8,16},{10,18},{12,20},{14,22},{16,24},... | collective-permute-start | bytes 393224 | tf_op jit(solution)/shard_map/ppermute | solution.py:302
  67.9 30.0 %collective-permute-start.9 = (bf16[4,2,2,128,128]{4,3,2,1,0:T(8,128)(2,1)S(1)}, bf16[4,2,2,128,128]{4,3,2,1,0:T(8,128)(2,1)S(1)}, u32[]{:S(2)}, u32[]{:S(2)}) collective-permute-start(bf16[4,2,2,128,128]{4,3,2,1,0:T(8,128)(2,1)S(1)} %pad_maximum_fusion.refs_0_), channel_id=1, source_target_pairs={{0,2},{2,4},{4,6},{6,8},{8,10},{10,12},{12,14},{14,16},{16,18},{18... | collective-permute-start | bytes 1572872 | tf_op jit(solution)/shard_map/ppermute | solution.py:302
  75.8 25.5 %collective-permute-start.8 = (bf16[4,2,2,128,128]{4,3,2,1,0:T(8,128)(2,1)S(1)}, bf16[4,2,2,128,128]{4,3,2,1,0:T(8,128)(2,1)S(1)}, u32[]{:S(2)}, u32[]{:S(2)}) collective-permute-start(bf16[4,2,2,128,128]{4,3,2,1,0:T(8,128)(2,1)S(1)} %pad_maximum_fusion.refs_0_), channel_id=1, source_target_pairs={{0,30},{2,0},{4,2},{6,4},{8,6},{10,8},{12,10},{14,12},{16,14},{18,... | collective-permute-start | bytes 1572872 | tf_op jit(solution)/shard_map/ppermute | solution.py:302
  85.1 22.9 %collective-permute-start.7 = (bf16[2,2,2,128,128]{4,3,2,1,0:T(8,128)(2,1)S(1)}, bf16[2,2,2,128,128]{4,3,2,1,0:T(8,128)(2,1)S(1)}, u32[]{:S(2)}, u32[]{:S(2)}) collective-permute-start(bf16[2,2,2,128,128]{4,3,2,1,0:T(8,128)(2,1)S(1)} %get-tuple-element.46), channel_id=1, source_target_pairs={{0,4},{2,6},{4,8},{6,10},{8,12},{10,14},{12,16},{14,18},{16,20},{1... | collective-permute-start | bytes 786440 | tf_op jit(solution)/shard_map/ppermute | solution.py:302
  87.0 21.0 %collective-permute-start.6 = (bf16[2,2,2,128,128]{4,3,2,1,0:T(8,128)(2,1)S(1)}, bf16[2,2,2,128,128]{4,3,2,1,0:T(8,128)(2,1)S(1)}, u32[]{:S(2)}, u32[]{:S(2)}) collective-permute-start(bf16[2,2,2,128,128]{4,3,2,1,0:T(8,128)(2,1)S(1)} %get-tuple-element.47), channel_id=1, source_target_pairs={{0,28},{2,30},{4,0},{6,2},{8,4},{10,6},{12,8},{14,10},{16,12},{18,... | collective-permute-start | bytes 786440 | tf_op jit(solution)/shard_map/ppermute | solution.py:302
  117.2 37.4 %collective-permute-start.14 = (bf16[2,2,2,128,128]{4,3,2,1,0:T(8,128)(2,1)S(1)}, bf16[2,2,2,128,128]{4,3,2,1,0:T(8,128)(2,1)S(1)}, u32[]{:S(2)}, u32[]{:S(2)}) collective-permute-start(bf16[2,2,2,128,128]{4,3,2,1,0:T(8,128)(2,1)S(1)} %get-tuple-element.35), channel_id=1, source_target_pairs={{0,4},{2,6},{4,8},{6,10},{8,12},{10,14},{12,16},{14,18},{16,20},{1... | collective-permute-start | bytes 786440 | tf_op jit(solution)/shard_map/ppermute | solution.py:302
  119.1 35.5 %collective-permute-start.15 = (bf16[2,2,2,128,128]{4,3,2,1,0:T(8,128)(2,1)S(1)}, bf16[2,2,2,128,128]{4,3,2,1,0:T(8,128)(2,1)S(1)}, u32[]{:S(2)}, u32[]{:S(2)}) collective-permute-start(bf16[2,2,2,128,128]{4,3,2,1,0:T(8,128)(2,1)S(1)} %get-tuple-element.36), channel_id=1, source_target_pairs={{0,28},{2,30},{4,0},{6,2},{8,4},{10,6},{12,8},{14,10},{16,12},{18,... | collective-permute-start | bytes 786440 | tf_op jit(solution)/shard_map/ppermute | solution.py:302
  130.2 15.0 %collective-permute-start.12 = (bf16[4,2,2,128,128]{4,3,2,1,0:T(8,128)(2,1)S(1)}, bf16[4,2,2,128,128]{4,3,2,1,0:T(8,128)(2,1)S(1)}, u32[]{:S(2)}, u32[]{:S(2)}) collective-permute-start(bf16[4,2,2,128,128]{4,3,2,1,0:T(8,128)(2,1)S(1)} %get-tuple-element.33), channel_id=1, source_target_pairs={{0,2},{2,4},{4,6},{6,8},{8,10},{10,12},{12,14},{14,16},{16,18},{18... | collective-permute-start | bytes 1572872 | tf_op jit(solution)/shard_map/ppermute | solution.py:302
  137.5 12.2 %collective-permute-start.13 = (bf16[4,2,2,128,128]{4,3,2,1,0:T(8,128)(2,1)S(1)}, bf16[4,2,2,128,128]{4,3,2,1,0:T(8,128)(2,1)S(1)}, u32[]{:S(2)}, u32[]{:S(2)}) collective-permute-start(bf16[4,2,2,128,128]{4,3,2,1,0:T(8,128)(2,1)S(1)} %get-tuple-element.34), channel_id=1, source_target_pairs={{0,30},{2,0},{4,2},{6,4},{8,6},{10,8},{12,10},{14,12},{16,14},{18,... | collective-permute-start | bytes 1572872 | tf_op jit(solution)/shard_map/ppermute | solution.py:302
  150.0 26.5 %collective-permute-start.18 = (bf16[2,2,128,128]{3,2,1,0:T(8,128)(2,1)S(1)}, bf16[2,2,128,128]{3,2,1,0:T(8,128)(2,1)S(1)}, u32[]{:S(2)}, u32[]{:S(2)}) collective-permute-start(bf16[2,2,128,128]{3,2,1,0:T(8,128)(2,1)S(1)} %fusion.9), channel_id=1, source_target_pairs={{0,16},{2,18},{4,20},{6,22},{8,24},{10,26},{12,28},{14,30},{16,0},... | collective-permute-start | bytes 393224 | tf_op jit(solution)/shard_map/ppermute | solution.py:302
  154.7 27.9 %collective-permute-start.16 = (bf16[2,2,128,128]{3,2,1,0:T(8,128)(2,1)S(1)}, bf16[2,2,128,128]{3,2,1,0:T(8,128)(2,1)S(1)}, u32[]{:S(2)}, u32[]{:S(2)}) collective-permute-start(bf16[2,2,128,128]{3,2,1,0:T(8,128)(2,1)S(1)} %get-tuple-element.40), channel_id=1, source_target_pairs={{0,24},{2,26},{4,28},{6,30},{8,0},{10,2},{12,4},{14,6},{16,8},{18,... | collective-permute-start | bytes 393224 | tf_op jit(solution)/shard_map/ppermute | solution.py:302
  157.2 25.4 %collective-permute-start.17 = (bf16[2,2,128,128]{3,2,1,0:T(8,128)(2,1)S(1)}, bf16[2,2,128,128]{3,2,1,0:T(8,128)(2,1)S(1)}, u32[]{:S(2)}, u32[]{:S(2)}) collective-permute-start(bf16[2,2,128,128]{3,2,1,0:T(8,128)(2,1)S(1)} %get-tuple-element.41), channel_id=1, source_target_pairs={{0,8},{2,10},{4,12},{6,14},{8,16},{10,18},{12,20},{14,22},{16,24},... | collective-permute-start | bytes 393224 | tf_op jit(solution)/shard_map/ppermute | solution.py:302
  164.2 5.3 %collective-permute-start.10 = (bf16[4,64,128]{2,1,0:T(8,128)(2,1)S(1)}, bf16[4,64,128]{2,1,0:T(8,128)(2,1)S(1)}, u32[]{:S(2)}, u32[]{:S(2)}) collective-permute-start(bf16[4,64,128]{2,1,0:T(8,128)(2,1)S(1)} %fusion.14), channel_id=1, source_target_pairs={{0,32},{32,0},{1,33},{33,1},{2,34},{34,2},{3,35},{35,3},{4,36},{36... | collective-permute-start | bytes 196616 | tf_op jit(solution)/shard_map/ppermute | solution.py:339
  170.3 22.0 %collective-permute-start.11 = (bf16[4,64,128]{2,1,0:T(8,128)(2,1)S(1)}, bf16[4,64,128]{2,1,0:T(8,128)(2,1)S(1)}, u32[]{:S(2)}, u32[]{:S(2)}) collective-permute-start(bf16[4,64,128]{2,1,0:T(8,128)(2,1)S(1)} %get-tuple-element.31), channel_id=1, source_target_pairs={{0,1},{1,0},{2,3},{3,2},{4,5},{5,4},{6,7},{7,6},{8,9},{9,8},{10,11... | collective-permute-start | bytes 196616 | tf_op jit(solution)/shard_map/ppermute | solution.py:343
  182.7 5.0 %collective-permute-start.19 = (bf16[2,128,128]{2,1,0:T(8,128)(2,1)S(1)}, bf16[2,128,128]{2,1,0:T(8,128)(2,1)S(1)}, u32[]{:S(2)}, u32[]{:S(2)}) collective-permute-start(bf16[2,128,128]{2,1,0:T(8,128)(2,1)S(1)} %fusion.13), channel_id=1, source_target_pairs={{0,32},{32,0},{1,33},{33,1},{2,34},{34,2},{3,35},{35,3},{4,36},{36... | collective-permute-start | bytes 196616 | tf_op jit(solution)/shard_map/ppermute | solution.py:351
  188.6 4.5 %collective-permute-start.20 = (bf16[4,128,128]{2,1,0:T(8,128)(2,1)S(1)}, bf16[4,128,128]{2,1,0:T(8,128)(2,1)S(1)}, u32[]{:S(2)}, u32[]{:S(2)}) collective-permute-start(bf16[4,128,128]{2,1,0:T(8,128)(2,1)S(1)} %get-tuple-element.39), channel_id=1, source_target_pairs={{0,1},{1,0},{2,3},{3,2},{4,5},{5,4},{6,7},{7,6},{8,9},{9,8},{10,11... | collective-permute-start | bytes 393224 | tf_op jit(solution)/shard_map/ppermute | solution.py:360
  (6 other events, 71.1 us)
Sparse Core Ops, SparseCore 0:
  25.5 46.0 all-gather.2

commit v3 on v2

--- a/solution.py
+++ b/solution.py
@@ -50,12 +50,12 @@
     return jnp.dot(a, b, preferred_element_type=F32)
 
 
-def bias_kernel(ids, bias, keep, send):
-    xl = ids[1]
+def bias_kernel(bias, send):
     for j in range(4):
-        cols = pl.ds(j * 128, 128)
-        keep[j] = bias[xl, :, cols].T
-        send[j] = bias[1 - xl, :, cols].T
+        for h in range(2):
+            block = bias[h, :, 128 * j : 128 * j + 128].T
+            send[h, j] = block
+            send[2 + h, j] = block
 
 
 def norm(x):
@@ -116,7 +116,7 @@
     for u in units:
         zk = (ids[0] + first + 4 * (u // 2) + 32) % 16
         xk = jnp.where(u % 2 == 0, ids[1], 1 - ids[1])
-        b.append(bias[zk // 4, jnp.where(xk == ids[3], 0, 1), half, zk % 4].astype(F32))
+        b.append(bias[zk // 4, xk, jnp.where(half == 0, ids[1], 1 - ids[1]), zk % 4].astype(F32))
     keys = [k[0] if len(k) == 1 else jnp.concatenate(k, axis=0) for k in keys]
     return keys, b[0] if len(b) == 1 else jnp.concatenate(b, axis=0)
 
@@ -234,10 +234,22 @@
         send[r] = jnp.where(c == 0, high, low).astype(BF16)
 
 
+def sum_kernel(ids, d_own, r_up, r_down, r_up2, r_down2, out):
+    m = ids[0] // 4
+    for e in range(4):
+        total = d_own[e].astype(F32) + r_up[e].astype(F32) + r_down[e].astype(F32)
+        if e in (1, 2):
+            total += r_up2[e - 1].astype(F32)
+        if e in (0, 1):
+            total += r_down2[e].astype(F32)
+        out[(m + e + 3) % 4] = total.astype(BF16)
+
+
 def proj_kernel(ids, oq_own, oq_other, dkv_own, dkv_other, gate, go, w_proj, keep, send, dp):
     xl = ids[1]
     for p in range(2):
-        mine_kv, theirs_kv = dkv_own[p].astype(F32).T, dkv_other[p].astype(F32).T
+        mine_kv = sum(dkv_own[m, 0, p].astype(F32) for m in range(4)).T
+        theirs_kv = dkv_other[p].astype(F32).T
         for i in range(2):
             r = 2 * p + i
             for oq, kvt, h in (
@@ -303,8 +315,7 @@
 
 
 def per_device(pair, gain, w_proj, w_out, tri_bias, active, d_out):
-    z, xl, c, xh = (lax.axis_index(name) for name in ("z", "xl", "c", "xh"))
-    ids = jnp.stack([z, xl, c, xh]).astype(jnp.int32)
+    ids = jnp.stack([lax.axis_index(name) for name in ("z", "xl", "c")]).astype(jnp.int32)
     gain = gain.reshape(1, 128)
     pack, pack_send, gate, go = call(
         prep_kernel,
@@ -314,9 +325,10 @@
         [pltpu.VMEM((2, 256, 128), F32)],
     )(ids, pair, gain, w_proj, w_out, d_out)
     pack_other = lax.ppermute(pack_send, "xl", SWAP)
-    bias_keep, bias_send = call(bias_kernel, [((4, 128, 128), BF16)] * 2, 1, 1)(ids, tri_bias)
-    bias = jnp.stack([bias_keep, lax.ppermute(bias_send, "xl", SWAP)])
-    bias = jnp.stack([bias, lax.ppermute(bias, "xh", SWAP)])
+    tri_bias, _ = lax.optimization_barrier((tri_bias, pack_send))
+    (bias,) = call(bias_kernel, [((4, 4, 128, 128), BF16)], 0, 1)(tri_bias)
+    bias = lax.all_to_all(bias, ("xh", "xl"), 0, 0, tiled=True).reshape(2, 2, 4, 128, 128)
+    bias, pack_other = lax.optimization_barrier((bias, pack_other))
     bias = lax.all_gather(bias, "y")
     kv = jnp.stack([pack[:256].reshape(2, 128, 128), pack_other[:256].reshape(2, 128, 128)])
     own = jnp.stack([to_z(kv, 4), kv, to_z(kv, -4), to_z(kv, 8)])
@@ -326,14 +338,13 @@
     state = stats_call((-4,), True, False, ids, active, (own,), rest)
     state = stats_call((-3, -5), False, False, ids, active, (up, down), rest + (state,))
     stats = stats_call((2, -6), False, True, ids, active, (up2, down2), rest + (state,))
-    rest = rest + (stats,)
-    (d_up2, d_down2), oq2 = back_call((2, -6), ids, active, (up2, down2), rest)
+    (d_up,), oq1 = back_call((-3,), ids, active, (up,), rest + (stats,))
+    r_up = to_z(d_up, 1)
+    (d_down,), oq3 = back_call((-5,), ids, active, (down,), rest + (stats,))
+    r_down = to_z(d_down, -1)
+    (d_up2, d_down2), oq2 = back_call((2, -6), ids, active, (up2, down2), rest + (stats,))
     r_up2, r_down2 = to_z(d_up2, 2), to_z(d_down2, -2)
-    (d_up,), oq1 = back_call((-3,), ids, active, (up,), rest)
-    r_up = to_z(d_up, 1)
-    (d_down,), oq3 = back_call((-5,), ids, active, (down,), rest)
-    r_down = to_z(d_down, -1)
-    (d_own,), oq0 = back_call((-4,), ids, active, (own,), rest)
+    (d_own,), oq0 = back_call((-4,), ids, active, (own,), rest + (stats,))
     oq = oq0 + oq1 + oq2 + oq3
     oq = jnp.concatenate([oq[:, :, :32] * SCALE, oq[:, :, 32:]], axis=2)
     oq_other = lax.ppermute(oq[1].astype(BF16), "xl", SWAP)
@@ -341,21 +352,20 @@
         out_kernel, [((4, 64, 128), F32), ((4, 64, 128), BF16)], 1, 4
     )(ids, oq, oq_other, gate, w_out)
     out = (out_keep + lax.ppermute(out_send, "c", SWAP).astype(F32)).astype(BF16)
-    f = lambda x: x.astype(F32)
-    sums = f(d_own) + f(r_up) + f(r_down)
-    s0 = (sums[0] + f(r_down2[0])).astype(BF16)
-    s1 = sums[1] + f(r_up2[0]) + f(r_down2[1])
-    s2 = (sums[2] + f(r_up2[1])).astype(BF16)
-    s3 = sums[3].astype(BF16)
-    dkv = s1 + f(to_z(s0, -4)) + f(to_z(s2, 4)) + f(to_z(s3, 8))
-    dkv_other = lax.ppermute(dkv[1].astype(BF16), "xl", SWAP)
+    (sums,) = call(sum_kernel, [((4, 2, 2, 128, 128), BF16)], 1, 5)(
+        ids, d_own, r_up, r_down, r_up2, r_down2
+    )
+    groups = [[k + 4 * m for m in range(4)] for k in range(4)]
+    dkv = lax.all_to_all(sums, "z", 0, 0, axis_index_groups=groups, tiled=True)
+    theirs = jnp.sum(dkv[:, 1].astype(F32), axis=0).astype(BF16)
+    dkv_other = lax.ppermute(theirs, "xl", SWAP)
     part, part_send = call(
         proj_kernel,
         [((4, 128, 128), F32), ((4, 128, 128), BF16)],
         1,
         7,
         [pltpu.VMEM((256, 128), F32)],
-    )(ids, oq, oq_other, dkv[0], dkv_other, gate, go, w_proj)
+    )(ids, oq, oq_other, dkv, dkv_other, gate, go, w_proj)
     (pair_gradient,) = call(final_kernel, [((4, 128, 128), BF16)], 0, 4)(
         pair, gain, part, lax.ppermute(part_send, "c", SWAP)
     )

time: 202 us -> 205 us (1.015)
  waiting for transfers between devices: 38.2 us -> 47 us
  Pallas kernels: 40.9 us -> 35 us
  local copies, waits for them, and re-layouts: 2.61 us -> 7.4 us
  starting transfers between devices: 103 us -> 98.3 us
    all_to_all x0 -> x2, waiting for transfers between devices: none -> 25 us  [the longest x1 24.9 us: per_device(): dkv = lax.all_to_all(sums, 'z', 0, 0, axis_index_groups=groups, tiled=True)]
    all_to_all x0 -> x2, starting transfers between devices: none -> 16.7 us  [the longest x1 11.8 us: per_device(): dkv = lax.all_to_all(sums, 'z', 0, 0, axis_index_groups=groups, tiled=True)]
    ppermute x3 -> x1, starting transfers between devices: 11.4 us -> 2.2 us  [per_device(): dkv_other = lax.ppermute(theirs, 'xl', SWAP)]
    ppermute x3 -> x1, waiting for transfers between devices: 9.1 us -> 0.01 us  [per_device(): dkv_other = lax.ppermute(theirs, 'xl', SWAP)]
    ppermute x14 -> x11, starting transfers between devices: 75.7 us -> 68.2 us  [to_z(): return lax.ppermute(x, 'z', [(j, (j + step) % 16) for j in range(16)])]
    ppermute x14 -> x11, waiting for transfers between devices: 23.6 us -> 18.1 us  [to_z(): return lax.ppermute(x, 'z', [(j, (j + step) % 16) for j in range(16)])]
    unnamed x16 -> x28, local copies, waits for them, and re-layouts: 2.56 us -> 7.39 us
    pallas_call x4, Pallas kernels: 22.1 us -> 17.5 us  [back_call(): call(functools.partial(back_kernel, firsts), [(kv.shape, BF16) for kv in...]
  transfers between devices with their start and end apart: 22 -> 19, of which waited for: 11 -> 10; matrix products, arithmetic and copies ran while one was open for 1% -> 1% of each run, Pallas kernels for 15% -> 11%
where the time goes in v3:
time: 205 us; the launch traced here: 204 us
  starting transfers between devices  98.3 us (48%)
  waiting for transfers between devices  47 us (23%)
  Pallas kernels  35 us (17%)
  between operations  14.4 us (7%)
  local copies, waits for them, and re-layouts  7.4 us (4%)
    ppermute x11, starting transfers between devices, to_z(): return lax.ppermute(x, 'z', [(j, (j + step) % 16) for j in range(16)])  68.2 us
    all_to_all x1, waiting for transfers between devices, per_device(): dkv = lax.all_to_all(sums, 'z', 0, 0, axis_index_groups=groups, tiled=True)  24.9 us
    ppermute x11, waiting for transfers between devices, to_z(): return lax.ppermute(x, 'z', [(j, (j + step) % 16) for j in range(16)])  18.1 us
    pallas_call x4, Pallas kernels, back_call(): call(functools.partial(back_kernel, firsts), [(kv.shape, BF16) for kv in...  17.5 us
    all_to_all x1, starting transfers between devices, per_device(): dkv = lax.all_to_all(sums, 'z', 0, 0, axis_index_groups=groups, tiled=True)  11.8 us
    pallas_call x3, Pallas kernels, stats_call(): call(functools.partial(stats_kernel, firsts, begin, end), [out], 2, len(k...  11 us
    unnamed x28, local copies, waits for them, and re-layouts  7.39 us
    all_to_all x1, starting transfers between devices, per_device(): lax.all_to_all(bias, ('xh', 'xl'), 0, 0, tiled=True)  4.97 us
  transfers between devices with their start and end apart: 19, of which 10 were waited for; matrix products, arithmetic and copies ran while one was open for 1% of the time, Pallas kernels for 11%

profile of v3, /device:TPU:1, one launch (start us, length us, event | category | flops | bytes accessed | tf_op | source)
XLA Modules:
  0.0 203.7 jit_solution(17134834623695679974)
XLA Ops:
  14.3 5.0 %all-to-all-start = ((bf16[4,4,128,128]{3,2,1,0:T(8,128)(2,1)}), bf16[4,4,128,128]{3,2,1,0:T(8,128)(2,1)S(1)}, u32[]{:S(2)}, u32[]{:S(2)}) async-start(bf16[4,4,128,128]{3,2,1,0:T(8,128)(2,1)} %shard_map.87), calls=%async_computation | async-start | bytes 1048576 | tf_op jit(solution)/shard_map/all_to_all | solution.py:330
  19.3 3.4 %collective-permute-start = (bf16[512,128]{1,0:T(8,128)(2,1)S(1)}, bf16[512,128]{1,0:T(8,128)(2,1)S(1)}, u32[]{:S(2)}, u32[]{:S(2)}) collective-permute-start(bf16[512,128]{1,0:T(8,128)(2,1)S(1)} %get-tuple-element.23), channel_id=1, source_target_pairs={{0,32},{32,0},{1,33},{33,1},{2,34},{34,2},{3,35},{35,3},{4,36},{36... | collective-permute-start | bytes 393224 | tf_op jit(solution)/shard_map/ppermute | solution.py:327
  22.6 3.5 %collective-permute-done.refs_3_.refs_4_ = bf16[512,128]{1,0:T(8,128)(2,1)S(1)} collective-permute-done((bf16[512,128]{1,0:T(8,128)(2,1)S(1)}, bf16[512,128]{1,0:T(8,128)(2,1)S(1)}, u32[]{:S(2)}, u32[]{:S(2)}) %collective-permute-start) | collective-permute-done | bytes 131104 | tf_op jit(solution)/shard_map/ppermute | solution.py:327
  27.1 15.4 %collective-permute-start.2 = (bf16[2,2,128,128]{3,2,1,0:T(8,128)(2,1)S(1)}, bf16[2,2,128,128]{3,2,1,0:T(8,128)(2,1)S(1)}, u32[]{:S(2)}, u32[]{:S(2)}) collective-permute-start(bf16[2,2,128,128]{3,2,1,0:T(8,128)(2,1)S(1)} %get-tuple-element.47), channel_id=1, source_target_pairs={{0,24},{2,26},{4,28},{6,30},{8,0},{10,2},{12,4},{14,6},{16,8},{18,... | collective-permute-start | bytes 393224 | tf_op jit(solution)/shard_map/ppermute | solution.py:314
  42.5 4.9 %collective-permute-start.3 = (bf16[2,2,128,128]{3,2,1,0:T(8,128)(2,1)S(1)}, bf16[2,2,128,128]{3,2,1,0:T(8,128)(2,1)S(1)}, u32[]{:S(2)}, u32[]{:S(2)}) collective-permute-start(bf16[2,2,128,128]{3,2,1,0:T(8,128)(2,1)S(1)} %get-tuple-element.47), channel_id=1, source_target_pairs={{0,16},{2,18},{4,20},{6,22},{8,24},{10,26},{12,28},{14,30},{16,0},... | collective-permute-start | bytes 393224 | tf_op jit(solution)/shard_map/ppermute | solution.py:314
  47.4 7.3 %collective-permute-start.1 = (bf16[2,2,128,128]{3,2,1,0:T(8,128)(2,1)S(1)}, bf16[2,2,128,128]{3,2,1,0:T(8,128)(2,1)S(1)}, u32[]{:S(2)}, u32[]{:S(2)}) collective-permute-start(bf16[2,2,128,128]{3,2,1,0:T(8,128)(2,1)S(1)} %get-tuple-element.47), channel_id=1, source_target_pairs={{0,8},{2,10},{4,12},{6,14},{8,16},{10,18},{12,20},{14,22},{16,24},... | collective-permute-start | bytes 393224 | tf_op jit(solution)/shard_map/ppermute | solution.py:314
  57.4 5.5 %collective-permute-done.1 = bf16[2,2,128,128]{3,2,1,0:T(8,128)(2,1)S(1)} collective-permute-done((bf16[2,2,128,128]{3,2,1,0:T(8,128)(2,1)S(1)}, bf16[2,2,128,128]{3,2,1,0:T(8,128)(2,1)S(1)}, u32[]{:S(2)}, u32[]{:S(2)}) %collective-permute-start.1) | collective-permute-done | bytes 131104 | tf_op jit(solution)/shard_map/ppermute | solution.py:314
  63.0 8.1 %collective-permute-start.7 = (bf16[4,2,2,128,128]{4,3,2,1,0:T(8,128)(2,1)S(1)}, bf16[4,2,2,128,128]{4,3,2,1,0:T(8,128)(2,1)S(1)}, u32[]{:S(2)}, u32[]{:S(2)}) collective-permute-start(bf16[4,2,2,128,128]{4,3,2,1,0:T(8,128)(2,1)S(1)} %pad_maximum_fusion.refs_0_), channel_id=1, source_target_pairs={{0,2},{2,4},{4,6},{6,8},{8,10},{10,12},{12,14},{14,16},{16,18},{18... | collective-permute-start | bytes 1572872 | tf_op jit(solution)/shard_map/ppermute | solution.py:314
  71.1 10.4 %collective-permute-start.6 = (bf16[4,2,2,128,128]{4,3,2,1,0:T(8,128)(2,1)S(1)}, bf16[4,2,2,128,128]{4,3,2,1,0:T(8,128)(2,1)S(1)}, u32[]{:S(2)}, u32[]{:S(2)}) collective-permute-start(bf16[4,2,2,128,128]{4,3,2,1,0:T(8,128)(2,1)S(1)} %pad_maximum_fusion.refs_0_), channel_id=1, source_target_pairs={{0,30},{2,0},{4,2},{6,4},{8,6},{10,8},{12,10},{14,12},{16,14},{18,... | collective-permute-start | bytes 1572872 | tf_op jit(solution)/shard_map/ppermute | solution.py:314
  84.2 5.5 %collective-permute-start.4 = (bf16[2,2,2,128,128]{4,3,2,1,0:T(8,128)(2,1)S(1)}, bf16[2,2,2,128,128]{4,3,2,1,0:T(8,128)(2,1)S(1)}, u32[]{:S(2)}, u32[]{:S(2)}) collective-permute-start(bf16[2,2,2,128,128]{4,3,2,1,0:T(8,128)(2,1)S(1)} %get-tuple-element.45), channel_id=1, source_target_pairs={{0,28},{2,30},{4,0},{6,2},{8,4},{10,6},{12,8},{14,10},{16,12},{18,... | collective-permute-start | bytes 786440 | tf_op jit(solution)/shard_map/ppermute | solution.py:314
  91.3 3.2 %shard_map.88.refs_5_ = f32[3,2,4,8,128]{4,3,2,1,0:T(8,128)S(1)} custom-call(s32[3]{0:T(128)S(1)} %pad_add_fusion.ids, s32[16,16]{1,0:T(8,128)S(1)} %copy-done.12, bf16[4,2,2,128,128]{4,3,2,1,0:T(8,128)(2,1)S(1)} %pad_maximum_fusion.refs_0_, bf16[4,2,2,4,128,128]{5,4,3,2,1,0:T(8,128)(2,1)S(1)} %bitcast.19, ...), custom_call_target="tpu_custom_call" | custom-call | flops 1000000000 | bytes 10000000 | tf_op jit(solution)/shard_map/pallas_call | solution.py:281
  94.5 3.4 %collective-permute-done.6.refs_0_ = bf16[4,2,2,128,128]{4,3,2,1,0:T(8,128)(2,1)S(1)} collective-permute-done((bf16[4,2,2,128,128]{4,3,2,1,0:T(8,128)(2,1)S(1)}, bf16[4,2,2,128,128]{4,3,2,1,0:T(8,128)(2,1)S(1)}, u32[]{:S(2)}, u32[]{:S(2)}) %collective-permute-start.6) | collective-permute-done | bytes 524320 | tf_op jit(solution)/shard_map/ppermute | solution.py:314
  97.9 5.0 %shard_map.89.refs_5_ = f32[3,2,4,8,128]{4,3,2,1,0:T(8,128)S(1)} custom-call(s32[3]{0:T(128)S(1)} %pad_add_fusion.ids, s32[16,16]{1,0:T(8,128)S(1)} %copy-done.12, bf16[4,2,2,128,128]{4,3,2,1,0:T(8,128)(2,1)S(1)} %collective-permute-done.6.refs_0_, bf16[4,2,2,128,128]{4,3,2,1,0:T(8,128)(2,1)S(1)} %collective-permute-done.7.refs_1_.refs_0_, ...), custom_call_target="tpu_custom_call" | custom-call | flops 1000000000 | bytes 10000000 | tf_op jit(solution)/shard_map/pallas_call | solution.py:281
  103.5 2.8 %shard_map.90.refs_4_.refs_5_ = f32[2,4,2,128]{3,2,1,0:T(2,128)S(1)} custom-call(s32[3]{0:T(128)S(1)} %pad_add_fusion.ids, s32[16,16]{1,0:T(8,128)S(1)} %copy-done.12, bf16[2,2,2,128,128]{4,3,2,1,0:T(8,128)(2,1)S(1)} %collective-permute-done.4.refs_0_, bf16[2,2,2,128,128]{4,3,2,1,0:T(8,128)(2,1)S(1)} %collective-permute-done.5.refs_1_, ...), custom_call_target="tpu_custom_call" | custom-call | flops 1000000000 | bytes 10000000 | tf_op jit(solution)/shard_map/pallas_call | solution.py:281
  106.3 4.8 %shard_map.92 = (bf16[4,2,2,128,128]{4,3,2,1,0:T(8,128)(2,1)S(1)}, f32[2,4,64,128]{3,2,1,0:T(8,128)S(1)}) custom-call(s32[3]{0:T(128)S(1)} %pad_add_fusion.ids, s32[16,16]{1,0:T(8,128)S(1)} %copy-done.12, bf16[4,2,2,128,128]{4,3,2,1,0:T(8,128)(2,1)S(1)} %collective-permute-done.6.refs_0_, bf16[4,2,2,4,128,128]{5,4,3,2,1,0:T(8,128)(2,1)S(1)} %bitcast.22, ...), custom_call_target="tpu_custom_call" | custom-call | flops 2000000000 | bytes 20000000 | tf_op jit(solution)/shard_map/pallas_call | solution.py:297
  113.1 3.7 %shard_map.94 = (bf16[4,2,2,128,128]{4,3,2,1,0:T(8,128)(2,1)S(1)}, f32[2,4,64,128]{3,2,1,0:T(8,128)S(1)}) custom-call(s32[3]{0:T(128)S(1)} %pad_add_fusion.ids, s32[16,16]{1,0:T(8,128)S(1)} %copy-done.12, bf16[4,2,2,128,128]{4,3,2,1,0:T(8,128)(2,1)S(1)} %collective-permute-done.7.refs_1_.refs_0_, bf16[4,2,2,4,128,128]{5,4,3,2,1,0:T(8,128)(2,1)S(1)} %bitcast.23, ...), custom_call_target="tpu_custom_call" | custom-call | flops 2000000000 | bytes 20000000 | tf_op jit(solution)/shard_map/pallas_call | solution.py:297
  116.7 5.4 %collective-permute-start.11 = (bf16[4,2,2,128,128]{4,3,2,1,0:T(8,128)(2,1)S(1)}, bf16[4,2,2,128,128]{4,3,2,1,0:T(8,128)(2,1)S(1)}, u32[]{:S(2)}, u32[]{:S(2)}) collective-permute-start(bf16[4,2,2,128,128]{4,3,2,1,0:T(8,128)(2,1)S(1)} %get-tuple-element.36), channel_id=1, source_target_pairs={{0,30},{2,0},{4,2},{6,4},{8,6},{10,8},{12,10},{14,12},{16,14},{18,... | collective-permute-start | bytes 1572872 | tf_op jit(solution)/shard_map/ppermute | solution.py:314
  122.2 4.2 %shard_map.93 = (bf16[2,2,2,128,128]{4,3,2,1,0:T(8,128)(2,1)S(1)}, bf16[2,2,2,128,128]{4,3,2,1,0:T(8,128)(2,1)S(1)}, f32[2,4,64,128]{3,2,1,0:T(8,128)S(1)}) custom-call(s32[3]{0:T(128)S(1)} %pad_add_fusion.ids, s32[16,16]{1,0:T(8,128)S(1)} %copy-done.12, bf16[2,2,2,128,128]{4,3,2,1,0:T(8,128)(2,1)S(1)} %collective-permute-done.4.refs_0_, ...), custom_call_target="tpu_custom_call" | custom-call | flops 2000000000 | bytes 20000000 | tf_op jit(solution)/shard_map/pallas_call | solution.py:297
  126.3 5.2 %collective-permute-start.12 = (bf16[2,2,2,128,128]{4,3,2,1,0:T(8,128)(2,1)S(1)}, bf16[2,2,2,128,128]{4,3,2,1,0:T(8,128)(2,1)S(1)}, u32[]{:S(2)}, u32[]{:S(2)}) collective-permute-start(bf16[2,2,2,128,128]{4,3,2,1,0:T(8,128)(2,1)S(1)} %get-tuple-element.37), channel_id=1, source_target_pairs={{0,4},{2,6},{4,8},{6,10},{8,12},{10,14},{12,16},{14,18},{16,20},{1... | collective-permute-start | bytes 786440 | tf_op jit(solution)/shard_map/ppermute | solution.py:314
  133.7 4.8 %shard_map.91 = (bf16[4,2,2,128,128]{4,3,2,1,0:T(8,128)(2,1)S(1)}, f32[2,4,64,128]{3,2,1,0:T(8,128)S(1)}) custom-call(s32[3]{0:T(128)S(1)} %pad_add_fusion.ids, s32[16,16]{1,0:T(8,128)S(1)} %copy-done.12, bf16[4,2,2,128,128]{4,3,2,1,0:T(8,128)(2,1)S(1)} %pad_maximum_fusion.refs_0_, bf16[4,2,2,4,128,128]{5,4,3,2,1,0:T(8,128)(2,1)S(1)} %bitcast.25, ...), custom_call_target="tpu_custom_call" | custom-call | flops 2000000000 | bytes 20000000 | tf_op jit(solution)/shard_map/pallas_call | solution.py:297
  138.6 4.8 %collective-permute-done.12.r_up2 = bf16[2,2,2,128,128]{4,3,2,1,0:T(8,128)(2,1)S(1)} collective-permute-done((bf16[2,2,2,128,128]{4,3,2,1,0:T(8,128)(2,1)S(1)}, bf16[2,2,2,128,128]{4,3,2,1,0:T(8,128)(2,1)S(1)}, u32[]{:S(2)}, u32[]{:S(2)}) %collective-permute-start.12) | collective-permute-done | bytes 262176 | tf_op jit(solution)/shard_map/ppermute | solution.py:314
  146.1 11.8 %all-to-all-start.1 = ((bf16[4,2,2,128,128]{4,3,2,1,0:T(8,128)(2,1)}), bf16[4,2,2,128,128]{4,3,2,1,0:T(8,128)(2,1)S(1)}, u32[]{:S(2)}, u32[]{:S(2)}) async-start(bf16[4,2,2,128,128]{4,3,2,1,0:T(8,128)(2,1)} %shard_map.96), calls=%async_computation.1 | async-start | bytes 1048576 | tf_op jit(solution)/shard_map/all_to_all | solution.py:359
  160.2 24.9 %all-to-all-done.1.dkv_own = bf16[4,2,2,128,128]{4,3,2,1,0:T(8,128)(2,1)S(1)} async-done(((bf16[4,2,2,128,128]{4,3,2,1,0:T(8,128)(2,1)}), bf16[4,2,2,128,128]{4,3,2,1,0:T(8,128)(2,1)S(1)}, u32[]{:S(2)}, u32[]{:S(2)}) %all-to-all-start.1) | async-done | bytes 524320 | tf_op jit(solution)/shard_map/all_to_all | solution.py:359
  188.2 2.8 %collective-permute-start.9 = (bf16[4,64,128]{2,1,0:T(8,128)(2,1)S(1)}, bf16[4,64,128]{2,1,0:T(8,128)(2,1)S(1)}, u32[]{:S(2)}, u32[]{:S(2)}) collective-permute-start(bf16[4,64,128]{2,1,0:T(8,128)(2,1)S(1)} %get-tuple-element.33), channel_id=1, source_target_pairs={{0,1},{1,0},{2,3},{3,2},{4,5},{5,4},{6,7},{7,6},{8,9},{9,8},{10,11... | collective-permute-start | bytes 196616 | tf_op jit(solution)/shard_map/ppermute | solution.py:354
  (68 shorter events, 33.6 us)
Async XLA Ops:
  14.3 75.4 %copy-start.12 = (s32[16,16]{1,0:T(8,128)S(1)}, s32[16,16]{1,0:T(8,128)}, u32[]{:S(2)}) copy-start(s32[16,16]{1,0:T(8,128)} %act.13) | copy-start | bytes 3076
  14.3 11.9 %all-to-all-start = ((bf16[4,4,128,128]{3,2,1,0:T(8,128)(2,1)}), bf16[4,4,128,128]{3,2,1,0:T(8,128)(2,1)S(1)}, u32[]{:S(2)}, u32[]{:S(2)}) async-start(bf16[4,4,128,128]{3,2,1,0:T(8,128)(2,1)} %shard_map.87), calls=%async_computation | async-start | bytes 1048576 | tf_op jit(solution)/shard_map/all_to_all | solution.py:330
  19.3 70.4 %all-gather.3.cloned.1.call-start = ((), (), s32[]{:S(2)}) async-start(), calls=%async_computation.2 | async-start | bytes 2621440 | tf_op jit(solution)/shard_map/all_gather | solution.py:332
  19.3 6.8 %collective-permute-start = (bf16[512,128]{1,0:T(8,128)(2,1)S(1)}, bf16[512,128]{1,0:T(8,128)(2,1)S(1)}, u32[]{:S(2)}, u32[]{:S(2)}) collective-permute-start(bf16[512,128]{1,0:T(8,128)(2,1)S(1)} %get-tuple-element.23), channel_id=1, source_target_pairs={{0,32},{32,0},{1,33},{33,1},{2,34},{34,2},{3,35},{35,3},{4,36},{36... | collective-permute-start | bytes 393224 | tf_op jit(solution)/shard_map/ppermute | solution.py:327
  27.1 27.6 %collective-permute-start.2 = (bf16[2,2,128,128]{3,2,1,0:T(8,128)(2,1)S(1)}, bf16[2,2,128,128]{3,2,1,0:T(8,128)(2,1)S(1)}, u32[]{:S(2)}, u32[]{:S(2)}) collective-permute-start(bf16[2,2,128,128]{3,2,1,0:T(8,128)(2,1)S(1)} %get-tuple-element.47), channel_id=1, source_target_pairs={{0,24},{2,26},{4,28},{6,30},{8,0},{10,2},{12,4},{14,6},{16,8},{18,... | collective-permute-start | bytes 393224 | tf_op jit(solution)/shard_map/ppermute | solution.py:314
  42.5 14.9 %collective-permute-start.3 = (bf16[2,2,128,128]{3,2,1,0:T(8,128)(2,1)S(1)}, bf16[2,2,128,128]{3,2,1,0:T(8,128)(2,1)S(1)}, u32[]{:S(2)}, u32[]{:S(2)}) collective-permute-start(bf16[2,2,128,128]{3,2,1,0:T(8,128)(2,1)S(1)} %get-tuple-element.47), channel_id=1, source_target_pairs={{0,16},{2,18},{4,20},{6,22},{8,24},{10,26},{12,28},{14,30},{16,0},... | collective-permute-start | bytes 393224 | tf_op jit(solution)/shard_map/ppermute | solution.py:314
  47.4 15.5 %collective-permute-start.1 = (bf16[2,2,128,128]{3,2,1,0:T(8,128)(2,1)S(1)}, bf16[2,2,128,128]{3,2,1,0:T(8,128)(2,1)S(1)}, u32[]{:S(2)}, u32[]{:S(2)}) collective-permute-start(bf16[2,2,128,128]{3,2,1,0:T(8,128)(2,1)S(1)} %get-tuple-element.47), channel_id=1, source_target_pairs={{0,8},{2,10},{4,12},{6,14},{8,16},{10,18},{12,20},{14,22},{16,24},... | collective-permute-start | bytes 393224 | tf_op jit(solution)/shard_map/ppermute | solution.py:314
  63.0 31.5 %collective-permute-start.7 = (bf16[4,2,2,128,128]{4,3,2,1,0:T(8,128)(2,1)S(1)}, bf16[4,2,2,128,128]{4,3,2,1,0:T(8,128)(2,1)S(1)}, u32[]{:S(2)}, u32[]{:S(2)}) collective-permute-start(bf16[4,2,2,128,128]{4,3,2,1,0:T(8,128)(2,1)S(1)} %pad_maximum_fusion.refs_0_), channel_id=1, source_target_pairs={{0,2},{2,4},{4,6},{6,8},{8,10},{10,12},{12,14},{14,16},{16,18},{18... | collective-permute-start | bytes 1572872 | tf_op jit(solution)/shard_map/ppermute | solution.py:314
  71.1 26.8 %collective-permute-start.6 = (bf16[4,2,2,128,128]{4,3,2,1,0:T(8,128)(2,1)S(1)}, bf16[4,2,2,128,128]{4,3,2,1,0:T(8,128)(2,1)S(1)}, u32[]{:S(2)}, u32[]{:S(2)}) collective-permute-start(bf16[4,2,2,128,128]{4,3,2,1,0:T(8,128)(2,1)S(1)} %pad_maximum_fusion.refs_0_), channel_id=1, source_target_pairs={{0,30},{2,0},{4,2},{6,4},{8,6},{10,8},{12,10},{14,12},{16,14},{18,... | collective-permute-start | bytes 1572872 | tf_op jit(solution)/shard_map/ppermute | solution.py:314
  82.3 21.3 %collective-permute-start.5 = (bf16[2,2,2,128,128]{4,3,2,1,0:T(8,128)(2,1)}, bf16[2,2,2,128,128]{4,3,2,1,0:T(8,128)(2,1)S(1)}, u32[]{:S(2)}, u32[]{:S(2)}) collective-permute-start(bf16[2,2,2,128,128]{4,3,2,1,0:T(8,128)(2,1)} %get-tuple-element.44), channel_id=1, source_target_pairs={{0,4},{2,6},{4,8},{6,10},{8,12},{10,14},{12,16},{14,18},{16,20},{1... | collective-permute-start | bytes 786440 | tf_op jit(solution)/shard_map/ppermute | solution.py:314
  84.2 19.3 %collective-permute-start.4 = (bf16[2,2,2,128,128]{4,3,2,1,0:T(8,128)(2,1)S(1)}, bf16[2,2,2,128,128]{4,3,2,1,0:T(8,128)(2,1)S(1)}, u32[]{:S(2)}, u32[]{:S(2)}) collective-permute-start(bf16[2,2,2,128,128]{4,3,2,1,0:T(8,128)(2,1)S(1)} %get-tuple-element.45), channel_id=1, source_target_pairs={{0,28},{2,30},{4,0},{6,2},{8,4},{10,6},{12,8},{14,10},{16,12},{18,... | collective-permute-start | bytes 786440 | tf_op jit(solution)/shard_map/ppermute | solution.py:314
  111.1 33.4 %collective-permute-start.10 = (bf16[4,2,2,128,128]{4,3,2,1,0:T(8,128)(2,1)S(1)}, bf16[4,2,2,128,128]{4,3,2,1,0:T(8,128)(2,1)S(1)}, u32[]{:S(2)}, u32[]{:S(2)}) collective-permute-start(bf16[4,2,2,128,128]{4,3,2,1,0:T(8,128)(2,1)S(1)} %get-tuple-element.35), channel_id=1, source_target_pairs={{0,2},{2,4},{4,6},{6,8},{8,10},{10,12},{12,14},{14,16},{16,18},{18... | collective-permute-start | bytes 1572872 | tf_op jit(solution)/shard_map/ppermute | solution.py:314
  116.7 27.8 %collective-permute-start.11 = (bf16[4,2,2,128,128]{4,3,2,1,0:T(8,128)(2,1)S(1)}, bf16[4,2,2,128,128]{4,3,2,1,0:T(8,128)(2,1)S(1)}, u32[]{:S(2)}, u32[]{:S(2)}) collective-permute-start(bf16[4,2,2,128,128]{4,3,2,1,0:T(8,128)(2,1)S(1)} %get-tuple-element.36), channel_id=1, source_target_pairs={{0,30},{2,0},{4,2},{6,4},{8,6},{10,8},{12,10},{14,12},{16,14},{18,... | collective-permute-start | bytes 1572872 | tf_op jit(solution)/shard_map/ppermute | solution.py:314
  126.3 17.1 %collective-permute-start.12 = (bf16[2,2,2,128,128]{4,3,2,1,0:T(8,128)(2,1)S(1)}, bf16[2,2,2,128,128]{4,3,2,1,0:T(8,128)(2,1)S(1)}, u32[]{:S(2)}, u32[]{:S(2)}) collective-permute-start(bf16[2,2,2,128,128]{4,3,2,1,0:T(8,128)(2,1)S(1)} %get-tuple-element.37), channel_id=1, source_target_pairs={{0,4},{2,6},{4,8},{6,10},{8,12},{10,14},{12,16},{14,18},{16,20},{1... | collective-permute-start | bytes 786440 | tf_op jit(solution)/shard_map/ppermute | solution.py:314
  131.5 13.0 %collective-permute-start.13 = (bf16[2,2,2,128,128]{4,3,2,1,0:T(8,128)(2,1)S(1)}, bf16[2,2,2,128,128]{4,3,2,1,0:T(8,128)(2,1)S(1)}, u32[]{:S(2)}, u32[]{:S(2)}) collective-permute-start(bf16[2,2,2,128,128]{4,3,2,1,0:T(8,128)(2,1)S(1)} %get-tuple-element.38), channel_id=1, source_target_pairs={{0,28},{2,30},{4,0},{6,2},{8,4},{10,6},{12,8},{14,10},{16,12},{18,... | collective-permute-start | bytes 786440 | tf_op jit(solution)/shard_map/ppermute | solution.py:314
  146.1 41.3 %copy-start.7 = (bf16[64,128]{1,0:T(8,128)(2,1)S(1)}, bf16[64,128]{1,0:T(8,128)(2,1)}, u32[]{:S(2)}) copy-start(bf16[64,128]{1,0:T(8,128)(2,1)} %w_out.3) | copy-start | bytes 49156
  146.1 44.9 %copy-start.4 = (bf16[128,256]{1,0:T(8,128)(2,1)S(1)}, bf16[128,256]{1,0:T(8,128)(2,1)}, u32[]{:S(2)}) copy-start(bf16[128,256]{1,0:T(8,128)(2,1)} %w_proj.3) | copy-start | bytes 196612
  146.1 39.0 %all-to-all-start.1 = ((bf16[4,2,2,128,128]{4,3,2,1,0:T(8,128)(2,1)}), bf16[4,2,2,128,128]{4,3,2,1,0:T(8,128)(2,1)S(1)}, u32[]{:S(2)}, u32[]{:S(2)}) async-start(bf16[4,2,2,128,128]{4,3,2,1,0:T(8,128)(2,1)} %shard_map.96), calls=%async_computation.1 | async-start | bytes 1048576 | tf_op jit(solution)/shard_map/all_to_all | solution.py:359
  157.9 37.8 %copy-start.1 = (bf16[4,128,128]{2,1,0:T(8,128)(2,1)S(1)}, bf16[4,128,128]{2,1,0:T(8,128)(2,1)}, u32[]{:S(2)}) copy-start(bf16[4,128,128]{2,1,0:T(8,128)(2,1)} %pair.3) | copy-start | bytes 393220
  157.9 37.8 %copy-start.9 = (f32[128]{0:T(128)S(1)}, f32[128]{0:T(128)}, u32[]{:S(2)}) copy-start(f32[128]{0:T(128)} %param.8) | copy-start | bytes 1540
  158.0 29.4 %collective-permute-start.8 = (bf16[4,64,128]{2,1,0:T(8,128)(2,1)S(1)}, bf16[4,64,128]{2,1,0:T(8,128)(2,1)S(1)}, u32[]{:S(2)}, u32[]{:S(2)}) collective-permute-start(bf16[4,64,128]{2,1,0:T(8,128)(2,1)S(1)} %fusion.3), channel_id=1, source_target_pairs={{0,32},{32,0},{1,33},{33,1},{2,34},{34,2},{3,35},{35,3},{4,36},{36... | collective-permute-start | bytes 196616 | tf_op jit(solution)/shard_map/ppermute | solution.py:350
  185.2 5.8 %collective-permute-start.14 = (bf16[2,128,128]{2,1,0:T(8,128)(2,1)S(1)}, bf16[2,128,128]{2,1,0:T(8,128)(2,1)S(1)}, u32[]{:S(2)}, u32[]{:S(2)}) collective-permute-start(bf16[2,128,128]{2,1,0:T(8,128)(2,1)S(1)} %slice_reduce_fusion), channel_id=1, source_target_pairs={{0,32},{32,0},{1,33},{33,1},{2,34},{34,2},{3,35},{35,3},{4,36},{36... | collective-permute-start | bytes 196616 | tf_op jit(solution)/shard_map/ppermute | solution.py:361
  188.2 6.6 %collective-permute-start.9 = (bf16[4,64,128]{2,1,0:T(8,128)(2,1)S(1)}, bf16[4,64,128]{2,1,0:T(8,128)(2,1)S(1)}, u32[]{:S(2)}, u32[]{:S(2)}) collective-permute-start(bf16[4,64,128]{2,1,0:T(8,128)(2,1)S(1)} %get-tuple-element.33), channel_id=1, source_target_pairs={{0,1},{1,0},{2,3},{3,2},{4,5},{5,4},{6,7},{7,6},{8,9},{9,8},{10,11... | collective-permute-start | bytes 196616 | tf_op jit(solution)/shard_map/ppermute | solution.py:354
  192.0 3.8 %collective-permute-start.15 = (bf16[4,128,128]{2,1,0:T(8,128)(2,1)S(1)}, bf16[4,128,128]{2,1,0:T(8,128)(2,1)S(1)}, u32[]{:S(2)}, u32[]{:S(2)}) collective-permute-start(bf16[4,128,128]{2,1,0:T(8,128)(2,1)S(1)} %get-tuple-element.41), channel_id=1, source_target_pairs={{0,1},{1,0},{2,3},{3,2},{4,5},{5,4},{6,7},{7,6},{8,9},{9,8},{10,11... | collective-permute-start | bytes 393224 | tf_op jit(solution)/shard_map/ppermute | solution.py:370
  (9 other events, 24.4 us)
Sparse Core Ops, SparseCore 0:
  27.2 46.7 all-gather.2

commit v4 on v3

--- a/solution.py
+++ b/solution.py
@@ -50,14 +50,6 @@
     return jnp.dot(a, b, preferred_element_type=F32)
 
 
-def bias_kernel(bias, send):
-    for j in range(4):
-        for h in range(2):
-            block = bias[h, :, 128 * j : 128 * j + 128].T
-            send[h, j] = block
-            send[2 + h, j] = block
-
-
 def norm(x):
     mean = jnp.mean(x, axis=-1, keepdims=True)
     centred = x - mean
@@ -65,7 +57,15 @@
     return centred * inv, inv
 
 
-def prep_kernel(ids, pair, gain, w_proj, w_out, d_out, keep, send, gate_out, go_out, proj_s):
+def prep_kernel(ids, *refs):
+    here, (keep, send, gate_out, go_out, bias_out) = refs[:6], refs[6:11]
+    pair, gain, w_proj, w_out, d_out, bias = local = refs[11:17]
+    proj_s, sems = refs[17:]
+    copies = [pltpu.make_async_copy(s, d, sems.at[k]) for k, (s, d) in enumerate(zip(here, local))]
+    for copy in copies:
+        copy.start()
+    for copy in copies[:5]:
+        copy.wait()
     xl = ids[1]
     w_t = w_proj[...].T
     for p in range(2):
@@ -85,6 +85,12 @@
         for ref, h in ((keep, xl), (send, 1 - xl)):
             ref[p * 128 : (p + 1) * 128] = proj_s[h, 0:128].T.astype(BF16)
             ref[256 + p * 128 : 384 + p * 128] = proj_s[h, 128:256].astype(BF16)
+    copies[5].wait()
+    for j in range(4):
+        for h in range(2):
+            block = bias[h, :, 128 * j : 128 * j + 128].T
+            bias_out[h, j] = block
+            bias_out[2 + h, j] = block
 
 
 def fill_queries(qd, packs):
@@ -102,7 +108,7 @@
 
 def list_units(ids, act, lst, a, first, count):
     def step(u, n):
-        zk = (ids[0] + first + 4 * (u // 2) + 32) % 16
+        zk = (ids[0] + first[0] + 16) % 4 + 4 * (u // 2 + first[1])
         xk = jnp.where(u % 2 == 0, ids[1], 1 - ids[1])
         lst[n] = u
         return n + act[a, tile_of(zk, xk)]
@@ -114,7 +120,7 @@
     keys = [[kv[u // 2, u % 2, p] for u in units] for p in range(2)]
     b = []
     for u in units:
-        zk = (ids[0] + first + 4 * (u // 2) + 32) % 16
+        zk = (ids[0] + first[0] + 16) % 4 + 4 * (u // 2 + first[1])
         xk = jnp.where(u % 2 == 0, ids[1], 1 - ids[1])
         b.append(bias[zk // 4, xk, jnp.where(half == 0, ids[1], 1 - ids[1]), zk % 4].astype(F32))
     keys = [k[0] if len(k) == 1 else jnp.concatenate(k, axis=0) for k in keys]
@@ -234,15 +240,11 @@
         send[r] = jnp.where(c == 0, high, low).astype(BF16)
 
 
-def sum_kernel(ids, d_own, r_up, r_down, r_up2, r_down2, out):
-    m = ids[0] // 4
-    for e in range(4):
-        total = d_own[e].astype(F32) + r_up[e].astype(F32) + r_down[e].astype(F32)
-        if e in (1, 2):
-            total += r_up2[e - 1].astype(F32)
-        if e in (0, 1):
-            total += r_down2[e].astype(F32)
-        out[(m + e + 3) % 4] = total.astype(BF16)
+def sum_kernel(d_own, r_up, r_down, r_up2, r_down2, out):
+    for m in range(4):
+        total = d_own[m].astype(F32) + r_up[m].astype(F32) + r_down[m].astype(F32)
+        total += (r_up2[m] if m < 2 else r_down2[m - 2]).astype(F32)
+        out[m] = total.astype(BF16)
 
 
 def proj_kernel(ids, oq_own, oq_other, dkv_own, dkv_other, gate, go, w_proj, keep, send, dp):
@@ -317,46 +319,51 @@
 def per_device(pair, gain, w_proj, w_out, tri_bias, active, d_out):
     ids = jnp.stack([lax.axis_index(name) for name in ("z", "xl", "c")]).astype(jnp.int32)
     gain = gain.reshape(1, 128)
-    pack, pack_send, gate, go = call(
+    args = (pair, gain, w_proj, w_out, d_out, tri_bias)
+    pack, pack_send, gate, go, bias = pl.pallas_call(
         prep_kernel,
-        [((512, 128), BF16)] * 2 + [((4, 64, 128), F32)] * 2,
-        1,
-        5,
-        [pltpu.VMEM((2, 256, 128), F32)],
-    )(ids, pair, gain, w_proj, w_out, d_out)
+        out_shape=shapes(
+            *[((512, 128), BF16)] * 2, *[((4, 64, 128), F32)] * 2, ((4, 4, 128, 128), BF16)
+        ),
+        in_specs=[smem()] + [pl.BlockSpec(memory_space=pl.ANY)] * 6,
+        out_specs=[vmem()] * 5,
+        scratch_shapes=[pltpu.VMEM(a.shape, a.dtype) for a in args]
+        + [pltpu.VMEM((2, 256, 128), F32), pltpu.SemaphoreType.DMA((6,))],
+        compiler_params=pltpu.CompilerParams(vmem_limit_bytes=56 * 1024 * 1024),
+    )(ids, *args)
     pack_other = lax.ppermute(pack_send, "xl", SWAP)
-    tri_bias, _ = lax.optimization_barrier((tri_bias, pack_send))
-    (bias,) = call(bias_kernel, [((4, 4, 128, 128), BF16)], 0, 1)(tri_bias)
     bias = lax.all_to_all(bias, ("xh", "xl"), 0, 0, tiled=True).reshape(2, 2, 4, 128, 128)
     bias, pack_other = lax.optimization_barrier((bias, pack_other))
     bias = lax.all_gather(bias, "y")
     kv = jnp.stack([pack[:256].reshape(2, 128, 128), pack_other[:256].reshape(2, 128, 128)])
-    own = jnp.stack([to_z(kv, 4), kv, to_z(kv, -4), to_z(kv, 8)])
+    groups = [[k + 4 * m for m in range(4)] for k in range(4)]
+    own = lax.all_gather(kv, "z", axis_index_groups=groups)
     up, down = to_z(own, -1), to_z(own, 1)
-    up2, down2 = to_z(own[1:3], -2), to_z(own[0:2], 2)
+    up2, down2 = to_z(own[0:2], -2), to_z(own[2:4], 2)
     rest = (bias, pack, pack_other)
-    state = stats_call((-4,), True, False, ids, active, (own,), rest)
-    state = stats_call((-3, -5), False, False, ids, active, (up, down), rest + (state,))
-    stats = stats_call((2, -6), False, True, ids, active, (up2, down2), rest + (state,))
-    (d_up,), oq1 = back_call((-3,), ids, active, (up,), rest + (stats,))
+    state = stats_call(((0, 0),), True, False, ids, active, (own,), rest)
+    state = stats_call(((1, 0), (-1, 0)), False, False, ids, active, (up, down), rest + (state,))
+    stats = stats_call(((2, 0), (-2, 2)), False, True, ids, active, (up2, down2), rest + (state,))
+    (d_up,), oq1 = back_call(((1, 0),), ids, active, (up,), rest + (stats,))
     r_up = to_z(d_up, 1)
-    (d_down,), oq3 = back_call((-5,), ids, active, (down,), rest + (stats,))
+    (d_down,), oq3 = back_call(((-1, 0),), ids, active, (down,), rest + (stats,))
     r_down = to_z(d_down, -1)
-    (d_up2, d_down2), oq2 = back_call((2, -6), ids, active, (up2, down2), rest + (stats,))
+    (d_up2, d_down2), oq2 = back_call(((2, 0), (-2, 2)), ids, active, (up2, down2), rest + (stats,))
     r_up2, r_down2 = to_z(d_up2, 2), to_z(d_down2, -2)
-    (d_own,), oq0 = back_call((-4,), ids, active, (own,), rest + (stats,))
+    (d_own,), oq0 = back_call(((0, 0),), ids, active, (own,), rest + (stats,))
     oq = oq0 + oq1 + oq2 + oq3
     oq = jnp.concatenate([oq[:, :, :32] * SCALE, oq[:, :, 32:]], axis=2)
     oq_other = lax.ppermute(oq[1].astype(BF16), "xl", SWAP)
     out_keep, out_send = call(
         out_kernel, [((4, 64, 128), F32), ((4, 64, 128), BF16)], 1, 4
     )(ids, oq, oq_other, gate, w_out)
-    out = (out_keep + lax.ppermute(out_send, "c", SWAP).astype(F32)).astype(BF16)
-    (sums,) = call(sum_kernel, [((4, 2, 2, 128, 128), BF16)], 1, 5)(
-        ids, d_own, r_up, r_down, r_up2, r_down2
+    out_other = lax.ppermute(out_send, "c", SWAP)
+    out = (out_keep + out_other.astype(F32)).astype(BF16)
+    (sums,) = call(sum_kernel, [((4, 2, 2, 128, 128), BF16)], 0, 5)(
+        d_own, r_up, r_down, r_up2, r_down2
     )
-    groups = [[k + 4 * m for m in range(4)] for k in range(4)]
     dkv = lax.all_to_all(sums, "z", 0, 0, axis_index_groups=groups, tiled=True)
+    dkv, _ = lax.optimization_barrier((dkv, out_other))
     theirs = jnp.sum(dkv[:, 1].astype(F32), axis=0).astype(BF16)
     dkv_other = lax.ppermute(theirs, "xl", SWAP)
     part, part_send = call(

time: 205 us -> 188 us (0.917)
  the two profiles are of different devices: /device:TPU:1 before, /device:TPU:85 now
where the time goes in v4:
time: 188 us; the launch traced here: 187 us
  starting transfers between devices  80.5 us (43%)
  Pallas kernels  40.6 us (22%)
  blocking collectives  28.6 us (15%)
  waiting for transfers between devices  18.7 us (10%)
  between operations  14.3 us (8%)
  local copies, waits for them, and re-layouts  3.34 us (2%)
    all_gather x1, blocking collectives, per_device(): own = lax.all_gather(kv, 'z', axis_index_groups=groups)  28.6 us
    ppermute x8, starting transfers between devices, to_z(): return lax.ppermute(x, 'z', [(j, (j + step) % 16) for j in range(16)])  27.3 us
    ppermute x1, starting transfers between devices, per_device(): out_other = lax.ppermute(out_send, 'c', SWAP)  24.8 us
    pallas_call x4, Pallas kernels, back_call(): call(functools.partial(back_kernel, firsts), [(kv.shape, BF16) for kv in...  20.4 us
    pallas_call x3, Pallas kernels, stats_call(): call(functools.partial(stats_kernel, firsts, begin, end), [out], 2, len(k...  12.8 us
    ppermute x1, starting transfers between devices, per_device(): lax.ppermute(part_send, 'c', SWAP)  9.6 us
    all_to_all x1, starting transfers between devices, per_device(): dkv = lax.all_to_all(sums, 'z', 0, 0, axis_index_groups=groups, tiled=True)  6.52 us
    ppermute x1, waiting for transfers between devices, per_device(): pack_other = lax.ppermute(pack_send, 'xl', SWAP)  6.21 us
  transfers between devices with their start and end apart: 16, of which 7 were waited for; matrix products, arithmetic and copies ran while one was open for 1% of the time, Pallas kernels for 13%

profile of v4, /device:TPU:85, one launch (start us, length us, event | category | flops | bytes accessed | tf_op | source)
XLA Modules:
  0.0 187.5 jit_solution(9604120340796958401)
XLA Ops:
  7.8 3.5 %shard_map.86 = (bf16[512,128]{1,0:T(8,128)(2,1)}, bf16[512,128]{1,0:T(8,128)(2,1)}, f32[4,64,128]{2,1,0:T(8,128)}, f32[4,64,128]{2,1,0:T(8,128)}, bf16[4,4,128,128]{3,2,1,0:T(8,128)(2,1)}) custom-call(s32[3]{0:T(128)} %pad_add_fusion.ids, bf16[4,128,128]{2,1,0:T(8,128)(2,1)} %pair.1, f32[1,128]{1,0:T(1,128)} %bitcast.19, bf16[128,256]{1,0:T(8,128)(2,1)} %w_proj.1, ...), custom_call_target="tpu_custom_call" | custom-call | tf_op jit(solution)/shard_map/pallas_call | solution.py:323
  11.3 4.4 %all-to-all-start = ((bf16[4,4,128,128]{3,2,1,0:T(8,128)(2,1)}), bf16[4,4,128,128]{3,2,1,0:T(8,128)(2,1)S(1)}, u32[]{:S(2)}, u32[]{:S(2)}) async-start(bf16[4,4,128,128]{3,2,1,0:T(8,128)(2,1)} %get-tuple-element.24), calls=%async_computation | async-start | bytes 1048576 | tf_op jit(solution)/shard_map/all_to_all | solution.py:335
  15.7 2.8 %collective-permute-start = (bf16[512,128]{1,0:T(8,128)(2,1)}, bf16[512,128]{1,0:T(8,128)(2,1)S(1)}, u32[]{:S(2)}, u32[]{:S(2)}) collective-permute-start(bf16[512,128]{1,0:T(8,128)(2,1)} %get-tuple-element.25), channel_id=1, source_target_pairs={{0,32},{32,0},{1,33},{33,1},{2,34},{34,2},{3,35},{35,3},{4,36},{36... | collective-permute-start | bytes 393224 | tf_op jit(solution)/shard_map/ppermute | solution.py:334
  18.4 6.2 %collective-permute-done.refs_3_.refs_4_ = bf16[512,128]{1,0:T(8,128)(2,1)S(1)} collective-permute-done((bf16[512,128]{1,0:T(8,128)(2,1)}, bf16[512,128]{1,0:T(8,128)(2,1)S(1)}, u32[]{:S(2)}, u32[]{:S(2)}) %collective-permute-start) | collective-permute-done | bytes 131104 | tf_op jit(solution)/shard_map/ppermute | solution.py:334
  26.4 28.6 %all-gather = bf16[8,2,128,128]{3,2,1,0:T(8,128)(2,1)S(1)} all-gather(bf16[2,2,128,128]{3,2,1,0:T(8,128)(2,1)S(1)} %pad_maximum_fusion.1), channel_id=2, replica_groups={{0,8,16,24},{2,10,18,26},{4,12,20,28},{6,14,22,30},{1,9,17,25},{3,11,19..., dimensions={0}, use_global_device_ids=true | all-gather | bytes 655360 | tf_op jit(solution)/shard_map/all_gather | solution.py:340
  55.0 3.0 %collective-permute-start.4 = (bf16[4,2,2,128,128]{4,3,2,1,0:T(8,128)(2,1)S(1)}, bf16[4,2,2,128,128]{4,3,2,1,0:T(8,128)(2,1)S(1)}, u32[]{:S(2)}, u32[]{:S(2)}) collective-permute-start(bf16[4,2,2,128,128]{4,3,2,1,0:T(8,128)(2,1)S(1)} %bitcast.15), channel_id=1, source_target_pairs={{0,2},{2,4},{4,6},{6,8},{8,10},{10,12},{12,14},{14,16},{16,18},{18... | collective-permute-start | bytes 1572872 | tf_op jit(solution)/shard_map/ppermute | solution.py:316
  60.3 4.8 %collective-permute-start.1 = (bf16[2,2,2,128,128]{4,3,2,1,0:T(8,128)(2,1)S(1)}, bf16[2,2,2,128,128]{4,3,2,1,0:T(8,128)(2,1)S(1)}, u32[]{:S(2)}, u32[]{:S(2)}) collective-permute-start(bf16[2,2,2,128,128]{4,3,2,1,0:T(8,128)(2,1)S(1)} %bitcast.32), channel_id=1, source_target_pairs={{0,28},{2,30},{4,0},{6,2},{8,4},{10,6},{12,8},{14,10},{16,12},{18,... | collective-permute-start | bytes 786440 | tf_op jit(solution)/shard_map/ppermute | solution.py:316
  65.1 2.6 %collective-permute-start.2 = (bf16[2,2,2,128,128]{4,3,2,1,0:T(8,128)(2,1)S(1)}, bf16[2,2,2,128,128]{4,3,2,1,0:T(8,128)(2,1)S(1)}, u32[]{:S(2)}, u32[]{:S(2)}) collective-permute-start(bf16[2,2,2,128,128]{4,3,2,1,0:T(8,128)(2,1)S(1)} %bitcast.31), channel_id=1, source_target_pairs={{0,4},{2,6},{4,8},{6,10},{8,12},{10,14},{12,16},{14,18},{16,20},{1... | collective-permute-start | bytes 786440 | tf_op jit(solution)/shard_map/ppermute | solution.py:316
  69.5 3.6 %shard_map.87.refs_5_ = f32[3,2,4,8,128]{4,3,2,1,0:T(8,128)S(1)} custom-call(s32[3]{0:T(128)S(1)} %copy-done.6, s32[16,16]{1,0:T(8,128)S(1)} %copy-done.10, bf16[4,2,2,128,128]{4,3,2,1,0:T(8,128)(2,1)S(1)} %bitcast.17, bf16[4,2,2,4,128,128]{5,4,3,2,1,0:T(8,128)(2,1)S(1)} %bitcast.21, bf16[512,128]{1,0:T(8,128)(2,1)S(1)} %copy-done.5, ...), custom_call_target="tpu_custom_call" | custom-call | flops 1000000000 | bytes 10000000 | tf_op jit(solution)/shard_map/pallas_call | solution.py:283
  73.1 6.0 %shard_map.88.refs_5_ = f32[3,2,4,8,128]{4,3,2,1,0:T(8,128)S(1)} custom-call(s32[3]{0:T(128)S(1)} %copy-done.6, s32[16,16]{1,0:T(8,128)S(1)} %copy-done.10, bf16[4,2,2,128,128]{4,3,2,1,0:T(8,128)(2,1)S(1)} %collective-permute-done.3.refs_0_, bf16[4,2,2,128,128]{4,3,2,1,0:T(8,128)(2,1)S(1)} %collective-permute-done.4.refs_1_.refs_0_, ...), custom_call_target="tpu_custom_call" | custom-call | flops 1000000000 | bytes 10000000 | tf_op jit(solution)/shard_map/pallas_call | solution.py:283
  79.1 3.3 %shard_map.89.refs_4_.refs_5_ = f32[2,4,2,128]{3,2,1,0:T(2,128)S(1)} custom-call(s32[3]{0:T(128)S(1)} %copy-done.6, s32[16,16]{1,0:T(8,128)S(1)} %copy-done.10, bf16[2,2,2,128,128]{4,3,2,1,0:T(8,128)(2,1)S(1)} %collective-permute-done.1.refs_0_, bf16[2,2,2,128,128]{4,3,2,1,0:T(8,128)(2,1)S(1)} %collective-permute-done.2.refs_1_, ...), custom_call_target="tpu_custom_call" | custom-call | flops 1000000000 | bytes 10000000 | tf_op jit(solution)/shard_map/pallas_call | solution.py:283
  82.4 5.4 %shard_map.91 = (bf16[4,2,2,128,128]{4,3,2,1,0:T(8,128)(2,1)S(1)}, f32[2,4,64,128]{3,2,1,0:T(8,128)S(1)}) custom-call(s32[3]{0:T(128)S(1)} %copy-done.6, s32[16,16]{1,0:T(8,128)S(1)} %copy-done.10, bf16[4,2,2,128,128]{4,3,2,1,0:T(8,128)(2,1)S(1)} %collective-permute-done.3.refs_0_, bf16[4,2,2,4,128,128]{5,4,3,2,1,0:T(8,128)(2,1)S(1)} %bitcast.24, ...), custom_call_target="tpu_custom_call" | custom-call | flops 2000000000 | bytes 20000000 | tf_op jit(solution)/shard_map/pallas_call | solution.py:299
  87.8 2.6 %collective-permute-start.7 = (bf16[4,2,2,128,128]{4,3,2,1,0:T(8,128)(2,1)S(1)}, bf16[4,2,2,128,128]{4,3,2,1,0:T(8,128)(2,1)S(1)}, u32[]{:S(2)}, u32[]{:S(2)}) collective-permute-start(bf16[4,2,2,128,128]{4,3,2,1,0:T(8,128)(2,1)S(1)} %get-tuple-element.36), channel_id=1, source_target_pairs={{0,2},{2,4},{4,6},{6,8},{8,10},{10,12},{12,14},{14,16},{16,18},{18... | collective-permute-start | bytes 1572872 | tf_op jit(solution)/shard_map/ppermute | solution.py:316
  90.4 4.8 %shard_map.93 = (bf16[4,2,2,128,128]{4,3,2,1,0:T(8,128)(2,1)S(1)}, f32[2,4,64,128]{3,2,1,0:T(8,128)S(1)}) custom-call(s32[3]{0:T(128)S(1)} %copy-done.6, s32[16,16]{1,0:T(8,128)S(1)} %copy-done.10, bf16[4,2,2,128,128]{4,3,2,1,0:T(8,128)(2,1)S(1)} %collective-permute-done.4.refs_1_.refs_0_, bf16[4,2,2,4,128,128]{5,4,3,2,1,0:T(8,128)(2,1)S(1)} %bitcast.25, ...), custom_call_target="tpu_custom_call" | custom-call | flops 2000000000 | bytes 20000000 | tf_op jit(solution)/shard_map/pallas_call | solution.py:299
  97.7 4.8 %shard_map.92 = (bf16[2,2,2,128,128]{4,3,2,1,0:T(8,128)(2,1)S(1)}, bf16[2,2,2,128,128]{4,3,2,1,0:T(8,128)(2,1)S(1)}, f32[2,4,64,128]{3,2,1,0:T(8,128)S(1)}) custom-call(s32[3]{0:T(128)S(1)} %copy-done.6, s32[16,16]{1,0:T(8,128)S(1)} %copy-done.10, bf16[2,2,2,128,128]{4,3,2,1,0:T(8,128)(2,1)S(1)} %collective-permute-done.1.refs_0_, ...), custom_call_target="tpu_custom_call" | custom-call | flops 2000000000 | bytes 20000000 | tf_op jit(solution)/shard_map/pallas_call | solution.py:299
  102.5 3.2 %collective-permute-start.9 = (bf16[2,2,2,128,128]{4,3,2,1,0:T(8,128)(2,1)S(1)}, bf16[2,2,2,128,128]{4,3,2,1,0:T(8,128)(2,1)S(1)}, u32[]{:S(2)}, u32[]{:S(2)}) collective-permute-start(bf16[2,2,2,128,128]{4,3,2,1,0:T(8,128)(2,1)S(1)} %get-tuple-element.38), channel_id=1, source_target_pairs={{0,4},{2,6},{4,8},{6,10},{8,12},{10,14},{12,16},{14,18},{16,20},{1... | collective-permute-start | bytes 786440 | tf_op jit(solution)/shard_map/ppermute | solution.py:316
  105.7 6.4 %collective-permute-start.10 = (bf16[2,2,2,128,128]{4,3,2,1,0:T(8,128)(2,1)S(1)}, bf16[2,2,2,128,128]{4,3,2,1,0:T(8,128)(2,1)S(1)}, u32[]{:S(2)}, u32[]{:S(2)}) collective-permute-start(bf16[2,2,2,128,128]{4,3,2,1,0:T(8,128)(2,1)S(1)} %get-tuple-element.39), channel_id=1, source_target_pairs={{0,28},{2,30},{4,0},{6,2},{8,4},{10,6},{12,8},{14,10},{16,12},{18,... | collective-permute-start | bytes 786440 | tf_op jit(solution)/shard_map/ppermute | solution.py:316
  112.2 5.4 %shard_map.90 = (bf16[4,2,2,128,128]{4,3,2,1,0:T(8,128)(2,1)S(1)}, f32[2,4,64,128]{3,2,1,0:T(8,128)S(1)}) custom-call(s32[3]{0:T(128)S(1)} %copy-done.6, s32[16,16]{1,0:T(8,128)S(1)} %copy-done.10, bf16[4,2,2,128,128]{4,3,2,1,0:T(8,128)(2,1)S(1)} %bitcast.18, bf16[4,2,2,4,128,128]{5,4,3,2,1,0:T(8,128)(2,1)S(1)} %bitcast.27, bf16[512,128]{1,0:T(8,128)(2,1)S(1)} %copy-done.5, ...), custom_call_target="tpu_custom_call" | custom-call | flops 2000000000 | bytes 20000000 | tf_op jit(solution)/shard_map/pallas_call | solution.py:299
  117.6 5.9 %collective-permute-done.10.r_down2 = bf16[2,2,2,128,128]{4,3,2,1,0:T(8,128)(2,1)S(1)} collective-permute-done((bf16[2,2,2,128,128]{4,3,2,1,0:T(8,128)(2,1)S(1)}, bf16[2,2,2,128,128]{4,3,2,1,0:T(8,128)(2,1)S(1)}, u32[]{:S(2)}, u32[]{:S(2)}) %collective-permute-start.10) | collective-permute-done | bytes 262176 | tf_op jit(solution)/shard_map/ppermute | solution.py:316
  124.6 6.5 %all-to-all-start.1 = ((bf16[4,2,2,128,128]{4,3,2,1,0:T(8,128)(2,1)}), bf16[4,2,2,128,128]{4,3,2,1,0:T(8,128)(2,1)S(1)}, u32[]{:S(2)}, u32[]{:S(2)}) async-start(bf16[4,2,2,128,128]{4,3,2,1,0:T(8,128)(2,1)} %shard_map.95), calls=%async_computation.1 | async-start | bytes 1048576 | tf_op jit(solution)/shard_map/all_to_all | solution.py:365
  131.2 3.2 %collective-permute-start.5 = (bf16[4,64,128]{2,1,0:T(8,128)(2,1)S(1)}, bf16[4,64,128]{2,1,0:T(8,128)(2,1)S(1)}, u32[]{:S(2)}, u32[]{:S(2)}) collective-permute-start(bf16[4,64,128]{2,1,0:T(8,128)(2,1)S(1)} %fusion.3), channel_id=1, source_target_pairs={{0,32},{32,0},{1,33},{33,1},{2,34},{34,2},{3,35},{35,3},{4,36},{36... | collective-permute-start | bytes 196616 | tf_op jit(solution)/shard_map/ppermute | solution.py:356
  137.0 24.8 %collective-permute-start.6 = (bf16[4,64,128]{2,1,0:T(8,128)(2,1)S(1)}, bf16[4,64,128]{2,1,0:T(8,128)(2,1)S(1)}, u32[]{:S(2)}, u32[]{:S(2)}) collective-permute-start(bf16[4,64,128]{2,1,0:T(8,128)(2,1)S(1)} %get-tuple-element.34), channel_id=1, source_target_pairs={{0,1},{1,0},{2,3},{3,2},{4,5},{5,4},{6,7},{7,6},{8,9},{9,8},{10,11... | collective-permute-start | bytes 196616 | tf_op jit(solution)/shard_map/ppermute | solution.py:360
  164.6 3.4 %collective-permute-done.11.dkv_other = bf16[2,128,128]{2,1,0:T(8,128)(2,1)S(1)} collective-permute-done((bf16[2,128,128]{2,1,0:T(8,128)(2,1)S(1)}, bf16[2,128,128]{2,1,0:T(8,128)(2,1)S(1)}, u32[]{:S(2)}, u32[]{:S(2)}) %collective-permute-start.11) | collective-permute-done | bytes 65568 | tf_op jit(solution)/shard_map/ppermute | solution.py:368
  168.9 9.6 %collective-permute-start.12 = (bf16[4,128,128]{2,1,0:T(8,128)(2,1)S(1)}, bf16[4,128,128]{2,1,0:T(8,128)(2,1)S(1)}, u32[]{:S(2)}, u32[]{:S(2)}) collective-permute-start(bf16[4,128,128]{2,1,0:T(8,128)(2,1)S(1)} %get-tuple-element.43), channel_id=1, source_target_pairs={{0,1},{1,0},{2,3},{3,2},{4,5},{5,4},{6,7},{7,6},{8,9},{9,8},{10,11... | collective-permute-start | bytes 393224 | tf_op jit(solution)/shard_map/ppermute | solution.py:377
  (57 shorter events, 18.5 us)
Async XLA Ops:
  7.8 60.2 %copy-start.6 = (s32[3]{0:T(128)S(1)}, s32[3]{0:T(128)}, u32[]{:S(2)}) copy-start(s32[3]{0:T(128)} %pad_add_fusion.ids) | copy-start | bytes 40
  7.8 60.2 %copy-start.10 = (s32[16,16]{1,0:T(8,128)S(1)}, s32[16,16]{1,0:T(8,128)}, u32[]{:S(2)}) copy-start(s32[16,16]{1,0:T(8,128)} %act.13) | copy-start | bytes 3076
  11.3 56.7 %copy-start.5 = (bf16[512,128]{1,0:T(8,128)(2,1)S(1)}, bf16[512,128]{1,0:T(8,128)(2,1)}, u32[]{:S(2)}) copy-start(bf16[512,128]{1,0:T(8,128)(2,1)} %get-tuple-element.23.refs_2_.refs_3_) | copy-start | bytes 393220
  11.3 13.4 %all-to-all-start = ((bf16[4,4,128,128]{3,2,1,0:T(8,128)(2,1)}), bf16[4,4,128,128]{3,2,1,0:T(8,128)(2,1)S(1)}, u32[]{:S(2)}, u32[]{:S(2)}) async-start(bf16[4,4,128,128]{3,2,1,0:T(8,128)(2,1)} %get-tuple-element.24), calls=%async_computation | async-start | bytes 1048576 | tf_op jit(solution)/shard_map/all_to_all | solution.py:335
  15.6 52.3 %all-gather.4.cloned.1.call-start = ((), (), s32[]{:S(2)}) async-start(), calls=%async_computation.2 | async-start | bytes 2621440 | tf_op jit(solution)/shard_map/all_gather | solution.py:337
  15.7 9.0 %collective-permute-start = (bf16[512,128]{1,0:T(8,128)(2,1)}, bf16[512,128]{1,0:T(8,128)(2,1)S(1)}, u32[]{:S(2)}, u32[]{:S(2)}) collective-permute-start(bf16[512,128]{1,0:T(8,128)(2,1)} %get-tuple-element.25), channel_id=1, source_target_pairs={{0,32},{32,0},{1,33},{33,1},{2,34},{34,2},{3,35},{35,3},{4,36},{36... | collective-permute-start | bytes 393224 | tf_op jit(solution)/shard_map/ppermute | solution.py:334
  55.0 18.1 %collective-permute-start.4 = (bf16[4,2,2,128,128]{4,3,2,1,0:T(8,128)(2,1)S(1)}, bf16[4,2,2,128,128]{4,3,2,1,0:T(8,128)(2,1)S(1)}, u32[]{:S(2)}, u32[]{:S(2)}) collective-permute-start(bf16[4,2,2,128,128]{4,3,2,1,0:T(8,128)(2,1)S(1)} %bitcast.15), channel_id=1, source_target_pairs={{0,2},{2,4},{4,6},{6,8},{8,10},{10,12},{12,14},{14,16},{16,18},{18... | collective-permute-start | bytes 1572872 | tf_op jit(solution)/shard_map/ppermute | solution.py:316
  58.0 15.1 %collective-permute-start.3 = (bf16[4,2,2,128,128]{4,3,2,1,0:T(8,128)(2,1)S(1)}, bf16[4,2,2,128,128]{4,3,2,1,0:T(8,128)(2,1)S(1)}, u32[]{:S(2)}, u32[]{:S(2)}) collective-permute-start(bf16[4,2,2,128,128]{4,3,2,1,0:T(8,128)(2,1)S(1)} %bitcast.16), channel_id=1, source_target_pairs={{0,30},{2,0},{4,2},{6,4},{8,6},{10,8},{12,10},{14,12},{16,14},{18,... | collective-permute-start | bytes 1572872 | tf_op jit(solution)/shard_map/ppermute | solution.py:316
  60.3 18.8 %collective-permute-start.1 = (bf16[2,2,2,128,128]{4,3,2,1,0:T(8,128)(2,1)S(1)}, bf16[2,2,2,128,128]{4,3,2,1,0:T(8,128)(2,1)S(1)}, u32[]{:S(2)}, u32[]{:S(2)}) collective-permute-start(bf16[2,2,2,128,128]{4,3,2,1,0:T(8,128)(2,1)S(1)} %bitcast.32), channel_id=1, source_target_pairs={{0,28},{2,30},{4,0},{6,2},{8,4},{10,6},{12,8},{14,10},{16,12},{18,... | collective-permute-start | bytes 786440 | tf_op jit(solution)/shard_map/ppermute | solution.py:316
  65.1 14.0 %collective-permute-start.2 = (bf16[2,2,2,128,128]{4,3,2,1,0:T(8,128)(2,1)S(1)}, bf16[2,2,2,128,128]{4,3,2,1,0:T(8,128)(2,1)S(1)}, u32[]{:S(2)}, u32[]{:S(2)}) collective-permute-start(bf16[2,2,2,128,128]{4,3,2,1,0:T(8,128)(2,1)S(1)} %bitcast.31), channel_id=1, source_target_pairs={{0,4},{2,6},{4,8},{6,10},{8,12},{10,14},{12,16},{14,18},{16,20},{1... | collective-permute-start | bytes 786440 | tf_op jit(solution)/shard_map/ppermute | solution.py:316
  87.8 35.7 %collective-permute-start.7 = (bf16[4,2,2,128,128]{4,3,2,1,0:T(8,128)(2,1)S(1)}, bf16[4,2,2,128,128]{4,3,2,1,0:T(8,128)(2,1)S(1)}, u32[]{:S(2)}, u32[]{:S(2)}) collective-permute-start(bf16[4,2,2,128,128]{4,3,2,1,0:T(8,128)(2,1)S(1)} %get-tuple-element.36), channel_id=1, source_target_pairs={{0,2},{2,4},{4,6},{6,8},{8,10},{10,12},{12,14},{14,16},{16,18},{18... | collective-permute-start | bytes 1572872 | tf_op jit(solution)/shard_map/ppermute | solution.py:316
  95.2 17.0 %copy-start.9 = (bf16[8,2,4,128,128]{4,3,2,1,0:T(8,128)(2,1)S(1)}, bf16[8,2,4,128,128]{4,3,2,1,0:T(8,128)(2,1)}, u32[]{:S(2)}) copy-start(bf16[8,2,4,128,128]{4,3,2,1,0:T(8,128)(2,1)} %all-gather.4.cloned.1.call-done) | copy-start | bytes 6291460
  95.2 28.3 %collective-permute-start.8 = (bf16[4,2,2,128,128]{4,3,2,1,0:T(8,128)(2,1)S(1)}, bf16[4,2,2,128,128]{4,3,2,1,0:T(8,128)(2,1)S(1)}, u32[]{:S(2)}, u32[]{:S(2)}) collective-permute-start(bf16[4,2,2,128,128]{4,3,2,1,0:T(8,128)(2,1)S(1)} %get-tuple-element.37), channel_id=1, source_target_pairs={{0,30},{2,0},{4,2},{6,4},{8,6},{10,8},{12,10},{14,12},{16,14},{18,... | collective-permute-start | bytes 1572872 | tf_op jit(solution)/shard_map/ppermute | solution.py:316
  102.5 15.1 %collective-permute-start.9 = (bf16[2,2,2,128,128]{4,3,2,1,0:T(8,128)(2,1)S(1)}, bf16[2,2,2,128,128]{4,3,2,1,0:T(8,128)(2,1)S(1)}, u32[]{:S(2)}, u32[]{:S(2)}) collective-permute-start(bf16[2,2,2,128,128]{4,3,2,1,0:T(8,128)(2,1)S(1)} %get-tuple-element.38), channel_id=1, source_target_pairs={{0,4},{2,6},{4,8},{6,10},{8,12},{10,14},{12,16},{14,18},{16,20},{1... | collective-permute-start | bytes 786440 | tf_op jit(solution)/shard_map/ppermute | solution.py:316
  105.7 17.8 %collective-permute-start.10 = (bf16[2,2,2,128,128]{4,3,2,1,0:T(8,128)(2,1)S(1)}, bf16[2,2,2,128,128]{4,3,2,1,0:T(8,128)(2,1)S(1)}, u32[]{:S(2)}, u32[]{:S(2)}) collective-permute-start(bf16[2,2,2,128,128]{4,3,2,1,0:T(8,128)(2,1)S(1)} %get-tuple-element.39), channel_id=1, source_target_pairs={{0,28},{2,30},{4,0},{6,2},{8,4},{10,6},{12,8},{14,10},{16,12},{18,... | collective-permute-start | bytes 786440 | tf_op jit(solution)/shard_map/ppermute | solution.py:316
  124.6 43.4 %copy-start.2 = (bf16[128,256]{1,0:T(8,128)(2,1)S(1)}, bf16[128,256]{1,0:T(8,128)(2,1)}, u32[]{:S(2)}) copy-start(bf16[128,256]{1,0:T(8,128)(2,1)} %w_proj.1) | copy-start | bytes 196612
  124.6 43.4 %copy-start.3 = (f32[4,64,128]{2,1,0:T(8,128)S(1)}, f32[4,64,128]{2,1,0:T(8,128)}, u32[]{:S(2)}) copy-start(f32[4,64,128]{2,1,0:T(8,128)} %get-tuple-element.41.go) | copy-start | bytes 393220
  124.6 38.1 %all-to-all-start.1 = ((bf16[4,2,2,128,128]{4,3,2,1,0:T(8,128)(2,1)}), bf16[4,2,2,128,128]{4,3,2,1,0:T(8,128)(2,1)S(1)}, u32[]{:S(2)}, u32[]{:S(2)}) async-start(bf16[4,2,2,128,128]{4,3,2,1,0:T(8,128)(2,1)} %shard_map.95), calls=%async_computation.1 | async-start | bytes 1048576 | tf_op jit(solution)/shard_map/all_to_all | solution.py:365
  131.2 48.4 %copy-start.1 = (bf16[4,128,128]{2,1,0:T(8,128)(2,1)S(1)}, bf16[4,128,128]{2,1,0:T(8,128)(2,1)}, u32[]{:S(2)}) copy-start(bf16[4,128,128]{2,1,0:T(8,128)(2,1)} %pair.1) | copy-start | bytes 393220
  131.2 48.4 %copy-start.7 = (f32[128]{0:T(128)S(1)}, f32[128]{0:T(128)}, u32[]{:S(2)}) copy-start(f32[128]{0:T(128)} %param.8) | copy-start | bytes 1540
  131.2 5.0 %collective-permute-start.5 = (bf16[4,64,128]{2,1,0:T(8,128)(2,1)S(1)}, bf16[4,64,128]{2,1,0:T(8,128)(2,1)S(1)}, u32[]{:S(2)}, u32[]{:S(2)}) collective-permute-start(bf16[4,64,128]{2,1,0:T(8,128)(2,1)S(1)} %fusion.3), channel_id=1, source_target_pairs={{0,32},{32,0},{1,33},{33,1},{2,34},{34,2},{3,35},{35,3},{4,36},{36... | collective-permute-start | bytes 196616 | tf_op jit(solution)/shard_map/ppermute | solution.py:356
  137.0 25.6 %collective-permute-start.6 = (bf16[4,64,128]{2,1,0:T(8,128)(2,1)S(1)}, bf16[4,64,128]{2,1,0:T(8,128)(2,1)S(1)}, u32[]{:S(2)}, u32[]{:S(2)}) collective-permute-start(bf16[4,64,128]{2,1,0:T(8,128)(2,1)S(1)} %get-tuple-element.34), channel_id=1, source_target_pairs={{0,1},{1,0},{2,3},{3,2},{4,5},{5,4},{6,7},{7,6},{8,9},{9,8},{10,11... | collective-permute-start | bytes 196616 | tf_op jit(solution)/shard_map/ppermute | solution.py:360
  162.7 5.3 %collective-permute-start.11 = (bf16[2,128,128]{2,1,0:T(8,128)(2,1)S(1)}, bf16[2,128,128]{2,1,0:T(8,128)(2,1)S(1)}, u32[]{:S(2)}, u32[]{:S(2)}) collective-permute-start(bf16[2,128,128]{2,1,0:T(8,128)(2,1)S(1)} %slice_reduce_fusion), channel_id=1, source_target_pairs={{0,32},{32,0},{1,33},{33,1},{2,34},{34,2},{3,35},{35,3},{4,36},{36... | collective-permute-start | bytes 196616 | tf_op jit(solution)/shard_map/ppermute | solution.py:368
  168.9 10.6 %collective-permute-start.12 = (bf16[4,128,128]{2,1,0:T(8,128)(2,1)S(1)}, bf16[4,128,128]{2,1,0:T(8,128)(2,1)S(1)}, u32[]{:S(2)}, u32[]{:S(2)}) collective-permute-start(bf16[4,128,128]{2,1,0:T(8,128)(2,1)S(1)} %get-tuple-element.43), channel_id=1, source_target_pairs={{0,1},{1,0},{2,3},{3,2},{4,5},{5,4},{6,7},{7,6},{8,9},{9,8},{10,11... | collective-permute-start | bytes 393224 | tf_op jit(solution)/shard_map/ppermute | solution.py:377
  (4 other events, 25.7 us)
Sparse Core Ops, SparseCore 0:
  25.6 42.2 all-gather.3

commit v5 on v4

--- a/solution.py
+++ b/solution.py
@@ -16,6 +16,8 @@
 F32 = jnp.float32
 BF16 = jnp.bfloat16
 SWAP = [(0, 1), (1, 0)]
+OWN, UP, DOWN, UP2, DOWN2 = range(5)
+ARRAYS = ((0, 0, 4), (1, 0, 4), (-1, 0, 4), (2, 0, 2), (-2, 2, 2))
 
 
 def vmem():
@@ -106,46 +108,51 @@
     return zk // 2 + 8 * xk
 
 
-def list_units(ids, act, lst, a, first, count):
-    def step(u, n):
-        zk = (ids[0] + first[0] + 16) % 4 + 4 * (u // 2 + first[1])
-        xk = jnp.where(u % 2 == 0, ids[1], 1 - ids[1])
-        lst[n] = u
-        return n + act[a, tile_of(zk, xk)]
-
-    return lax.fori_loop(0, 2 * count, step, 0)
-
-
-def load_units(ids, kv, bias, first, half, units):
+def setup_kernel(ids, act, pack0, pack1, lists, qd):
+    fill_queries(qd, (pack0, pack1))
+    for k, (step, low, count) in enumerate(ARRAYS):
+        for half in range(2):
+            a = tile_of(ids[0], ids[1] if half == 0 else 1 - ids[1])
+            base = 9 * (2 * k + half)
+            n = 0
+            for u in range(2 * count):
+                zk = (ids[0] + step + 16) % 4 + 4 * (u // 2 + low)
+                xk = ids[1] if u % 2 == 0 else 1 - ids[1]
+                lists[base + n] = u
+                n = n + act[a, tile_of(zk, xk)]
+            lists[base + 8] = n
+
+
+def load_units(ids, kv, bias, which, half, units):
+    step, low, _ = ARRAYS[which]
     keys = [[kv[u // 2, u % 2, p] for u in units] for p in range(2)]
     b = []
     for u in units:
-        zk = (ids[0] + first[0] + 16) % 4 + 4 * (u // 2 + first[1])
         xk = jnp.where(u % 2 == 0, ids[1], 1 - ids[1])
-        b.append(bias[zk // 4, xk, jnp.where(half == 0, ids[1], 1 - ids[1]), zk % 4].astype(F32))
+        xq = jnp.where(half == 0, ids[1], 1 - ids[1])
+        b.append(bias[u // 2 + low, xk, xq, (ids[0] + step + 16) % 4].astype(F32))
     keys = [k[0] if len(k) == 1 else jnp.concatenate(k, axis=0) for k in keys]
     return keys, b[0] if len(b) == 1 else jnp.concatenate(b, axis=0)
 
 
-def over_units(ids, act, lst, first, count, half, body):
-    a = tile_of(ids[0], jnp.where(half == 0, ids[1], 1 - ids[1]))
-    n = list_units(ids, act, lst, a, first, count)
+def over_units(lists, which, half, body):
+    base = 9 * (2 * which + half)
+    n = lists[base + 8]
 
     @pl.loop(0, n // 2)
     def _(k):
-        body([lst[2 * k], lst[2 * k + 1]])
+        body([lists[base + 2 * k], lists[base + 2 * k + 1]])
 
     @pl.when(n % 2 == 1)
     def _():
-        body([lst[n - 1]])
-
-
-def stats_kernel(firsts, begin, end, ids, act, *refs):
-    n = len(firsts)
-    kvs, (bias, pack0, pack1), refs = refs[:n], refs[n : n + 3], refs[n + 3 :]
+        body([lists[base + n - 1]])
+
+
+def stats_kernel(names, begin, end, ids, lists, *refs):
+    n = len(names)
+    kvs, (bias, qd), refs = refs[:n], refs[n : n + 2], refs[n + 2 :]
     before, refs = (None, refs) if begin else (refs[0], refs[1:])
-    out, qd, lst, st = refs
-    fill_queries(qd, (pack0, pack1))
+    out, st = refs
     if begin:
         st[0] = jnp.full(st.shape[1:], NEG, F32)
         st[1:3] = jnp.zeros((2,) + st.shape[1:], F32)
@@ -154,10 +161,10 @@
 
     @pl.loop(0, 2)
     def _(half):
-        for kv, first in zip(kvs, firsts):
-
-            def body(units, kv=kv, first=first):
-                keys, b = load_units(ids, kv, bias, first, half, units)
+        for kv, which in zip(kvs, names):
+
+            def body(units, kv=kv, which=which):
+                keys, b = load_units(ids, kv, bias, which, half, units)
                 rows = b.shape[0] // 8
                 for p in range(2):
                     sd = [nn(keys[p], qd[half, 2 * p + i]) for i in range(2)]
@@ -173,7 +180,7 @@
                         st[2, half, r] = st[2, half, r] * c + jnp.sum(e * dp, axis=0)
                         st[0, half, r] = m_new
 
-            over_units(ids, act, lst, first, kv.shape[0], half, body)
+            over_units(lists, which, half, body)
 
     if not end:
         out[...] = st[...]
@@ -188,20 +195,19 @@
             out[half, r, 1:2] = jnp.sum(st[2, half, r] * f, axis=0, keepdims=True) / total
 
 
-def back_kernel(firsts, ids, act, *refs):
-    n = len(firsts)
-    kvs, (bias, pack0, pack1, stats) = refs[:n], refs[n : n + 4]
-    dkvs, (oq, qd, lst, acc) = refs[n + 4 : 2 * n + 4], refs[2 * n + 4 :]
-    fill_queries(qd, (pack0, pack1))
+def back_kernel(names, ids, lists, *refs):
+    n = len(names)
+    kvs, (bias, qd, stats) = refs[:n], refs[n : n + 3]
+    dkvs, (oq, acc) = refs[n + 3 : 2 * n + 3], refs[2 * n + 3 :]
     oq[...] = jnp.zeros_like(oq)
-    for kv, dkv, first in zip(kvs, dkvs, firsts):
+    for kv, dkv, which in zip(kvs, dkvs, names):
         count = kv.shape[0]
         acc[0:count] = jnp.zeros((count,) + acc.shape[1:], F32)
 
         @pl.loop(0, 2)
         def _(half):
             def body(units):
-                keys, b = load_units(ids, kv, bias, first, half, units)
+                keys, b = load_units(ids, kv, bias, which, half, units)
                 for p in range(2):
                     keys_t = keys[p].T
                     qs = [qd[half, 2 * p + i] for i in range(2)]
@@ -221,7 +227,7 @@
                         oq[half, r, 0:32] += t[0:32, 0:128]
                         oq[half, r, 32:64] += t[32:64, 128:256]
 
-            over_units(ids, act, lst, first, count, half, body)
+            over_units(lists, which, half, body)
 
         dkv[...] = acc[0:count].astype(BF16)
 
@@ -278,37 +284,29 @@
         out[r] = (inv * (g - mean - xhat * along)).astype(BF16)
 
 
-def stats_call(firsts, begin, end, ids, active, kvs, rest):
+def stats_call(names, begin, end, ids, lists, kvs, rest):
     out = ((2, 4, 2, 128), F32) if end else ((3, 2, 4, 8, 128), F32)
     return call(
-        functools.partial(stats_kernel, firsts, begin, end),
+        functools.partial(stats_kernel, names, begin, end),
         [out],
         2,
         len(kvs) + len(rest),
-        [
-            pltpu.VMEM((2, 4, 128, 256), BF16),
-            pltpu.SMEM((9,), jnp.int32),
-            pltpu.VMEM((3, 2, 4, 8, 128), F32),
-        ],
+        [pltpu.VMEM((3, 2, 4, 8, 128), F32)],
         flops=10 ** 9,
         nbytes=10 ** 7,
-    )(ids, active, *kvs, *rest)[0]
-
-
-def back_call(firsts, ids, active, kvs, rest):
+    )(ids, lists, *kvs, *rest)[0]
+
+
+def back_call(names, ids, lists, kvs, rest):
     res = call(
-        functools.partial(back_kernel, firsts),
+        functools.partial(back_kernel, names),
         [(kv.shape, BF16) for kv in kvs] + [((2, 4, 64, 128), F32)],
         2,
         len(kvs) + len(rest),
-        [
-            pltpu.VMEM((2, 4, 128, 256), BF16),
-            pltpu.SMEM((9,), jnp.int32),
-            pltpu.VMEM((4, 2, 2, 128, 128), F32),
-        ],
+        [pltpu.VMEM((4, 2, 2, 128, 128), F32)],
         flops=2 * 10 ** 9,
         nbytes=2 * 10 ** 7,
-    )(ids, active, *kvs, *rest)
+    )(ids, lists, *kvs, *rest)
     return res[:-1], res[-1]
 
 
@@ -340,17 +338,26 @@
     own = lax.all_gather(kv, "z", axis_index_groups=groups)
     up, down = to_z(own, -1), to_z(own, 1)
     up2, down2 = to_z(own[0:2], -2), to_z(own[2:4], 2)
-    rest = (bias, pack, pack_other)
-    state = stats_call(((0, 0),), True, False, ids, active, (own,), rest)
-    state = stats_call(((1, 0), (-1, 0)), False, False, ids, active, (up, down), rest + (state,))
-    stats = stats_call(((2, 0), (-2, 2)), False, True, ids, active, (up2, down2), rest + (state,))
-    (d_up,), oq1 = back_call(((1, 0),), ids, active, (up,), rest + (stats,))
+    lists, qd = pl.pallas_call(
+        setup_kernel,
+        out_shape=shapes(((90,), jnp.int32), ((2, 4, 128, 256), BF16)),
+        in_specs=[smem()] * 2 + [vmem()] * 2,
+        out_specs=[smem(), vmem()],
+        compiler_params=pltpu.CompilerParams(vmem_limit_bytes=24 * 1024 * 1024),
+    )(ids, active, pack, pack_other)
+    rest = (bias, qd)
+    state = stats_call((OWN,), True, False, ids, lists, (own,), rest)
+    stats = stats_call(
+        (UP, DOWN, UP2, DOWN2), False, True, ids, lists, (up, down, up2, down2), rest + (state,)
+    )
+    rest = rest + (stats,)
+    (d_up2, d_down2), oq2 = back_call((UP2, DOWN2), ids, lists, (up2, down2), rest)
+    r_up2, r_down2 = to_z(d_up2, 2), to_z(d_down2, -2)
+    (d_up,), oq1 = back_call((UP,), ids, lists, (up,), rest)
     r_up = to_z(d_up, 1)
-    (d_down,), oq3 = back_call(((-1, 0),), ids, active, (down,), rest + (stats,))
+    (d_down,), oq3 = back_call((DOWN,), ids, lists, (down,), rest)
     r_down = to_z(d_down, -1)
-    (d_up2, d_down2), oq2 = back_call(((2, 0), (-2, 2)), ids, active, (up2, down2), rest + (stats,))
-    r_up2, r_down2 = to_z(d_up2, 2), to_z(d_down2, -2)
-    (d_own,), oq0 = back_call(((0, 0),), ids, active, (own,), rest + (stats,))
+    (d_own,), oq0 = back_call((OWN,), ids, lists, (own,), rest)
     oq = oq0 + oq1 + oq2 + oq3
     oq = jnp.concatenate([oq[:, :, :32] * SCALE, oq[:, :, 32:]], axis=2)
     oq_other = lax.ppermute(oq[1].astype(BF16), "xl", SWAP)

time: 188 us -> 182 us (0.968)
  the two profiles are of different devices: /device:TPU:85 before, /device:TPU:1 now
where the time goes in v5:
time: 182 us; the launch traced here: 179 us
  starting transfers between devices  78.4 us (43%)
  blocking collectives  33 us (18%)
  Pallas kernels  28.2 us (15%)
  waiting for transfers between devices  20.5 us (11%)
  between operations  14.3 us (8%)
  local copies, waits for them, and re-layouts  3.33 us (2%)
    all_gather x1, blocking collectives, per_device(): own = lax.all_gather(kv, 'z', axis_index_groups=groups)  33 us
    ppermute x8, starting transfers between devices, to_z(): return lax.ppermute(x, 'z', [(j, (j + step) % 16) for j in range(16)])  32.3 us
    ppermute x1, starting transfers between devices, per_device(): lax.ppermute(part_send, 'c', SWAP)  14.8 us
    pallas_call x4, Pallas kernels, back_call(): call(functools.partial(back_kernel, names), [(kv.shape, BF16) for kv in k...  12.4 us
    ppermute x8, waiting for transfers between devices, to_z(): return lax.ppermute(x, 'z', [(j, (j + step) % 16) for j in range(16)])  12 us
    ppermute x1, starting transfers between devices, per_device(): out_other = lax.ppermute(out_send, 'c', SWAP)  11.4 us
    pallas_call x2, Pallas kernels, stats_call(): call(functools.partial(stats_kernel, names, begin, end), [out], 2, len(kv...  6.89 us
    all_to_all x1, starting transfers between devices, per_device(): lax.all_to_all(bias, ('xh', 'xl'), 0, 0, tiled=True)  4.99 us
  transfers between devices with their start and end apart: 16, of which 9 were waited for; matrix products, arithmetic and copies ran while one was open for 1% of the time, Pallas kernels for 7%

profile of v5, /device:TPU:1, one launch (start us, length us, event | category | flops | bytes accessed | tf_op | source)
XLA Modules:
  0.0 179.0 jit_solution(8757010461266082421)
XLA Ops:
  7.8 3.5 %shard_map.86 = (bf16[512,128]{1,0:T(8,128)(2,1)}, bf16[512,128]{1,0:T(8,128)(2,1)}, f32[4,64,128]{2,1,0:T(8,128)}, f32[4,64,128]{2,1,0:T(8,128)}, bf16[4,4,128,128]{3,2,1,0:T(8,128)(2,1)}) custom-call(s32[3]{0:T(128)} %pad_add_fusion.ids, bf16[4,128,128]{2,1,0:T(8,128)(2,1)} %pair.1, f32[1,128]{1,0:T(1,128)} %bitcast.25, bf16[128,256]{1,0:T(8,128)(2,1)} %w_proj.1, ...), custom_call_target="tpu_custom_call" | custom-call | tf_op jit(solution)/shard_map/pallas_call | solution.py:321
  11.2 5.0 %all-to-all-start = ((bf16[4,4,128,128]{3,2,1,0:T(8,128)(2,1)}), bf16[4,4,128,128]{3,2,1,0:T(8,128)(2,1)S(1)}, u32[]{:S(2)}, u32[]{:S(2)}) async-start(bf16[4,4,128,128]{3,2,1,0:T(8,128)(2,1)} %get-tuple-element.26), calls=%async_computation | async-start | bytes 1048576 | tf_op jit(solution)/shard_map/all_to_all | solution.py:333
  16.2 3.4 %collective-permute-start = (bf16[512,128]{1,0:T(8,128)(2,1)}, bf16[512,128]{1,0:T(8,128)(2,1)S(1)}, u32[]{:S(2)}, u32[]{:S(2)}) collective-permute-start(bf16[512,128]{1,0:T(8,128)(2,1)} %get-tuple-element.27), channel_id=1, source_target_pairs={{0,32},{32,0},{1,33},{33,1},{2,34},{34,2},{3,35},{35,3},{4,36},{36... | collective-permute-start | bytes 393224 | tf_op jit(solution)/shard_map/ppermute | solution.py:332
  19.6 3.5 %collective-permute-done.pack1 = bf16[512,128]{1,0:T(8,128)(2,1)S(1)} collective-permute-done((bf16[512,128]{1,0:T(8,128)(2,1)}, bf16[512,128]{1,0:T(8,128)(2,1)S(1)}, u32[]{:S(2)}, u32[]{:S(2)}) %collective-permute-start) | collective-permute-done | bytes 131104 | tf_op jit(solution)/shard_map/ppermute | solution.py:332
  24.9 33.0 %all-gather = bf16[8,2,128,128]{3,2,1,0:T(8,128)(2,1)S(1)} all-gather(bf16[2,2,128,128]{3,2,1,0:T(8,128)(2,1)S(1)} %pad_maximum_fusion.1), channel_id=2, replica_groups={{0,8,16,24},{2,10,18,26},{4,12,20,28},{6,14,22,30},{1,9,17,25},{3,11,19..., dimensions={0}, use_global_device_ids=true | all-gather | bytes 655360 | tf_op jit(solution)/shard_map/all_gather | solution.py:338
  57.8 2.9 %collective-permute-start.2 = (bf16[4,2,2,128,128]{4,3,2,1,0:T(8,128)(2,1)S(1)}, bf16[4,2,2,128,128]{4,3,2,1,0:T(8,128)(2,1)S(1)}, u32[]{:S(2)}, u32[]{:S(2)}) collective-permute-start(bf16[4,2,2,128,128]{4,3,2,1,0:T(8,128)(2,1)S(1)} %bitcast.21), channel_id=1, source_target_pairs={{0,2},{2,4},{4,6},{6,8},{8,10},{10,12},{12,14},{14,16},{16,18},{18... | collective-permute-start | bytes 1572872 | tf_op jit(solution)/shard_map/ppermute | solution.py:314
  60.8 3.5 %collective-permute-start.1 = (bf16[4,2,2,128,128]{4,3,2,1,0:T(8,128)(2,1)S(1)}, bf16[4,2,2,128,128]{4,3,2,1,0:T(8,128)(2,1)S(1)}, u32[]{:S(2)}, u32[]{:S(2)}) collective-permute-start(bf16[4,2,2,128,128]{4,3,2,1,0:T(8,128)(2,1)S(1)} %bitcast.22), channel_id=1, source_target_pairs={{0,30},{2,0},{4,2},{6,4},{8,6},{10,8},{12,10},{14,12},{16,14},{18,... | collective-permute-start | bytes 1572872 | tf_op jit(solution)/shard_map/ppermute | solution.py:314
  64.4 2.9 %collective-permute-start.3 = (bf16[2,2,2,128,128]{4,3,2,1,0:T(8,128)(2,1)S(1)}, bf16[2,2,2,128,128]{4,3,2,1,0:T(8,128)(2,1)S(1)}, u32[]{:S(2)}, u32[]{:S(2)}) collective-permute-start(bf16[2,2,2,128,128]{4,3,2,1,0:T(8,128)(2,1)S(1)} %bitcast.31), channel_id=1, source_target_pairs={{0,28},{2,30},{4,0},{6,2},{8,4},{10,6},{12,8},{14,10},{16,12},{18,... | collective-permute-start | bytes 786440 | tf_op jit(solution)/shard_map/ppermute | solution.py:314
  67.3 3.2 %collective-permute-start.4 = (bf16[2,2,2,128,128]{4,3,2,1,0:T(8,128)(2,1)S(1)}, bf16[2,2,2,128,128]{4,3,2,1,0:T(8,128)(2,1)S(1)}, u32[]{:S(2)}, u32[]{:S(2)}) collective-permute-start(bf16[2,2,2,128,128]{4,3,2,1,0:T(8,128)(2,1)S(1)} %bitcast.30), channel_id=1, source_target_pairs={{0,4},{2,6},{4,8},{6,10},{8,12},{10,14},{12,16},{14,18},{16,20},{1... | collective-permute-start | bytes 786440 | tf_op jit(solution)/shard_map/ppermute | solution.py:314
  76.2 3.6 %collective-permute-done.3.refs_2_.refs_0_ = bf16[2,2,2,128,128]{4,3,2,1,0:T(8,128)(2,1)S(1)} collective-permute-done((bf16[2,2,2,128,128]{4,3,2,1,0:T(8,128)(2,1)S(1)}, bf16[2,2,2,128,128]{4,3,2,1,0:T(8,128)(2,1)S(1)}, u32[]{:S(2)}, u32[]{:S(2)}) %collective-permute-start.3) | collective-permute-done | bytes 262176 | tf_op jit(solution)/shard_map/ppermute | solution.py:314
  81.2 4.5 %shard_map.89.refs_3_.refs_4_ = f32[2,4,2,128]{3,2,1,0:T(2,128)S(1)} custom-call(s32[3]{0:T(128)S(1)} %copy-done.8, s32[90]{0:T(128)S(1)} %get-tuple-element.29.lists, bf16[4,2,2,128,128]{4,3,2,1,0:T(8,128)(2,1)S(1)} %collective-permute-done.1.refs_0_, bf16[4,2,2,128,128]{4,3,2,1,0:T(8,128)(2,1)S(1)} %collective-permute-done.2.refs_1_.refs_0_, ...), custom_call_target="tpu_custom_call" | custom-call | flops 1000000000 | bytes 10000000 | tf_op jit(solution)/shard_map/pallas_call | solution.py:289
  85.7 3.7 %shard_map.91 = (bf16[4,2,2,128,128]{4,3,2,1,0:T(8,128)(2,1)S(1)}, f32[2,4,64,128]{3,2,1,0:T(8,128)S(1)}) custom-call(s32[3]{0:T(128)S(1)} %copy-done.8, s32[90]{0:T(128)S(1)} %get-tuple-element.29.lists, bf16[4,2,2,128,128]{4,3,2,1,0:T(8,128)(2,1)S(1)} %collective-permute-done.1.refs_0_, bf16[4,2,2,4,128,128]{5,4,3,2,1,0:T(8,128)(2,1)S(1)} %bitcast.17, ...), custom_call_target="tpu_custom_call" | custom-call | flops 2000000000 | bytes 20000000 | tf_op jit(solution)/shard_map/pallas_call | solution.py:301
  89.4 2.4 %collective-permute-start.7 = (bf16[4,2,2,128,128]{4,3,2,1,0:T(8,128)(2,1)S(1)}, bf16[4,2,2,128,128]{4,3,2,1,0:T(8,128)(2,1)S(1)}, u32[]{:S(2)}, u32[]{:S(2)}) collective-permute-start(bf16[4,2,2,128,128]{4,3,2,1,0:T(8,128)(2,1)S(1)} %get-tuple-element.40), channel_id=1, source_target_pairs={{0,2},{2,4},{4,6},{6,8},{8,10},{10,12},{12,14},{14,16},{16,18},{18... | collective-permute-start | bytes 1572872 | tf_op jit(solution)/shard_map/ppermute | solution.py:314
  91.8 2.5 %shard_map.93 = (bf16[4,2,2,128,128]{4,3,2,1,0:T(8,128)(2,1)S(1)}, f32[2,4,64,128]{3,2,1,0:T(8,128)S(1)}) custom-call(s32[3]{0:T(128)S(1)} %copy-done.8, s32[90]{0:T(128)S(1)} %get-tuple-element.29.lists, bf16[4,2,2,128,128]{4,3,2,1,0:T(8,128)(2,1)S(1)} %collective-permute-done.2.refs_1_.refs_0_, bf16[4,2,2,4,128,128]{5,4,3,2,1,0:T(8,128)(2,1)S(1)} %bitcast.18, ...), custom_call_target="tpu_custom_call" | custom-call | flops 2000000000 | bytes 20000000 | tf_op jit(solution)/shard_map/pallas_call | solution.py:301
  94.3 9.0 %collective-permute-start.8 = (bf16[4,2,2,128,128]{4,3,2,1,0:T(8,128)(2,1)S(1)}, bf16[4,2,2,128,128]{4,3,2,1,0:T(8,128)(2,1)S(1)}, u32[]{:S(2)}, u32[]{:S(2)}) collective-permute-start(bf16[4,2,2,128,128]{4,3,2,1,0:T(8,128)(2,1)S(1)} %get-tuple-element.41), channel_id=1, source_target_pairs={{0,30},{2,0},{4,2},{6,4},{8,6},{10,8},{12,10},{14,12},{16,14},{18,... | collective-permute-start | bytes 1572872 | tf_op jit(solution)/shard_map/ppermute | solution.py:314
  103.3 2.5 %shard_map.92 = (bf16[2,2,2,128,128]{4,3,2,1,0:T(8,128)(2,1)S(1)}, bf16[2,2,2,128,128]{4,3,2,1,0:T(8,128)(2,1)S(1)}, f32[2,4,64,128]{3,2,1,0:T(8,128)S(1)}) custom-call(s32[3]{0:T(128)S(1)} %copy-done.8, s32[90]{0:T(128)S(1)} %get-tuple-element.29.lists, bf16[2,2,2,128,128]{4,3,2,1,0:T(8,128)(2,1)S(1)} %collective-permute-done.3.refs_2_.refs_0_, ...), custom_call_target="tpu_custom_call" | custom-call | flops 2000000000 | bytes 20000000 | tf_op jit(solution)/shard_map/pallas_call | solution.py:301
  107.8 6.3 %collective-permute-start.10 = (bf16[2,2,2,128,128]{4,3,2,1,0:T(8,128)(2,1)S(1)}, bf16[2,2,2,128,128]{4,3,2,1,0:T(8,128)(2,1)S(1)}, u32[]{:S(2)}, u32[]{:S(2)}) collective-permute-start(bf16[2,2,2,128,128]{4,3,2,1,0:T(8,128)(2,1)S(1)} %get-tuple-element.43), channel_id=1, source_target_pairs={{0,28},{2,30},{4,0},{6,2},{8,4},{10,6},{12,8},{14,10},{16,12},{18,... | collective-permute-start | bytes 786440 | tf_op jit(solution)/shard_map/ppermute | solution.py:314
  114.1 3.7 %shard_map.90 = (bf16[4,2,2,128,128]{4,3,2,1,0:T(8,128)(2,1)S(1)}, f32[2,4,64,128]{3,2,1,0:T(8,128)S(1)}) custom-call(s32[3]{0:T(128)S(1)} %copy-done.8, s32[90]{0:T(128)S(1)} %get-tuple-element.29.lists, bf16[4,2,2,128,128]{4,3,2,1,0:T(8,128)(2,1)S(1)} %bitcast.24, bf16[4,2,2,4,128,128]{5,4,3,2,1,0:T(8,128)(2,1)S(1)} %bitcast.20, ...), custom_call_target="tpu_custom_call" | custom-call | flops 2000000000 | bytes 20000000 | tf_op jit(solution)/shard_map/pallas_call | solution.py:301
  117.9 7.0 %collective-permute-done.10.r_down2 = bf16[2,2,2,128,128]{4,3,2,1,0:T(8,128)(2,1)S(1)} collective-permute-done((bf16[2,2,2,128,128]{4,3,2,1,0:T(8,128)(2,1)S(1)}, bf16[2,2,2,128,128]{4,3,2,1,0:T(8,128)(2,1)S(1)}, u32[]{:S(2)}, u32[]{:S(2)}) %collective-permute-start.10) | collective-permute-done | bytes 262176 | tf_op jit(solution)/shard_map/ppermute | solution.py:314
  126.0 4.8 %all-to-all-start.1 = ((bf16[4,2,2,128,128]{4,3,2,1,0:T(8,128)(2,1)}), bf16[4,2,2,128,128]{4,3,2,1,0:T(8,128)(2,1)S(1)}, u32[]{:S(2)}, u32[]{:S(2)}) async-start(bf16[4,2,2,128,128]{4,3,2,1,0:T(8,128)(2,1)} %shard_map.95), calls=%async_computation.1 | async-start | bytes 1048576 | tf_op jit(solution)/shard_map/all_to_all | solution.py:372
  130.9 3.3 %collective-permute-start.5 = (bf16[4,64,128]{2,1,0:T(8,128)(2,1)S(1)}, bf16[4,64,128]{2,1,0:T(8,128)(2,1)S(1)}, u32[]{:S(2)}, u32[]{:S(2)}) collective-permute-start(bf16[4,64,128]{2,1,0:T(8,128)(2,1)S(1)} %fusion.3), channel_id=1, source_target_pairs={{0,32},{32,0},{1,33},{33,1},{2,34},{34,2},{3,35},{35,3},{4,36},{36... | collective-permute-start | bytes 196616 | tf_op jit(solution)/shard_map/ppermute | solution.py:363
  136.7 11.4 %collective-permute-start.6 = (bf16[4,64,128]{2,1,0:T(8,128)(2,1)S(1)}, bf16[4,64,128]{2,1,0:T(8,128)(2,1)S(1)}, u32[]{:S(2)}, u32[]{:S(2)}) collective-permute-start(bf16[4,64,128]{2,1,0:T(8,128)(2,1)S(1)} %get-tuple-element.38), channel_id=1, source_target_pairs={{0,1},{1,0},{2,3},{3,2},{4,5},{5,4},{6,7},{7,6},{8,9},{9,8},{10,11... | collective-permute-start | bytes 196616 | tf_op jit(solution)/shard_map/ppermute | solution.py:367
  149.0 3.4 %collective-permute-start.11 = (bf16[2,128,128]{2,1,0:T(8,128)(2,1)S(1)}, bf16[2,128,128]{2,1,0:T(8,128)(2,1)S(1)}, u32[]{:S(2)}, u32[]{:S(2)}) collective-permute-start(bf16[2,128,128]{2,1,0:T(8,128)(2,1)S(1)} %slice_reduce_fusion), channel_id=1, source_target_pairs={{0,32},{32,0},{1,33},{33,1},{2,34},{34,2},{3,35},{35,3},{4,36},{36... | collective-permute-start | bytes 196616 | tf_op jit(solution)/shard_map/ppermute | solution.py:375
  155.3 14.8 %collective-permute-start.12 = (bf16[4,128,128]{2,1,0:T(8,128)(2,1)S(1)}, bf16[4,128,128]{2,1,0:T(8,128)(2,1)S(1)}, u32[]{:S(2)}, u32[]{:S(2)}) collective-permute-start(bf16[4,128,128]{2,1,0:T(8,128)(2,1)S(1)} %get-tuple-element.47), channel_id=1, source_target_pairs={{0,1},{1,0},{2,3},{3,2},{4,5},{5,4},{6,7},{7,6},{8,9},{9,8},{10,11... | collective-permute-start | bytes 393224 | tf_op jit(solution)/shard_map/ppermute | solution.py:384
  (57 shorter events, 20.8 us)
Async XLA Ops:
  7.7 62.8 %copy-start.8 = (s32[3]{0:T(128)S(1)}, s32[3]{0:T(128)}, u32[]{:S(2)}) copy-start(s32[3]{0:T(128)} %pad_add_fusion.ids) | copy-start | bytes 40
  7.8 62.8 %copy-start.9 = (s32[16,16]{1,0:T(8,128)S(1)}, s32[16,16]{1,0:T(8,128)}, u32[]{:S(2)}) copy-start(s32[16,16]{1,0:T(8,128)} %act.1) | copy-start | bytes 3076
  11.2 59.4 %copy-start.4 = (bf16[512,128]{1,0:T(8,128)(2,1)S(1)}, bf16[512,128]{1,0:T(8,128)(2,1)}, u32[]{:S(2)}) copy-start(bf16[512,128]{1,0:T(8,128)(2,1)} %get-tuple-element.25.pack0) | copy-start | bytes 393220
  11.2 11.9 %all-to-all-start = ((bf16[4,4,128,128]{3,2,1,0:T(8,128)(2,1)}), bf16[4,4,128,128]{3,2,1,0:T(8,128)(2,1)S(1)}, u32[]{:S(2)}, u32[]{:S(2)}) async-start(bf16[4,4,128,128]{3,2,1,0:T(8,128)(2,1)} %get-tuple-element.26), calls=%async_computation | async-start | bytes 1048576 | tf_op jit(solution)/shard_map/all_to_all | solution.py:333
  16.2 56.0 %all-gather.4.cloned.1.call-start = ((), (), s32[]{:S(2)}) async-start(), calls=%async_computation.2 | async-start | bytes 2621440 | tf_op jit(solution)/shard_map/all_gather | solution.py:335
  16.2 6.8 %collective-permute-start = (bf16[512,128]{1,0:T(8,128)(2,1)}, bf16[512,128]{1,0:T(8,128)(2,1)S(1)}, u32[]{:S(2)}, u32[]{:S(2)}) collective-permute-start(bf16[512,128]{1,0:T(8,128)(2,1)} %get-tuple-element.27), channel_id=1, source_target_pairs={{0,32},{32,0},{1,33},{33,1},{2,34},{34,2},{3,35},{35,3},{4,36},{36... | collective-permute-start | bytes 393224 | tf_op jit(solution)/shard_map/ppermute | solution.py:332
  57.8 23.4 %collective-permute-start.2 = (bf16[4,2,2,128,128]{4,3,2,1,0:T(8,128)(2,1)S(1)}, bf16[4,2,2,128,128]{4,3,2,1,0:T(8,128)(2,1)S(1)}, u32[]{:S(2)}, u32[]{:S(2)}) collective-permute-start(bf16[4,2,2,128,128]{4,3,2,1,0:T(8,128)(2,1)S(1)} %bitcast.21), channel_id=1, source_target_pairs={{0,2},{2,4},{4,6},{6,8},{8,10},{10,12},{12,14},{14,16},{16,18},{18... | collective-permute-start | bytes 1572872 | tf_op jit(solution)/shard_map/ppermute | solution.py:314
  60.8 20.4 %collective-permute-start.1 = (bf16[4,2,2,128,128]{4,3,2,1,0:T(8,128)(2,1)S(1)}, bf16[4,2,2,128,128]{4,3,2,1,0:T(8,128)(2,1)S(1)}, u32[]{:S(2)}, u32[]{:S(2)}) collective-permute-start(bf16[4,2,2,128,128]{4,3,2,1,0:T(8,128)(2,1)S(1)} %bitcast.22), channel_id=1, source_target_pairs={{0,30},{2,0},{4,2},{6,4},{8,6},{10,8},{12,10},{14,12},{16,14},{18,... | collective-permute-start | bytes 1572872 | tf_op jit(solution)/shard_map/ppermute | solution.py:314
  64.4 15.4 %collective-permute-start.3 = (bf16[2,2,2,128,128]{4,3,2,1,0:T(8,128)(2,1)S(1)}, bf16[2,2,2,128,128]{4,3,2,1,0:T(8,128)(2,1)S(1)}, u32[]{:S(2)}, u32[]{:S(2)}) collective-permute-start(bf16[2,2,2,128,128]{4,3,2,1,0:T(8,128)(2,1)S(1)} %bitcast.31), channel_id=1, source_target_pairs={{0,28},{2,30},{4,0},{6,2},{8,4},{10,6},{12,8},{14,10},{16,12},{18,... | collective-permute-start | bytes 786440 | tf_op jit(solution)/shard_map/ppermute | solution.py:314
  67.3 13.9 %collective-permute-start.4 = (bf16[2,2,2,128,128]{4,3,2,1,0:T(8,128)(2,1)S(1)}, bf16[2,2,2,128,128]{4,3,2,1,0:T(8,128)(2,1)S(1)}, u32[]{:S(2)}, u32[]{:S(2)}) collective-permute-start(bf16[2,2,2,128,128]{4,3,2,1,0:T(8,128)(2,1)S(1)} %bitcast.30), channel_id=1, source_target_pairs={{0,4},{2,6},{4,8},{6,10},{8,12},{10,14},{12,16},{14,18},{16,20},{1... | collective-permute-start | bytes 786440 | tf_op jit(solution)/shard_map/ppermute | solution.py:314
  89.4 35.5 %collective-permute-start.7 = (bf16[4,2,2,128,128]{4,3,2,1,0:T(8,128)(2,1)S(1)}, bf16[4,2,2,128,128]{4,3,2,1,0:T(8,128)(2,1)S(1)}, u32[]{:S(2)}, u32[]{:S(2)}) collective-permute-start(bf16[4,2,2,128,128]{4,3,2,1,0:T(8,128)(2,1)S(1)} %get-tuple-element.40), channel_id=1, source_target_pairs={{0,2},{2,4},{4,6},{6,8},{8,10},{10,12},{12,14},{14,16},{16,18},{18... | collective-permute-start | bytes 1572872 | tf_op jit(solution)/shard_map/ppermute | solution.py:314
  94.3 30.6 %collective-permute-start.8 = (bf16[4,2,2,128,128]{4,3,2,1,0:T(8,128)(2,1)S(1)}, bf16[4,2,2,128,128]{4,3,2,1,0:T(8,128)(2,1)S(1)}, u32[]{:S(2)}, u32[]{:S(2)}) collective-permute-start(bf16[4,2,2,128,128]{4,3,2,1,0:T(8,128)(2,1)S(1)} %get-tuple-element.41), channel_id=1, source_target_pairs={{0,30},{2,0},{4,2},{6,4},{8,6},{10,8},{12,10},{14,12},{16,14},{18,... | collective-permute-start | bytes 1572872 | tf_op jit(solution)/shard_map/ppermute | solution.py:314
  105.9 12.0 %collective-permute-start.9 = (bf16[2,2,2,128,128]{4,3,2,1,0:T(8,128)(2,1)S(1)}, bf16[2,2,2,128,128]{4,3,2,1,0:T(8,128)(2,1)S(1)}, u32[]{:S(2)}, u32[]{:S(2)}) collective-permute-start(bf16[2,2,2,128,128]{4,3,2,1,0:T(8,128)(2,1)S(1)} %get-tuple-element.42), channel_id=1, source_target_pairs={{0,4},{2,6},{4,8},{6,10},{8,12},{10,14},{12,16},{14,18},{16,20},{1... | collective-permute-start | bytes 786440 | tf_op jit(solution)/shard_map/ppermute | solution.py:314
  107.8 17.1 %collective-permute-start.10 = (bf16[2,2,2,128,128]{4,3,2,1,0:T(8,128)(2,1)S(1)}, bf16[2,2,2,128,128]{4,3,2,1,0:T(8,128)(2,1)S(1)}, u32[]{:S(2)}, u32[]{:S(2)}) collective-permute-start(bf16[2,2,2,128,128]{4,3,2,1,0:T(8,128)(2,1)S(1)} %get-tuple-element.43), channel_id=1, source_target_pairs={{0,28},{2,30},{4,0},{6,2},{8,4},{10,6},{12,8},{14,10},{16,12},{18,... | collective-permute-start | bytes 786440 | tf_op jit(solution)/shard_map/ppermute | solution.py:314
  126.0 10.0 %copy-start.7 = (bf16[64,128]{1,0:T(8,128)(2,1)S(1)}, bf16[64,128]{1,0:T(8,128)(2,1)}, u32[]{:S(2)}) copy-start(bf16[64,128]{1,0:T(8,128)(2,1)} %w_out.1) | copy-start | bytes 49156
  126.0 28.4 %copy-start.5 = (bf16[128,256]{1,0:T(8,128)(2,1)S(1)}, bf16[128,256]{1,0:T(8,128)(2,1)}, u32[]{:S(2)}) copy-start(bf16[128,256]{1,0:T(8,128)(2,1)} %w_proj.1) | copy-start | bytes 196612
  126.0 28.4 %copy-start.6 = (f32[4,64,128]{2,1,0:T(8,128)S(1)}, f32[4,64,128]{2,1,0:T(8,128)}, u32[]{:S(2)}) copy-start(f32[4,64,128]{2,1,0:T(8,128)} %get-tuple-element.45.go) | copy-start | bytes 393220
  126.0 23.0 %all-to-all-start.1 = ((bf16[4,2,2,128,128]{4,3,2,1,0:T(8,128)(2,1)}), bf16[4,2,2,128,128]{4,3,2,1,0:T(8,128)(2,1)S(1)}, u32[]{:S(2)}, u32[]{:S(2)}) async-start(bf16[4,2,2,128,128]{4,3,2,1,0:T(8,128)(2,1)} %shard_map.95), calls=%async_computation.1 | async-start | bytes 1048576 | tf_op jit(solution)/shard_map/all_to_all | solution.py:372
  130.8 40.2 %copy-start.3 = (bf16[4,128,128]{2,1,0:T(8,128)(2,1)S(1)}, bf16[4,128,128]{2,1,0:T(8,128)(2,1)}, u32[]{:S(2)}) copy-start(bf16[4,128,128]{2,1,0:T(8,128)(2,1)} %pair.1) | copy-start | bytes 393220
  130.8 40.2 %copy-start.10 = (f32[128]{0:T(128)S(1)}, f32[128]{0:T(128)}, u32[]{:S(2)}) copy-start(f32[128]{0:T(128)} %param.8) | copy-start | bytes 1540
  130.9 5.0 %collective-permute-start.5 = (bf16[4,64,128]{2,1,0:T(8,128)(2,1)S(1)}, bf16[4,64,128]{2,1,0:T(8,128)(2,1)S(1)}, u32[]{:S(2)}, u32[]{:S(2)}) collective-permute-start(bf16[4,64,128]{2,1,0:T(8,128)(2,1)S(1)} %fusion.3), channel_id=1, source_target_pairs={{0,32},{32,0},{1,33},{33,1},{2,34},{34,2},{3,35},{35,3},{4,36},{36... | collective-permute-start | bytes 196616 | tf_op jit(solution)/shard_map/ppermute | solution.py:363
  136.7 12.3 %collective-permute-start.6 = (bf16[4,64,128]{2,1,0:T(8,128)(2,1)S(1)}, bf16[4,64,128]{2,1,0:T(8,128)(2,1)S(1)}, u32[]{:S(2)}, u32[]{:S(2)}) collective-permute-start(bf16[4,64,128]{2,1,0:T(8,128)(2,1)S(1)} %get-tuple-element.38), channel_id=1, source_target_pairs={{0,1},{1,0},{2,3},{3,2},{4,5},{5,4},{6,7},{7,6},{8,9},{9,8},{10,11... | collective-permute-start | bytes 196616 | tf_op jit(solution)/shard_map/ppermute | solution.py:367
  149.0 5.4 %collective-permute-start.11 = (bf16[2,128,128]{2,1,0:T(8,128)(2,1)S(1)}, bf16[2,128,128]{2,1,0:T(8,128)(2,1)S(1)}, u32[]{:S(2)}, u32[]{:S(2)}) collective-permute-start(bf16[2,128,128]{2,1,0:T(8,128)(2,1)S(1)} %slice_reduce_fusion), channel_id=1, source_target_pairs={{0,32},{32,0},{1,33},{33,1},{2,34},{34,2},{3,35},{35,3},{4,36},{36... | collective-permute-start | bytes 196616 | tf_op jit(solution)/shard_map/ppermute | solution.py:375
  155.3 15.7 %collective-permute-start.12 = (bf16[4,128,128]{2,1,0:T(8,128)(2,1)S(1)}, bf16[4,128,128]{2,1,0:T(8,128)(2,1)S(1)}, u32[]{:S(2)}, u32[]{:S(2)}) collective-permute-start(bf16[4,128,128]{2,1,0:T(8,128)(2,1)S(1)} %get-tuple-element.47), channel_id=1, source_target_pairs={{0,1},{1,0},{2,3},{3,2},{4,5},{5,4},{6,7},{7,6},{8,9},{9,8},{10,11... | collective-permute-start | bytes 393224 | tf_op jit(solution)/shard_map/ppermute | solution.py:384
  (4 other events, 19.7 us)
Sparse Core Ops, SparseCore 0:
  24.1 46.7 all-gather.3

commit v6 on v5

--- a/solution.py
+++ b/solution.py
@@ -18,6 +18,10 @@
 SWAP = [(0, 1), (1, 0)]
 OWN, UP, DOWN, UP2, DOWN2 = range(5)
 ARRAYS = ((0, 0, 4), (1, 0, 4), (-1, 0, 4), (2, 0, 2), (-2, 2, 2))
+
+
+def place():
+    return [lax.axis_index(name) for name in ("z", "xl", "c")]
 
 
 def vmem():
@@ -59,7 +63,8 @@
     return centred * inv, inv
 
 
-def prep_kernel(ids, *refs):
+def prep_kernel(*refs):
+    ids = place()
     here, (keep, send, gate_out, go_out, bias_out) = refs[:6], refs[6:11]
     pair, gain, w_proj, w_out, d_out, bias = local = refs[11:17]
     proj_s, sems = refs[17:]
@@ -108,7 +113,8 @@
     return zk // 2 + 8 * xk
 
 
-def setup_kernel(ids, act, pack0, pack1, lists, qd):
+def setup_kernel(act, pack0, pack1, lists, qd):
+    ids = place()
     fill_queries(qd, (pack0, pack1))
     for k, (step, low, count) in enumerate(ARRAYS):
         for half in range(2):
@@ -148,8 +154,8 @@
         body([lists[base + n - 1]])
 
 
-def stats_kernel(names, begin, end, ids, lists, *refs):
-    n = len(names)
+def stats_kernel(names, begin, end, lists, *refs):
+    n, ids = len(names), place()
     kvs, (bias, qd), refs = refs[:n], refs[n : n + 2], refs[n + 2 :]
     before, refs = (None, refs) if begin else (refs[0], refs[1:])
     out, st = refs
@@ -195,8 +201,8 @@
             out[half, r, 1:2] = jnp.sum(st[2, half, r] * f, axis=0, keepdims=True) / total
 
 
-def back_kernel(names, ids, lists, *refs):
-    n = len(names)
+def back_kernel(names, lists, *refs):
+    n, ids = len(names), place()
     kvs, (bias, qd, stats) = refs[:n], refs[n : n + 3]
     dkvs, (oq, acc) = refs[n + 3 : 2 * n + 3], refs[2 * n + 3 :]
     oq[...] = jnp.zeros_like(oq)
@@ -232,8 +238,8 @@
         dkv[...] = acc[0:count].astype(BF16)
 
 
-def out_kernel(ids, oq_own, oq_other, gate, w_out, keep, send):
-    xl, c = ids[1], ids[2]
+def out_kernel(oq_own, oq_other, gate, w_out, keep, send):
+    _, xl, c = place()
     w_t = w_out[...].T
     for r in range(4):
         mine, theirs = oq_own[0, r, 32:64], oq_other[r, 32:64].astype(F32)
@@ -246,17 +252,17 @@
         send[r] = jnp.where(c == 0, high, low).astype(BF16)
 
 
-def sum_kernel(d_own, r_up, r_down, r_up2, r_down2, out):
+def sum_kernel(d_own, r_up, r_down, r_up2, r_down2, own, other):
     for m in range(4):
         total = d_own[m].astype(F32) + r_up[m].astype(F32) + r_down[m].astype(F32)
         total += (r_up2[m] if m < 2 else r_down2[m - 2]).astype(F32)
-        out[m] = total.astype(BF16)
-
-
-def proj_kernel(ids, oq_own, oq_other, dkv_own, dkv_other, gate, go, w_proj, keep, send, dp):
-    xl = ids[1]
+        own[m], other[m] = total[0].astype(BF16), total[1].astype(BF16)
+
+
+def proj_kernel(oq_own, oq_other, dkv_own, dkv_other, gate, go, w_proj, keep, send, dp):
+    _, xl, _ = place()
     for p in range(2):
-        mine_kv = sum(dkv_own[m, 0, p].astype(F32) for m in range(4)).T
+        mine_kv = sum(dkv_own[m, p].astype(F32) for m in range(4)).T
         theirs_kv = dkv_other[p].astype(F32).T
         for i in range(2):
             r = 2 * p + i
@@ -284,29 +290,29 @@
         out[r] = (inv * (g - mean - xhat * along)).astype(BF16)
 
 
-def stats_call(names, begin, end, ids, lists, kvs, rest):
+def stats_call(names, begin, end, lists, kvs, rest):
     out = ((2, 4, 2, 128), F32) if end else ((3, 2, 4, 8, 128), F32)
     return call(
         functools.partial(stats_kernel, names, begin, end),
         [out],
-        2,
+        1,
         len(kvs) + len(rest),
         [pltpu.VMEM((3, 2, 4, 8, 128), F32)],
         flops=10 ** 9,
         nbytes=10 ** 7,
-    )(ids, lists, *kvs, *rest)[0]
-
-
-def back_call(names, ids, lists, kvs, rest):
+    )(lists, *kvs, *rest)[0]
+
+
+def back_call(names, lists, kvs, rest):
     res = call(
         functools.partial(back_kernel, names),
         [(kv.shape, BF16) for kv in kvs] + [((2, 4, 64, 128), F32)],
-        2,
+        1,
         len(kvs) + len(rest),
         [pltpu.VMEM((4, 2, 2, 128, 128), F32)],
         flops=2 * 10 ** 9,
         nbytes=2 * 10 ** 7,
-    )(ids, lists, *kvs, *rest)
+    )(lists, *kvs, *rest)
     return res[:-1], res[-1]
 
 
@@ -315,7 +321,6 @@
 
 
 def per_device(pair, gain, w_proj, w_out, tri_bias, active, d_out):
-    ids = jnp.stack([lax.axis_index(name) for name in ("z", "xl", "c")]).astype(jnp.int32)
     gain = gain.reshape(1, 128)
     args = (pair, gain, w_proj, w_out, d_out, tri_bias)
     pack, pack_send, gate, go, bias = pl.pallas_call(
@@ -323,12 +328,12 @@
         out_shape=shapes(
             *[((512, 128), BF16)] * 2, *[((4, 64, 128), F32)] * 2, ((4, 4, 128, 128), BF16)
         ),
-        in_specs=[smem()] + [pl.BlockSpec(memory_space=pl.ANY)] * 6,
+        in_specs=[pl.BlockSpec(memory_space=pl.ANY)] * 6,
         out_specs=[vmem()] * 5,
         scratch_shapes=[pltpu.VMEM(a.shape, a.dtype) for a in args]
         + [pltpu.VMEM((2, 256, 128), F32), pltpu.SemaphoreType.DMA((6,))],
         compiler_params=pltpu.CompilerParams(vmem_limit_bytes=56 * 1024 * 1024),
-    )(ids, *args)
+    )(*args)
     pack_other = lax.ppermute(pack_send, "xl", SWAP)
     bias = lax.all_to_all(bias, ("xh", "xl"), 0, 0, tiled=True).reshape(2, 2, 4, 128, 128)
     bias, pack_other = lax.optimization_barrier((bias, pack_other))
@@ -341,45 +346,47 @@
     lists, qd = pl.pallas_call(
         setup_kernel,
         out_shape=shapes(((90,), jnp.int32), ((2, 4, 128, 256), BF16)),
-        in_specs=[smem()] * 2 + [vmem()] * 2,
+        in_specs=[smem()] + [vmem()] * 2,
         out_specs=[smem(), vmem()],
         compiler_params=pltpu.CompilerParams(vmem_limit_bytes=24 * 1024 * 1024),
-    )(ids, active, pack, pack_other)
+    )(active, pack, pack_other)
     rest = (bias, qd)
-    state = stats_call((OWN,), True, False, ids, lists, (own,), rest)
-    stats = stats_call(
-        (UP, DOWN, UP2, DOWN2), False, True, ids, lists, (up, down, up2, down2), rest + (state,)
-    )
+    state = stats_call((OWN,), True, False, lists, (own,), rest)
+    state = stats_call((UP, DOWN), False, False, lists, (up, down), rest + (state,))
+    stats = stats_call((UP2, DOWN2), False, True, lists, (up2, down2), rest + (state,))
     rest = rest + (stats,)
-    (d_up2, d_down2), oq2 = back_call((UP2, DOWN2), ids, lists, (up2, down2), rest)
+    (d_up2, d_down2), oq2 = back_call((UP2, DOWN2), lists, (up2, down2), rest)
     r_up2, r_down2 = to_z(d_up2, 2), to_z(d_down2, -2)
-    (d_up,), oq1 = back_call((UP,), ids, lists, (up,), rest)
+    (d_up,), oq1 = back_call((UP,), lists, (up,), rest)
     r_up = to_z(d_up, 1)
-    (d_down,), oq3 = back_call((DOWN,), ids, lists, (down,), rest)
+    (d_down,), oq3 = back_call((DOWN,), lists, (down,), rest)
     r_down = to_z(d_down, -1)
-    (d_own,), oq0 = back_call((OWN,), ids, lists, (own,), rest)
+    (d_own,), oq0 = back_call((OWN,), lists, (own,), rest)
     oq = oq0 + oq1 + oq2 + oq3
     oq = jnp.concatenate([oq[:, :, :32] * SCALE, oq[:, :, 32:]], axis=2)
     oq_other = lax.ppermute(oq[1].astype(BF16), "xl", SWAP)
     out_keep, out_send = call(
-        out_kernel, [((4, 64, 128), F32), ((4, 64, 128), BF16)], 1, 4
-    )(ids, oq, oq_other, gate, w_out)
+        out_kernel, [((4, 64, 128), F32), ((4, 64, 128), BF16)], 0, 4
+    )(oq, oq_other, gate, w_out)
     out_other = lax.ppermute(out_send, "c", SWAP)
     out = (out_keep + out_other.astype(F32)).astype(BF16)
-    (sums,) = call(sum_kernel, [((4, 2, 2, 128, 128), BF16)], 0, 5)(
+    sums, sums_other = call(sum_kernel, [((4, 2, 128, 128), BF16)] * 2, 0, 5)(
         d_own, r_up, r_down, r_up2, r_down2
     )
-    dkv = lax.all_to_all(sums, "z", 0, 0, axis_index_groups=groups, tiled=True)
-    dkv, _ = lax.optimization_barrier((dkv, out_other))
-    theirs = jnp.sum(dkv[:, 1].astype(F32), axis=0).astype(BF16)
+    exchange = functools.partial(
+        lax.all_to_all, axis_name="z", split_axis=0, concat_axis=0, axis_index_groups=groups, tiled=True
+    )
+    theirs = jnp.sum(exchange(sums_other).astype(F32), axis=0).astype(BF16)
     dkv_other = lax.ppermute(theirs, "xl", SWAP)
+    dkv = exchange(sums)
+    dkv, _, _ = lax.optimization_barrier((dkv, out_other, dkv_other))
     part, part_send = call(
         proj_kernel,
         [((4, 128, 128), F32), ((4, 128, 128), BF16)],
-        1,
+        0,
         7,
         [pltpu.VMEM((256, 128), F32)],
-    )(ids, oq, oq_other, dkv, dkv_other, gate, go, w_proj)
+    )(oq, oq_other, dkv, dkv_other, gate, go, w_proj)
     (pair_gradient,) = call(final_kernel, [((4, 128, 128), BF16)], 0, 4)(
         pair, gain, part, lax.ppermute(part_send, "c", SWAP)
     )

time: 182 us -> 187 us (1.027)
  blocking collectives: 33 us -> 56.1 us
  starting transfers between devices: 78.4 us -> 58.9 us
  Pallas kernels: 28.2 us -> 42.6 us
  waiting for transfers between devices: 20.5 us -> 8.9 us
    all_to_all x0 -> x1, blocking collectives: none -> 23 us  [per_device(): theirs = jnp.sum(exchange(sums_other).astype(F32), axis=0).astype(BF16)]
    ppermute x8, waiting for transfers between devices: 12 us -> 0.69 us  [to_z(): return lax.ppermute(x, 'z', [(j, (j + step) % 16) for j in range(16)])]
    ppermute x1, starting transfers between devices: 14.8 us -> 3.99 us  [per_device(): lax.ppermute(part_send, 'c', SWAP)]
    pallas_call x4, Pallas kernels: 12.4 us -> 22.2 us  [back_call(): call(functools.partial(back_kernel, names), [(kv.shape, BF16) for kv in k...]
    ppermute x8, starting transfers between devices: 32.3 us -> 25.5 us  [to_z(): return lax.ppermute(x, 'z', [(j, (j + step) % 16) for j in range(16)])]
    pallas_call x5 -> x6, Pallas kernels: 9.62 us -> 15.1 us  [the longest x3 13.5 us: stats_call(): call(functools.partial(stats_kernel, names, begin, end), [out], 1, len(kv...]
    ppermute x1, starting transfers between devices: 11.4 us -> 8.65 us  [per_device(): out_other = lax.ppermute(out_send, 'c', SWAP)]
    ppermute x1, starting transfers between devices: 3.28 us -> 6.02 us  [per_device(): oq_other = lax.ppermute(oq[1].astype(BF16), 'xl', SWAP)]
  transfers between devices with their start and end apart: 16 -> 16, of which waited for: 9 -> 7; matrix products, arithmetic and copies ran while one was open for 1% -> 1% of each run, Pallas kernels for 7% -> 15%
where the time goes in v6:
time: 187 us; the launch traced here: 185 us
  starting transfers between devices  58.9 us (31%)
  blocking collectives  56.1 us (30%)
  Pallas kernels  42.6 us (23%)
  between operations  14.4 us (8%)
  waiting for transfers between devices  8.9 us (5%)
  local copies, waits for them, and re-layouts  3.33 us (2%)
    all_gather x1, blocking collectives, per_device(): own = lax.all_gather(kv, 'z', axis_index_groups=groups)  33.1 us
    ppermute x8, starting transfers between devices, to_z(): return lax.ppermute(x, 'z', [(j, (j + step) % 16) for j in range(16)])  25.5 us
    all_to_all x1, blocking collectives, per_device(): theirs = jnp.sum(exchange(sums_other).astype(F32), axis=0).astype(BF16)  23 us
    pallas_call x4, Pallas kernels, back_call(): call(functools.partial(back_kernel, names), [(kv.shape, BF16) for kv in k...  22.2 us
    pallas_call x3, Pallas kernels, stats_call(): call(functools.partial(stats_kernel, names, begin, end), [out], 1, len(kv...  13.5 us
    ppermute x1, starting transfers between devices, per_device(): out_other = lax.ppermute(out_send, 'c', SWAP)  8.65 us
    ppermute x1, starting transfers between devices, per_device(): oq_other = lax.ppermute(oq[1].astype(BF16), 'xl', SWAP)  6.02 us
    all_to_all x1, starting transfers between devices, per_device(): lax.all_to_all(bias, ('xh', 'xl'), 0, 0, tiled=True)  4.99 us
  transfers between devices with their start and end apart: 16, of which 7 were waited for; matrix products, arithmetic and copies ran while one was open for 1% of the time, Pallas kernels for 15%

profile of v6, /device:TPU:1, one launch (start us, length us, event | category | flops | bytes accessed | tf_op | source)
XLA Modules:
  0.0 185.1 jit_solution(5957379050499510155)
XLA Ops:
  7.2 2.7 %shard_map.86 = (bf16[512,128]{1,0:T(8,128)(2,1)}, bf16[512,128]{1,0:T(8,128)(2,1)}, f32[4,64,128]{2,1,0:T(8,128)}, f32[4,64,128]{2,1,0:T(8,128)}, bf16[4,4,128,128]{3,2,1,0:T(8,128)(2,1)}) custom-call(bf16[4,128,128]{2,1,0:T(8,128)(2,1)} %pair.1, f32[1,128]{1,0:T(1,128)} %bitcast.23, bf16[128,256]{1,0:T(8,128)(2,1)} %w_proj.1, bf16[64,128]{1,0:T(8,128)(2,1)} %w_out.1, ...), custom_call_target="tpu_custom_call" | custom-call | tf_op jit(solution)/shard_map/pallas_call | solution.py:326
  9.9 5.0 %all-to-all-start = ((bf16[4,4,128,128]{3,2,1,0:T(8,128)(2,1)}), bf16[4,4,128,128]{3,2,1,0:T(8,128)(2,1)S(1)}, u32[]{:S(2)}, u32[]{:S(2)}) async-start(bf16[4,4,128,128]{3,2,1,0:T(8,128)(2,1)} %get-tuple-element.28), calls=%async_computation | async-start | bytes 1048576 | tf_op jit(solution)/shard_map/all_to_all | solution.py:338
  14.9 3.4 %collective-permute-start = (bf16[512,128]{1,0:T(8,128)(2,1)}, bf16[512,128]{1,0:T(8,128)(2,1)S(1)}, u32[]{:S(2)}, u32[]{:S(2)}) collective-permute-start(bf16[512,128]{1,0:T(8,128)(2,1)} %get-tuple-element.29), channel_id=1, source_target_pairs={{0,32},{32,0},{1,33},{33,1},{2,34},{34,2},{3,35},{35,3},{4,36},{36... | collective-permute-start | bytes 393224 | tf_op jit(solution)/shard_map/ppermute | solution.py:337
  18.2 3.5 %collective-permute-done.pack1 = bf16[512,128]{1,0:T(8,128)(2,1)S(1)} collective-permute-done((bf16[512,128]{1,0:T(8,128)(2,1)}, bf16[512,128]{1,0:T(8,128)(2,1)S(1)}, u32[]{:S(2)}, u32[]{:S(2)}) %collective-permute-start) | collective-permute-done | bytes 131104 | tf_op jit(solution)/shard_map/ppermute | solution.py:337
  23.5 33.1 %all-gather = bf16[8,2,128,128]{3,2,1,0:T(8,128)(2,1)S(1)} all-gather(bf16[2,2,128,128]{3,2,1,0:T(8,128)(2,1)S(1)} %pad_maximum_fusion.1), channel_id=2, replica_groups={{0,8,16,24},{2,10,18,26},{4,12,20,28},{6,14,22,30},{1,9,17,25},{3,11,19..., dimensions={0}, use_global_device_ids=true | all-gather | bytes 655360 | tf_op jit(solution)/shard_map/all_gather | solution.py:343
  58.8 4.3 %collective-permute-start.3 = (bf16[4,2,2,128,128]{4,3,2,1,0:T(8,128)(2,1)S(1)}, bf16[4,2,2,128,128]{4,3,2,1,0:T(8,128)(2,1)S(1)}, u32[]{:S(2)}, u32[]{:S(2)}) collective-permute-start(bf16[4,2,2,128,128]{4,3,2,1,0:T(8,128)(2,1)S(1)} %bitcast.13), channel_id=1, source_target_pairs={{0,30},{2,0},{4,2},{6,4},{8,6},{10,8},{12,10},{14,12},{16,14},{18,... | collective-permute-start | bytes 1572872 | tf_op jit(solution)/shard_map/ppermute | solution.py:320
  63.2 2.8 %collective-permute-start.1 = (bf16[2,2,2,128,128]{4,3,2,1,0:T(8,128)(2,1)S(1)}, bf16[2,2,2,128,128]{4,3,2,1,0:T(8,128)(2,1)S(1)}, u32[]{:S(2)}, u32[]{:S(2)}) collective-permute-start(bf16[2,2,2,128,128]{4,3,2,1,0:T(8,128)(2,1)S(1)} %bitcast.29), channel_id=1, source_target_pairs={{0,28},{2,30},{4,0},{6,2},{8,4},{10,6},{12,8},{14,10},{16,12},{18,... | collective-permute-start | bytes 786440 | tf_op jit(solution)/shard_map/ppermute | solution.py:320
  66.0 3.4 %collective-permute-start.2 = (bf16[2,2,2,128,128]{4,3,2,1,0:T(8,128)(2,1)S(1)}, bf16[2,2,2,128,128]{4,3,2,1,0:T(8,128)(2,1)S(1)}, u32[]{:S(2)}, u32[]{:S(2)}) collective-permute-start(bf16[2,2,2,128,128]{4,3,2,1,0:T(8,128)(2,1)S(1)} %bitcast.28), channel_id=1, source_target_pairs={{0,4},{2,6},{4,8},{6,10},{8,12},{10,14},{12,16},{14,18},{16,20},{1... | collective-permute-start | bytes 786440 | tf_op jit(solution)/shard_map/ppermute | solution.py:320
  72.6 3.6 %shard_map.88.refs_4_ = f32[3,2,4,8,128]{4,3,2,1,0:T(8,128)S(1)} custom-call(s32[90]{0:T(128)S(1)} %get-tuple-element.31.lists, bf16[4,2,2,128,128]{4,3,2,1,0:T(8,128)(2,1)S(1)} %bitcast.14, bf16[4,2,2,4,128,128]{5,4,3,2,1,0:T(8,128)(2,1)S(1)} %bitcast.16, bf16[2,4,128,256]{3,2,1,0:T(8,128)(2,1)S(1)} %get-tuple-element.33.refs_2_.refs_3_), custom_call_target="tpu_custom_call" | custom-call | flops 1000000000 | bytes 10000000 | tf_op jit(solution)/shard_map/pallas_call | solution.py:295
  76.2 6.4 %shard_map.89.refs_4_ = f32[3,2,4,8,128]{4,3,2,1,0:T(8,128)S(1)} custom-call(s32[90]{0:T(128)S(1)} %get-tuple-element.31.lists, bf16[4,2,2,128,128]{4,3,2,1,0:T(8,128)(2,1)S(1)} %collective-permute-done.3.refs_0_, bf16[4,2,2,128,128]{4,3,2,1,0:T(8,128)(2,1)S(1)} %collective-permute-done.4.refs_1_.refs_0_, bf16[4,2,2,4,128,128]{5,4,3,2,1,0:T(8,128)(2,1)S(1)} %bitcast.17, ...), custom_call_target="tpu_custom_call" | custom-call | flops 1000000000 | bytes 10000000 | tf_op jit(solution)/shard_map/pallas_call | solution.py:295
  82.7 3.4 %shard_map.90.refs_3_.refs_4_ = f32[2,4,2,128]{3,2,1,0:T(2,128)S(1)} custom-call(s32[90]{0:T(128)S(1)} %get-tuple-element.31.lists, bf16[2,2,2,128,128]{4,3,2,1,0:T(8,128)(2,1)S(1)} %collective-permute-done.1.refs_0_, bf16[2,2,2,128,128]{4,3,2,1,0:T(8,128)(2,1)S(1)} %collective-permute-done.2.refs_1_, bf16[4,2,2,4,128,128]{5,4,3,2,1,0:T(8,128)(2,1)S(1)} %bitcast.18, ...), custom_call_target="tpu_custom_call" | custom-call | flops 1000000000 | bytes 10000000 | tf_op jit(solution)/shard_map/pallas_call | solution.py:295
  86.1 5.6 %shard_map.92 = (bf16[4,2,2,128,128]{4,3,2,1,0:T(8,128)(2,1)S(1)}, f32[2,4,64,128]{3,2,1,0:T(8,128)S(1)}) custom-call(s32[90]{0:T(128)S(1)} %get-tuple-element.31.lists, bf16[4,2,2,128,128]{4,3,2,1,0:T(8,128)(2,1)S(1)} %collective-permute-done.3.refs_0_, bf16[4,2,2,4,128,128]{5,4,3,2,1,0:T(8,128)(2,1)S(1)} %bitcast.19, ...), custom_call_target="tpu_custom_call" | custom-call | flops 2000000000 | bytes 20000000 | tf_op jit(solution)/shard_map/pallas_call | solution.py:307
  93.7 5.5 %shard_map.94 = (bf16[4,2,2,128,128]{4,3,2,1,0:T(8,128)(2,1)S(1)}, f32[2,4,64,128]{3,2,1,0:T(8,128)S(1)}) custom-call(s32[90]{0:T(128)S(1)} %get-tuple-element.31.lists, bf16[4,2,2,128,128]{4,3,2,1,0:T(8,128)(2,1)S(1)} %collective-permute-done.4.refs_1_.refs_0_, bf16[4,2,2,4,128,128]{5,4,3,2,1,0:T(8,128)(2,1)S(1)} %bitcast.20, ...), custom_call_target="tpu_custom_call" | custom-call | flops 2000000000 | bytes 20000000 | tf_op jit(solution)/shard_map/pallas_call | solution.py:307
  99.1 3.5 %collective-permute-start.8 = (bf16[4,2,2,128,128]{4,3,2,1,0:T(8,128)(2,1)S(1)}, bf16[4,2,2,128,128]{4,3,2,1,0:T(8,128)(2,1)S(1)}, u32[]{:S(2)}, u32[]{:S(2)}) collective-permute-start(bf16[4,2,2,128,128]{4,3,2,1,0:T(8,128)(2,1)S(1)} %get-tuple-element.43), channel_id=1, source_target_pairs={{0,30},{2,0},{4,2},{6,4},{8,6},{10,8},{12,10},{14,12},{16,14},{18,... | collective-permute-start | bytes 1572872 | tf_op jit(solution)/shard_map/ppermute | solution.py:320
  102.7 5.5 %shard_map.93 = (bf16[2,2,2,128,128]{4,3,2,1,0:T(8,128)(2,1)S(1)}, bf16[2,2,2,128,128]{4,3,2,1,0:T(8,128)(2,1)S(1)}, f32[2,4,64,128]{3,2,1,0:T(8,128)S(1)}) custom-call(s32[90]{0:T(128)S(1)} %get-tuple-element.31.lists, bf16[2,2,2,128,128]{4,3,2,1,0:T(8,128)(2,1)S(1)} %collective-permute-done.1.refs_0_, ...), custom_call_target="tpu_custom_call" | custom-call | flops 2000000000 | bytes 20000000 | tf_op jit(solution)/shard_map/pallas_call | solution.py:307
  110.1 5.5 %collective-permute-start.10 = (bf16[2,2,2,128,128]{4,3,2,1,0:T(8,128)(2,1)S(1)}, bf16[2,2,2,128,128]{4,3,2,1,0:T(8,128)(2,1)S(1)}, u32[]{:S(2)}, u32[]{:S(2)}) collective-permute-start(bf16[2,2,2,128,128]{4,3,2,1,0:T(8,128)(2,1)S(1)} %get-tuple-element.45), channel_id=1, source_target_pairs={{0,28},{2,30},{4,0},{6,2},{8,4},{10,6},{12,8},{14,10},{16,12},{18,... | collective-permute-start | bytes 786440 | tf_op jit(solution)/shard_map/ppermute | solution.py:320
  115.6 5.6 %shard_map.91 = (bf16[4,2,2,128,128]{4,3,2,1,0:T(8,128)(2,1)S(1)}, f32[2,4,64,128]{3,2,1,0:T(8,128)S(1)}) custom-call(s32[90]{0:T(128)S(1)} %get-tuple-element.31.lists, bf16[4,2,2,128,128]{4,3,2,1,0:T(8,128)(2,1)S(1)} %bitcast.15, bf16[4,2,2,4,128,128]{5,4,3,2,1,0:T(8,128)(2,1)S(1)} %bitcast.22, ...), custom_call_target="tpu_custom_call" | custom-call | flops 2000000000 | bytes 20000000 | tf_op jit(solution)/shard_map/pallas_call | solution.py:307
  122.8 23.0 %all_to_all.15 = bf16[4,2,128,128]{3,2,1,0:T(8,128)(2,1)S(1)} all-to-all(bf16[4,2,128,128]{3,2,1,0:T(8,128)(2,1)S(1)} %get-tuple-element.47), channel_id=1, replica_groups={{0,8,16,24},{2,10,18,26},{4,12,20,28},{6,14,22,30},{1,9,17,25},{3,11,19..., dimensions={0} | all-to-all | bytes 524288 | tf_op jit(solution)/shard_map/all_to_all | solution.py:379
  145.8 3.5 %all-to-all-start.1 = ((bf16[4,2,128,128]{3,2,1,0:T(8,128)(2,1)}), bf16[4,2,128,128]{3,2,1,0:T(8,128)(2,1)S(1)}, u32[]{:S(2)}, u32[]{:S(2)}) async-start(bf16[4,2,128,128]{3,2,1,0:T(8,128)(2,1)} %get-tuple-element.46), calls=%async_computation.1 | async-start | bytes 524288 | tf_op jit(solution)/shard_map/all_to_all | solution.py:381
  149.5 6.0 %collective-permute-start.5 = (bf16[4,64,128]{2,1,0:T(8,128)(2,1)S(1)}, bf16[4,64,128]{2,1,0:T(8,128)(2,1)S(1)}, u32[]{:S(2)}, u32[]{:S(2)}) collective-permute-start(bf16[4,64,128]{2,1,0:T(8,128)(2,1)S(1)} %fusion.3), channel_id=1, source_target_pairs={{0,32},{32,0},{1,33},{33,1},{2,34},{34,2},{3,35},{35,3},{4,36},{36... | collective-permute-start | bytes 196616 | tf_op jit(solution)/shard_map/ppermute | solution.py:367
  157.4 8.7 %collective-permute-start.6 = (bf16[4,64,128]{2,1,0:T(8,128)(2,1)S(1)}, bf16[4,64,128]{2,1,0:T(8,128)(2,1)S(1)}, u32[]{:S(2)}, u32[]{:S(2)}) collective-permute-start(bf16[4,64,128]{2,1,0:T(8,128)(2,1)S(1)} %get-tuple-element.40), channel_id=1, source_target_pairs={{0,1},{1,0},{2,3},{3,2},{4,5},{5,4},{6,7},{7,6},{8,9},{9,8},{10,11... | collective-permute-start | bytes 196616 | tf_op jit(solution)/shard_map/ppermute | solution.py:371
  166.1 2.9 %collective-permute-start.11 = (bf16[2,128,128]{2,1,0:T(8,128)(2,1)S(1)}, bf16[2,128,128]{2,1,0:T(8,128)(2,1)S(1)}, u32[]{:S(2)}, u32[]{:S(2)}) collective-permute-start(bf16[2,128,128]{2,1,0:T(8,128)(2,1)S(1)} %reduce_sum.12), channel_id=1, source_target_pairs={{0,32},{32,0},{1,33},{33,1},{2,34},{34,2},{3,35},{35,3},{4,36},{36... | collective-permute-start | bytes 196616 | tf_op jit(solution)/shard_map/ppermute | solution.py:380
  169.0 2.7 %collective-permute-done.11.dkv_other = bf16[2,128,128]{2,1,0:T(8,128)(2,1)S(1)} collective-permute-done((bf16[2,128,128]{2,1,0:T(8,128)(2,1)S(1)}, bf16[2,128,128]{2,1,0:T(8,128)(2,1)S(1)}, u32[]{:S(2)}, u32[]{:S(2)}) %collective-permute-start.11) | collective-permute-done | bytes 65568 | tf_op jit(solution)/shard_map/ppermute | solution.py:380
  172.2 4.0 %collective-permute-start.12 = (bf16[4,128,128]{2,1,0:T(8,128)(2,1)S(1)}, bf16[4,128,128]{2,1,0:T(8,128)(2,1)S(1)}, u32[]{:S(2)}, u32[]{:S(2)}) collective-permute-start(bf16[4,128,128]{2,1,0:T(8,128)(2,1)S(1)} %get-tuple-element.51), channel_id=1, source_target_pairs={{0,1},{1,0},{2,3},{3,2},{4,5},{5,4},{6,7},{7,6},{8,9},{9,8},{10,11... | collective-permute-start | bytes 393224 | tf_op jit(solution)/shard_map/ppermute | solution.py:391
  (54 shorter events, 17.2 us)
Async XLA Ops:
  7.2 62.2 %copy-start.7 = (s32[16,16]{1,0:T(8,128)S(1)}, s32[16,16]{1,0:T(8,128)}, u32[]{:S(2)}) copy-start(s32[16,16]{1,0:T(8,128)} %act.1) | copy-start | bytes 3076
  9.9 59.5 %copy-start.3 = (bf16[512,128]{1,0:T(8,128)(2,1)S(1)}, bf16[512,128]{1,0:T(8,128)(2,1)}, u32[]{:S(2)}) copy-start(bf16[512,128]{1,0:T(8,128)(2,1)} %get-tuple-element.27.pack0) | copy-start | bytes 393220
  9.9 11.9 %all-to-all-start = ((bf16[4,4,128,128]{3,2,1,0:T(8,128)(2,1)}), bf16[4,4,128,128]{3,2,1,0:T(8,128)(2,1)S(1)}, u32[]{:S(2)}, u32[]{:S(2)}) async-start(bf16[4,4,128,128]{3,2,1,0:T(8,128)(2,1)} %get-tuple-element.28), calls=%async_computation | async-start | bytes 1048576 | tf_op jit(solution)/shard_map/all_to_all | solution.py:338
  14.9 56.1 %all-gather.4.cloned.1.call-start = ((), (), s32[]{:S(2)}) async-start(), calls=%async_computation.3 | async-start | bytes 2621440 | tf_op jit(solution)/shard_map/all_gather | solution.py:340
  14.9 6.8 %collective-permute-start = (bf16[512,128]{1,0:T(8,128)(2,1)}, bf16[512,128]{1,0:T(8,128)(2,1)S(1)}, u32[]{:S(2)}, u32[]{:S(2)}) collective-permute-start(bf16[512,128]{1,0:T(8,128)(2,1)} %get-tuple-element.29), channel_id=1, source_target_pairs={{0,32},{32,0},{1,33},{33,1},{2,34},{34,2},{3,35},{35,3},{4,36},{36... | collective-permute-start | bytes 393224 | tf_op jit(solution)/shard_map/ppermute | solution.py:337
  56.6 19.6 %collective-permute-start.4 = (bf16[4,2,2,128,128]{4,3,2,1,0:T(8,128)(2,1)S(1)}, bf16[4,2,2,128,128]{4,3,2,1,0:T(8,128)(2,1)S(1)}, u32[]{:S(2)}, u32[]{:S(2)}) collective-permute-start(bf16[4,2,2,128,128]{4,3,2,1,0:T(8,128)(2,1)S(1)} %bitcast.12), channel_id=1, source_target_pairs={{0,2},{2,4},{4,6},{6,8},{8,10},{10,12},{12,14},{14,16},{16,18},{18... | collective-permute-start | bytes 1572872 | tf_op jit(solution)/shard_map/ppermute | solution.py:320
  58.8 17.4 %collective-permute-start.3 = (bf16[4,2,2,128,128]{4,3,2,1,0:T(8,128)(2,1)S(1)}, bf16[4,2,2,128,128]{4,3,2,1,0:T(8,128)(2,1)S(1)}, u32[]{:S(2)}, u32[]{:S(2)}) collective-permute-start(bf16[4,2,2,128,128]{4,3,2,1,0:T(8,128)(2,1)S(1)} %bitcast.13), channel_id=1, source_target_pairs={{0,30},{2,0},{4,2},{6,4},{8,6},{10,8},{12,10},{14,12},{16,14},{18,... | collective-permute-start | bytes 1572872 | tf_op jit(solution)/shard_map/ppermute | solution.py:320
  63.2 19.5 %collective-permute-start.1 = (bf16[2,2,2,128,128]{4,3,2,1,0:T(8,128)(2,1)S(1)}, bf16[2,2,2,128,128]{4,3,2,1,0:T(8,128)(2,1)S(1)}, u32[]{:S(2)}, u32[]{:S(2)}) collective-permute-start(bf16[2,2,2,128,128]{4,3,2,1,0:T(8,128)(2,1)S(1)} %bitcast.29), channel_id=1, source_target_pairs={{0,28},{2,30},{4,0},{6,2},{8,4},{10,6},{12,8},{14,10},{16,12},{18,... | collective-permute-start | bytes 786440 | tf_op jit(solution)/shard_map/ppermute | solution.py:320
  66.0 16.7 %collective-permute-start.2 = (bf16[2,2,2,128,128]{4,3,2,1,0:T(8,128)(2,1)S(1)}, bf16[2,2,2,128,128]{4,3,2,1,0:T(8,128)(2,1)S(1)}, u32[]{:S(2)}, u32[]{:S(2)}) collective-permute-start(bf16[2,2,2,128,128]{4,3,2,1,0:T(8,128)(2,1)S(1)} %bitcast.28), channel_id=1, source_target_pairs={{0,4},{2,6},{4,8},{6,10},{8,12},{10,14},{12,16},{14,18},{16,20},{1... | collective-permute-start | bytes 786440 | tf_op jit(solution)/shard_map/ppermute | solution.py:320
  91.7 30.1 %collective-permute-start.7 = (bf16[4,2,2,128,128]{4,3,2,1,0:T(8,128)(2,1)S(1)}, bf16[4,2,2,128,128]{4,3,2,1,0:T(8,128)(2,1)S(1)}, u32[]{:S(2)}, u32[]{:S(2)}) collective-permute-start(bf16[4,2,2,128,128]{4,3,2,1,0:T(8,128)(2,1)S(1)} %get-tuple-element.42), channel_id=1, source_target_pairs={{0,2},{2,4},{4,6},{6,8},{8,10},{10,12},{12,14},{14,16},{16,18},{18... | collective-permute-start | bytes 1572872 | tf_op jit(solution)/shard_map/ppermute | solution.py:320
  99.1 22.7 %collective-permute-start.8 = (bf16[4,2,2,128,128]{4,3,2,1,0:T(8,128)(2,1)S(1)}, bf16[4,2,2,128,128]{4,3,2,1,0:T(8,128)(2,1)S(1)}, u32[]{:S(2)}, u32[]{:S(2)}) collective-permute-start(bf16[4,2,2,128,128]{4,3,2,1,0:T(8,128)(2,1)S(1)} %get-tuple-element.43), channel_id=1, source_target_pairs={{0,30},{2,0},{4,2},{6,4},{8,6},{10,8},{12,10},{14,12},{16,14},{18,... | collective-permute-start | bytes 1572872 | tf_op jit(solution)/shard_map/ppermute | solution.py:320
  108.2 13.4 %collective-permute-start.9 = (bf16[2,2,2,128,128]{4,3,2,1,0:T(8,128)(2,1)S(1)}, bf16[2,2,2,128,128]{4,3,2,1,0:T(8,128)(2,1)S(1)}, u32[]{:S(2)}, u32[]{:S(2)}) collective-permute-start(bf16[2,2,2,128,128]{4,3,2,1,0:T(8,128)(2,1)S(1)} %get-tuple-element.44), channel_id=1, source_target_pairs={{0,4},{2,6},{4,8},{6,10},{8,12},{10,14},{12,16},{14,18},{16,20},{1... | collective-permute-start | bytes 786440 | tf_op jit(solution)/shard_map/ppermute | solution.py:320
  110.1 11.8 %collective-permute-start.10 = (bf16[2,2,2,128,128]{4,3,2,1,0:T(8,128)(2,1)S(1)}, bf16[2,2,2,128,128]{4,3,2,1,0:T(8,128)(2,1)S(1)}, u32[]{:S(2)}, u32[]{:S(2)}) collective-permute-start(bf16[2,2,2,128,128]{4,3,2,1,0:T(8,128)(2,1)S(1)} %get-tuple-element.45), channel_id=1, source_target_pairs={{0,28},{2,30},{4,0},{6,2},{8,4},{10,6},{12,8},{14,10},{16,12},{18,... | collective-permute-start | bytes 786440 | tf_op jit(solution)/shard_map/ppermute | solution.py:320
  122.8 34.4 %copy-start.1 = (f32[4,64,128]{2,1,0:T(8,128)S(1)}, f32[4,64,128]{2,1,0:T(8,128)}, u32[]{:S(2)}) copy-start(f32[4,64,128]{2,1,0:T(8,128)} %get-tuple-element.38.gate) | copy-start | bytes 393220
  122.8 34.4 %copy-start.6 = (bf16[64,128]{1,0:T(8,128)(2,1)S(1)}, bf16[64,128]{1,0:T(8,128)(2,1)}, u32[]{:S(2)}) copy-start(bf16[64,128]{1,0:T(8,128)(2,1)} %w_out.1) | copy-start | bytes 49156
  145.8 25.9 %copy-start.4 = (bf16[128,256]{1,0:T(8,128)(2,1)S(1)}, bf16[128,256]{1,0:T(8,128)(2,1)}, u32[]{:S(2)}) copy-start(bf16[128,256]{1,0:T(8,128)(2,1)} %w_proj.1) | copy-start | bytes 196612
  145.8 25.9 %copy-start.5 = (f32[4,64,128]{2,1,0:T(8,128)S(1)}, f32[4,64,128]{2,1,0:T(8,128)}, u32[]{:S(2)}) copy-start(f32[4,64,128]{2,1,0:T(8,128)} %get-tuple-element.49.go) | copy-start | bytes 393220
  145.8 23.2 %all-to-all-start.1 = ((bf16[4,2,128,128]{3,2,1,0:T(8,128)(2,1)}), bf16[4,2,128,128]{3,2,1,0:T(8,128)(2,1)S(1)}, u32[]{:S(2)}, u32[]{:S(2)}) async-start(bf16[4,2,128,128]{3,2,1,0:T(8,128)(2,1)} %get-tuple-element.46), calls=%async_computation.1 | async-start | bytes 524288 | tf_op jit(solution)/shard_map/all_to_all | solution.py:381
  149.3 27.8 %copy-start.2 = (bf16[4,128,128]{2,1,0:T(8,128)(2,1)S(1)}, bf16[4,128,128]{2,1,0:T(8,128)(2,1)}, u32[]{:S(2)}) copy-start(bf16[4,128,128]{2,1,0:T(8,128)(2,1)} %pair.1) | copy-start | bytes 393220
  149.4 27.8 %copy-start.8 = (f32[128]{0:T(128)S(1)}, f32[128]{0:T(128)}, u32[]{:S(2)}) copy-start(f32[128]{0:T(128)} %param.8) | copy-start | bytes 1540
  149.5 7.7 %collective-permute-start.5 = (bf16[4,64,128]{2,1,0:T(8,128)(2,1)S(1)}, bf16[4,64,128]{2,1,0:T(8,128)(2,1)S(1)}, u32[]{:S(2)}, u32[]{:S(2)}) collective-permute-start(bf16[4,64,128]{2,1,0:T(8,128)(2,1)S(1)} %fusion.3), channel_id=1, source_target_pairs={{0,32},{32,0},{1,33},{33,1},{2,34},{34,2},{3,35},{35,3},{4,36},{36... | collective-permute-start | bytes 196616 | tf_op jit(solution)/shard_map/ppermute | solution.py:367
  157.4 11.6 %collective-permute-start.6 = (bf16[4,64,128]{2,1,0:T(8,128)(2,1)S(1)}, bf16[4,64,128]{2,1,0:T(8,128)(2,1)S(1)}, u32[]{:S(2)}, u32[]{:S(2)}) collective-permute-start(bf16[4,64,128]{2,1,0:T(8,128)(2,1)S(1)} %get-tuple-element.40), channel_id=1, source_target_pairs={{0,1},{1,0},{2,3},{3,2},{4,5},{5,4},{6,7},{7,6},{8,9},{9,8},{10,11... | collective-permute-start | bytes 196616 | tf_op jit(solution)/shard_map/ppermute | solution.py:371
  166.1 5.6 %collective-permute-start.11 = (bf16[2,128,128]{2,1,0:T(8,128)(2,1)S(1)}, bf16[2,128,128]{2,1,0:T(8,128)(2,1)S(1)}, u32[]{:S(2)}, u32[]{:S(2)}) collective-permute-start(bf16[2,128,128]{2,1,0:T(8,128)(2,1)S(1)} %reduce_sum.12), channel_id=1, source_target_pairs={{0,32},{32,0},{1,33},{33,1},{2,34},{34,2},{3,35},{35,3},{4,36},{36... | collective-permute-start | bytes 196616 | tf_op jit(solution)/shard_map/ppermute | solution.py:380
  172.2 5.0 %collective-permute-start.12 = (bf16[4,128,128]{2,1,0:T(8,128)(2,1)S(1)}, bf16[4,128,128]{2,1,0:T(8,128)(2,1)S(1)}, u32[]{:S(2)}, u32[]{:S(2)}) collective-permute-start(bf16[4,128,128]{2,1,0:T(8,128)(2,1)S(1)} %get-tuple-element.51), channel_id=1, source_target_pairs={{0,1},{1,0},{2,3},{3,2},{4,5},{5,4},{6,7},{7,6},{8,9},{9,8},{10,11... | collective-permute-start | bytes 393224 | tf_op jit(solution)/shard_map/ppermute | solution.py:391
  (2 other events, 2.4 us)
Sparse Core Ops, SparseCore 0:
  22.7 46.7 all-gather.3

commit v7 on v6

--- a/solution.py
+++ b/solution.py
@@ -113,8 +113,11 @@
     return zk // 2 + 8 * xk
 
 
-def setup_kernel(act, pack0, pack1, lists, qd):
+def setup_kernel(act, pack0, pack1, lists, qd, kv):
     ids = place()
+    for p in range(2):
+        kv[0, p] = pack0[128 * p : 128 * p + 128]
+        kv[1, p] = pack1[128 * p : 128 * p + 128]
     fill_queries(qd, (pack0, pack1))
     for k, (step, low, count) in enumerate(ARRAYS):
         for half in range(2):
@@ -252,18 +255,18 @@
         send[r] = jnp.where(c == 0, high, low).astype(BF16)
 
 
-def sum_kernel(d_own, r_up, r_down, r_up2, r_down2, own, other):
+def sum_kernel(d_own, r_up, r_down, r_up2, r_down2, out):
     for m in range(4):
         total = d_own[m].astype(F32) + r_up[m].astype(F32) + r_down[m].astype(F32)
         total += (r_up2[m] if m < 2 else r_down2[m - 2]).astype(F32)
-        own[m], other[m] = total[0].astype(BF16), total[1].astype(BF16)
-
-
-def proj_kernel(oq_own, oq_other, dkv_own, dkv_other, gate, go, w_proj, keep, send, dp):
+        out[m] = total.astype(BF16)
+
+
+def proj_kernel(oq_own, oq_other, dkv_own, dkv_other, gate, go, w_proj, send, dp):
     _, xl, _ = place()
     for p in range(2):
-        mine_kv = sum(dkv_own[m, p].astype(F32) for m in range(4)).T
-        theirs_kv = dkv_other[p].astype(F32).T
+        mine_kv = sum(dkv_own[m, 0, p].astype(F32) for m in range(4)).T
+        theirs_kv = dkv_other[1 - xl, p].astype(F32).T
         for i in range(2):
             r = 2 * p + i
             for oq, kvt, h in (
@@ -276,15 +279,13 @@
                 dp[pl.ds(base, 32)] = oq[0:32]
                 dp[pl.ds(base + 32, 64)] = kvt[64 * i : 64 * i + 64]
                 dp[pl.ds(base + 96, 32)] = go[r, pl.ds(low, DH)] * oq[32:64] * g * (1.0 - g)
-            part = nn(w_proj[...], dp[...].astype(BF16)).T
-            keep[r] = part
-            send[r] = part.astype(BF16)
-
-
-def final_kernel(pair, gain, part, other, out):
+            send[r] = nn(w_proj[...], dp[...].astype(BF16)).T.astype(BF16)
+
+
+def final_kernel(pair, gain, parts, out):
     for r in range(4):
         xhat, inv = norm(pair[r].astype(F32))
-        g = (part[r].astype(BF16).astype(F32) + other[r].astype(F32)) * gain[...]
+        g = (parts[0, r].astype(F32) + parts[1, r].astype(F32)) * gain[...]
         mean = jnp.mean(g, axis=-1, keepdims=True)
         along = jnp.mean(g * xhat, axis=-1, keepdims=True)
         out[r] = (inv * (g - mean - xhat * along)).astype(BF16)
@@ -338,18 +339,19 @@
     bias = lax.all_to_all(bias, ("xh", "xl"), 0, 0, tiled=True).reshape(2, 2, 4, 128, 128)
     bias, pack_other = lax.optimization_barrier((bias, pack_other))
     bias = lax.all_gather(bias, "y")
-    kv = jnp.stack([pack[:256].reshape(2, 128, 128), pack_other[:256].reshape(2, 128, 128)])
+    lists, qd, kv = pl.pallas_call(
+        setup_kernel,
+        out_shape=shapes(
+            ((90,), jnp.int32), ((2, 4, 128, 256), BF16), ((2, 2, 128, 128), BF16)
+        ),
+        in_specs=[smem()] + [vmem()] * 2,
+        out_specs=[smem(), vmem(), vmem()],
+        compiler_params=pltpu.CompilerParams(vmem_limit_bytes=24 * 1024 * 1024),
+    )(active, pack, pack_other)
     groups = [[k + 4 * m for m in range(4)] for k in range(4)]
     own = lax.all_gather(kv, "z", axis_index_groups=groups)
     up, down = to_z(own, -1), to_z(own, 1)
     up2, down2 = to_z(own[0:2], -2), to_z(own[2:4], 2)
-    lists, qd = pl.pallas_call(
-        setup_kernel,
-        out_shape=shapes(((90,), jnp.int32), ((2, 4, 128, 256), BF16)),
-        in_specs=[smem()] + [vmem()] * 2,
-        out_specs=[smem(), vmem()],
-        compiler_params=pltpu.CompilerParams(vmem_limit_bytes=24 * 1024 * 1024),
-    )(active, pack, pack_other)
     rest = (bias, qd)
     state = stats_call((OWN,), True, False, lists, (own,), rest)
     state = stats_call((UP, DOWN), False, False, lists, (up, down), rest + (state,))
@@ -370,25 +372,17 @@
     )(oq, oq_other, gate, w_out)
     out_other = lax.ppermute(out_send, "c", SWAP)
     out = (out_keep + out_other.astype(F32)).astype(BF16)
-    sums, sums_other = call(sum_kernel, [((4, 2, 128, 128), BF16)] * 2, 0, 5)(
+    (sums,) = call(sum_kernel, [((4, 2, 2, 128, 128), BF16)], 0, 5)(
         d_own, r_up, r_down, r_up2, r_down2
     )
-    exchange = functools.partial(
-        lax.all_to_all, axis_name="z", split_axis=0, concat_axis=0, axis_index_groups=groups, tiled=True
-    )
-    theirs = jnp.sum(exchange(sums_other).astype(F32), axis=0).astype(BF16)
-    dkv_other = lax.ppermute(theirs, "xl", SWAP)
-    dkv = exchange(sums)
-    dkv, _, _ = lax.optimization_barrier((dkv, out_other, dkv_other))
-    part, part_send = call(
-        proj_kernel,
-        [((4, 128, 128), F32), ((4, 128, 128), BF16)],
-        0,
-        7,
-        [pltpu.VMEM((256, 128), F32)],
-    )(oq, oq_other, dkv, dkv_other, gate, go, w_proj)
-    (pair_gradient,) = call(final_kernel, [((4, 128, 128), BF16)], 0, 4)(
-        pair, gain, part, lax.ppermute(part_send, "c", SWAP)
+    dkv = lax.all_to_all(sums, "z", 0, 0, axis_index_groups=groups, tiled=True)
+    dkv, out = lax.optimization_barrier((dkv, out))
+    theirs = jnp.sum(dkv[:, 1].astype(F32), axis=0).astype(BF16)
+    (part,) = call(
+        proj_kernel, [((4, 128, 128), BF16)], 0, 7, [pltpu.VMEM((256, 128), F32)]
+    )(oq, oq_other, dkv, lax.all_gather(theirs, "xl"), gate, go, w_proj)
+    (pair_gradient,) = call(final_kernel, [((4, 128, 128), BF16)], 0, 3)(
+        pair, gain, lax.all_gather(part, "c")
     )
     return jnp.swapaxes(out, 1, 2), pair_gradient
 

time: 187 us -> 179 us (0.957)
  the two profiles are of different devices: /device:TPU:1 before, /device:TPU:13 now
where the time goes in v7:
time: 179 us; the launch traced here: 178 us
  starting transfers between devices  57.1 us (32%)
  blocking collectives  51.5 us (29%)
  Pallas kernels  33.2 us (19%)
  waiting for transfers between devices  17.9 us (10%)
  between operations  14.3 us (8%)
  local copies, waits for them, and re-layouts  3.36 us (2%)
    all_gather x1, blocking collectives, per_device(): own = lax.all_gather(kv, 'z', axis_index_groups=groups)  30.9 us
    ppermute x8, starting transfers between devices, to_z(): return lax.ppermute(x, 'z', [(j, (j + step) % 16) for j in range(16)])  27.2 us
    pallas_call x4, Pallas kernels, back_call(): call(functools.partial(back_kernel, names), [(kv.shape, BF16) for kv in k...  16.2 us
    all_gather x1, blocking collectives, per_device(): lax.all_gather(theirs, 'xl')  11.1 us
    all_to_all x1, starting transfers between devices, per_device(): dkv = lax.all_to_all(sums, 'z', 0, 0, axis_index_groups=groups, tiled=True)  10.4 us
    ppermute x1, starting transfers between devices, per_device(): out_other = lax.ppermute(out_send, 'c', SWAP)  10.4 us
    pallas_call x3, Pallas kernels, stats_call(): call(functools.partial(stats_kernel, names, begin, end), [out], 1, len(kv...  9.95 us
    all_gather x1, blocking collectives, per_device(): lax.all_gather(part, 'c')  9.52 us
  transfers between devices with their start and end apart: 14, of which 7 were waited for; matrix products, arithmetic and copies ran while one was open for 0% of the time, Pallas kernels for 12%

profile of v7, /device:TPU:13, one launch (start us, length us, event | category | flops | bytes accessed | tf_op | source)
XLA Modules:
  0.0 178.2 jit_solution(12885990560473755867)
XLA Ops:
  7.2 2.7 %shard_map.86 = (bf16[512,128]{1,0:T(8,128)(2,1)}, bf16[512,128]{1,0:T(8,128)(2,1)}, f32[4,64,128]{2,1,0:T(8,128)}, f32[4,64,128]{2,1,0:T(8,128)}, bf16[4,4,128,128]{3,2,1,0:T(8,128)(2,1)}) custom-call(bf16[4,128,128]{2,1,0:T(8,128)(2,1)} %pair.1, f32[1,128]{1,0:T(1,128)} %bitcast.24, bf16[128,256]{1,0:T(8,128)(2,1)} %w_proj.1, bf16[64,128]{1,0:T(8,128)(2,1)} %w_out.1, ...), custom_call_target="tpu_custom_call" | custom-call | tf_op jit(solution)/shard_map/pallas_call | solution.py:327
  9.9 4.2 %all-to-all-start = ((bf16[4,4,128,128]{3,2,1,0:T(8,128)(2,1)}), bf16[4,4,128,128]{3,2,1,0:T(8,128)(2,1)S(1)}, u32[]{:S(2)}, u32[]{:S(2)}) async-start(bf16[4,4,128,128]{3,2,1,0:T(8,128)(2,1)} %get-tuple-element.26), calls=%async_computation | async-start | bytes 1048576 | tf_op jit(solution)/shard_map/all_to_all | solution.py:339
  14.1 2.8 %collective-permute-start = (bf16[512,128]{1,0:T(8,128)(2,1)}, bf16[512,128]{1,0:T(8,128)(2,1)S(1)}, u32[]{:S(2)}, u32[]{:S(2)}) collective-permute-start(bf16[512,128]{1,0:T(8,128)(2,1)} %get-tuple-element.27), channel_id=1, source_target_pairs={{0,32},{32,0},{1,33},{33,1},{2,34},{34,2},{3,35},{35,3},{4,36},{36... | collective-permute-start | bytes 393224 | tf_op jit(solution)/shard_map/ppermute | solution.py:338
  16.9 6.2 %collective-permute-done.pack1 = bf16[512,128]{1,0:T(8,128)(2,1)S(1)} collective-permute-done((bf16[512,128]{1,0:T(8,128)(2,1)}, bf16[512,128]{1,0:T(8,128)(2,1)S(1)}, u32[]{:S(2)}, u32[]{:S(2)}) %collective-permute-start) | collective-permute-done | bytes 131104 | tf_op jit(solution)/shard_map/ppermute | solution.py:338
  26.4 30.9 %all-gather = bf16[8,2,128,128]{3,2,1,0:T(8,128)(2,1)S(1)} all-gather(bf16[2,2,128,128]{3,2,1,0:T(8,128)(2,1)S(1)} %get-tuple-element.30), channel_id=2, replica_groups={{0,8,16,24},{2,10,18,26},{4,12,20,28},{6,14,22,30},{1,9,17,25},{3,11,19..., dimensions={0}, use_global_device_ids=true | all-gather | bytes 655360 | tf_op jit(solution)/shard_map/all_gather | solution.py:352
  59.2 4.6 %collective-permute-start.3 = (bf16[4,2,2,128,128]{4,3,2,1,0:T(8,128)(2,1)S(1)}, bf16[4,2,2,128,128]{4,3,2,1,0:T(8,128)(2,1)S(1)}, u32[]{:S(2)}, u32[]{:S(2)}) collective-permute-start(bf16[4,2,2,128,128]{4,3,2,1,0:T(8,128)(2,1)S(1)} %bitcast.12), channel_id=1, source_target_pairs={{0,30},{2,0},{4,2},{6,4},{8,6},{10,8},{12,10},{14,12},{16,14},{18,... | collective-permute-start | bytes 1572872 | tf_op jit(solution)/shard_map/ppermute | solution.py:321
  65.8 4.3 %collective-permute-start.2 = (bf16[2,2,2,128,128]{4,3,2,1,0:T(8,128)(2,1)S(1)}, bf16[2,2,2,128,128]{4,3,2,1,0:T(8,128)(2,1)S(1)}, u32[]{:S(2)}, u32[]{:S(2)}) collective-permute-start(bf16[2,2,2,128,128]{4,3,2,1,0:T(8,128)(2,1)S(1)} %bitcast.27), channel_id=1, source_target_pairs={{0,4},{2,6},{4,8},{6,10},{8,12},{10,14},{12,16},{14,18},{16,20},{1... | collective-permute-start | bytes 786440 | tf_op jit(solution)/shard_map/ppermute | solution.py:321
  71.7 2.7 %shard_map.88.refs_4_ = f32[3,2,4,8,128]{4,3,2,1,0:T(8,128)S(1)} custom-call(s32[90]{0:T(128)S(1)} %get-tuple-element.29.lists, bf16[4,2,2,128,128]{4,3,2,1,0:T(8,128)(2,1)S(1)} %bitcast.13, bf16[4,2,2,4,128,128]{5,4,3,2,1,0:T(8,128)(2,1)S(1)} %bitcast.15, bf16[2,4,128,256]{3,2,1,0:T(8,128)(2,1)S(1)} %get-tuple-element.32.refs_2_.refs_3_), custom_call_target="tpu_custom_call" | custom-call | flops 1000000000 | bytes 10000000 | tf_op jit(solution)/shard_map/pallas_call | solution.py:296
  74.4 4.7 %shard_map.89.refs_4_ = f32[3,2,4,8,128]{4,3,2,1,0:T(8,128)S(1)} custom-call(s32[90]{0:T(128)S(1)} %get-tuple-element.29.lists, bf16[4,2,2,128,128]{4,3,2,1,0:T(8,128)(2,1)S(1)} %collective-permute-done.3.refs_0_, bf16[4,2,2,128,128]{4,3,2,1,0:T(8,128)(2,1)S(1)} %collective-permute-done.4.refs_1_.refs_0_, bf16[4,2,2,4,128,128]{5,4,3,2,1,0:T(8,128)(2,1)S(1)} %bitcast.16, ...), custom_call_target="tpu_custom_call" | custom-call | flops 1000000000 | bytes 10000000 | tf_op jit(solution)/shard_map/pallas_call | solution.py:296
  81.2 2.6 %shard_map.90.refs_3_.refs_4_ = f32[2,4,2,128]{3,2,1,0:T(2,128)S(1)} custom-call(s32[90]{0:T(128)S(1)} %get-tuple-element.29.lists, bf16[2,2,2,128,128]{4,3,2,1,0:T(8,128)(2,1)S(1)} %collective-permute-done.1.refs_0_, bf16[2,2,2,128,128]{4,3,2,1,0:T(8,128)(2,1)S(1)} %collective-permute-done.2.refs_1_, bf16[4,2,2,4,128,128]{5,4,3,2,1,0:T(8,128)(2,1)S(1)} %bitcast.17, ...), custom_call_target="tpu_custom_call" | custom-call | flops 1000000000 | bytes 10000000 | tf_op jit(solution)/shard_map/pallas_call | solution.py:296
  83.8 4.3 %shard_map.92 = (bf16[4,2,2,128,128]{4,3,2,1,0:T(8,128)(2,1)S(1)}, f32[2,4,64,128]{3,2,1,0:T(8,128)S(1)}) custom-call(s32[90]{0:T(128)S(1)} %get-tuple-element.29.lists, bf16[4,2,2,128,128]{4,3,2,1,0:T(8,128)(2,1)S(1)} %collective-permute-done.3.refs_0_, bf16[4,2,2,4,128,128]{5,4,3,2,1,0:T(8,128)(2,1)S(1)} %bitcast.18, ...), custom_call_target="tpu_custom_call" | custom-call | flops 2000000000 | bytes 20000000 | tf_op jit(solution)/shard_map/pallas_call | solution.py:308
  88.1 3.4 %collective-permute-start.5 = (bf16[4,2,2,128,128]{4,3,2,1,0:T(8,128)(2,1)S(1)}, bf16[4,2,2,128,128]{4,3,2,1,0:T(8,128)(2,1)S(1)}, u32[]{:S(2)}, u32[]{:S(2)}) collective-permute-start(bf16[4,2,2,128,128]{4,3,2,1,0:T(8,128)(2,1)S(1)} %get-tuple-element.34), channel_id=1, source_target_pairs={{0,2},{2,4},{4,6},{6,8},{8,10},{10,12},{12,14},{14,16},{16,18},{18... | collective-permute-start | bytes 1572872 | tf_op jit(solution)/shard_map/ppermute | solution.py:321
  91.5 3.8 %shard_map.93 = (bf16[4,2,2,128,128]{4,3,2,1,0:T(8,128)(2,1)S(1)}, f32[2,4,64,128]{3,2,1,0:T(8,128)S(1)}) custom-call(s32[90]{0:T(128)S(1)} %get-tuple-element.29.lists, bf16[4,2,2,128,128]{4,3,2,1,0:T(8,128)(2,1)S(1)} %collective-permute-done.4.refs_1_.refs_0_, bf16[4,2,2,4,128,128]{5,4,3,2,1,0:T(8,128)(2,1)S(1)} %bitcast.19, ...), custom_call_target="tpu_custom_call" | custom-call | flops 2000000000 | bytes 20000000 | tf_op jit(solution)/shard_map/pallas_call | solution.py:308
  95.3 3.8 %collective-permute-start.6 = (bf16[4,2,2,128,128]{4,3,2,1,0:T(8,128)(2,1)S(1)}, bf16[4,2,2,128,128]{4,3,2,1,0:T(8,128)(2,1)S(1)}, u32[]{:S(2)}, u32[]{:S(2)}) collective-permute-start(bf16[4,2,2,128,128]{4,3,2,1,0:T(8,128)(2,1)S(1)} %get-tuple-element.35), channel_id=1, source_target_pairs={{0,30},{2,0},{4,2},{6,4},{8,6},{10,8},{12,10},{14,12},{16,14},{18,... | collective-permute-start | bytes 1572872 | tf_op jit(solution)/shard_map/ppermute | solution.py:321
  99.1 3.8 %shard_map.94 = (bf16[2,2,2,128,128]{4,3,2,1,0:T(8,128)(2,1)S(1)}, bf16[2,2,2,128,128]{4,3,2,1,0:T(8,128)(2,1)S(1)}, f32[2,4,64,128]{3,2,1,0:T(8,128)S(1)}) custom-call(s32[90]{0:T(128)S(1)} %get-tuple-element.29.lists, bf16[2,2,2,128,128]{4,3,2,1,0:T(8,128)(2,1)S(1)} %collective-permute-done.1.refs_0_, ...), custom_call_target="tpu_custom_call" | custom-call | flops 2000000000 | bytes 20000000 | tf_op jit(solution)/shard_map/pallas_call | solution.py:308
  102.9 2.2 %collective-permute-start.7 = (bf16[2,2,2,128,128]{4,3,2,1,0:T(8,128)(2,1)S(1)}, bf16[2,2,2,128,128]{4,3,2,1,0:T(8,128)(2,1)S(1)}, u32[]{:S(2)}, u32[]{:S(2)}) collective-permute-start(bf16[2,2,2,128,128]{4,3,2,1,0:T(8,128)(2,1)S(1)} %get-tuple-element.36), channel_id=1, source_target_pairs={{0,4},{2,6},{4,8},{6,10},{8,12},{10,14},{12,16},{14,18},{16,20},{1... | collective-permute-start | bytes 786440 | tf_op jit(solution)/shard_map/ppermute | solution.py:321
  105.1 5.1 %collective-permute-start.8 = (bf16[2,2,2,128,128]{4,3,2,1,0:T(8,128)(2,1)S(1)}, bf16[2,2,2,128,128]{4,3,2,1,0:T(8,128)(2,1)S(1)}, u32[]{:S(2)}, u32[]{:S(2)}) collective-permute-start(bf16[2,2,2,128,128]{4,3,2,1,0:T(8,128)(2,1)S(1)} %get-tuple-element.37), channel_id=1, source_target_pairs={{0,28},{2,30},{4,0},{6,2},{8,4},{10,6},{12,8},{14,10},{16,12},{18,... | collective-permute-start | bytes 786440 | tf_op jit(solution)/shard_map/ppermute | solution.py:321
  110.3 4.3 %shard_map.91 = (bf16[4,2,2,128,128]{4,3,2,1,0:T(8,128)(2,1)S(1)}, f32[2,4,64,128]{3,2,1,0:T(8,128)S(1)}) custom-call(s32[90]{0:T(128)S(1)} %get-tuple-element.29.lists, bf16[4,2,2,128,128]{4,3,2,1,0:T(8,128)(2,1)S(1)} %bitcast.14, bf16[4,2,2,4,128,128]{5,4,3,2,1,0:T(8,128)(2,1)S(1)} %bitcast.21, ...), custom_call_target="tpu_custom_call" | custom-call | flops 2000000000 | bytes 20000000 | tf_op jit(solution)/shard_map/pallas_call | solution.py:308
  114.6 5.5 %collective-permute-done.8.r_down2 = bf16[2,2,2,128,128]{4,3,2,1,0:T(8,128)(2,1)S(1)} collective-permute-done((bf16[2,2,2,128,128]{4,3,2,1,0:T(8,128)(2,1)S(1)}, bf16[2,2,2,128,128]{4,3,2,1,0:T(8,128)(2,1)S(1)}, u32[]{:S(2)}, u32[]{:S(2)}) %collective-permute-start.8) | collective-permute-done | bytes 262176 | tf_op jit(solution)/shard_map/ppermute | solution.py:321
  121.2 10.4 %all-to-all-start.1 = ((bf16[4,2,2,128,128]{4,3,2,1,0:T(8,128)(2,1)}), bf16[4,2,2,128,128]{4,3,2,1,0:T(8,128)(2,1)S(1)}, u32[]{:S(2)}, u32[]{:S(2)}) async-start(bf16[4,2,2,128,128]{4,3,2,1,0:T(8,128)(2,1)} %shard_map.95), calls=%async_computation.1 | async-start | bytes 1048576 | tf_op jit(solution)/shard_map/all_to_all | solution.py:378
  133.8 3.1 %collective-permute-done.9.oq_other = bf16[4,64,128]{2,1,0:T(8,128)(2,1)S(1)} collective-permute-done((bf16[4,64,128]{2,1,0:T(8,128)(2,1)S(1)}, bf16[4,64,128]{2,1,0:T(8,128)(2,1)S(1)}, u32[]{:S(2)}, u32[]{:S(2)}) %collective-permute-start.9) | collective-permute-done | bytes 65568 | tf_op jit(solution)/shard_map/ppermute | solution.py:369
  137.1 10.4 %collective-permute-start.10 = (bf16[4,64,128]{2,1,0:T(8,128)(2,1)S(1)}, bf16[4,64,128]{2,1,0:T(8,128)(2,1)S(1)}, u32[]{:S(2)}, u32[]{:S(2)}) collective-permute-start(bf16[4,64,128]{2,1,0:T(8,128)(2,1)S(1)} %get-tuple-element.44), channel_id=1, source_target_pairs={{0,1},{1,0},{2,3},{3,2},{4,5},{5,4},{6,7},{7,6},{8,9},{9,8},{10,11... | collective-permute-start | bytes 196616 | tf_op jit(solution)/shard_map/ppermute | solution.py:373
  149.1 11.1 %all-gather.2 = bf16[4,128,128]{2,1,0:T(8,128)(2,1)S(1)} all-gather(bf16[2,128,128]{2,1,0:T(8,128)(2,1)S(1)} %slice_reduce_fusion), channel_id=4, replica_groups=mesh['xh'=2,'y'=4,'xl'=2,'z'=16,'c'=2] {'xl'}, dimensions={0}, use_global_device_ids=true | all-gather | bytes 196608 | tf_op jit(solution)/shard_map/all_gather | solution.py:383
  160.7 9.5 %all-gather.3 = bf16[8,128,128]{2,1,0:T(8,128)(2,1)S(1)} all-gather(bf16[4,128,128]{2,1,0:T(8,128)(2,1)S(1)} %shard_map.97), channel_id=5, replica_groups=mesh['xh'=2,'y'=4,'xl'=2,'z'=16,'c'=2] {'c'}, dimensions={0}, use_global_device_ids=true | all-gather | bytes 393216 | tf_op jit(solution)/shard_map/all_gather | solution.py:385
  (48 shorter events, 17.6 us)
Async XLA Ops:
  7.2 16.8 %copy-start.7 = (s32[16,16]{1,0:T(8,128)S(1)}, s32[16,16]{1,0:T(8,128)}, u32[]{:S(2)}) copy-start(s32[16,16]{1,0:T(8,128)} %act.1) | copy-start | bytes 3076
  9.9 13.3 %all-to-all-start = ((bf16[4,4,128,128]{3,2,1,0:T(8,128)(2,1)}), bf16[4,4,128,128]{3,2,1,0:T(8,128)(2,1)S(1)}, u32[]{:S(2)}, u32[]{:S(2)}) async-start(bf16[4,4,128,128]{3,2,1,0:T(8,128)(2,1)} %get-tuple-element.26), calls=%async_computation | async-start | bytes 1048576 | tf_op jit(solution)/shard_map/all_to_all | solution.py:339
  14.1 56.0 %all-gather.6.cloned.1.call-start = ((), (), s32[]{:S(2)}) async-start(), calls=%async_computation.2 | async-start | bytes 2621440 | tf_op jit(solution)/shard_map/all_gather | solution.py:341
  14.1 9.0 %collective-permute-start = (bf16[512,128]{1,0:T(8,128)(2,1)}, bf16[512,128]{1,0:T(8,128)(2,1)S(1)}, u32[]{:S(2)}, u32[]{:S(2)}) collective-permute-start(bf16[512,128]{1,0:T(8,128)(2,1)} %get-tuple-element.27), channel_id=1, source_target_pairs={{0,32},{32,0},{1,33},{33,1},{2,34},{34,2},{3,35},{35,3},{4,36},{36... | collective-permute-start | bytes 393224 | tf_op jit(solution)/shard_map/ppermute | solution.py:338
  23.1 0.8 copy-start.9
  23.9 0.9 copy-start.4
  57.3 17.1 %collective-permute-start.4 = (bf16[4,2,2,128,128]{4,3,2,1,0:T(8,128)(2,1)S(1)}, bf16[4,2,2,128,128]{4,3,2,1,0:T(8,128)(2,1)S(1)}, u32[]{:S(2)}, u32[]{:S(2)}) collective-permute-start(bf16[4,2,2,128,128]{4,3,2,1,0:T(8,128)(2,1)S(1)} %bitcast.11), channel_id=1, source_target_pairs={{0,2},{2,4},{4,6},{6,8},{8,10},{10,12},{12,14},{14,16},{16,18},{18... | collective-permute-start | bytes 1572872 | tf_op jit(solution)/shard_map/ppermute | solution.py:321
  59.2 15.2 %collective-permute-start.3 = (bf16[4,2,2,128,128]{4,3,2,1,0:T(8,128)(2,1)S(1)}, bf16[4,2,2,128,128]{4,3,2,1,0:T(8,128)(2,1)S(1)}, u32[]{:S(2)}, u32[]{:S(2)}) collective-permute-start(bf16[4,2,2,128,128]{4,3,2,1,0:T(8,128)(2,1)S(1)} %bitcast.12), channel_id=1, source_target_pairs={{0,30},{2,0},{4,2},{6,4},{8,6},{10,8},{12,10},{14,12},{16,14},{18,... | collective-permute-start | bytes 1572872 | tf_op jit(solution)/shard_map/ppermute | solution.py:321
  63.9 16.1 %collective-permute-start.1 = (bf16[2,2,2,128,128]{4,3,2,1,0:T(8,128)(2,1)S(1)}, bf16[2,2,2,128,128]{4,3,2,1,0:T(8,128)(2,1)S(1)}, u32[]{:S(2)}, u32[]{:S(2)}) collective-permute-start(bf16[2,2,2,128,128]{4,3,2,1,0:T(8,128)(2,1)S(1)} %bitcast.28), channel_id=1, source_target_pairs={{0,28},{2,30},{4,0},{6,2},{8,4},{10,6},{12,8},{14,10},{16,12},{18,... | collective-permute-start | bytes 786440 | tf_op jit(solution)/shard_map/ppermute | solution.py:321
  65.8 15.5 %collective-permute-start.2 = (bf16[2,2,2,128,128]{4,3,2,1,0:T(8,128)(2,1)S(1)}, bf16[2,2,2,128,128]{4,3,2,1,0:T(8,128)(2,1)S(1)}, u32[]{:S(2)}, u32[]{:S(2)}) collective-permute-start(bf16[2,2,2,128,128]{4,3,2,1,0:T(8,128)(2,1)S(1)} %bitcast.27), channel_id=1, source_target_pairs={{0,4},{2,6},{4,8},{6,10},{8,12},{10,14},{12,16},{14,18},{16,20},{1... | collective-permute-start | bytes 786440 | tf_op jit(solution)/shard_map/ppermute | solution.py:321
  70.1 1.6 copy-start
  88.1 32.0 %collective-permute-start.5 = (bf16[4,2,2,128,128]{4,3,2,1,0:T(8,128)(2,1)S(1)}, bf16[4,2,2,128,128]{4,3,2,1,0:T(8,128)(2,1)S(1)}, u32[]{:S(2)}, u32[]{:S(2)}) collective-permute-start(bf16[4,2,2,128,128]{4,3,2,1,0:T(8,128)(2,1)S(1)} %get-tuple-element.34), channel_id=1, source_target_pairs={{0,2},{2,4},{4,6},{6,8},{8,10},{10,12},{12,14},{14,16},{16,18},{18... | collective-permute-start | bytes 1572872 | tf_op jit(solution)/shard_map/ppermute | solution.py:321
  95.3 24.8 %collective-permute-start.6 = (bf16[4,2,2,128,128]{4,3,2,1,0:T(8,128)(2,1)S(1)}, bf16[4,2,2,128,128]{4,3,2,1,0:T(8,128)(2,1)S(1)}, u32[]{:S(2)}, u32[]{:S(2)}) collective-permute-start(bf16[4,2,2,128,128]{4,3,2,1,0:T(8,128)(2,1)S(1)} %get-tuple-element.35), channel_id=1, source_target_pairs={{0,30},{2,0},{4,2},{6,4},{8,6},{10,8},{12,10},{14,12},{16,14},{18,... | collective-permute-start | bytes 1572872 | tf_op jit(solution)/shard_map/ppermute | solution.py:321
  102.9 11.7 %collective-permute-start.7 = (bf16[2,2,2,128,128]{4,3,2,1,0:T(8,128)(2,1)S(1)}, bf16[2,2,2,128,128]{4,3,2,1,0:T(8,128)(2,1)S(1)}, u32[]{:S(2)}, u32[]{:S(2)}) collective-permute-start(bf16[2,2,2,128,128]{4,3,2,1,0:T(8,128)(2,1)S(1)} %get-tuple-element.36), channel_id=1, source_target_pairs={{0,4},{2,6},{4,8},{6,10},{8,12},{10,14},{12,16},{14,18},{16,20},{1... | collective-permute-start | bytes 786440 | tf_op jit(solution)/shard_map/ppermute | solution.py:321
  105.1 15.0 %collective-permute-start.8 = (bf16[2,2,2,128,128]{4,3,2,1,0:T(8,128)(2,1)S(1)}, bf16[2,2,2,128,128]{4,3,2,1,0:T(8,128)(2,1)S(1)}, u32[]{:S(2)}, u32[]{:S(2)}) collective-permute-start(bf16[2,2,2,128,128]{4,3,2,1,0:T(8,128)(2,1)S(1)} %get-tuple-element.37), channel_id=1, source_target_pairs={{0,28},{2,30},{4,0},{6,2},{8,4},{10,6},{12,8},{14,10},{16,12},{18,... | collective-permute-start | bytes 786440 | tf_op jit(solution)/shard_map/ppermute | solution.py:321
  121.2 15.7 %copy-start.2 = (f32[4,64,128]{2,1,0:T(8,128)S(1)}, f32[4,64,128]{2,1,0:T(8,128)}, u32[]{:S(2)}) copy-start(f32[4,64,128]{2,1,0:T(8,128)} %get-tuple-element.42.gate) | copy-start | bytes 393220
  121.2 15.7 %copy-start.6 = (bf16[64,128]{1,0:T(8,128)(2,1)S(1)}, bf16[64,128]{1,0:T(8,128)(2,1)}, u32[]{:S(2)}) copy-start(bf16[64,128]{1,0:T(8,128)(2,1)} %w_out.1) | copy-start | bytes 49156
  121.2 27.9 %all-to-all-start.1 = ((bf16[4,2,2,128,128]{4,3,2,1,0:T(8,128)(2,1)}), bf16[4,2,2,128,128]{4,3,2,1,0:T(8,128)(2,1)S(1)}, u32[]{:S(2)}, u32[]{:S(2)}) async-start(bf16[4,2,2,128,128]{4,3,2,1,0:T(8,128)(2,1)} %shard_map.95), calls=%async_computation.1 | async-start | bytes 1048576 | tf_op jit(solution)/shard_map/all_to_all | solution.py:378
  131.6 28.7 %copy-start.3 = (bf16[128,256]{1,0:T(8,128)(2,1)S(1)}, bf16[128,256]{1,0:T(8,128)(2,1)}, u32[]{:S(2)}) copy-start(bf16[128,256]{1,0:T(8,128)(2,1)} %w_proj.1) | copy-start | bytes 196612
  131.6 28.7 %copy-start.5 = (f32[4,64,128]{2,1,0:T(8,128)S(1)}, f32[4,64,128]{2,1,0:T(8,128)}, u32[]{:S(2)}) copy-start(f32[4,64,128]{2,1,0:T(8,128)} %get-tuple-element.47.go) | copy-start | bytes 393220
  131.7 38.6 %copy-start.1 = (bf16[4,128,128]{2,1,0:T(8,128)(2,1)S(1)}, bf16[4,128,128]{2,1,0:T(8,128)(2,1)}, u32[]{:S(2)}) copy-start(bf16[4,128,128]{2,1,0:T(8,128)(2,1)} %pair.1) | copy-start | bytes 393220
  131.7 38.5 %copy-start.8 = (f32[128]{0:T(128)S(1)}, f32[128]{0:T(128)}, u32[]{:S(2)}) copy-start(f32[128]{0:T(128)} %param.8) | copy-start | bytes 1540
  131.7 5.1 %collective-permute-start.9 = (bf16[4,64,128]{2,1,0:T(8,128)(2,1)S(1)}, bf16[4,64,128]{2,1,0:T(8,128)(2,1)S(1)}, u32[]{:S(2)}, u32[]{:S(2)}) collective-permute-start(bf16[4,64,128]{2,1,0:T(8,128)(2,1)S(1)} %fusion.2), channel_id=1, source_target_pairs={{0,32},{32,0},{1,33},{33,1},{2,34},{34,2},{3,35},{35,3},{4,36},{36... | collective-permute-start | bytes 196616 | tf_op jit(solution)/shard_map/ppermute | solution.py:369
  137.1 11.3 %collective-permute-start.10 = (bf16[4,64,128]{2,1,0:T(8,128)(2,1)S(1)}, bf16[4,64,128]{2,1,0:T(8,128)(2,1)S(1)}, u32[]{:S(2)}, u32[]{:S(2)}) collective-permute-start(bf16[4,64,128]{2,1,0:T(8,128)(2,1)S(1)} %get-tuple-element.44), channel_id=1, source_target_pairs={{0,1},{1,0},{2,3},{3,2},{4,5},{5,4},{6,7},{7,6},{8,9},{9,8},{10,11... | collective-permute-start | bytes 196616 | tf_op jit(solution)/shard_map/ppermute | solution.py:373
Sparse Core Ops, SparseCore 0:
  24.1 43.3 all-gather.5

commit v8 on v7

--- a/solution.py
+++ b/solution.py
@@ -63,14 +63,30 @@
     return centred * inv, inv
 
 
+def make_lists(ids, act, lists):
+    for k, (step, low, count) in enumerate(ARRAYS):
+        for half in range(2):
+            a = tile_of(ids[0], ids[1] if half == 0 else 1 - ids[1])
+            base = 9 * (2 * k + half)
+            n = 0
+            for u in range(2 * count):
+                zk = (ids[0] + step + 16) % 4 + 4 * (u // 2 + low)
+                xk = ids[1] if u % 2 == 0 else 1 - ids[1]
+                lists[base + n] = u
+                n = n + act[a, tile_of(zk, xk)]
+            lists[base + 8] = n
+
+
 def prep_kernel(*refs):
     ids = place()
-    here, (keep, send, gate_out, go_out, bias_out) = refs[:6], refs[6:11]
-    pair, gain, w_proj, w_out, d_out, bias = local = refs[11:17]
-    proj_s, sems = refs[17:]
+    here, (keep, send, gate_out, go_out, bias_out, lists) = refs[:7], refs[7:13]
+    pair, gain, w_proj, w_out, d_out, bias, act = local = refs[13:20]
+    proj_s, sems = refs[20:]
     copies = [pltpu.make_async_copy(s, d, sems.at[k]) for k, (s, d) in enumerate(zip(here, local))]
-    for copy in copies:
+    for copy in reversed(copies):
         copy.start()
+    copies[6].wait()
+    make_lists(ids, act, lists)
     for copy in copies[:5]:
         copy.wait()
     xl = ids[1]
@@ -113,23 +129,11 @@
     return zk // 2 + 8 * xk
 
 
-def setup_kernel(act, pack0, pack1, lists, qd, kv):
-    ids = place()
+def setup_kernel(pack0, pack1, qd, kv):
     for p in range(2):
         kv[0, p] = pack0[128 * p : 128 * p + 128]
         kv[1, p] = pack1[128 * p : 128 * p + 128]
     fill_queries(qd, (pack0, pack1))
-    for k, (step, low, count) in enumerate(ARRAYS):
-        for half in range(2):
-            a = tile_of(ids[0], ids[1] if half == 0 else 1 - ids[1])
-            base = 9 * (2 * k + half)
-            n = 0
-            for u in range(2 * count):
-                zk = (ids[0] + step + 16) % 4 + 4 * (u // 2 + low)
-                xk = ids[1] if u % 2 == 0 else 1 - ids[1]
-                lists[base + n] = u
-                n = n + act[a, tile_of(zk, xk)]
-            lists[base + 8] = n
 
 
 def load_units(ids, kv, bias, which, half, units):
@@ -241,6 +245,11 @@
         dkv[...] = acc[0:count].astype(BF16)
 
 
+def mid_kernel(lists, up2, down2, up, down, bias, qd, before, stats, d_up, d_down, oq, st, acc):
+    stats_kernel((UP2, DOWN2), False, True, lists, up2, down2, bias, qd, before, stats, st)
+    back_kernel((UP, DOWN), lists, up, down, bias, qd, stats, d_up, d_down, oq, acc)
+
+
 def out_kernel(oq_own, oq_other, gate, w_out, keep, send):
     _, xl, c = place()
     w_t = w_out[...].T
@@ -323,31 +332,27 @@
 
 def per_device(pair, gain, w_proj, w_out, tri_bias, active, d_out):
     gain = gain.reshape(1, 128)
-    args = (pair, gain, w_proj, w_out, d_out, tri_bias)
-    pack, pack_send, gate, go, bias = pl.pallas_call(
+    args = (pair, gain, w_proj, w_out, d_out, tri_bias, active)
+    pack, pack_send, gate, go, bias, lists = pl.pallas_call(
         prep_kernel,
         out_shape=shapes(
-            *[((512, 128), BF16)] * 2, *[((4, 64, 128), F32)] * 2, ((4, 4, 128, 128), BF16)
+            *[((512, 128), BF16)] * 2, *[((4, 64, 128), F32)] * 2, ((4, 4, 128, 128), BF16),
+            ((90,), jnp.int32),
         ),
-        in_specs=[pl.BlockSpec(memory_space=pl.ANY)] * 6,
-        out_specs=[vmem()] * 5,
-        scratch_shapes=[pltpu.VMEM(a.shape, a.dtype) for a in args]
-        + [pltpu.VMEM((2, 256, 128), F32), pltpu.SemaphoreType.DMA((6,))],
+        in_specs=[pl.BlockSpec(memory_space=pl.ANY)] * 7,
+        out_specs=[vmem()] * 5 + [smem()],
+        scratch_shapes=[pltpu.VMEM(a.shape, a.dtype) for a in args[:6]]
+        + [pltpu.SMEM(active.shape, active.dtype)]
+        + [pltpu.VMEM((2, 256, 128), F32), pltpu.SemaphoreType.DMA((7,))],
         compiler_params=pltpu.CompilerParams(vmem_limit_bytes=56 * 1024 * 1024),
     )(*args)
     pack_other = lax.ppermute(pack_send, "xl", SWAP)
     bias = lax.all_to_all(bias, ("xh", "xl"), 0, 0, tiled=True).reshape(2, 2, 4, 128, 128)
     bias, pack_other = lax.optimization_barrier((bias, pack_other))
     bias = lax.all_gather(bias, "y")
-    lists, qd, kv = pl.pallas_call(
-        setup_kernel,
-        out_shape=shapes(
-            ((90,), jnp.int32), ((2, 4, 128, 256), BF16), ((2, 2, 128, 128), BF16)
-        ),
-        in_specs=[smem()] + [vmem()] * 2,
-        out_specs=[smem(), vmem(), vmem()],
-        compiler_params=pltpu.CompilerParams(vmem_limit_bytes=24 * 1024 * 1024),
-    )(active, pack, pack_other)
+    qd, kv = call(
+        setup_kernel, [((2, 4, 128, 256), BF16), ((2, 2, 128, 128), BF16)], 0, 2
+    )(pack, pack_other)
     groups = [[k + 4 * m for m in range(4)] for k in range(4)]
     own = lax.all_gather(kv, "z", axis_index_groups=groups)
     up, down = to_z(own, -1), to_z(own, 1)
@@ -355,16 +360,21 @@
     rest = (bias, qd)
     state = stats_call((OWN,), True, False, lists, (own,), rest)
     state = stats_call((UP, DOWN), False, False, lists, (up, down), rest + (state,))
-    stats = stats_call((UP2, DOWN2), False, True, lists, (up2, down2), rest + (state,))
+    stats, d_up, d_down, oq1 = call(
+        mid_kernel,
+        [((2, 4, 2, 128), F32), (up.shape, BF16), (down.shape, BF16), ((2, 4, 64, 128), F32)],
+        1,
+        7,
+        [pltpu.VMEM((3, 2, 4, 8, 128), F32), pltpu.VMEM((4, 2, 2, 128, 128), F32)],
+        flops=3 * 10 ** 9,
+        nbytes=3 * 10 ** 7,
+    )(lists, up2, down2, up, down, bias, qd, state)
+    r_up, r_down = to_z(d_up, 1), to_z(d_down, -1)
     rest = rest + (stats,)
     (d_up2, d_down2), oq2 = back_call((UP2, DOWN2), lists, (up2, down2), rest)
     r_up2, r_down2 = to_z(d_up2, 2), to_z(d_down2, -2)
-    (d_up,), oq1 = back_call((UP,), lists, (up,), rest)
-    r_up = to_z(d_up, 1)
-    (d_down,), oq3 = back_call((DOWN,), lists, (down,), rest)
-    r_down = to_z(d_down, -1)
     (d_own,), oq0 = back_call((OWN,), lists, (own,), rest)
-    oq = oq0 + oq1 + oq2 + oq3
+    oq = oq0 + oq1 + oq2
     oq = jnp.concatenate([oq[:, :, :32] * SCALE, oq[:, :, 32:]], axis=2)
     oq_other = lax.ppermute(oq[1].astype(BF16), "xl", SWAP)
     out_keep, out_send = call(

time: 179 us -> 171 us (0.955)
  the two profiles are of different devices: /device:TPU:13 before, /device:TPU:19 now
where the time goes in v8:
time: 171 us; the launch traced here: 170 us
  starting transfers between devices  53.5 us (31%)
  blocking collectives  41.4 us (24%)
  waiting for transfers between devices  29.1 us (17%)
  Pallas kernels  27.8 us (16%)
  between operations  14.3 us (8%)
  local copies, waits for them, and re-layouts  3.37 us (2%)
    all_gather x1, blocking collectives, per_device(): own = lax.all_gather(kv, 'z', axis_index_groups=groups)  28.5 us
    ppermute x8, starting transfers between devices, to_z(): return lax.ppermute(x, 'z', [(j, (j + step) % 16) for j in range(16)])  27.4 us
    ppermute x1, starting transfers between devices, per_device(): out_other = lax.ppermute(out_send, 'c', SWAP)  10.3 us
    ppermute x8, waiting for transfers between devices, to_z(): return lax.ppermute(x, 'z', [(j, (j + step) % 16) for j in range(16)])  9.54 us
    all_to_all x1, waiting for transfers between devices, per_device(): dkv = lax.all_to_all(sums, 'z', 0, 0, axis_index_groups=groups, tiled=True)  9.24 us
    all_gather x1, blocking collectives, per_device(): lax.all_gather(part, 'c')  8.78 us
    pallas_call x1, Pallas kernels, per_device(): call(mid_kernel, [((2, 4, 2, 128), F32), (up.shape, BF16), (down.shape, B...  8.44 us
    pallas_call x2, Pallas kernels, back_call(): call(functools.partial(back_kernel, names), [(kv.shape, BF16) for kv in k...  7.34 us
  transfers between devices with their start and end apart: 14, of which 9 were waited for; matrix products, arithmetic and copies ran while one was open for 0% of the time, Pallas kernels for 8%

profile of v8, /device:TPU:19, one launch (start us, length us, event | category | flops | bytes accessed | tf_op | source)
XLA Modules:
  0.0 170.3 jit_solution(13549362199215061572)
XLA Ops:
  7.2 2.8 %shard_map.86 = (bf16[512,128]{1,0:T(8,128)(2,1)}, bf16[512,128]{1,0:T(8,128)(2,1)}, f32[4,64,128]{2,1,0:T(8,128)}, f32[4,64,128]{2,1,0:T(8,128)}, bf16[4,4,128,128]{3,2,1,0:T(8,128)(2,1)}, /*index=5*/s32[90]{0:T(128)}) custom-call(bf16[4,128,128]{2,1,0:T(8,128)(2,1)} %pair.1, f32[1,128]{1,0:T(1,128)} %bitcast.22, bf16[128,256]{1,0:T(8,128)(2,1)} %w_proj.1, ...), custom_call_target="tpu_custom_call" | custom-call | tf_op jit(solution)/shard_map/pallas_call | solution.py:336
  10.0 4.3 %all-to-all-start = ((bf16[4,4,128,128]{3,2,1,0:T(8,128)(2,1)}), bf16[4,4,128,128]{3,2,1,0:T(8,128)(2,1)S(1)}, u32[]{:S(2)}, u32[]{:S(2)}) async-start(bf16[4,4,128,128]{3,2,1,0:T(8,128)(2,1)} %get-tuple-element.27), calls=%async_computation | async-start | bytes 1048576 | tf_op jit(solution)/shard_map/all_to_all | solution.py:350
  16.2 6.8 %collective-permute-done.pack1 = bf16[512,128]{1,0:T(8,128)(2,1)S(1)} collective-permute-done((bf16[512,128]{1,0:T(8,128)(2,1)}, bf16[512,128]{1,0:T(8,128)(2,1)S(1)}, u32[]{:S(2)}, u32[]{:S(2)}) %collective-permute-start) | collective-permute-done | bytes 131104 | tf_op jit(solution)/shard_map/ppermute | solution.py:349
  24.8 28.5 %all-gather = bf16[8,2,128,128]{3,2,1,0:T(8,128)(2,1)S(1)} all-gather(bf16[2,2,128,128]{3,2,1,0:T(8,128)(2,1)S(1)} %get-tuple-element.30), channel_id=2, replica_groups={{0,8,16,24},{2,10,18,26},{4,12,20,28},{6,14,22,30},{1,9,17,25},{3,11,19..., dimensions={0}, use_global_device_ids=true | all-gather | bytes 655360 | tf_op jit(solution)/shard_map/all_gather | solution.py:357
  53.3 4.5 %collective-permute-start.4 = (bf16[4,2,2,128,128]{4,3,2,1,0:T(8,128)(2,1)S(1)}, bf16[4,2,2,128,128]{4,3,2,1,0:T(8,128)(2,1)S(1)}, u32[]{:S(2)}, u32[]{:S(2)}) collective-permute-start(bf16[4,2,2,128,128]{4,3,2,1,0:T(8,128)(2,1)S(1)} %bitcast.11), channel_id=1, source_target_pairs={{0,2},{2,4},{4,6},{6,8},{8,10},{10,12},{12,14},{14,16},{16,18},{18... | collective-permute-start | bytes 1572872 | tf_op jit(solution)/shard_map/ppermute | solution.py:330
  57.7 2.7 %collective-permute-start.3 = (bf16[4,2,2,128,128]{4,3,2,1,0:T(8,128)(2,1)S(1)}, bf16[4,2,2,128,128]{4,3,2,1,0:T(8,128)(2,1)S(1)}, u32[]{:S(2)}, u32[]{:S(2)}) collective-permute-start(bf16[4,2,2,128,128]{4,3,2,1,0:T(8,128)(2,1)S(1)} %bitcast.12), channel_id=1, source_target_pairs={{0,30},{2,0},{4,2},{6,4},{8,6},{10,8},{12,10},{14,12},{16,14},{18,... | collective-permute-start | bytes 1572872 | tf_op jit(solution)/shard_map/ppermute | solution.py:330
  60.4 4.4 %collective-permute-start.1 = (bf16[2,2,2,128,128]{4,3,2,1,0:T(8,128)(2,1)S(1)}, bf16[2,2,2,128,128]{4,3,2,1,0:T(8,128)(2,1)S(1)}, u32[]{:S(2)}, u32[]{:S(2)}) collective-permute-start(bf16[2,2,2,128,128]{4,3,2,1,0:T(8,128)(2,1)S(1)} %bitcast.26), channel_id=1, source_target_pairs={{0,28},{2,30},{4,0},{6,2},{8,4},{10,6},{12,8},{14,10},{16,12},{18,... | collective-permute-start | bytes 786440 | tf_op jit(solution)/shard_map/ppermute | solution.py:330
  68.8 2.4 %shard_map.88.refs_4_ = f32[3,2,4,8,128]{4,3,2,1,0:T(8,128)S(1)} custom-call(s32[90]{0:T(128)S(1)} %copy-done.8, bf16[4,2,2,128,128]{4,3,2,1,0:T(8,128)(2,1)S(1)} %bitcast.13, bf16[4,2,2,4,128,128]{5,4,3,2,1,0:T(8,128)(2,1)S(1)} %bitcast.15, bf16[2,4,128,256]{3,2,1,0:T(8,128)(2,1)S(1)} %get-tuple-element.32.refs_2_.refs_3_.qd), custom_call_target="tpu_custom_call" | custom-call | flops 1000000000 | bytes 10000000 | tf_op jit(solution)/shard_map/pallas_call | solution.py:305
  71.2 4.0 %shard_map.89.before = f32[3,2,4,8,128]{4,3,2,1,0:T(8,128)S(1)} custom-call(s32[90]{0:T(128)S(1)} %copy-done.8, bf16[4,2,2,128,128]{4,3,2,1,0:T(8,128)(2,1)S(1)} %collective-permute-done.3.refs_0_.up, bf16[4,2,2,128,128]{4,3,2,1,0:T(8,128)(2,1)S(1)} %collective-permute-done.4.refs_1_.down, bf16[4,2,2,4,128,128]{5,4,3,2,1,0:T(8,128)(2,1)S(1)} %bitcast.16, ...), custom_call_target="tpu_custom_call" | custom-call | flops 1000000000 | bytes 10000000 | tf_op jit(solution)/shard_map/pallas_call | solution.py:305
  77.8 8.4 %shard_map.90 = (f32[2,4,2,128]{3,2,1,0:T(2,128)S(1)}, bf16[4,2,2,128,128]{4,3,2,1,0:T(8,128)(2,1)S(1)}, bf16[4,2,2,128,128]{4,3,2,1,0:T(8,128)(2,1)S(1)}, f32[2,4,64,128]{3,2,1,0:T(8,128)S(1)}) custom-call(s32[90]{0:T(128)S(1)} %copy-done.8, bf16[2,2,2,128,128]{4,3,2,1,0:T(8,128)(2,1)S(1)} %collective-permute-done.1.up2.refs_0_, ...), custom_call_target="tpu_custom_call" | custom-call | flops 3000000000 | bytes 30000000 | tf_op jit(solution)/shard_map/pallas_call | solution.py:363
  86.3 2.1 %collective-permute-start.5 = (bf16[4,2,2,128,128]{4,3,2,1,0:T(8,128)(2,1)S(1)}, bf16[4,2,2,128,128]{4,3,2,1,0:T(8,128)(2,1)S(1)}, u32[]{:S(2)}, u32[]{:S(2)}) collective-permute-start(bf16[4,2,2,128,128]{4,3,2,1,0:T(8,128)(2,1)S(1)} %get-tuple-element.35), channel_id=1, source_target_pairs={{0,2},{2,4},{4,6},{6,8},{8,10},{10,12},{12,14},{14,16},{16,18},{18... | collective-permute-start | bytes 1572872 | tf_op jit(solution)/shard_map/ppermute | solution.py:330
  88.4 4.4 %collective-permute-start.6 = (bf16[4,2,2,128,128]{4,3,2,1,0:T(8,128)(2,1)S(1)}, bf16[4,2,2,128,128]{4,3,2,1,0:T(8,128)(2,1)S(1)}, u32[]{:S(2)}, u32[]{:S(2)}) collective-permute-start(bf16[4,2,2,128,128]{4,3,2,1,0:T(8,128)(2,1)S(1)} %get-tuple-element.36), channel_id=1, source_target_pairs={{0,30},{2,0},{4,2},{6,4},{8,6},{10,8},{12,10},{14,12},{16,14},{18,... | collective-permute-start | bytes 1572872 | tf_op jit(solution)/shard_map/ppermute | solution.py:330
  92.8 3.7 %shard_map.92 = (bf16[2,2,2,128,128]{4,3,2,1,0:T(8,128)(2,1)S(1)}, bf16[2,2,2,128,128]{4,3,2,1,0:T(8,128)(2,1)S(1)}, f32[2,4,64,128]{3,2,1,0:T(8,128)S(1)}) custom-call(s32[90]{0:T(128)S(1)} %copy-done.8, bf16[2,2,2,128,128]{4,3,2,1,0:T(8,128)(2,1)S(1)} %collective-permute-done.1.up2.refs_0_, ...), custom_call_target="tpu_custom_call" | custom-call | flops 2000000000 | bytes 20000000 | tf_op jit(solution)/shard_map/pallas_call | solution.py:317
  96.5 3.0 %collective-permute-start.7 = (bf16[2,2,2,128,128]{4,3,2,1,0:T(8,128)(2,1)S(1)}, bf16[2,2,2,128,128]{4,3,2,1,0:T(8,128)(2,1)S(1)}, u32[]{:S(2)}, u32[]{:S(2)}) collective-permute-start(bf16[2,2,2,128,128]{4,3,2,1,0:T(8,128)(2,1)S(1)} %get-tuple-element.37), channel_id=1, source_target_pairs={{0,4},{2,6},{4,8},{6,10},{8,12},{10,14},{12,16},{14,18},{16,20},{1... | collective-permute-start | bytes 786440 | tf_op jit(solution)/shard_map/ppermute | solution.py:330
  99.4 4.4 %collective-permute-start.8 = (bf16[2,2,2,128,128]{4,3,2,1,0:T(8,128)(2,1)S(1)}, bf16[2,2,2,128,128]{4,3,2,1,0:T(8,128)(2,1)S(1)}, u32[]{:S(2)}, u32[]{:S(2)}) collective-permute-start(bf16[2,2,2,128,128]{4,3,2,1,0:T(8,128)(2,1)S(1)} %get-tuple-element.38), channel_id=1, source_target_pairs={{0,28},{2,30},{4,0},{6,2},{8,4},{10,6},{12,8},{14,10},{16,12},{18,... | collective-permute-start | bytes 786440 | tf_op jit(solution)/shard_map/ppermute | solution.py:330
  103.9 3.7 %shard_map.91 = (bf16[4,2,2,128,128]{4,3,2,1,0:T(8,128)(2,1)S(1)}, f32[2,4,64,128]{3,2,1,0:T(8,128)S(1)}) custom-call(s32[90]{0:T(128)S(1)} %copy-done.8, bf16[4,2,2,128,128]{4,3,2,1,0:T(8,128)(2,1)S(1)} %bitcast.14, bf16[4,2,2,4,128,128]{5,4,3,2,1,0:T(8,128)(2,1)S(1)} %bitcast.19, bf16[2,4,128,256]{3,2,1,0:T(8,128)(2,1)S(1)} %get-tuple-element.32.refs_2_.refs_3_.qd, ...), custom_call_target="tpu_custom_call" | custom-call | flops 2000000000 | bytes 20000000 | tf_op jit(solution)/shard_map/pallas_call | solution.py:317
  107.9 6.6 %collective-permute-done.8.r_down2 = bf16[2,2,2,128,128]{4,3,2,1,0:T(8,128)(2,1)S(1)} collective-permute-done((bf16[2,2,2,128,128]{4,3,2,1,0:T(8,128)(2,1)S(1)}, bf16[2,2,2,128,128]{4,3,2,1,0:T(8,128)(2,1)S(1)}, u32[]{:S(2)}, u32[]{:S(2)}) %collective-permute-start.8) | collective-permute-done | bytes 262176 | tf_op jit(solution)/shard_map/ppermute | solution.py:330
  115.6 6.8 %all-to-all-start.1 = ((bf16[4,2,2,128,128]{4,3,2,1,0:T(8,128)(2,1)}), bf16[4,2,2,128,128]{4,3,2,1,0:T(8,128)(2,1)S(1)}, u32[]{:S(2)}, u32[]{:S(2)}) async-start(bf16[4,2,2,128,128]{4,3,2,1,0:T(8,128)(2,1)} %shard_map.93), calls=%async_computation.1 | async-start | bytes 1048576 | tf_op jit(solution)/shard_map/all_to_all | solution.py:388
  122.5 2.9 %collective-permute-start.9 = (bf16[4,64,128]{2,1,0:T(8,128)(2,1)S(1)}, bf16[4,64,128]{2,1,0:T(8,128)(2,1)S(1)}, u32[]{:S(2)}, u32[]{:S(2)}) collective-permute-start(bf16[4,64,128]{2,1,0:T(8,128)(2,1)S(1)} %fusion.2), channel_id=1, source_target_pairs={{0,32},{32,0},{1,33},{33,1},{2,34},{34,2},{3,35},{35,3},{4,36},{36... | collective-permute-start | bytes 196616 | tf_op jit(solution)/shard_map/ppermute | solution.py:379
  125.4 2.2 %collective-permute-done.9.oq_other = bf16[4,64,128]{2,1,0:T(8,128)(2,1)S(1)} collective-permute-done((bf16[4,64,128]{2,1,0:T(8,128)(2,1)S(1)}, bf16[4,64,128]{2,1,0:T(8,128)(2,1)S(1)}, u32[]{:S(2)}, u32[]{:S(2)}) %collective-permute-start.9) | collective-permute-done | bytes 65568 | tf_op jit(solution)/shard_map/ppermute | solution.py:379
  127.9 10.3 %collective-permute-start.10 = (bf16[4,64,128]{2,1,0:T(8,128)(2,1)S(1)}, bf16[4,64,128]{2,1,0:T(8,128)(2,1)S(1)}, u32[]{:S(2)}, u32[]{:S(2)}) collective-permute-start(bf16[4,64,128]{2,1,0:T(8,128)(2,1)S(1)} %get-tuple-element.44), channel_id=1, source_target_pairs={{0,1},{1,0},{2,3},{3,2},{4,5},{5,4},{6,7},{7,6},{8,9},{9,8},{10,11... | collective-permute-start | bytes 196616 | tf_op jit(solution)/shard_map/ppermute | solution.py:383
  139.7 9.2 %all-to-all-done.1.dkv_own = bf16[4,2,2,128,128]{4,3,2,1,0:T(8,128)(2,1)S(1)} async-done(((bf16[4,2,2,128,128]{4,3,2,1,0:T(8,128)(2,1)}), bf16[4,2,2,128,128]{4,3,2,1,0:T(8,128)(2,1)S(1)}, u32[]{:S(2)}, u32[]{:S(2)}) %all-to-all-start.1) | async-done | bytes 524320 | tf_op jit(solution)/shard_map/all_to_all | solution.py:388
  149.0 4.1 %all-gather.2 = bf16[4,128,128]{2,1,0:T(8,128)(2,1)S(1)} all-gather(bf16[2,128,128]{2,1,0:T(8,128)(2,1)S(1)} %slice_reduce_fusion), channel_id=4, replica_groups=mesh['xh'=2,'y'=4,'xl'=2,'z'=16,'c'=2] {'xl'}, dimensions={0}, use_global_device_ids=true | all-gather | bytes 196608 | tf_op jit(solution)/shard_map/all_gather | solution.py:393
  153.5 8.8 %all-gather.3 = bf16[8,128,128]{2,1,0:T(8,128)(2,1)S(1)} all-gather(bf16[4,128,128]{2,1,0:T(8,128)(2,1)S(1)} %shard_map.95), channel_id=5, replica_groups=mesh['xh'=2,'y'=4,'xl'=2,'z'=16,'c'=2] {'c'}, dimensions={0}, use_global_device_ids=true | all-gather | bytes 393216 | tf_op jit(solution)/shard_map/all_gather | solution.py:395
  (46 shorter events, 15.1 us)
Async XLA Ops:
  9.9 57.3 %copy-start.8 = (s32[90]{0:T(128)S(1)}, s32[90]{0:T(128)}, u32[]{:S(2)}) copy-start(s32[90]{0:T(128)} %get-tuple-element.25.lists) | copy-start | bytes 1084
  10.0 13.0 %all-to-all-start = ((bf16[4,4,128,128]{3,2,1,0:T(8,128)(2,1)}), bf16[4,4,128,128]{3,2,1,0:T(8,128)(2,1)S(1)}, u32[]{:S(2)}, u32[]{:S(2)}) async-start(bf16[4,4,128,128]{3,2,1,0:T(8,128)(2,1)} %get-tuple-element.27), calls=%async_computation | async-start | bytes 1048576 | tf_op jit(solution)/shard_map/all_to_all | solution.py:350
  14.2 53.0 %all-gather.6.cloned.1.call-start = ((), (), s32[]{:S(2)}) async-start(), calls=%async_computation.2 | async-start | bytes 2621440 | tf_op jit(solution)/shard_map/all_gather | solution.py:352
  14.2 8.7 %collective-permute-start = (bf16[512,128]{1,0:T(8,128)(2,1)}, bf16[512,128]{1,0:T(8,128)(2,1)S(1)}, u32[]{:S(2)}, u32[]{:S(2)}) collective-permute-start(bf16[512,128]{1,0:T(8,128)(2,1)} %get-tuple-element.28), channel_id=1, source_target_pairs={{0,32},{32,0},{1,33},{33,1},{2,34},{34,2},{3,35},{35,3},{4,36},{36... | collective-permute-start | bytes 393224 | tf_op jit(solution)/shard_map/ppermute | solution.py:349
  23.0 0.8 copy-start.9
  23.8 0.9 copy-start.4
  53.3 17.9 %collective-permute-start.4 = (bf16[4,2,2,128,128]{4,3,2,1,0:T(8,128)(2,1)S(1)}, bf16[4,2,2,128,128]{4,3,2,1,0:T(8,128)(2,1)S(1)}, u32[]{:S(2)}, u32[]{:S(2)}) collective-permute-start(bf16[4,2,2,128,128]{4,3,2,1,0:T(8,128)(2,1)S(1)} %bitcast.11), channel_id=1, source_target_pairs={{0,2},{2,4},{4,6},{6,8},{8,10},{10,12},{12,14},{14,16},{16,18},{18... | collective-permute-start | bytes 1572872 | tf_op jit(solution)/shard_map/ppermute | solution.py:330
  57.7 13.5 %collective-permute-start.3 = (bf16[4,2,2,128,128]{4,3,2,1,0:T(8,128)(2,1)S(1)}, bf16[4,2,2,128,128]{4,3,2,1,0:T(8,128)(2,1)S(1)}, u32[]{:S(2)}, u32[]{:S(2)}) collective-permute-start(bf16[4,2,2,128,128]{4,3,2,1,0:T(8,128)(2,1)S(1)} %bitcast.12), channel_id=1, source_target_pairs={{0,30},{2,0},{4,2},{6,4},{8,6},{10,8},{12,10},{14,12},{16,14},{18,... | collective-permute-start | bytes 1572872 | tf_op jit(solution)/shard_map/ppermute | solution.py:330
  60.4 16.3 %collective-permute-start.1 = (bf16[2,2,2,128,128]{4,3,2,1,0:T(8,128)(2,1)S(1)}, bf16[2,2,2,128,128]{4,3,2,1,0:T(8,128)(2,1)S(1)}, u32[]{:S(2)}, u32[]{:S(2)}) collective-permute-start(bf16[2,2,2,128,128]{4,3,2,1,0:T(8,128)(2,1)S(1)} %bitcast.26), channel_id=1, source_target_pairs={{0,28},{2,30},{4,0},{6,2},{8,4},{10,6},{12,8},{14,10},{16,12},{18,... | collective-permute-start | bytes 786440 | tf_op jit(solution)/shard_map/ppermute | solution.py:330
  64.9 13.0 %collective-permute-start.2 = (bf16[2,2,2,128,128]{4,3,2,1,0:T(8,128)(2,1)S(1)}, bf16[2,2,2,128,128]{4,3,2,1,0:T(8,128)(2,1)S(1)}, u32[]{:S(2)}, u32[]{:S(2)}) collective-permute-start(bf16[2,2,2,128,128]{4,3,2,1,0:T(8,128)(2,1)S(1)} %bitcast.25), channel_id=1, source_target_pairs={{0,4},{2,6},{4,8},{6,10},{8,12},{10,14},{12,16},{14,18},{16,20},{1... | collective-permute-start | bytes 786440 | tf_op jit(solution)/shard_map/ppermute | solution.py:330
  67.2 1.6 copy-start
  86.3 28.2 %collective-permute-start.5 = (bf16[4,2,2,128,128]{4,3,2,1,0:T(8,128)(2,1)S(1)}, bf16[4,2,2,128,128]{4,3,2,1,0:T(8,128)(2,1)S(1)}, u32[]{:S(2)}, u32[]{:S(2)}) collective-permute-start(bf16[4,2,2,128,128]{4,3,2,1,0:T(8,128)(2,1)S(1)} %get-tuple-element.35), channel_id=1, source_target_pairs={{0,2},{2,4},{4,6},{6,8},{8,10},{10,12},{12,14},{14,16},{16,18},{18... | collective-permute-start | bytes 1572872 | tf_op jit(solution)/shard_map/ppermute | solution.py:330
  88.4 26.1 %collective-permute-start.6 = (bf16[4,2,2,128,128]{4,3,2,1,0:T(8,128)(2,1)S(1)}, bf16[4,2,2,128,128]{4,3,2,1,0:T(8,128)(2,1)S(1)}, u32[]{:S(2)}, u32[]{:S(2)}) collective-permute-start(bf16[4,2,2,128,128]{4,3,2,1,0:T(8,128)(2,1)S(1)} %get-tuple-element.36), channel_id=1, source_target_pairs={{0,30},{2,0},{4,2},{6,4},{8,6},{10,8},{12,10},{14,12},{16,14},{18,... | collective-permute-start | bytes 1572872 | tf_op jit(solution)/shard_map/ppermute | solution.py:330
  96.5 11.5 %collective-permute-start.7 = (bf16[2,2,2,128,128]{4,3,2,1,0:T(8,128)(2,1)S(1)}, bf16[2,2,2,128,128]{4,3,2,1,0:T(8,128)(2,1)S(1)}, u32[]{:S(2)}, u32[]{:S(2)}) collective-permute-start(bf16[2,2,2,128,128]{4,3,2,1,0:T(8,128)(2,1)S(1)} %get-tuple-element.37), channel_id=1, source_target_pairs={{0,4},{2,6},{4,8},{6,10},{8,12},{10,14},{12,16},{14,18},{16,20},{1... | collective-permute-start | bytes 786440 | tf_op jit(solution)/shard_map/ppermute | solution.py:330
  99.4 15.1 %collective-permute-start.8 = (bf16[2,2,2,128,128]{4,3,2,1,0:T(8,128)(2,1)S(1)}, bf16[2,2,2,128,128]{4,3,2,1,0:T(8,128)(2,1)S(1)}, u32[]{:S(2)}, u32[]{:S(2)}) collective-permute-start(bf16[2,2,2,128,128]{4,3,2,1,0:T(8,128)(2,1)S(1)} %get-tuple-element.38), channel_id=1, source_target_pairs={{0,28},{2,30},{4,0},{6,2},{8,4},{10,6},{12,8},{14,10},{16,12},{18,... | collective-permute-start | bytes 786440 | tf_op jit(solution)/shard_map/ppermute | solution.py:330
  115.6 12.1 %copy-start.2 = (f32[4,64,128]{2,1,0:T(8,128)S(1)}, f32[4,64,128]{2,1,0:T(8,128)}, u32[]{:S(2)}) copy-start(f32[4,64,128]{2,1,0:T(8,128)} %get-tuple-element.42.gate) | copy-start | bytes 393220
  115.6 12.1 %copy-start.6 = (bf16[64,128]{1,0:T(8,128)(2,1)S(1)}, bf16[64,128]{1,0:T(8,128)(2,1)}, u32[]{:S(2)}) copy-start(bf16[64,128]{1,0:T(8,128)(2,1)} %w_out.1) | copy-start | bytes 49156
  115.6 33.4 %all-to-all-start.1 = ((bf16[4,2,2,128,128]{4,3,2,1,0:T(8,128)(2,1)}), bf16[4,2,2,128,128]{4,3,2,1,0:T(8,128)(2,1)S(1)}, u32[]{:S(2)}, u32[]{:S(2)}) async-start(bf16[4,2,2,128,128]{4,3,2,1,0:T(8,128)(2,1)} %shard_map.93), calls=%async_computation.1 | async-start | bytes 1048576 | tf_op jit(solution)/shard_map/all_to_all | solution.py:388
  122.4 30.7 %copy-start.3 = (bf16[128,256]{1,0:T(8,128)(2,1)S(1)}, bf16[128,256]{1,0:T(8,128)(2,1)}, u32[]{:S(2)}) copy-start(bf16[128,256]{1,0:T(8,128)(2,1)} %w_proj.1) | copy-start | bytes 196612
  122.4 30.7 %copy-start.5 = (f32[4,64,128]{2,1,0:T(8,128)S(1)}, f32[4,64,128]{2,1,0:T(8,128)}, u32[]{:S(2)}) copy-start(f32[4,64,128]{2,1,0:T(8,128)} %get-tuple-element.47.go) | copy-start | bytes 393220
  122.4 39.9 %copy-start.1 = (bf16[4,128,128]{2,1,0:T(8,128)(2,1)S(1)}, bf16[4,128,128]{2,1,0:T(8,128)(2,1)}, u32[]{:S(2)}) copy-start(bf16[4,128,128]{2,1,0:T(8,128)(2,1)} %pair.1) | copy-start | bytes 393220
  122.5 39.9 %copy-start.7 = (f32[128]{0:T(128)S(1)}, f32[128]{0:T(128)}, u32[]{:S(2)}) copy-start(f32[128]{0:T(128)} %param.8) | copy-start | bytes 1540
  122.5 5.1 %collective-permute-start.9 = (bf16[4,64,128]{2,1,0:T(8,128)(2,1)S(1)}, bf16[4,64,128]{2,1,0:T(8,128)(2,1)S(1)}, u32[]{:S(2)}, u32[]{:S(2)}) collective-permute-start(bf16[4,64,128]{2,1,0:T(8,128)(2,1)S(1)} %fusion.2), channel_id=1, source_target_pairs={{0,32},{32,0},{1,33},{33,1},{2,34},{34,2},{3,35},{35,3},{4,36},{36... | collective-permute-start | bytes 196616 | tf_op jit(solution)/shard_map/ppermute | solution.py:379
  127.9 11.2 %collective-permute-start.10 = (bf16[4,64,128]{2,1,0:T(8,128)(2,1)S(1)}, bf16[4,64,128]{2,1,0:T(8,128)(2,1)S(1)}, u32[]{:S(2)}, u32[]{:S(2)}) collective-permute-start(bf16[4,64,128]{2,1,0:T(8,128)(2,1)S(1)} %get-tuple-element.44), channel_id=1, source_target_pairs={{0,1},{1,0},{2,3},{3,2},{4,5},{5,4},{6,7},{7,6},{8,9},{9,8},{10,11... | collective-permute-start | bytes 196616 | tf_op jit(solution)/shard_map/ppermute | solution.py:383
Sparse Core Ops, SparseCore 0:
  23.9 43.2 all-gather.5

commit v9 on v8

--- a/solution.py
+++ b/solution.py
@@ -152,9 +152,13 @@
     base = 9 * (2 * which + half)
     n = lists[base + 8]
 
-    @pl.loop(0, n // 2)
+    @pl.loop(0, n // 4)
     def _(k):
-        body([lists[base + 2 * k], lists[base + 2 * k + 1]])
+        body([lists[base + 4 * k + j] for j in range(4)])
+
+    @pl.when(n % 4 >= 2)
+    def _():
+        body([lists[base + n // 4 * 4], lists[base + n // 4 * 4 + 1]])
 
     @pl.when(n % 2 == 1)
     def _():
@@ -178,20 +182,18 @@
 
             def body(units, kv=kv, which=which):
                 keys, b = load_units(ids, kv, bias, which, half, units)
-                rows = b.shape[0] // 8
-                for p in range(2):
-                    sd = [nn(keys[p], qd[half, 2 * p + i]) for i in range(2)]
-                    for i in range(2):
-                        r = 2 * p + i
-                        s = (sd[i][:, :128] + b).reshape(rows, 8, 128)
-                        dp = sd[i][:, 128:].reshape(rows, 8, 128)
-                        m_old = st[0, half, r]
-                        m_new = jnp.maximum(m_old, jnp.max(s, axis=0))
+                for r in range(4):
+                    sd = nn(keys[r // 2], qd[half, r])
+                    m, l, d = (st[k, half, r] for k in range(3))
+                    for low in range(0, b.shape[0], 64):
+                        rows = slice(low, low + 64)
+                        s = (sd[rows, :128] + b[rows]).reshape(-1, 8, 128)
+                        dp = sd[rows, 128:].reshape(-1, 8, 128)
+                        m_new = jnp.maximum(m, jnp.max(s, axis=0))
                         e = jnp.exp(s - m_new[None])
-                        c = jnp.exp(m_old - m_new)
-                        st[1, half, r] = st[1, half, r] * c + jnp.sum(e, axis=0)
-                        st[2, half, r] = st[2, half, r] * c + jnp.sum(e * dp, axis=0)
-                        st[0, half, r] = m_new
+                        c = jnp.exp(m - m_new)
+                        m, l, d = m_new, l * c + jnp.sum(e, axis=0), d * c + jnp.sum(e * dp, axis=0)
+                    st[0, half, r], st[1, half, r], st[2, half, r] = m, l, d
 
             over_units(lists, which, half, body)
 

time: 171 us -> 174 us (1.018)
  the two profiles are of different devices: /device:TPU:19 before, /device:TPU:1 now
where the time goes in v9:
time: 174 us
  starting transfers between devices  62.4 us (36%)
  blocking collectives  44.7 us (26%)
  waiting for transfers between devices  29.4 us (17%)
  Pallas kernels  19.2 us (11%)
  between operations  14.3 us (8%)
  local copies, waits for them, and re-layouts  3.37 us (2%)
    all_gather x1, blocking collectives, per_device(): own = lax.all_gather(kv, 'z', axis_index_groups=groups)  32.9 us
    ppermute x8, starting transfers between devices, to_z(): return lax.ppermute(x, 'z', [(j, (j + step) % 16) for j in range(16)])  31.6 us
    all_to_all x1, starting transfers between devices, per_device(): dkv = lax.all_to_all(sums, 'z', 0, 0, axis_index_groups=groups, tiled=True)  15.1 us
    all_to_all x1, waiting for transfers between devices, per_device(): dkv = lax.all_to_all(sums, 'z', 0, 0, axis_index_groups=groups, tiled=True)  10.8 us
    ppermute x8, waiting for transfers between devices, to_z(): return lax.ppermute(x, 'z', [(j, (j + step) % 16) for j in range(16)])  10.7 us
    all_gather x1, blocking collectives, per_device(): lax.all_gather(theirs, 'xl')  7.5 us
    ppermute x1, starting transfers between devices, per_device(): out_other = lax.ppermute(out_send, 'c', SWAP)  5.43 us
    pallas_call x2, Pallas kernels, back_call(): call(functools.partial(back_kernel, names), [(kv.shape, BF16) for kv in k...  5.03 us
  transfers between devices with their start and end apart: 14, of which 9 were waited for; matrix products, arithmetic and copies ran while one was open for 0% of the time, Pallas kernels for 5%

profile of v9, /device:TPU:1, one launch (start us, length us, event | category | flops | bytes accessed | tf_op | source)
XLA Modules:
  0.0 174.1 jit_solution(3815071618304745043)
XLA Ops:
  7.2 2.8 %shard_map.86 = (bf16[512,128]{1,0:T(8,128)(2,1)}, bf16[512,128]{1,0:T(8,128)(2,1)}, f32[4,64,128]{2,1,0:T(8,128)}, f32[4,64,128]{2,1,0:T(8,128)}, bf16[4,4,128,128]{3,2,1,0:T(8,128)(2,1)}, /*index=5*/s32[90]{0:T(128)}) custom-call(bf16[4,128,128]{2,1,0:T(8,128)(2,1)} %pair.1, f32[1,128]{1,0:T(1,128)} %bitcast.22, bf16[128,256]{1,0:T(8,128)(2,1)} %w_proj.1, ...), custom_call_target="tpu_custom_call" | custom-call | tf_op jit(solution)/shard_map/pallas_call | solution.py:338
  10.0 4.9 %all-to-all-start = ((bf16[4,4,128,128]{3,2,1,0:T(8,128)(2,1)}), bf16[4,4,128,128]{3,2,1,0:T(8,128)(2,1)S(1)}, u32[]{:S(2)}, u32[]{:S(2)}) async-start(bf16[4,4,128,128]{3,2,1,0:T(8,128)(2,1)} %get-tuple-element.27), calls=%async_computation | async-start | bytes 1048576 | tf_op jit(solution)/shard_map/all_to_all | solution.py:352
  14.8 3.4 %collective-permute-start = (bf16[512,128]{1,0:T(8,128)(2,1)}, bf16[512,128]{1,0:T(8,128)(2,1)S(1)}, u32[]{:S(2)}, u32[]{:S(2)}) collective-permute-start(bf16[512,128]{1,0:T(8,128)(2,1)} %get-tuple-element.28), channel_id=1, source_target_pairs={{0,32},{32,0},{1,33},{33,1},{2,34},{34,2},{3,35},{35,3},{4,36},{36... | collective-permute-start | bytes 393224 | tf_op jit(solution)/shard_map/ppermute | solution.py:351
  18.2 3.5 %collective-permute-done.pack1 = bf16[512,128]{1,0:T(8,128)(2,1)S(1)} collective-permute-done((bf16[512,128]{1,0:T(8,128)(2,1)}, bf16[512,128]{1,0:T(8,128)(2,1)S(1)}, u32[]{:S(2)}, u32[]{:S(2)}) %collective-permute-start) | collective-permute-done | bytes 131104 | tf_op jit(solution)/shard_map/ppermute | solution.py:351
  23.5 32.9 %all-gather = bf16[8,2,128,128]{3,2,1,0:T(8,128)(2,1)S(1)} all-gather(bf16[2,2,128,128]{3,2,1,0:T(8,128)(2,1)S(1)} %get-tuple-element.30), channel_id=2, replica_groups={{0,8,16,24},{2,10,18,26},{4,12,20,28},{6,14,22,30},{1,9,17,25},{3,11,19..., dimensions={0}, use_global_device_ids=true | all-gather | bytes 655360 | tf_op jit(solution)/shard_map/all_gather | solution.py:359
  56.5 2.9 %collective-permute-start.4 = (bf16[4,2,2,128,128]{4,3,2,1,0:T(8,128)(2,1)S(1)}, bf16[4,2,2,128,128]{4,3,2,1,0:T(8,128)(2,1)S(1)}, u32[]{:S(2)}, u32[]{:S(2)}) collective-permute-start(bf16[4,2,2,128,128]{4,3,2,1,0:T(8,128)(2,1)S(1)} %bitcast.11), channel_id=1, source_target_pairs={{0,2},{2,4},{4,6},{6,8},{8,10},{10,12},{12,14},{14,16},{16,18},{18... | collective-permute-start | bytes 1572872 | tf_op jit(solution)/shard_map/ppermute | solution.py:332
  59.4 3.5 %collective-permute-start.3 = (bf16[4,2,2,128,128]{4,3,2,1,0:T(8,128)(2,1)S(1)}, bf16[4,2,2,128,128]{4,3,2,1,0:T(8,128)(2,1)S(1)}, u32[]{:S(2)}, u32[]{:S(2)}) collective-permute-start(bf16[4,2,2,128,128]{4,3,2,1,0:T(8,128)(2,1)S(1)} %bitcast.12), channel_id=1, source_target_pairs={{0,30},{2,0},{4,2},{6,4},{8,6},{10,8},{12,10},{14,12},{16,14},{18,... | collective-permute-start | bytes 1572872 | tf_op jit(solution)/shard_map/ppermute | solution.py:332
  63.0 3.0 %collective-permute-start.1 = (bf16[2,2,2,128,128]{4,3,2,1,0:T(8,128)(2,1)S(1)}, bf16[2,2,2,128,128]{4,3,2,1,0:T(8,128)(2,1)S(1)}, u32[]{:S(2)}, u32[]{:S(2)}) collective-permute-start(bf16[2,2,2,128,128]{4,3,2,1,0:T(8,128)(2,1)S(1)} %bitcast.26), channel_id=1, source_target_pairs={{0,28},{2,30},{4,0},{6,2},{8,4},{10,6},{12,8},{14,10},{16,12},{18,... | collective-permute-start | bytes 786440 | tf_op jit(solution)/shard_map/ppermute | solution.py:332
  66.0 3.2 %collective-permute-start.2 = (bf16[2,2,2,128,128]{4,3,2,1,0:T(8,128)(2,1)S(1)}, bf16[2,2,2,128,128]{4,3,2,1,0:T(8,128)(2,1)S(1)}, u32[]{:S(2)}, u32[]{:S(2)}) collective-permute-start(bf16[2,2,2,128,128]{4,3,2,1,0:T(8,128)(2,1)S(1)} %bitcast.25), channel_id=1, source_target_pairs={{0,4},{2,6},{4,8},{6,10},{8,12},{10,14},{12,16},{14,18},{16,20},{1... | collective-permute-start | bytes 786440 | tf_op jit(solution)/shard_map/ppermute | solution.py:332
  74.8 4.5 %collective-permute-done.1.up2.refs_0_ = bf16[2,2,2,128,128]{4,3,2,1,0:T(8,128)(2,1)S(1)} collective-permute-done((bf16[2,2,2,128,128]{4,3,2,1,0:T(8,128)(2,1)S(1)}, bf16[2,2,2,128,128]{4,3,2,1,0:T(8,128)(2,1)S(1)}, u32[]{:S(2)}, u32[]{:S(2)}) %collective-permute-start.1) | collective-permute-done | bytes 262176 | tf_op jit(solution)/shard_map/ppermute | solution.py:332
  79.4 4.9 %shard_map.90 = (f32[2,4,2,128]{3,2,1,0:T(2,128)S(1)}, bf16[4,2,2,128,128]{4,3,2,1,0:T(8,128)(2,1)S(1)}, bf16[4,2,2,128,128]{4,3,2,1,0:T(8,128)(2,1)S(1)}, f32[2,4,64,128]{3,2,1,0:T(8,128)S(1)}) custom-call(s32[90]{0:T(128)S(1)} %copy-done.8, bf16[2,2,2,128,128]{4,3,2,1,0:T(8,128)(2,1)S(1)} %collective-permute-done.1.up2.refs_0_, ...), custom_call_target="tpu_custom_call" | custom-call | flops 3000000000 | bytes 30000000 | tf_op jit(solution)/shard_map/pallas_call | solution.py:365
  84.2 6.3 %collective-permute-start.5 = (bf16[4,2,2,128,128]{4,3,2,1,0:T(8,128)(2,1)S(1)}, bf16[4,2,2,128,128]{4,3,2,1,0:T(8,128)(2,1)S(1)}, u32[]{:S(2)}, u32[]{:S(2)}) collective-permute-start(bf16[4,2,2,128,128]{4,3,2,1,0:T(8,128)(2,1)S(1)} %get-tuple-element.35), channel_id=1, source_target_pairs={{0,2},{2,4},{4,6},{6,8},{8,10},{10,12},{12,14},{14,16},{16,18},{18... | collective-permute-start | bytes 1572872 | tf_op jit(solution)/shard_map/ppermute | solution.py:332
  90.5 5.3 %collective-permute-start.6 = (bf16[4,2,2,128,128]{4,3,2,1,0:T(8,128)(2,1)S(1)}, bf16[4,2,2,128,128]{4,3,2,1,0:T(8,128)(2,1)S(1)}, u32[]{:S(2)}, u32[]{:S(2)}) collective-permute-start(bf16[4,2,2,128,128]{4,3,2,1,0:T(8,128)(2,1)S(1)} %get-tuple-element.36), channel_id=1, source_target_pairs={{0,30},{2,0},{4,2},{6,4},{8,6},{10,8},{12,10},{14,12},{16,14},{18,... | collective-permute-start | bytes 1572872 | tf_op jit(solution)/shard_map/ppermute | solution.py:332
  95.8 2.5 %shard_map.92 = (bf16[2,2,2,128,128]{4,3,2,1,0:T(8,128)(2,1)S(1)}, bf16[2,2,2,128,128]{4,3,2,1,0:T(8,128)(2,1)S(1)}, f32[2,4,64,128]{3,2,1,0:T(8,128)S(1)}) custom-call(s32[90]{0:T(128)S(1)} %copy-done.8, bf16[2,2,2,128,128]{4,3,2,1,0:T(8,128)(2,1)S(1)} %collective-permute-done.1.up2.refs_0_, ...), custom_call_target="tpu_custom_call" | custom-call | flops 2000000000 | bytes 20000000 | tf_op jit(solution)/shard_map/pallas_call | solution.py:319
  98.3 2.3 %collective-permute-start.7 = (bf16[2,2,2,128,128]{4,3,2,1,0:T(8,128)(2,1)S(1)}, bf16[2,2,2,128,128]{4,3,2,1,0:T(8,128)(2,1)S(1)}, u32[]{:S(2)}, u32[]{:S(2)}) collective-permute-start(bf16[2,2,2,128,128]{4,3,2,1,0:T(8,128)(2,1)S(1)} %get-tuple-element.37), channel_id=1, source_target_pairs={{0,4},{2,6},{4,8},{6,10},{8,12},{10,14},{12,16},{14,18},{16,20},{1... | collective-permute-start | bytes 786440 | tf_op jit(solution)/shard_map/ppermute | solution.py:332
  100.7 5.1 %collective-permute-start.8 = (bf16[2,2,2,128,128]{4,3,2,1,0:T(8,128)(2,1)S(1)}, bf16[2,2,2,128,128]{4,3,2,1,0:T(8,128)(2,1)S(1)}, u32[]{:S(2)}, u32[]{:S(2)}) collective-permute-start(bf16[2,2,2,128,128]{4,3,2,1,0:T(8,128)(2,1)S(1)} %get-tuple-element.38), channel_id=1, source_target_pairs={{0,28},{2,30},{4,0},{6,2},{8,4},{10,6},{12,8},{14,10},{16,12},{18,... | collective-permute-start | bytes 786440 | tf_op jit(solution)/shard_map/ppermute | solution.py:332
  105.7 2.5 %shard_map.91 = (bf16[4,2,2,128,128]{4,3,2,1,0:T(8,128)(2,1)S(1)}, f32[2,4,64,128]{3,2,1,0:T(8,128)S(1)}) custom-call(s32[90]{0:T(128)S(1)} %copy-done.8, bf16[4,2,2,128,128]{4,3,2,1,0:T(8,128)(2,1)S(1)} %bitcast.14, bf16[4,2,2,4,128,128]{5,4,3,2,1,0:T(8,128)(2,1)S(1)} %bitcast.19, bf16[2,4,128,256]{3,2,1,0:T(8,128)(2,1)S(1)} %get-tuple-element.32.refs_2_.refs_3_.qd, ...), custom_call_target="tpu_custom_call" | custom-call | flops 2000000000 | bytes 20000000 | tf_op jit(solution)/shard_map/pallas_call | solution.py:319
  108.3 4.2 %collective-permute-done.7.r_up2 = bf16[2,2,2,128,128]{4,3,2,1,0:T(8,128)(2,1)S(1)} collective-permute-done((bf16[2,2,2,128,128]{4,3,2,1,0:T(8,128)(2,1)S(1)}, bf16[2,2,2,128,128]{4,3,2,1,0:T(8,128)(2,1)S(1)}, u32[]{:S(2)}, u32[]{:S(2)}) %collective-permute-start.7) | collective-permute-done | bytes 262176 | tf_op jit(solution)/shard_map/ppermute | solution.py:332
  115.5 15.1 %all-to-all-start.1 = ((bf16[4,2,2,128,128]{4,3,2,1,0:T(8,128)(2,1)}), bf16[4,2,2,128,128]{4,3,2,1,0:T(8,128)(2,1)S(1)}, u32[]{:S(2)}, u32[]{:S(2)}) async-start(bf16[4,2,2,128,128]{4,3,2,1,0:T(8,128)(2,1)} %shard_map.93), calls=%async_computation.1 | async-start | bytes 1048576 | tf_op jit(solution)/shard_map/all_to_all | solution.py:390
  132.8 3.1 %collective-permute-done.9.oq_other = bf16[4,64,128]{2,1,0:T(8,128)(2,1)S(1)} collective-permute-done((bf16[4,64,128]{2,1,0:T(8,128)(2,1)S(1)}, bf16[4,64,128]{2,1,0:T(8,128)(2,1)S(1)}, u32[]{:S(2)}, u32[]{:S(2)}) %collective-permute-start.9) | collective-permute-done | bytes 65568 | tf_op jit(solution)/shard_map/ppermute | solution.py:381
  136.1 5.4 %collective-permute-start.10 = (bf16[4,64,128]{2,1,0:T(8,128)(2,1)S(1)}, bf16[4,64,128]{2,1,0:T(8,128)(2,1)S(1)}, u32[]{:S(2)}, u32[]{:S(2)}) collective-permute-start(bf16[4,64,128]{2,1,0:T(8,128)(2,1)S(1)} %get-tuple-element.44), channel_id=1, source_target_pairs={{0,1},{1,0},{2,3},{3,2},{4,5},{5,4},{6,7},{7,6},{8,9},{9,8},{10,11... | collective-permute-start | bytes 196616 | tf_op jit(solution)/shard_map/ppermute | solution.py:385
  143.1 10.8 %all-to-all-done.1.dkv_own = bf16[4,2,2,128,128]{4,3,2,1,0:T(8,128)(2,1)S(1)} async-done(((bf16[4,2,2,128,128]{4,3,2,1,0:T(8,128)(2,1)}), bf16[4,2,2,128,128]{4,3,2,1,0:T(8,128)(2,1)S(1)}, u32[]{:S(2)}, u32[]{:S(2)}) %all-to-all-start.1) | async-done | bytes 524320 | tf_op jit(solution)/shard_map/all_to_all | solution.py:390
  153.9 7.5 %all-gather.2 = bf16[4,128,128]{2,1,0:T(8,128)(2,1)S(1)} all-gather(bf16[2,128,128]{2,1,0:T(8,128)(2,1)S(1)} %slice_reduce_fusion), channel_id=4, replica_groups=mesh['xh'=2,'y'=4,'xl'=2,'z'=16,'c'=2] {'xl'}, dimensions={0}, use_global_device_ids=true | all-gather | bytes 196608 | tf_op jit(solution)/shard_map/all_gather | solution.py:395
  161.9 4.2 %all-gather.3 = bf16[8,128,128]{2,1,0:T(8,128)(2,1)S(1)} all-gather(bf16[4,128,128]{2,1,0:T(8,128)(2,1)S(1)} %shard_map.95), channel_id=5, replica_groups=mesh['xh'=2,'y'=4,'xl'=2,'z'=16,'c'=2] {'c'}, dimensions={0}, use_global_device_ids=true | all-gather | bytes 393216 | tf_op jit(solution)/shard_map/all_gather | solution.py:397
  (46 shorter events, 16.1 us)
Async XLA Ops:
  9.9 59.6 %copy-start.8 = (s32[90]{0:T(128)S(1)}, s32[90]{0:T(128)}, u32[]{:S(2)}) copy-start(s32[90]{0:T(128)} %get-tuple-element.25.lists) | copy-start | bytes 1084
  10.0 11.8 %all-to-all-start = ((bf16[4,4,128,128]{3,2,1,0:T(8,128)(2,1)}), bf16[4,4,128,128]{3,2,1,0:T(8,128)(2,1)S(1)}, u32[]{:S(2)}, u32[]{:S(2)}) async-start(bf16[4,4,128,128]{3,2,1,0:T(8,128)(2,1)} %get-tuple-element.27), calls=%async_computation | async-start | bytes 1048576 | tf_op jit(solution)/shard_map/all_to_all | solution.py:352
  14.8 54.7 %all-gather.6.cloned.1.call-start = ((), (), s32[]{:S(2)}) async-start(), calls=%async_computation.2 | async-start | bytes 2621440 | tf_op jit(solution)/shard_map/all_gather | solution.py:354
  14.8 6.8 %collective-permute-start = (bf16[512,128]{1,0:T(8,128)(2,1)}, bf16[512,128]{1,0:T(8,128)(2,1)S(1)}, u32[]{:S(2)}, u32[]{:S(2)}) collective-permute-start(bf16[512,128]{1,0:T(8,128)(2,1)} %get-tuple-element.28), channel_id=1, source_target_pairs={{0,32},{32,0},{1,33},{33,1},{2,34},{34,2},{3,35},{35,3},{4,36},{36... | collective-permute-start | bytes 393224 | tf_op jit(solution)/shard_map/ppermute | solution.py:351
  21.7 0.8 copy-start.9
  22.6 0.9 copy-start.4
  56.5 16.1 %collective-permute-start.4 = (bf16[4,2,2,128,128]{4,3,2,1,0:T(8,128)(2,1)S(1)}, bf16[4,2,2,128,128]{4,3,2,1,0:T(8,128)(2,1)S(1)}, u32[]{:S(2)}, u32[]{:S(2)}) collective-permute-start(bf16[4,2,2,128,128]{4,3,2,1,0:T(8,128)(2,1)S(1)} %bitcast.11), channel_id=1, source_target_pairs={{0,2},{2,4},{4,6},{6,8},{8,10},{10,12},{12,14},{14,16},{16,18},{18... | collective-permute-start | bytes 1572872 | tf_op jit(solution)/shard_map/ppermute | solution.py:332
  59.4 13.2 %collective-permute-start.3 = (bf16[4,2,2,128,128]{4,3,2,1,0:T(8,128)(2,1)S(1)}, bf16[4,2,2,128,128]{4,3,2,1,0:T(8,128)(2,1)S(1)}, u32[]{:S(2)}, u32[]{:S(2)}) collective-permute-start(bf16[4,2,2,128,128]{4,3,2,1,0:T(8,128)(2,1)S(1)} %bitcast.12), channel_id=1, source_target_pairs={{0,30},{2,0},{4,2},{6,4},{8,6},{10,8},{12,10},{14,12},{16,14},{18,... | collective-permute-start | bytes 1572872 | tf_op jit(solution)/shard_map/ppermute | solution.py:332
  63.0 16.3 %collective-permute-start.1 = (bf16[2,2,2,128,128]{4,3,2,1,0:T(8,128)(2,1)S(1)}, bf16[2,2,2,128,128]{4,3,2,1,0:T(8,128)(2,1)S(1)}, u32[]{:S(2)}, u32[]{:S(2)}) collective-permute-start(bf16[2,2,2,128,128]{4,3,2,1,0:T(8,128)(2,1)S(1)} %bitcast.26), channel_id=1, source_target_pairs={{0,28},{2,30},{4,0},{6,2},{8,4},{10,6},{12,8},{14,10},{16,12},{18,... | collective-permute-start | bytes 786440 | tf_op jit(solution)/shard_map/ppermute | solution.py:332
  66.0 13.3 %collective-permute-start.2 = (bf16[2,2,2,128,128]{4,3,2,1,0:T(8,128)(2,1)S(1)}, bf16[2,2,2,128,128]{4,3,2,1,0:T(8,128)(2,1)S(1)}, u32[]{:S(2)}, u32[]{:S(2)}) collective-permute-start(bf16[2,2,2,128,128]{4,3,2,1,0:T(8,128)(2,1)S(1)} %bitcast.25), channel_id=1, source_target_pairs={{0,4},{2,6},{4,8},{6,10},{8,12},{10,14},{12,16},{14,18},{16,20},{1... | collective-permute-start | bytes 786440 | tf_op jit(solution)/shard_map/ppermute | solution.py:332
  69.5 1.6 copy-start
  84.2 30.3 %collective-permute-start.5 = (bf16[4,2,2,128,128]{4,3,2,1,0:T(8,128)(2,1)S(1)}, bf16[4,2,2,128,128]{4,3,2,1,0:T(8,128)(2,1)S(1)}, u32[]{:S(2)}, u32[]{:S(2)}) collective-permute-start(bf16[4,2,2,128,128]{4,3,2,1,0:T(8,128)(2,1)S(1)} %get-tuple-element.35), channel_id=1, source_target_pairs={{0,2},{2,4},{4,6},{6,8},{8,10},{10,12},{12,14},{14,16},{16,18},{18... | collective-permute-start | bytes 1572872 | tf_op jit(solution)/shard_map/ppermute | solution.py:332
  90.5 24.0 %collective-permute-start.6 = (bf16[4,2,2,128,128]{4,3,2,1,0:T(8,128)(2,1)S(1)}, bf16[4,2,2,128,128]{4,3,2,1,0:T(8,128)(2,1)S(1)}, u32[]{:S(2)}, u32[]{:S(2)}) collective-permute-start(bf16[4,2,2,128,128]{4,3,2,1,0:T(8,128)(2,1)S(1)} %get-tuple-element.36), channel_id=1, source_target_pairs={{0,30},{2,0},{4,2},{6,4},{8,6},{10,8},{12,10},{14,12},{16,14},{18,... | collective-permute-start | bytes 1572872 | tf_op jit(solution)/shard_map/ppermute | solution.py:332
  98.3 14.2 %collective-permute-start.7 = (bf16[2,2,2,128,128]{4,3,2,1,0:T(8,128)(2,1)S(1)}, bf16[2,2,2,128,128]{4,3,2,1,0:T(8,128)(2,1)S(1)}, u32[]{:S(2)}, u32[]{:S(2)}) collective-permute-start(bf16[2,2,2,128,128]{4,3,2,1,0:T(8,128)(2,1)S(1)} %get-tuple-element.37), channel_id=1, source_target_pairs={{0,4},{2,6},{4,8},{6,10},{8,12},{10,14},{12,16},{14,18},{16,20},{1... | collective-permute-start | bytes 786440 | tf_op jit(solution)/shard_map/ppermute | solution.py:332
  100.7 13.8 %collective-permute-start.8 = (bf16[2,2,2,128,128]{4,3,2,1,0:T(8,128)(2,1)S(1)}, bf16[2,2,2,128,128]{4,3,2,1,0:T(8,128)(2,1)S(1)}, u32[]{:S(2)}, u32[]{:S(2)}) collective-permute-start(bf16[2,2,2,128,128]{4,3,2,1,0:T(8,128)(2,1)S(1)} %get-tuple-element.38), channel_id=1, source_target_pairs={{0,28},{2,30},{4,0},{6,2},{8,4},{10,6},{12,8},{14,10},{16,12},{18,... | collective-permute-start | bytes 786440 | tf_op jit(solution)/shard_map/ppermute | solution.py:332
  115.5 20.4 %copy-start.2 = (f32[4,64,128]{2,1,0:T(8,128)S(1)}, f32[4,64,128]{2,1,0:T(8,128)}, u32[]{:S(2)}) copy-start(f32[4,64,128]{2,1,0:T(8,128)} %get-tuple-element.42.gate) | copy-start | bytes 393220
  115.5 20.4 %copy-start.6 = (bf16[64,128]{1,0:T(8,128)(2,1)S(1)}, bf16[64,128]{1,0:T(8,128)(2,1)}, u32[]{:S(2)}) copy-start(bf16[64,128]{1,0:T(8,128)(2,1)} %w_out.1) | copy-start | bytes 49156
  115.5 38.4 %all-to-all-start.1 = ((bf16[4,2,2,128,128]{4,3,2,1,0:T(8,128)(2,1)}), bf16[4,2,2,128,128]{4,3,2,1,0:T(8,128)(2,1)S(1)}, u32[]{:S(2)}, u32[]{:S(2)}) async-start(bf16[4,2,2,128,128]{4,3,2,1,0:T(8,128)(2,1)} %shard_map.93), calls=%async_computation.1 | async-start | bytes 1048576 | tf_op jit(solution)/shard_map/all_to_all | solution.py:390
  130.6 30.8 %copy-start.3 = (bf16[128,256]{1,0:T(8,128)(2,1)S(1)}, bf16[128,256]{1,0:T(8,128)(2,1)}, u32[]{:S(2)}) copy-start(bf16[128,256]{1,0:T(8,128)(2,1)} %w_proj.1) | copy-start | bytes 196612
  130.6 30.8 %copy-start.5 = (f32[4,64,128]{2,1,0:T(8,128)S(1)}, f32[4,64,128]{2,1,0:T(8,128)}, u32[]{:S(2)}) copy-start(f32[4,64,128]{2,1,0:T(8,128)} %get-tuple-element.47.go) | copy-start | bytes 393220
  130.7 35.4 %copy-start.1 = (bf16[4,128,128]{2,1,0:T(8,128)(2,1)S(1)}, bf16[4,128,128]{2,1,0:T(8,128)(2,1)}, u32[]{:S(2)}) copy-start(bf16[4,128,128]{2,1,0:T(8,128)(2,1)} %pair.1) | copy-start | bytes 393220
  130.7 35.4 %copy-start.7 = (f32[128]{0:T(128)S(1)}, f32[128]{0:T(128)}, u32[]{:S(2)}) copy-start(f32[128]{0:T(128)} %param.8) | copy-start | bytes 1540
  130.7 5.1 %collective-permute-start.9 = (bf16[4,64,128]{2,1,0:T(8,128)(2,1)S(1)}, bf16[4,64,128]{2,1,0:T(8,128)(2,1)S(1)}, u32[]{:S(2)}, u32[]{:S(2)}) collective-permute-start(bf16[4,64,128]{2,1,0:T(8,128)(2,1)S(1)} %fusion.2), channel_id=1, source_target_pairs={{0,32},{32,0},{1,33},{33,1},{2,34},{34,2},{3,35},{35,3},{4,36},{36... | collective-permute-start | bytes 196616 | tf_op jit(solution)/shard_map/ppermute | solution.py:381
  136.1 6.3 %collective-permute-start.10 = (bf16[4,64,128]{2,1,0:T(8,128)(2,1)S(1)}, bf16[4,64,128]{2,1,0:T(8,128)(2,1)S(1)}, u32[]{:S(2)}, u32[]{:S(2)}) collective-permute-start(bf16[4,64,128]{2,1,0:T(8,128)(2,1)S(1)} %get-tuple-element.44), channel_id=1, source_target_pairs={{0,1},{1,0},{2,3},{3,2},{4,5},{5,4},{6,7},{7,6},{8,9},{9,8},{10,11... | collective-permute-start | bytes 196616 | tf_op jit(solution)/shard_map/ppermute | solution.py:385
Sparse Core Ops, SparseCore 0:
  22.7 46.7 all-gather.5

commit v10 on v9

--- a/solution.py
+++ b/solution.py
@@ -77,15 +77,26 @@
             lists[base + 8] = n
 
 
+def bias_kernel(here, out, bias, sem):
+    copy = pltpu.make_async_copy(here, bias, sem)
+    copy.start()
+    copy.wait()
+    for j in range(4):
+        for h in range(2):
+            block = bias[h, :, 128 * j : 128 * j + 128].T
+            out[h, j] = block
+            out[2 + h, j] = block
+
+
 def prep_kernel(*refs):
     ids = place()
-    here, (keep, send, gate_out, go_out, bias_out, lists) = refs[:7], refs[7:13]
-    pair, gain, w_proj, w_out, d_out, bias, act = local = refs[13:20]
-    proj_s, sems = refs[20:]
+    here, (keep, send, gate_out, go_out, lists) = refs[:6], refs[7:12]
+    pair, gain, w_proj, w_out, d_out, act = local = refs[12:18]
+    proj_s, sems = refs[18:]
     copies = [pltpu.make_async_copy(s, d, sems.at[k]) for k, (s, d) in enumerate(zip(here, local))]
     for copy in reversed(copies):
         copy.start()
-    copies[6].wait()
+    copies[5].wait()
     make_lists(ids, act, lists)
     for copy in copies[:5]:
         copy.wait()
@@ -108,12 +119,6 @@
         for ref, h in ((keep, xl), (send, 1 - xl)):
             ref[p * 128 : (p + 1) * 128] = proj_s[h, 0:128].T.astype(BF16)
             ref[256 + p * 128 : 384 + p * 128] = proj_s[h, 128:256].astype(BF16)
-    copies[5].wait()
-    for j in range(4):
-        for h in range(2):
-            block = bias[h, :, 128 * j : 128 * j + 128].T
-            bias_out[h, j] = block
-            bias_out[2 + h, j] = block
 
 
 def fill_queries(qd, packs):
@@ -334,20 +339,29 @@
 
 def per_device(pair, gain, w_proj, w_out, tri_bias, active, d_out):
     gain = gain.reshape(1, 128)
-    args = (pair, gain, w_proj, w_out, d_out, tri_bias, active)
-    pack, pack_send, gate, go, bias, lists = pl.pallas_call(
+    whole = pl.BlockSpec(memory_space=pl.ANY)
+    big = pltpu.CompilerParams(vmem_limit_bytes=56 * 1024 * 1024)
+    bias = pl.pallas_call(
+        bias_kernel,
+        out_shape=jax.ShapeDtypeStruct((4, 4, 128, 128), BF16),
+        in_specs=[whole],
+        out_specs=vmem(),
+        scratch_shapes=[pltpu.VMEM(tri_bias.shape, BF16), pltpu.SemaphoreType.DMA(())],
+        compiler_params=big,
+    )(tri_bias)
+    args = (pair, gain, w_proj, w_out, d_out, active)
+    pack, pack_send, gate, go, lists = pl.pallas_call(
         prep_kernel,
         out_shape=shapes(
-            *[((512, 128), BF16)] * 2, *[((4, 64, 128), F32)] * 2, ((4, 4, 128, 128), BF16),
-            ((90,), jnp.int32),
+            *[((512, 128), BF16)] * 2, *[((4, 64, 128), F32)] * 2, ((90,), jnp.int32)
         ),
-        in_specs=[pl.BlockSpec(memory_space=pl.ANY)] * 7,
-        out_specs=[vmem()] * 5 + [smem()],
-        scratch_shapes=[pltpu.VMEM(a.shape, a.dtype) for a in args[:6]]
+        in_specs=[whole] * 7,
+        out_specs=[vmem()] * 4 + [smem()],
+        scratch_shapes=[pltpu.VMEM(a.shape, a.dtype) for a in args[:5]]
         + [pltpu.SMEM(active.shape, active.dtype)]
-        + [pltpu.VMEM((2, 256, 128), F32), pltpu.SemaphoreType.DMA((7,))],
-        compiler_params=pltpu.CompilerParams(vmem_limit_bytes=56 * 1024 * 1024),
-    )(*args)
+        + [pltpu.VMEM((2, 256, 128), F32), pltpu.SemaphoreType.DMA((6,))],
+        compiler_params=big,
+    )(*args, bias)
     pack_other = lax.ppermute(pack_send, "xl", SWAP)
     bias = lax.all_to_all(bias, ("xh", "xl"), 0, 0, tiled=True).reshape(2, 2, 4, 128, 128)
     bias, pack_other = lax.optimization_barrier((bias, pack_other))

time: 174 us -> 170 us (0.977)
  starting transfers between devices: 62.4 us -> 52.2 us
  Pallas kernels: 19.2 us -> 23.9 us
    all_to_all x1, starting transfers between devices: 15.1 us -> 3.6 us  [per_device(): dkv = lax.all_to_all(sums, 'z', 0, 0, axis_index_groups=groups, tiled=True)]
    ppermute x8, waiting for transfers between devices: 10.7 us -> 16.4 us  [to_z(): return lax.ppermute(x, 'z', [(j, (j + step) % 16) for j in range(16)])]
    ppermute x8, starting transfers between devices: 31.6 us -> 26.7 us  [to_z(): return lax.ppermute(x, 'z', [(j, (j + step) % 16) for j in range(16)])]
    all_gather x1, blocking collectives: 4.22 us -> 7.94 us  [per_device(): lax.all_gather(part, 'c')]
    ppermute x1, starting transfers between devices: 2.05 us -> 5.72 us  [per_device(): oq_other = lax.ppermute(oq[1].astype(BF16), 'xl', SWAP)]
    all_gather x1, blocking collectives: 7.5 us -> 4.09 us  [per_device(): lax.all_gather(theirs, 'xl')]
    ppermute x1, starting transfers between devices: 5.43 us -> 7.9 us  [per_device(): out_other = lax.ppermute(out_send, 'c', SWAP)]
    all_to_all x1, waiting for transfers between devices: 10.8 us -> 8.42 us  [per_device(): dkv = lax.all_to_all(sums, 'z', 0, 0, axis_index_groups=groups, tiled=True)]
  transfers between devices with their start and end apart: 14 -> 14, of which waited for: 9 -> 8; matrix products, arithmetic and copies ran while one was open for 0% -> 0% of each run, Pallas kernels for 5% -> 8%
where the time goes in v10:
time: 170 us; the launch traced here: 169 us
  starting transfers between devices  52.2 us (31%)
  blocking collectives  43.3 us (25%)
  waiting for transfers between devices  30.9 us (18%)
  Pallas kernels  23.9 us (14%)
  between operations  14.3 us (8%)
  local copies, waits for them, and re-layouts  3.37 us (2%)
    all_gather x1, blocking collectives, per_device(): own = lax.all_gather(kv, 'z', axis_index_groups=groups)  31.3 us
    ppermute x8, starting transfers between devices, to_z(): return lax.ppermute(x, 'z', [(j, (j + step) % 16) for j in range(16)])  26.7 us
    ppermute x8, waiting for transfers between devices, to_z(): return lax.ppermute(x, 'z', [(j, (j + step) % 16) for j in range(16)])  16.4 us
    all_to_all x1, waiting for transfers between devices, per_device(): dkv = lax.all_to_all(sums, 'z', 0, 0, axis_index_groups=groups, tiled=True)  8.42 us
    all_gather x1, blocking collectives, per_device(): lax.all_gather(part, 'c')  7.94 us
    ppermute x1, starting transfers between devices, per_device(): out_other = lax.ppermute(out_send, 'c', SWAP)  7.9 us
    pallas_call x1, Pallas kernels, per_device(): call(mid_kernel, [((2, 4, 2, 128), F32), (up.shape, BF16), (down.shape, B...  6.3 us
    pallas_call x2, Pallas kernels, back_call(): call(functools.partial(back_kernel, names), [(kv.shape, BF16) for kv in k...  6.24 us
  transfers between devices with their start and end apart: 14, of which 8 were waited for; matrix products, arithmetic and copies ran while one was open for 0% of the time, Pallas kernels for 8%

profile of v10, /device:TPU:1, one launch (start us, length us, event | category | flops | bytes accessed | tf_op | source)
XLA Modules:
  0.0 168.7 jit_solution(6620195768124690591)
XLA Ops:
  9.0 4.9 %all-to-all-start = ((bf16[4,4,128,128]{3,2,1,0:T(8,128)(2,1)}), bf16[4,4,128,128]{3,2,1,0:T(8,128)(2,1)S(1)}, u32[]{:S(2)}, u32[]{:S(2)}) async-start(bf16[4,4,128,128]{3,2,1,0:T(8,128)(2,1)} %shard_map.86.refs_6_), calls=%async_computation | async-start | bytes 1048576 | tf_op jit(solution)/shard_map/all_to_all | solution.py:366
  13.9 2.4 %shard_map.87 = (bf16[512,128]{1,0:T(8,128)(2,1)}, bf16[512,128]{1,0:T(8,128)(2,1)}, f32[4,64,128]{2,1,0:T(8,128)}, f32[4,64,128]{2,1,0:T(8,128)}, s32[90]{0:T(128)}) custom-call(bf16[4,128,128]{2,1,0:T(8,128)(2,1)} %pair.1, f32[1,128]{1,0:T(1,128)} %bitcast.22, bf16[128,256]{1,0:T(8,128)(2,1)} %w_proj.1, bf16[64,128]{1,0:T(8,128)(2,1)} %w_out.1, ...), custom_call_target="tpu_custom_call" | custom-call | tf_op jit(solution)/shard_map/pallas_call | solution.py:353
  16.4 3.4 %collective-permute-start = (bf16[512,128]{1,0:T(8,128)(2,1)}, bf16[512,128]{1,0:T(8,128)(2,1)S(1)}, u32[]{:S(2)}, u32[]{:S(2)}) collective-permute-start(bf16[512,128]{1,0:T(8,128)(2,1)} %get-tuple-element.26), channel_id=1, source_target_pairs={{0,32},{32,0},{1,33},{33,1},{2,34},{34,2},{3,35},{35,3},{4,36},{36... | collective-permute-start | bytes 393224 | tf_op jit(solution)/shard_map/ppermute | solution.py:365
  19.7 3.6 %collective-permute-done.pack1 = bf16[512,128]{1,0:T(8,128)(2,1)S(1)} collective-permute-done((bf16[512,128]{1,0:T(8,128)(2,1)}, bf16[512,128]{1,0:T(8,128)(2,1)S(1)}, u32[]{:S(2)}, u32[]{:S(2)}) %collective-permute-start) | collective-permute-done | bytes 131104 | tf_op jit(solution)/shard_map/ppermute | solution.py:365
  25.2 31.3 %all-gather = bf16[8,2,128,128]{3,2,1,0:T(8,128)(2,1)S(1)} all-gather(bf16[2,2,128,128]{3,2,1,0:T(8,128)(2,1)S(1)} %get-tuple-element.28), channel_id=2, replica_groups={{0,8,16,24},{2,10,18,26},{4,12,20,28},{6,14,22,30},{1,9,17,25},{3,11,19..., dimensions={0}, use_global_device_ids=true | all-gather | bytes 655360 | tf_op jit(solution)/shard_map/all_gather | solution.py:373
  58.3 4.6 %collective-permute-start.3 = (bf16[4,2,2,128,128]{4,3,2,1,0:T(8,128)(2,1)S(1)}, bf16[4,2,2,128,128]{4,3,2,1,0:T(8,128)(2,1)S(1)}, u32[]{:S(2)}, u32[]{:S(2)}) collective-permute-start(bf16[4,2,2,128,128]{4,3,2,1,0:T(8,128)(2,1)S(1)} %bitcast.12), channel_id=1, source_target_pairs={{0,30},{2,0},{4,2},{6,4},{8,6},{10,8},{12,10},{14,12},{16,14},{18,... | collective-permute-start | bytes 1572872 | tf_op jit(solution)/shard_map/ppermute | solution.py:337
  63.0 1.9 %collective-permute-start.1 = (bf16[2,2,2,128,128]{4,3,2,1,0:T(8,128)(2,1)S(1)}, bf16[2,2,2,128,128]{4,3,2,1,0:T(8,128)(2,1)S(1)}, u32[]{:S(2)}, u32[]{:S(2)}) collective-permute-start(bf16[2,2,2,128,128]{4,3,2,1,0:T(8,128)(2,1)S(1)} %bitcast.26), channel_id=1, source_target_pairs={{0,28},{2,30},{4,0},{6,2},{8,4},{10,6},{12,8},{14,10},{16,12},{18,... | collective-permute-start | bytes 786440 | tf_op jit(solution)/shard_map/ppermute | solution.py:337
  64.9 4.3 %collective-permute-start.2 = (bf16[2,2,2,128,128]{4,3,2,1,0:T(8,128)(2,1)S(1)}, bf16[2,2,2,128,128]{4,3,2,1,0:T(8,128)(2,1)S(1)}, u32[]{:S(2)}, u32[]{:S(2)}) collective-permute-start(bf16[2,2,2,128,128]{4,3,2,1,0:T(8,128)(2,1)S(1)} %bitcast.25), channel_id=1, source_target_pairs={{0,4},{2,6},{4,8},{6,10},{8,12},{10,14},{12,16},{14,18},{16,20},{1... | collective-permute-start | bytes 786440 | tf_op jit(solution)/shard_map/ppermute | solution.py:337
  72.3 2.7 %shard_map.90.before = f32[3,2,4,8,128]{4,3,2,1,0:T(8,128)S(1)} custom-call(s32[90]{0:T(128)S(1)} %copy-done.8, bf16[4,2,2,128,128]{4,3,2,1,0:T(8,128)(2,1)S(1)} %collective-permute-done.3.refs_0_.up, bf16[4,2,2,128,128]{4,3,2,1,0:T(8,128)(2,1)S(1)} %collective-permute-done.4.refs_1_.down, bf16[4,2,2,4,128,128]{5,4,3,2,1,0:T(8,128)(2,1)S(1)} %bitcast.16, ...), custom_call_target="tpu_custom_call" | custom-call | flops 1000000000 | bytes 10000000 | tf_op jit(solution)/shard_map/pallas_call | solution.py:312
  75.0 5.2 %collective-permute-done.1.up2.refs_0_ = bf16[2,2,2,128,128]{4,3,2,1,0:T(8,128)(2,1)S(1)} collective-permute-done((bf16[2,2,2,128,128]{4,3,2,1,0:T(8,128)(2,1)S(1)}, bf16[2,2,2,128,128]{4,3,2,1,0:T(8,128)(2,1)S(1)}, u32[]{:S(2)}, u32[]{:S(2)}) %collective-permute-start.1) | collective-permute-done | bytes 262176 | tf_op jit(solution)/shard_map/ppermute | solution.py:337
  80.1 2.6 %collective-permute-done.2.down2.refs_1_ = bf16[2,2,2,128,128]{4,3,2,1,0:T(8,128)(2,1)S(1)} collective-permute-done((bf16[2,2,2,128,128]{4,3,2,1,0:T(8,128)(2,1)S(1)}, bf16[2,2,2,128,128]{4,3,2,1,0:T(8,128)(2,1)S(1)}, u32[]{:S(2)}, u32[]{:S(2)}) %collective-permute-start.2) | collective-permute-done | bytes 262176 | tf_op jit(solution)/shard_map/ppermute | solution.py:337
  82.7 6.3 %shard_map.91 = (f32[2,4,2,128]{3,2,1,0:T(2,128)S(1)}, bf16[4,2,2,128,128]{4,3,2,1,0:T(8,128)(2,1)S(1)}, bf16[4,2,2,128,128]{4,3,2,1,0:T(8,128)(2,1)S(1)}, f32[2,4,64,128]{3,2,1,0:T(8,128)S(1)}) custom-call(s32[90]{0:T(128)S(1)} %copy-done.8, bf16[2,2,2,128,128]{4,3,2,1,0:T(8,128)(2,1)S(1)} %collective-permute-done.1.up2.refs_0_, ...), custom_call_target="tpu_custom_call" | custom-call | flops 3000000000 | bytes 30000000 | tf_op jit(solution)/shard_map/pallas_call | solution.py:379
  90.9 4.8 %collective-permute-start.6 = (bf16[4,2,2,128,128]{4,3,2,1,0:T(8,128)(2,1)S(1)}, bf16[4,2,2,128,128]{4,3,2,1,0:T(8,128)(2,1)S(1)}, u32[]{:S(2)}, u32[]{:S(2)}) collective-permute-start(bf16[4,2,2,128,128]{4,3,2,1,0:T(8,128)(2,1)S(1)} %get-tuple-element.34), channel_id=1, source_target_pairs={{0,30},{2,0},{4,2},{6,4},{8,6},{10,8},{12,10},{14,12},{16,14},{18,... | collective-permute-start | bytes 1572872 | tf_op jit(solution)/shard_map/ppermute | solution.py:337
  95.7 3.7 %shard_map.93 = (bf16[2,2,2,128,128]{4,3,2,1,0:T(8,128)(2,1)S(1)}, bf16[2,2,2,128,128]{4,3,2,1,0:T(8,128)(2,1)S(1)}, f32[2,4,64,128]{3,2,1,0:T(8,128)S(1)}) custom-call(s32[90]{0:T(128)S(1)} %copy-done.8, bf16[2,2,2,128,128]{4,3,2,1,0:T(8,128)(2,1)S(1)} %collective-permute-done.1.up2.refs_0_, ...), custom_call_target="tpu_custom_call" | custom-call | flops 2000000000 | bytes 20000000 | tf_op jit(solution)/shard_map/pallas_call | solution.py:324
  101.4 5.5 %collective-permute-start.8 = (bf16[2,2,2,128,128]{4,3,2,1,0:T(8,128)(2,1)S(1)}, bf16[2,2,2,128,128]{4,3,2,1,0:T(8,128)(2,1)S(1)}, u32[]{:S(2)}, u32[]{:S(2)}) collective-permute-start(bf16[2,2,2,128,128]{4,3,2,1,0:T(8,128)(2,1)S(1)} %get-tuple-element.36), channel_id=1, source_target_pairs={{0,28},{2,30},{4,0},{6,2},{8,4},{10,6},{12,8},{14,10},{16,12},{18,... | collective-permute-start | bytes 786440 | tf_op jit(solution)/shard_map/ppermute | solution.py:337
  106.9 2.5 %shard_map.92 = (bf16[4,2,2,128,128]{4,3,2,1,0:T(8,128)(2,1)S(1)}, f32[2,4,64,128]{3,2,1,0:T(8,128)S(1)}) custom-call(s32[90]{0:T(128)S(1)} %copy-done.8, bf16[4,2,2,128,128]{4,3,2,1,0:T(8,128)(2,1)S(1)} %bitcast.14, bf16[4,2,2,4,128,128]{5,4,3,2,1,0:T(8,128)(2,1)S(1)} %bitcast.19, bf16[2,4,128,256]{3,2,1,0:T(8,128)(2,1)S(1)} %get-tuple-element.30.refs_2_.refs_3_.qd, ...), custom_call_target="tpu_custom_call" | custom-call | flops 2000000000 | bytes 20000000 | tf_op jit(solution)/shard_map/pallas_call | solution.py:324
  109.4 3.2 %collective-permute-done.7.r_up2 = bf16[2,2,2,128,128]{4,3,2,1,0:T(8,128)(2,1)S(1)} collective-permute-done((bf16[2,2,2,128,128]{4,3,2,1,0:T(8,128)(2,1)S(1)}, bf16[2,2,2,128,128]{4,3,2,1,0:T(8,128)(2,1)S(1)}, u32[]{:S(2)}, u32[]{:S(2)}) %collective-permute-start.7) | collective-permute-done | bytes 262176 | tf_op jit(solution)/shard_map/ppermute | solution.py:337
  112.6 5.4 %collective-permute-done.8.r_down2 = bf16[2,2,2,128,128]{4,3,2,1,0:T(8,128)(2,1)S(1)} collective-permute-done((bf16[2,2,2,128,128]{4,3,2,1,0:T(8,128)(2,1)S(1)}, bf16[2,2,2,128,128]{4,3,2,1,0:T(8,128)(2,1)S(1)}, u32[]{:S(2)}, u32[]{:S(2)}) %collective-permute-start.8) | collective-permute-done | bytes 262176 | tf_op jit(solution)/shard_map/ppermute | solution.py:337
  119.0 3.6 %all-to-all-start.1 = ((bf16[4,2,2,128,128]{4,3,2,1,0:T(8,128)(2,1)}), bf16[4,2,2,128,128]{4,3,2,1,0:T(8,128)(2,1)S(1)}, u32[]{:S(2)}, u32[]{:S(2)}) async-start(bf16[4,2,2,128,128]{4,3,2,1,0:T(8,128)(2,1)} %shard_map.94), calls=%async_computation.1 | async-start | bytes 1048576 | tf_op jit(solution)/shard_map/all_to_all | solution.py:404
  122.8 5.7 %collective-permute-start.9 = (bf16[4,64,128]{2,1,0:T(8,128)(2,1)S(1)}, bf16[4,64,128]{2,1,0:T(8,128)(2,1)S(1)}, u32[]{:S(2)}, u32[]{:S(2)}) collective-permute-start(bf16[4,64,128]{2,1,0:T(8,128)(2,1)S(1)} %fusion.2), channel_id=1, source_target_pairs={{0,32},{32,0},{1,33},{33,1},{2,34},{34,2},{3,35},{35,3},{4,36},{36... | collective-permute-start | bytes 196616 | tf_op jit(solution)/shard_map/ppermute | solution.py:395
  130.4 7.9 %collective-permute-start.10 = (bf16[4,64,128]{2,1,0:T(8,128)(2,1)S(1)}, bf16[4,64,128]{2,1,0:T(8,128)(2,1)S(1)}, u32[]{:S(2)}, u32[]{:S(2)}) collective-permute-start(bf16[4,64,128]{2,1,0:T(8,128)(2,1)S(1)} %get-tuple-element.42), channel_id=1, source_target_pairs={{0,1},{1,0},{2,3},{3,2},{4,5},{5,4},{6,7},{7,6},{8,9},{9,8},{10,11... | collective-permute-start | bytes 196616 | tf_op jit(solution)/shard_map/ppermute | solution.py:399
  139.8 8.4 %all-to-all-done.1.dkv_own = bf16[4,2,2,128,128]{4,3,2,1,0:T(8,128)(2,1)S(1)} async-done(((bf16[4,2,2,128,128]{4,3,2,1,0:T(8,128)(2,1)}), bf16[4,2,2,128,128]{4,3,2,1,0:T(8,128)(2,1)S(1)}, u32[]{:S(2)}, u32[]{:S(2)}) %all-to-all-start.1) | async-done | bytes 524320 | tf_op jit(solution)/shard_map/all_to_all | solution.py:404
  148.3 4.1 %all-gather.2 = bf16[4,128,128]{2,1,0:T(8,128)(2,1)S(1)} all-gather(bf16[2,128,128]{2,1,0:T(8,128)(2,1)S(1)} %slice_reduce_fusion), channel_id=4, replica_groups=mesh['xh'=2,'y'=4,'xl'=2,'z'=16,'c'=2] {'xl'}, dimensions={0}, use_global_device_ids=true | all-gather | bytes 196608 | tf_op jit(solution)/shard_map/all_gather | solution.py:409
  152.8 7.9 %all-gather.3 = bf16[8,128,128]{2,1,0:T(8,128)(2,1)S(1)} all-gather(bf16[4,128,128]{2,1,0:T(8,128)(2,1)S(1)} %shard_map.96), channel_id=5, replica_groups=mesh['xh'=2,'y'=4,'xl'=2,'z'=16,'c'=2] {'c'}, dimensions={0}, use_global_device_ids=true | all-gather | bytes 393216 | tf_op jit(solution)/shard_map/all_gather | solution.py:411
  (47 shorter events, 18.7 us)
Async XLA Ops:
  9.0 14.3 %all-to-all-start = ((bf16[4,4,128,128]{3,2,1,0:T(8,128)(2,1)}), bf16[4,4,128,128]{3,2,1,0:T(8,128)(2,1)S(1)}, u32[]{:S(2)}, u32[]{:S(2)}) async-start(bf16[4,4,128,128]{3,2,1,0:T(8,128)(2,1)} %shard_map.86.refs_6_), calls=%async_computation | async-start | bytes 1048576 | tf_op jit(solution)/shard_map/all_to_all | solution.py:366
  13.9 55.3 %all-gather.6.cloned.1.call-start = ((), (), s32[]{:S(2)}) async-start(), calls=%async_computation.2 | async-start | bytes 2621440 | tf_op jit(solution)/shard_map/all_gather | solution.py:368
  16.4 52.8 %copy-start.8 = (s32[90]{0:T(128)S(1)}, s32[90]{0:T(128)}, u32[]{:S(2)}) copy-start(s32[90]{0:T(128)} %get-tuple-element.24.lists) | copy-start | bytes 1084
  16.4 7.0 %collective-permute-start = (bf16[512,128]{1,0:T(8,128)(2,1)}, bf16[512,128]{1,0:T(8,128)(2,1)S(1)}, u32[]{:S(2)}, u32[]{:S(2)}) collective-permute-start(bf16[512,128]{1,0:T(8,128)(2,1)} %get-tuple-element.26), channel_id=1, source_target_pairs={{0,32},{32,0},{1,33},{33,1},{2,34},{34,2},{3,35},{35,3},{4,36},{36... | collective-permute-start | bytes 393224 | tf_op jit(solution)/shard_map/ppermute | solution.py:365
  23.4 0.8 copy-start.9
  24.2 0.9 copy-start.4
  56.4 15.9 %collective-permute-start.4 = (bf16[4,2,2,128,128]{4,3,2,1,0:T(8,128)(2,1)S(1)}, bf16[4,2,2,128,128]{4,3,2,1,0:T(8,128)(2,1)S(1)}, u32[]{:S(2)}, u32[]{:S(2)}) collective-permute-start(bf16[4,2,2,128,128]{4,3,2,1,0:T(8,128)(2,1)S(1)} %bitcast.11), channel_id=1, source_target_pairs={{0,2},{2,4},{4,6},{6,8},{8,10},{10,12},{12,14},{14,16},{16,18},{18... | collective-permute-start | bytes 1572872 | tf_op jit(solution)/shard_map/ppermute | solution.py:337
  58.3 14.0 %collective-permute-start.3 = (bf16[4,2,2,128,128]{4,3,2,1,0:T(8,128)(2,1)S(1)}, bf16[4,2,2,128,128]{4,3,2,1,0:T(8,128)(2,1)S(1)}, u32[]{:S(2)}, u32[]{:S(2)}) collective-permute-start(bf16[4,2,2,128,128]{4,3,2,1,0:T(8,128)(2,1)S(1)} %bitcast.12), channel_id=1, source_target_pairs={{0,30},{2,0},{4,2},{6,4},{8,6},{10,8},{12,10},{14,12},{16,14},{18,... | collective-permute-start | bytes 1572872 | tf_op jit(solution)/shard_map/ppermute | solution.py:337
  63.0 17.2 %collective-permute-start.1 = (bf16[2,2,2,128,128]{4,3,2,1,0:T(8,128)(2,1)S(1)}, bf16[2,2,2,128,128]{4,3,2,1,0:T(8,128)(2,1)S(1)}, u32[]{:S(2)}, u32[]{:S(2)}) collective-permute-start(bf16[2,2,2,128,128]{4,3,2,1,0:T(8,128)(2,1)S(1)} %bitcast.26), channel_id=1, source_target_pairs={{0,28},{2,30},{4,0},{6,2},{8,4},{10,6},{12,8},{14,10},{16,12},{18,... | collective-permute-start | bytes 786440 | tf_op jit(solution)/shard_map/ppermute | solution.py:337
  64.9 17.8 %collective-permute-start.2 = (bf16[2,2,2,128,128]{4,3,2,1,0:T(8,128)(2,1)S(1)}, bf16[2,2,2,128,128]{4,3,2,1,0:T(8,128)(2,1)S(1)}, u32[]{:S(2)}, u32[]{:S(2)}) collective-permute-start(bf16[2,2,2,128,128]{4,3,2,1,0:T(8,128)(2,1)S(1)} %bitcast.25), channel_id=1, source_target_pairs={{0,4},{2,6},{4,8},{6,10},{8,12},{10,14},{12,16},{14,18},{16,20},{1... | collective-permute-start | bytes 786440 | tf_op jit(solution)/shard_map/ppermute | solution.py:337
  69.2 1.6 copy-start
  89.0 29.0 %collective-permute-start.5 = (bf16[4,2,2,128,128]{4,3,2,1,0:T(8,128)(2,1)S(1)}, bf16[4,2,2,128,128]{4,3,2,1,0:T(8,128)(2,1)S(1)}, u32[]{:S(2)}, u32[]{:S(2)}) collective-permute-start(bf16[4,2,2,128,128]{4,3,2,1,0:T(8,128)(2,1)S(1)} %get-tuple-element.33), channel_id=1, source_target_pairs={{0,2},{2,4},{4,6},{6,8},{8,10},{10,12},{12,14},{14,16},{16,18},{18... | collective-permute-start | bytes 1572872 | tf_op jit(solution)/shard_map/ppermute | solution.py:337
  90.9 27.0 %collective-permute-start.6 = (bf16[4,2,2,128,128]{4,3,2,1,0:T(8,128)(2,1)S(1)}, bf16[4,2,2,128,128]{4,3,2,1,0:T(8,128)(2,1)S(1)}, u32[]{:S(2)}, u32[]{:S(2)}) collective-permute-start(bf16[4,2,2,128,128]{4,3,2,1,0:T(8,128)(2,1)S(1)} %get-tuple-element.34), channel_id=1, source_target_pairs={{0,30},{2,0},{4,2},{6,4},{8,6},{10,8},{12,10},{14,12},{16,14},{18,... | collective-permute-start | bytes 1572872 | tf_op jit(solution)/shard_map/ppermute | solution.py:337
  99.4 13.2 %collective-permute-start.7 = (bf16[2,2,2,128,128]{4,3,2,1,0:T(8,128)(2,1)S(1)}, bf16[2,2,2,128,128]{4,3,2,1,0:T(8,128)(2,1)S(1)}, u32[]{:S(2)}, u32[]{:S(2)}) collective-permute-start(bf16[2,2,2,128,128]{4,3,2,1,0:T(8,128)(2,1)S(1)} %get-tuple-element.35), channel_id=1, source_target_pairs={{0,4},{2,6},{4,8},{6,10},{8,12},{10,14},{12,16},{14,18},{16,20},{1... | collective-permute-start | bytes 786440 | tf_op jit(solution)/shard_map/ppermute | solution.py:337
  101.4 16.6 %collective-permute-start.8 = (bf16[2,2,2,128,128]{4,3,2,1,0:T(8,128)(2,1)S(1)}, bf16[2,2,2,128,128]{4,3,2,1,0:T(8,128)(2,1)S(1)}, u32[]{:S(2)}, u32[]{:S(2)}) collective-permute-start(bf16[2,2,2,128,128]{4,3,2,1,0:T(8,128)(2,1)S(1)} %get-tuple-element.36), channel_id=1, source_target_pairs={{0,28},{2,30},{4,0},{6,2},{8,4},{10,6},{12,8},{14,10},{16,12},{18,... | collective-permute-start | bytes 786440 | tf_op jit(solution)/shard_map/ppermute | solution.py:337
  119.0 11.1 %copy-start.2 = (f32[4,64,128]{2,1,0:T(8,128)S(1)}, f32[4,64,128]{2,1,0:T(8,128)}, u32[]{:S(2)}) copy-start(f32[4,64,128]{2,1,0:T(8,128)} %get-tuple-element.40.gate) | copy-start | bytes 393220
  119.0 11.1 %copy-start.6 = (bf16[64,128]{1,0:T(8,128)(2,1)S(1)}, bf16[64,128]{1,0:T(8,128)(2,1)}, u32[]{:S(2)}) copy-start(bf16[64,128]{1,0:T(8,128)(2,1)} %w_out.1) | copy-start | bytes 49156
  119.0 29.2 %all-to-all-start.1 = ((bf16[4,2,2,128,128]{4,3,2,1,0:T(8,128)(2,1)}), bf16[4,2,2,128,128]{4,3,2,1,0:T(8,128)(2,1)S(1)}, u32[]{:S(2)}, u32[]{:S(2)}) async-start(bf16[4,2,2,128,128]{4,3,2,1,0:T(8,128)(2,1)} %shard_map.94), calls=%async_computation.1 | async-start | bytes 1048576 | tf_op jit(solution)/shard_map/all_to_all | solution.py:404
  122.6 29.7 %copy-start.3 = (bf16[128,256]{1,0:T(8,128)(2,1)S(1)}, bf16[128,256]{1,0:T(8,128)(2,1)}, u32[]{:S(2)}) copy-start(bf16[128,256]{1,0:T(8,128)(2,1)} %w_proj.1) | copy-start | bytes 196612
  122.7 29.7 %copy-start.5 = (f32[4,64,128]{2,1,0:T(8,128)S(1)}, f32[4,64,128]{2,1,0:T(8,128)}, u32[]{:S(2)}) copy-start(f32[4,64,128]{2,1,0:T(8,128)} %get-tuple-element.45.go) | copy-start | bytes 393220
  122.8 38.0 %copy-start.1 = (bf16[4,128,128]{2,1,0:T(8,128)(2,1)S(1)}, bf16[4,128,128]{2,1,0:T(8,128)(2,1)}, u32[]{:S(2)}) copy-start(bf16[4,128,128]{2,1,0:T(8,128)(2,1)} %pair.1) | copy-start | bytes 393220
  122.8 38.0 %copy-start.7 = (f32[128]{0:T(128)S(1)}, f32[128]{0:T(128)}, u32[]{:S(2)}) copy-start(f32[128]{0:T(128)} %param.8) | copy-start | bytes 1540
  122.8 7.4 %collective-permute-start.9 = (bf16[4,64,128]{2,1,0:T(8,128)(2,1)S(1)}, bf16[4,64,128]{2,1,0:T(8,128)(2,1)S(1)}, u32[]{:S(2)}, u32[]{:S(2)}) collective-permute-start(bf16[4,64,128]{2,1,0:T(8,128)(2,1)S(1)} %fusion.2), channel_id=1, source_target_pairs={{0,32},{32,0},{1,33},{33,1},{2,34},{34,2},{3,35},{35,3},{4,36},{36... | collective-permute-start | bytes 196616 | tf_op jit(solution)/shard_map/ppermute | solution.py:395
  130.4 8.8 %collective-permute-start.10 = (bf16[4,64,128]{2,1,0:T(8,128)(2,1)S(1)}, bf16[4,64,128]{2,1,0:T(8,128)(2,1)S(1)}, u32[]{:S(2)}, u32[]{:S(2)}) collective-permute-start(bf16[4,64,128]{2,1,0:T(8,128)(2,1)S(1)} %get-tuple-element.42), channel_id=1, source_target_pairs={{0,1},{1,0},{2,3},{3,2},{4,5},{5,4},{6,7},{7,6},{8,9},{9,8},{10,11... | collective-permute-start | bytes 196616 | tf_op jit(solution)/shard_map/ppermute | solution.py:399
Sparse Core Ops, SparseCore 0:
  24.3 44.2 all-gather.5
